TPU v7x, 32 devices: a whole 2x2x4 slice. The times are simulated.
32 devices in a mesh: dp: 8 (over z, y), fsdp: 4 (over x, core).
Axes of the slice: x: 2, y: 2, z: 4, core: 2. Of those that a mesh axis runs over, the one named last changes fastest.
Arguments:
- tokens: bfloat16 [8192, 1024], P(('dp', 'fsdp')), may hold values from -6 to 6
- cotangent: bfloat16 [8192, 1024], P(('dp', 'fsdp')), may hold values from -6 to 6
- seq_lengths: int32 [32, 4], P(('dp', 'fsdp')), may hold values from 0 to 256, as said below
- att_master: float32 [1024, 4096], P(('dp', 'fsdp')), may hold values from -3 to 3
- ffn_master: float32 [2, 1024, 4096], P(None, ('dp', 'fsdp')), may hold values from -1 to 1
- norm_master: float32 [4, 1024], P(None, ('dp', 'fsdp')), may hold values from -2 to 2
- att_moment: float32 [1024, 4096], P(('dp', 'fsdp')), may hold values from -6 to 6
- ffn_moment: float32 [2, 1024, 4096], P(None, ('dp', 'fsdp')), may hold values from -16 to 16
- norm_moment: float32 [4, 1024], P(None, ('dp', 'fsdp')), may hold values from -56 to 56
- att_average: float32 [1024, 4096], P(('dp', 'fsdp')), may hold values from -0.75 to 0.75
- ffn_average: float32 [2, 1024, 4096], P(None, ('dp', 'fsdp')), may hold values from -0.4375 to 0.4375
- norm_average: float32 [4, 1024], P(None, ('dp', 'fsdp')), may hold values from -6 to 6
Outputs:
- layer_output: bfloat16 [8192, 1024], P(('dp', 'fsdp'))
- input_grad: float32 [8192, 1024], P(('dp', 'fsdp'))
- att_grad: float32 [1024, 4096], P(('dp', 'fsdp'))
- att_moment_new: float32 [1024, 4096], P(('dp', 'fsdp'))
- att_new: float32 [1024, 4096], P(('dp', 'fsdp'))
- att_average_new: float32 [1024, 4096], P(('dp', 'fsdp'))
- att_copy: bfloat16 [1024, 4096], P(('dp', 'fsdp'))
- ffn_grad: float32 [2, 1024, 4096], P(None, ('dp', 'fsdp'))
- ffn_moment_new: float32 [2, 1024, 4096], P(None, ('dp', 'fsdp'))
- ffn_new: float32 [2, 1024, 4096], P(None, ('dp', 'fsdp'))
- ffn_average_new: float32 [2, 1024, 4096], P(None, ('dp', 'fsdp'))
- ffn_copy: bfloat16 [2, 1024, 4096], P(None, ('dp', 'fsdp'))
- norm_grad: float32 [4, 1024], P(None, ('dp', 'fsdp'))
- norm_moment_new: float32 [4, 1024], P(None, ('dp', 'fsdp'))
- norm_new: float32 [4, 1024], P(None, ('dp', 'fsdp'))
- norm_average_new: float32 [4, 1024], P(None, ('dp', 'fsdp'))
- norm_copy: bfloat16 [4, 1024], P(None, ('dp', 'fsdp'))
Inputs may be any that keep to these rules, and one draw needn't show every extreme that they name: `seq_lengths`: row r holds the lengths of the sequences on device r in its first slots and zeros after them; they sum to at most 256; a row with one sequence has length 256, and some row in every draw is such.
All inputs are finite; a program needn't handle non-finite values.
Results may differ from a plain program's by a relative error of at most 0.018.
Values may be sent and summed in bfloat16 or wider, within the bound.
No kernel may reach another device: no remote copies, remote signals or barrier semaphores. Data moves between devices by JAX's collectives and lax.ppermute only.
A program may use at most 320 MiB of HBM per device.

v0:
```python
import math

import jax
import jax.numpy as jnp
from jax import lax
from jax.sharding import PartitionSpec as P

HEAD_DIM = 64
LAYERS = 2


head_group = 4


def normalize(values_in, gain_row, bias_row):
    centered = values_in - jnp.mean(values_in, axis=-1, keepdims=True)
    spread = jnp.mean(centered * centered, axis=-1, keepdims=True)
    return centered * lax.rsqrt(spread + 1e-05) * gain_row + bias_row


def gelu_tanh(inner_value):
    return jax.nn.gelu(inner_value, approximate=True)


def split_heads(head_block):
    return head_block.reshape(head_block.shape[0], -1, head_group, HEAD_DIM).transpose(1, 0, 2, 3)


def merge_heads(head_block):
    return head_block.transpose(1, 0, 2, 3).reshape(head_block.shape[1], -1)


def softmax_of(query_rows, key_rows, same_seq):
    scores = jnp.einsum(
        "qhd,khd->hqk", query_rows, key_rows, preferred_element_type=jnp.float32
    ) * HEAD_DIM ** (-0.5)
    scores = jnp.where(same_seq[None], scores, -1e30)
    row_peak = jnp.max(scores, axis=-1, keepdims=True)
    weights = jnp.exp(scores - row_peak)
    return weights / jnp.sum(weights, axis=-1, keepdims=True)


def head_parts(qkv_rows):
    model_width = qkv_rows.shape[1] // 3
    return (
        split_heads(qkv_rows[:, :model_width]),
        split_heads(qkv_rows[:, model_width : 2 * model_width]),
        split_heads(qkv_rows[:, 2 * model_width :]),
    )


def attend(qkv_rows, same_seq):

    def one_group(group_item):
        query_rows, key_rows, value_rows = group_item
        softmax_rows = softmax_of(query_rows, key_rows, same_seq)
        return jnp.einsum(
            "hqk,khd->qhd",
            softmax_rows.astype(jnp.bfloat16),
            value_rows,
            preferred_element_type=jnp.float32,
        )

    return merge_heads(lax.map(one_group, head_parts(qkv_rows)))


def attend_back(qkv_rows, grad_mixed, same_seq):
    query_all, key_all, value_all = head_parts(qkv_rows)

    def one_group(group_item):
        query_rows, key_rows, value_rows, grad_rows = group_item
        softmax_rows = softmax_of(query_rows, key_rows, same_seq)
        grad_probs = jnp.einsum(
            "qhd,khd->hqk", grad_rows, value_rows, preferred_element_type=jnp.float32
        )
        grad_value = jnp.einsum(
            "hqk,qhd->khd",
            softmax_rows.astype(jnp.bfloat16),
            grad_rows,
            preferred_element_type=jnp.float32,
        )
        grad_scores = softmax_rows * (
            grad_probs - jnp.sum(softmax_rows * grad_probs, axis=-1, keepdims=True)
        )
        grad_low = grad_scores.astype(jnp.bfloat16)
        grad_query = jnp.einsum(
            "hqk,khd->qhd", grad_low, key_rows, preferred_element_type=jnp.float32
        ) * HEAD_DIM ** (-0.5)
        grad_key = jnp.einsum(
            "hqk,qhd->khd", grad_low, query_rows, preferred_element_type=jnp.float32
        ) * HEAD_DIM ** (-0.5)
        return (grad_query, grad_key, grad_value)

    grad_query, grad_key, grad_value = lax.map(
        one_group, (query_all, key_all, value_all, split_heads(grad_mixed))
    )
    return jnp.concatenate(
        [merge_heads(grad_query), merge_heads(grad_key), merge_heads(grad_value)], axis=1
    ).astype(jnp.bfloat16)


def layer_states(rows_in, weights, same_seq):
    att_full, ffn_full, norm_full = weights
    model_width = att_full.shape[0]
    norm_values = norm_full.astype(jnp.float32)
    rows_low = rows_in.astype(jnp.bfloat16)
    qkv_rows = jnp.dot(
        rows_low, att_full[:, : 3 * model_width], preferred_element_type=jnp.float32
    ).astype(jnp.bfloat16)
    mixed_rows = attend(qkv_rows, same_seq).astype(jnp.bfloat16)
    branch = jnp.dot(mixed_rows, att_full[:, 3 * model_width :], preferred_element_type=jnp.float32)
    first_sum = rows_in + branch
    hidden = normalize(first_sum, norm_values[0], norm_values[1])
    hidden_low = hidden.astype(jnp.bfloat16)
    inner_rows = jnp.dot(hidden_low, ffn_full[0], preferred_element_type=jnp.float32)
    active = gelu_tanh(inner_rows).astype(jnp.bfloat16)
    second = hidden + jnp.einsum(
        "tf,df->td", active, ffn_full[1], preferred_element_type=jnp.float32
    )
    return (rows_low, qkv_rows, mixed_rows, first_sum, hidden_low, inner_rows, active, second)


def layer_out(rows_in, weights, same_seq):
    second = layer_states(rows_in, weights, same_seq)[7]
    norm_values = weights[2].astype(jnp.float32)
    return normalize(second, norm_values[2], norm_values[3])


def layer_back(rows_in, weights, same_seq, grad_out):
    att_full, ffn_full, norm_full = weights
    model_width = att_full.shape[0]
    norm_values = norm_full.astype(jnp.float32)
    rows_low, qkv_rows, mixed_rows, first_sum, hidden_low, inner_rows, active, second = (
        layer_states(rows_in, weights, same_seq)
    )
    second_value, second_back = jax.vjp(normalize, second, norm_values[2], norm_values[3])
    grad_second, grad_gain2, grad_bias2 = second_back(grad_out)
    grad_ffn_out = grad_second.astype(jnp.bfloat16)
    grad_down = jnp.einsum("td,tf->df", grad_ffn_out, active, preferred_element_type=jnp.float32)
    grad_active = jnp.dot(grad_ffn_out, ffn_full[1], preferred_element_type=jnp.float32)
    gelu_value, gelu_back = jax.vjp(gelu_tanh, inner_rows)
    grad_inner = gelu_back(grad_active)[0].astype(jnp.bfloat16)
    grad_up = jnp.einsum("td,tf->df", hidden_low, grad_inner, preferred_element_type=jnp.float32)
    grad_hidden = grad_second + jnp.einsum(
        "tf,df->td", grad_inner, ffn_full[0], preferred_element_type=jnp.float32
    )
    first_value, first_back = jax.vjp(normalize, first_sum, norm_values[0], norm_values[1])
    grad_first, grad_gain1, grad_bias1 = first_back(grad_hidden)
    grad_branch = grad_first.astype(jnp.bfloat16)
    grad_proj = jnp.einsum("td,te->de", mixed_rows, grad_branch, preferred_element_type=jnp.float32)
    grad_mixed = jnp.einsum(
        "te,de->td", grad_branch, att_full[:, 3 * model_width :], preferred_element_type=jnp.float32
    ).astype(jnp.bfloat16)
    grad_qkv = attend_back(qkv_rows, grad_mixed, same_seq)
    grad_inproj = jnp.einsum("td,te->de", rows_low, grad_qkv, preferred_element_type=jnp.float32)
    grad_rows = grad_first + jnp.einsum(
        "te,de->td", grad_qkv, att_full[:, : 3 * model_width], preferred_element_type=jnp.float32
    )
    grad_terms = (
        jnp.concatenate([grad_inproj, grad_proj], axis=1),
        grad_up,
        grad_down,
        jnp.stack([grad_gain1, grad_bias1, grad_gain2, grad_bias2]),
    )
    return (grad_rows, grad_terms)


def fetch_forward(pieces):
    return (
        lax.all_gather(pieces[0], ("dp", "fsdp"), axis=0, tiled=True),
        lax.all_gather(pieces[1], ("dp", "fsdp"), axis=1, tiled=True),
        lax.all_gather(pieces[2], ("dp", "fsdp"), axis=1, tiled=True),
    )


def fetch_backward(pieces):
    return (
        lax.all_gather(pieces[0], ("dp", "fsdp"), axis=0, tiled=True),
        lax.all_gather(pieces[1], ("dp", "fsdp"), axis=1, tiled=True),
        lax.all_gather(pieces[2], ("dp", "fsdp"), axis=1, tiled=True),
    )


def owner_sums(grad_terms):
    att_term, up_term, down_term, norm_term = grad_terms
    att_share, norm_share = (
        lax.psum_scatter(att_term, ("dp", "fsdp"), scatter_dimension=0, tiled=True),
        lax.psum_scatter(norm_term, ("dp", "fsdp"), scatter_dimension=1, tiled=True),
    )
    up_share = lax.psum_scatter(up_term, ("dp", "fsdp"), scatter_dimension=0, tiled=True)
    down_share = lax.psum_scatter(down_term, ("dp", "fsdp"), scatter_dimension=0, tiled=True)
    return (att_share, jnp.stack([up_share, down_share]), norm_share)


def update(gradient, master, moment, average, step_rate):
    moment_new = 0.9 * moment + gradient
    master_new = master - step_rate * (gradient + 0.9 * moment_new)
    average_new = 0.8 * average + 0.2 * master_new
    return (gradient, moment_new, master_new, average_new, master_new.astype(jnp.bfloat16))


def shards(
    tokens,
    cotangent,
    seq_lengths,
    att_master,
    ffn_master,
    norm_master,
    att_moment,
    ffn_moment,
    norm_moment,
    att_average,
    ffn_average,
    norm_average,
):
    row_count = tokens.shape[0]
    seq_ends = jnp.cumsum(seq_lengths[0])
    position = jnp.arange(row_count, dtype=jnp.int32)
    segment = jnp.sum((position[:, None] >= seq_ends[None, :]).astype(jnp.int32), axis=1)
    same_seq = segment[:, None] == segment[None, :]
    live_rows = (position < seq_ends[-1]).astype(jnp.float32)[:, None]
    pieces = (
        att_master.astype(jnp.bfloat16),
        ffn_master.astype(jnp.bfloat16),
        norm_master.astype(jnp.bfloat16),
    )
    stored = []
    current = tokens.astype(jnp.float32)
    for depth in range(LAYERS):
        weights = fetch_forward(pieces)
        stored.append(current)
        current = layer_out(current, weights, same_seq)
    grad_now = cotangent.astype(jnp.float32) * live_rows
    totals = (jnp.zeros_like(att_master), jnp.zeros_like(ffn_master), jnp.zeros_like(norm_master))
    for depth in reversed(range(LAYERS)):
        weights = fetch_backward(pieces)
        grad_now, grad_terms = layer_back(stored[depth], weights, same_seq, grad_now)
        shares = owner_sums(grad_terms)
        totals = jax.tree.map(jnp.add, totals, shares)
    step_rate = 0.1 / math.sqrt(row_count * lax.axis_size(("dp", "fsdp")))
    att_out = update(totals[0], att_master, att_moment, att_average, step_rate)
    ffn_out = update(totals[1], ffn_master, ffn_moment, ffn_average, step_rate)
    norm_out = update(totals[2], norm_master, norm_moment, norm_average, step_rate)
    return (
        current.astype(jnp.bfloat16),
        grad_now,
        att_out[0],
        att_out[1],
        att_out[2],
        att_out[3],
        att_out[4],
        ffn_out[0],
        ffn_out[1],
        ffn_out[2],
        ffn_out[3],
        ffn_out[4],
        norm_out[0],
        norm_out[1],
        norm_out[2],
        norm_out[3],
        norm_out[4],
    )


def solution(mesh):
    return jax.shard_map(
        shards,
        mesh=mesh,
        in_specs=(
            P(("dp", "fsdp"), None),
            P(("dp", "fsdp"), None),
            P(("dp", "fsdp"), None),
            P(("dp", "fsdp"), None),
            P(None, ("dp", "fsdp"), None),
            P(None, ("dp", "fsdp")),
            P(("dp", "fsdp"), None),
            P(None, ("dp", "fsdp"), None),
            P(None, ("dp", "fsdp")),
            P(("dp", "fsdp"), None),
            P(None, ("dp", "fsdp"), None),
            P(None, ("dp", "fsdp")),
        ),
        out_specs=(
            P(("dp", "fsdp"), None),
            P(("dp", "fsdp"), None),
            P(("dp", "fsdp"), None),
            P(("dp", "fsdp"), None),
            P(("dp", "fsdp"), None),
            P(("dp", "fsdp"), None),
            P(("dp", "fsdp"), None),
            P(None, ("dp", "fsdp"), None),
            P(None, ("dp", "fsdp"), None),
            P(None, ("dp", "fsdp"), None),
            P(None, ("dp", "fsdp"), None),
            P(None, ("dp", "fsdp"), None),
            P(None, ("dp", "fsdp")),
            P(None, ("dp", "fsdp")),
            P(None, ("dp", "fsdp")),
            P(None, ("dp", "fsdp")),
            P(None, ("dp", "fsdp")),
        ),
        check_vma=False,
    )
```

profile of v0, /device:TPU:0, one launch (start us, length us, event | category | flops | bytes accessed | tf_op | source)
XLA Modules:
  0.0 1418.5 jit_solution(2991864227352109479)
XLA Ops:
  12.7 43.5 %all-gather = bf16[32,32,4]{1,2,0:T(4,128)(2,1)S(1)} all-gather(bf16[1,32,4]{1,2,0:T(4,128)(2,1)S(1)} %convert_bitcast_fusion), channel_id=1, replica_groups=mesh['dp'=8,'fsdp'=4] {'dp','fsdp'}, dimensions={0}, use_global_device_ids=true | all-gather | bytes 8448 | tf_op jit(solution)/shard_map/all_gather | solution.py:172
  57.7 34.1 %all-gather.4.cloned.1.call-done = bf16[1024,4096]{1,0:T(8,128)(2,1)} async-done(((bf16[32,4096]{1,0:T(8,128)(2,1)}), bf16[1024,4096]{1,0:T(8,128)(2,1)}) %all-gather.4.cloned.1.call-update) | async-done | bytes 8388624 | tf_op jit(solution)/shard_map/all_gather | solution.py:170
  91.7 4.8 fusion.186
  98.1 9.8 while.60
  111.5 97.1 %all-gather.6.cloned.1.call-done = bf16[2,1024,4096]{2,1,0:T(8,128)(2,1)} async-done(((bf16[2,32,4096]{2,1,0:T(8,128)(2,1)}), bf16[2,1024,4096]{2,1,0:T(8,128)(2,1)}) %all-gather.6.cloned.1.call-update) | async-done | bytes 16777232 | tf_op jit(solution)/shard_map/all_gather | solution.py:171
  208.6 5.8 fusion.159
  214.5 7.9 fusion.271
  222.6 4.7 fusion.189
  233.1 19.7 %while.61 = (s32[]{:T(128)}, bf16[4,256,4,64]{1,3,2,0:T(8,128)(2,1)}, bf16[4,256,4,64]{1,3,2,0:T(8,128)(2,1)}, bf16[4,256,4,64]{1,3,2,0:T(8,128)(2,1)}, bf16[4,2...) while((s32[]{:T(128)}, bf16[4,256,4,64]{1,3,2,0:T(8,128)(2,1)}, ...), condition=%wide.region_13.14_spmd.clone, body=%wide.region_10.13_spmd.clone.sunk | while | flops 103089664 | bytes 4272205 | solution.py:64
  255.7 5.9 fusion.158
  261.6 7.9 fusion.273
  271.7 7.3 fusion.177
  279.0 5.9 multiply_reduce_fusion.5
  292.3 36.2 %while.62 = (s32[]{:T(128)}, bf16[4,256,4,64]{1,3,2,0:T(8,128)(2,1)}, bf16[4,256,4,64]{1,3,2,0:T(8,128)(2,1)}, bf16[4,256,4,64]{1,3,2,0:T(8,128)(2,1)}, bf16[4,2...) while((s32[]{:T(128)}, ...), condition=%wide.region_26.27_spmd.clone, body=%wide.region_22.26_spmd.clone.sunk | while | flops 205718016 | bytes 17398996 | solution.py:94
  328.6 5.9 multiply_reduce_fusion.2
  334.9 7.3 fusion.170
  347.1 9.8 fusion.232
  358.1 10.5 fusion.230
  369.8 10.4 fusion.228
  380.3 9.8 fusion.237
  396.8 4.1 fusion.231
  406.3 25.9 %while.63 = (s32[]{:T(128)}, bf16[4,256,4,64]{1,3,2,0:T(8,128)(2,1)}, bf16[4,256,4,64]{1,3,2,0:T(8,128)(2,1)}, bf16[4,256,4,64]{1,3,2,0:T(8,128)(2,1)}, bf16[4,2...) while((s32[]{:T(128)}, ...), condition=%wide.region_35.36_spmd.clone, body=%wide.region_31.35_spmd.clone.sunk | while | flops 205718016 | bytes 17398996 | solution.py:94
  435.7 6.5 fusion.219
  442.3 12.0 maximum_add_fusion
  455.7 5.9 fusion.201
  461.6 17.8 %reduce-scatter.19.cloned.1.call-done = f32[32,4]{1,0:T(8,128)} async-done(((f32[1024,4]{1,0:T(8,128)}), f32[32,4]{1,0:T(8,128)}) %reduce-scatter.19.cloned.1.call-update) | async-done | bytes 528
  481.4 179.1 %reduce-scatter.9.cloned.1.call-done = f32[32,4096]{1,0:T(8,128)} async-done(((f32[1024,4096]{1,0:T(8,128)}), f32[32,4096]{1,0:T(8,128)}) %reduce-scatter.9.cloned.1.call-update) | async-done | bytes 524304 | tf_op jit(solution)/shard_map/reduce_scatter | solution.py:190
  660.5 186.8 %reduce-scatter.15.cloned.1.call-done = f32[32,4096]{1,0:T(8,128)} async-done(((f32[1024,4096]{1,0:T(8,128)}), f32[32,4096]{1,0:T(8,128)}) %reduce-scatter.15.cloned.1.call-update) | async-done | bytes 524304 | tf_op jit(solution)/shard_map/reduce_scatter | solution.py:191
  847.3 186.7 %reduce-scatter.11.cloned.1.call-done = f32[32,4096]{1,0:T(8,128)} async-done(((f32[1024,4096]{1,0:T(8,128)}), f32[32,4096]{1,0:T(8,128)}) %reduce-scatter.11.cloned.1.call-update) | async-done | bytes 524304 | tf_op jit(solution)/shard_map/reduce_scatter | solution.py:191
  1033.9 187.0 %reduce-scatter.13.cloned.1.call-done = f32[32,4096]{1,0:T(8,128)} async-done(((f32[1024,4096]{1,0:T(8,128)}), f32[32,4096]{1,0:T(8,128)}) %reduce-scatter.13.cloned.1.call-update) | async-done | bytes 524304 | tf_op jit(solution)/shard_map/reduce_scatter | solution.py:190
  1221.0 3.8 fusion.241
  1227.5 180.9 %reduce-scatter.17.cloned.1.call-done = f32[32,4096]{1,0:T(8,128)} async-done(((f32[1024,4096]{1,0:T(8,128)}), f32[32,4096]{1,0:T(8,128)}) %reduce-scatter.17.cloned.1.call-update) | async-done | bytes 524304 | tf_op jit(solution)/shard_map/reduce_scatter | solution.py:187
  (329 shorter events, 153.2 us)
Async XLA Ops:
  7.2 84.5 %all-gather.4.cloned.1.call-start = ((), (), s32[]{:S(2)}) async-start(), calls=%async_computation.6 | async-start | bytes 8650752 | tf_op jit(solution)/shard_map/all_gather | solution.py:170
  9.0 199.6 %all-gather.6.cloned.1.call-start = ((), (), s32[]{:S(2)}) async-start(), calls=%async_computation.7 | async-start | bytes 17301504 | tf_op jit(solution)/shard_map/all_gather | solution.py:171
  11.2 468.2 %reduce-scatter.19.cloned.1.call-start = ((), (), s32[]{:S(2)}) async-start(), calls=%async_computation.13 | async-start | bytes 540672
  107.9 106.5 %copy-start.5 = (bf16[4,256,4,64]{1,3,2,0:T(8,128)(2,1)}, bf16[4,256,4,64]{1,3,2,0:T(8,128)(2,1)S(1)}, u32[]{:S(2)}) copy-start(bf16[4,256,4,64]{1,3,2,0:T(8,128)(2,1)S(1)} %get-tuple-element.724) | copy-start | bytes 1572868
  107.9 106.5 %copy-start.7 = (bf16[4,256,4,64]{1,3,2,0:T(8,128)(2,1)}, bf16[4,256,4,64]{1,3,2,0:T(8,128)(2,1)S(1)}, u32[]{:S(2)}) copy-start(bf16[4,256,4,64]{1,3,2,0:T(8,128)(2,1)S(1)} %get-tuple-element.203) | copy-start | bytes 1572868
  111.5 102.9 %copy-start.43 = (f32[256]{0:T(256)}, f32[256]{0:T(256)S(1)}, u32[]{:S(2)}) copy-start(f32[256]{0:T(256)S(1)} %multiply_reduce_fusion.13) | copy-start | bytes 3076
  214.4 7.9 copy-start.10
  255.4 29.6 %copy-start = (f32[256,1024]{1,0:T(8,128)}, f32[256,1024]{1,0:T(8,128)S(1)}, u32[]{:S(2)}) copy-start(f32[256,1024]{1,0:T(8,128)S(1)} %get-tuple-element.397) | copy-start | bytes 3145732
  261.6 10.1 copy-start.12
  261.6 8.2 copy-start.36
  271.7 7.3 copy-start.13
  328.6 13.6 slice-start
  328.6 13.6 slice-start.1
  334.8 7.3 copy-start.15
  334.9 7.3 slice-start.2
  334.9 7.3 slice-start.3
  347.0 313.4 %reduce-scatter.9.cloned.1.call-start = ((), (), s32[]{:S(2)}) async-start(), calls=%async_computation.8 | async-start | bytes 17301504 | tf_op jit(solution)/shard_map/reduce_scatter | solution.py:190
  356.9 490.4 %reduce-scatter.15.cloned.1.call-start = ((), (), s32[]{:S(2)}) async-start(), calls=%async_computation.11 | async-start | bytes 17301504 | tf_op jit(solution)/shard_map/reduce_scatter | solution.py:191
  368.6 665.3 %reduce-scatter.11.cloned.1.call-start = ((), (), s32[]{:S(2)}) async-start(), calls=%async_computation.9 | async-start | bytes 17301504 | tf_op jit(solution)/shard_map/reduce_scatter | solution.py:191
  380.3 840.7 %reduce-scatter.13.cloned.1.call-start = ((), (), s32[]{:S(2)}) async-start(), calls=%async_computation.10 | async-start | bytes 17301504 | tf_op jit(solution)/shard_map/reduce_scatter | solution.py:190
  390.1 1018.3 %reduce-scatter.17.cloned.1.call-start = ((), (), s32[]{:S(2)}) async-start(), calls=%async_computation.12 | async-start | bytes 17301504 | tf_op jit(solution)/shard_map/reduce_scatter | solution.py:187
  435.7 6.5 copy-start.2
  455.7 24.5 %copy-start.47 = (f32[4,32]{1,0:T(4,128)S(1)}, f32[4,32]{1,0:T(4,128)}, u32[]{:S(2)}) copy-start(f32[4,32]{1,0:T(4,128)} %param.25) | copy-start | bytes 1540
  455.7 24.5 %copy-start.49 = (f32[4,32]{1,0:T(4,128)S(1)}, f32[4,32]{1,0:T(4,128)}, u32[]{:S(2)}) copy-start(f32[4,32]{1,0:T(4,128)} %param.28) | copy-start | bytes 1540
  455.7 25.1 %copy-start.48 = (f32[4,32]{1,0:T(4,128)S(1)}, f32[4,32]{1,0:T(4,128)}, u32[]{:S(2)}) copy-start(f32[4,32]{1,0:T(4,128)} %param.31) | copy-start | bytes 1540
  455.7 765.2 %copy-start.18 = (f32[2,32,4096]{2,1,0:T(8,128)S(1)}, f32[2,32,4096]{2,1,0:T(8,128)}, u32[]{:S(2)}) copy-start(f32[2,32,4096]{2,1,0:T(8,128)} %param.24) | copy-start | bytes 3145732
  480.2 747.3 %copy-start.45 = (f32[4,32]{1,0:T(4,128)}, f32[4,32]{1,0:T(4,128)S(1)}, u32[]{:S(2)}) copy-start(f32[4,32]{1,0:T(4,128)S(1)} %copy.140) | copy-start | bytes 1540
  480.8 746.7 %copy-start.46 = (f32[4,32]{1,0:T(4,128)}, f32[4,32]{1,0:T(4,128)S(1)}, u32[]{:S(2)}) copy-start(f32[4,32]{1,0:T(4,128)S(1)} %get-tuple-element.356) | copy-start | bytes 1540
  1221.0 187.5 %copy-start.38 = (f32[32,4096]{1,0:T(8,128)S(1)}, f32[32,4096]{1,0:T(8,128)}, u32[]{:S(2)}) copy-start(f32[32,4096]{1,0:T(8,128)} %param.23) | copy-start | bytes 1572868
  1221.0 187.5 %copy-start.42 = (f32[32,4096]{1,0:T(8,128)S(1)}, f32[32,4096]{1,0:T(8,128)}, u32[]{:S(2)}) copy-start(f32[32,4096]{1,0:T(8,128)} %param.26) | copy-start | bytes 1572868
  1224.7 186.7 %copy-start.17 = (f32[2,32,4096]{2,1,0:T(8,128)}, f32[2,32,4096]{2,1,0:T(8,128)S(1)}, u32[]{:S(2)}) copy-start(f32[2,32,4096]{2,1,0:T(8,128)S(1)} %get-tuple-element.359) | copy-start | bytes 3145732
  1224.7 185.8 %copy-start.41 = (f32[32,4096]{1,0:T(8,128)S(1)}, f32[32,4096]{1,0:T(8,128)}, u32[]{:S(2)}) copy-start(f32[32,4096]{1,0:T(8,128)} %param.29) | copy-start | bytes 1572868
  (54 other events, 115.1 us)
Sparse Core Ops, SparseCore 0:
  11.5 80.2 all-gather.3
  95.2 113.3 all-gather.5
  347.1 132.2 reduce-scatter.18
  481.7 178.7 reduce-scatter.8
  662.7 184.5 reduce-scatter.14
  849.5 184.3 reduce-scatter.10
  1036.3 184.5 reduce-scatter.12
  1223.9 184.4 reduce-scatter.16
where the time goes:
time: 1420 us
  waiting for transfers between devices  1070 us (75%)
  matrix products  218 us (15%)
  blocking collectives  43.5 us (3%)
  other arithmetic  37.4 us (3%)
  local copies, waits for them, and re-layouts  32.4 us (2%)
  between operations  14.9 us (1%)
    reduce_scatter x2, waiting for transfers between devices, owner_sums(): lax.psum_scatter(down_term, ('dp', 'fsdp'), scatter_dimension=0, tiled=True)  373 us
    reduce_scatter x2, waiting for transfers between devices, owner_sums(): lax.psum_scatter(up_term, ('dp', 'fsdp'), scatter_dimension=0, tiled=True)  366 us
    reduce_scatter x1, waiting for transfers between devices, owner_sums(): lax.psum_scatter(att_term, ('dp', 'fsdp'), scatter_dimension=0, tiled=True)  181 us
    all_gather x1, waiting for transfers between devices, fetch_forward(): lax.all_gather(pieces[1], ('dp', 'fsdp'), axis=1, tiled=True)  97.1 us
    all_gather x1, blocking collectives, fetch_forward(): lax.all_gather(pieces[2], ('dp', 'fsdp'), axis=1, tiled=True)  43.5 us
    all_gather x1, waiting for transfers between devices, fetch_forward(): lax.all_gather(pieces[0], ('dp', 'fsdp'), axis=0, tiled=True)  34.1 us
  transfers between devices with their start and end apart: 8, of which 8 were waited for; matrix products, arithmetic and copies ran while one was open for 10% of the time, Pallas kernels for 0%

commit v1 on v0

--- a/solution.py
+++ b/solution.py
@@ -120,49 +120,47 @@
     return (rows_low, qkv_rows, mixed_rows, first_sum, hidden_low, inner_rows, active, second)
 
 
-def layer_out(rows_in, weights, same_seq):
-    second = layer_states(rows_in, weights, same_seq)[7]
-    norm_values = weights[2].astype(jnp.float32)
-    return normalize(second, norm_values[2], norm_values[3])
-
-
-def layer_back(rows_in, weights, same_seq, grad_out):
+def layer_back(states, weights, same_seq, grad_out):
     att_full, ffn_full, norm_full = weights
     model_width = att_full.shape[0]
     norm_values = norm_full.astype(jnp.float32)
     rows_low, qkv_rows, mixed_rows, first_sum, hidden_low, inner_rows, active, second = (
-        layer_states(rows_in, weights, same_seq)
+        states
     )
     second_value, second_back = jax.vjp(normalize, second, norm_values[2], norm_values[3])
     grad_second, grad_gain2, grad_bias2 = second_back(grad_out)
     grad_ffn_out = grad_second.astype(jnp.bfloat16)
-    grad_down = jnp.einsum("td,tf->df", grad_ffn_out, active, preferred_element_type=jnp.float32)
     grad_active = jnp.dot(grad_ffn_out, ffn_full[1], preferred_element_type=jnp.float32)
     gelu_value, gelu_back = jax.vjp(gelu_tanh, inner_rows)
     grad_inner = gelu_back(grad_active)[0].astype(jnp.bfloat16)
-    grad_up = jnp.einsum("td,tf->df", hidden_low, grad_inner, preferred_element_type=jnp.float32)
     grad_hidden = grad_second + jnp.einsum(
         "tf,df->td", grad_inner, ffn_full[0], preferred_element_type=jnp.float32
     )
     first_value, first_back = jax.vjp(normalize, first_sum, norm_values[0], norm_values[1])
     grad_first, grad_gain1, grad_bias1 = first_back(grad_hidden)
     grad_branch = grad_first.astype(jnp.bfloat16)
-    grad_proj = jnp.einsum("td,te->de", mixed_rows, grad_branch, preferred_element_type=jnp.float32)
     grad_mixed = jnp.einsum(
         "te,de->td", grad_branch, att_full[:, 3 * model_width :], preferred_element_type=jnp.float32
     ).astype(jnp.bfloat16)
     grad_qkv = attend_back(qkv_rows, grad_mixed, same_seq)
-    grad_inproj = jnp.einsum("td,te->de", rows_low, grad_qkv, preferred_element_type=jnp.float32)
     grad_rows = grad_first + jnp.einsum(
         "te,de->td", grad_qkv, att_full[:, : 3 * model_width], preferred_element_type=jnp.float32
     )
-    grad_terms = (
-        jnp.concatenate([grad_inproj, grad_proj], axis=1),
-        grad_up,
-        grad_down,
-        jnp.stack([grad_gain1, grad_bias1, grad_gain2, grad_bias2]),
-    )
-    return (grad_rows, grad_terms)
+    factors = (
+        (grad_ffn_out, active),
+        (hidden_low, grad_inner),
+        (mixed_rows, grad_branch),
+        (rows_low, grad_qkv),
+    )
+    return (grad_rows, factors, jnp.stack([grad_gain1, grad_bias1, grad_gain2, grad_bias2]))
+
+
+def weight_sum(layer_pairs):
+    left = jnp.concatenate([pair[0] for pair in layer_pairs])
+    right = jnp.concatenate([pair[1] for pair in layer_pairs])
+    return jnp.einsum("td,tf->df", left, right, preferred_element_type=jnp.float32).astype(
+        jnp.bfloat16
+    )
 
 
 def fetch_forward(pieces):
@@ -173,23 +171,10 @@
     )
 
 
-def fetch_backward(pieces):
-    return (
-        lax.all_gather(pieces[0], ("dp", "fsdp"), axis=0, tiled=True),
-        lax.all_gather(pieces[1], ("dp", "fsdp"), axis=1, tiled=True),
-        lax.all_gather(pieces[2], ("dp", "fsdp"), axis=1, tiled=True),
-    )
-
-
-def owner_sums(grad_terms):
-    att_term, up_term, down_term, norm_term = grad_terms
-    att_share, norm_share = (
-        lax.psum_scatter(att_term, ("dp", "fsdp"), scatter_dimension=0, tiled=True),
-        lax.psum_scatter(norm_term, ("dp", "fsdp"), scatter_dimension=1, tiled=True),
-    )
-    up_share = lax.psum_scatter(up_term, ("dp", "fsdp"), scatter_dimension=0, tiled=True)
-    down_share = lax.psum_scatter(down_term, ("dp", "fsdp"), scatter_dimension=0, tiled=True)
-    return (att_share, jnp.stack([up_share, down_share]), norm_share)
+def owner_sum(term, dim):
+    return lax.psum_scatter(term, ("dp", "fsdp"), scatter_dimension=dim, tiled=True).astype(
+        jnp.float32
+    )
 
 
 def update(gradient, master, moment, average, step_rate):
@@ -214,7 +199,8 @@
     norm_average,
 ):
     row_count = tokens.shape[0]
-    seq_ends = jnp.cumsum(seq_lengths[0])
+    lengths = [seq_lengths[0, slot] for slot in range(seq_lengths.shape[1])]
+    seq_ends = jnp.stack([sum(lengths[: slot + 1]) for slot in range(len(lengths))])
     position = jnp.arange(row_count, dtype=jnp.int32)
     segment = jnp.sum((position[:, None] >= seq_ends[None, :]).astype(jnp.int32), axis=1)
     same_seq = segment[:, None] == segment[None, :]
@@ -224,19 +210,23 @@
         ffn_master.astype(jnp.bfloat16),
         norm_master.astype(jnp.bfloat16),
     )
+    weights = fetch_forward(pieces)
+    norm_values = weights[2].astype(jnp.float32)
     stored = []
     current = tokens.astype(jnp.float32)
     for depth in range(LAYERS):
-        weights = fetch_forward(pieces)
-        stored.append(current)
-        current = layer_out(current, weights, same_seq)
+        stored.append(layer_states(current, weights, same_seq))
+        current = normalize(stored[depth][7], norm_values[2], norm_values[3])
     grad_now = cotangent.astype(jnp.float32) * live_rows
-    totals = (jnp.zeros_like(att_master), jnp.zeros_like(ffn_master), jnp.zeros_like(norm_master))
+    factors, norm_term = [], 0.0
     for depth in reversed(range(LAYERS)):
-        weights = fetch_backward(pieces)
-        grad_now, grad_terms = layer_back(stored[depth], weights, same_seq, grad_now)
-        shares = owner_sums(grad_terms)
-        totals = jax.tree.map(jnp.add, totals, shares)
+        grad_now, pairs, norm_part = layer_back(stored[depth], weights, same_seq, grad_now)
+        factors.append(pairs)
+        norm_term = norm_term + norm_part
+    down, up, proj, inproj = [weight_sum(pairs) for pairs in zip(*factors)]
+    ffn_total = jnp.stack([owner_sum(up, 0), owner_sum(down, 0)])
+    att_total = owner_sum(jnp.concatenate([inproj, proj], axis=1), 0)
+    totals = (att_total, ffn_total, owner_sum(norm_term, 1))
     step_rate = 0.1 / math.sqrt(row_count * lax.axis_size(("dp", "fsdp")))
     att_out = update(totals[0], att_master, att_moment, att_average, step_rate)
     ffn_out = update(totals[1], ffn_master, ffn_moment, ffn_average, step_rate)

time: 1420 us -> 933 us (0.66)
  waiting for transfers between devices: 1070 us -> 614 us
  matrix products: 218 us -> 185 us
    reduce_scatter x5 -> x3, waiting for transfers between devices: 921 us -> 433 us  [owner_sum(): lax.psum_scatter(term, ('dp', 'fsdp'), scatter_dimension=dim, tiled=True)]
    unnamed x9 -> x7, waiting for transfers between devices: 17.9 us -> 53.2 us
    dot_general x8 -> x4, matrix products: 57.4 us -> 30.1 us  [weight_sum(): jnp.einsum('td,tf->df', left, right, preferred_element_type=jnp.float32)]
  transfers between devices with their start and end apart: 8 -> 6, of which waited for: 8 -> 6; matrix products, arithmetic and copies ran while one was open for 10% -> 11% of each run, Pallas kernels for 0% -> 0%
where the time goes in v1:
time: 933 us; the launch traced here: 928 us
  waiting for transfers between devices  614 us (66%)
  matrix products  185 us (20%)
  blocking collectives  43.4 us (5%)
  local copies, waits for them, and re-layouts  34.3 us (4%)
  other arithmetic  31.8 us (3%)
  between operations  17.6 us (2%)
    reduce_scatter x3, waiting for transfers between devices, owner_sum(): lax.psum_scatter(term, ('dp', 'fsdp'), scatter_dimension=dim, tiled=True)  433 us
    all_gather x1, waiting for transfers between devices, fetch_forward(): lax.all_gather(pieces[1], ('dp', 'fsdp'), axis=1, tiled=True)  97 us
    unnamed x7, waiting for transfers between devices  53.2 us
    all_gather x1, blocking collectives, fetch_forward(): lax.all_gather(pieces[2], ('dp', 'fsdp'), axis=1, tiled=True)  43.4 us
    all_gather x1, waiting for transfers between devices, fetch_forward(): lax.all_gather(pieces[0], ('dp', 'fsdp'), axis=0, tiled=True)  31.4 us
    dot_general x4, matrix products, weight_sum(): jnp.einsum('td,tf->df', left, right, preferred_element_type=jnp.float32)  30.1 us
    dot_general x8, matrix products, one_group(): jnp.einsum('hqk,qhd->khd', softmax_rows.astype(jnp.bfloat16), grad_rows,...  19 us
  transfers between devices with their start and end apart: 6, of which 6 were waited for; matrix products, arithmetic and copies ran while one was open for 11% of the time, Pallas kernels for 0%

profile of v1, /device:TPU:0, one launch (start us, length us, event | category | flops | bytes accessed | tf_op | source)
XLA Modules:
  0.0 928.5 jit_solution(17027405955791544080)
XLA Ops:
  11.9 43.4 %all-gather = bf16[32,32,4]{1,2,0:T(4,128)(2,1)S(1)} all-gather(bf16[1,32,4]{1,2,0:T(4,128)(2,1)S(1)} %convert_bitcast_fusion), channel_id=1, replica_groups=mesh['dp'=8,'fsdp'=4] {'dp','fsdp'}, dimensions={0}, use_global_device_ids=true | all-gather | bytes 8448 | tf_op jit(solution)/shard_map/all_gather | solution.py:170
  60.2 31.4 %all-gather.4.cloned.1.call-done = bf16[1024,4096]{1,0:T(8,128)(2,1)} async-done(((bf16[32,4096]{1,0:T(8,128)(2,1)}), bf16[1024,4096]{1,0:T(8,128)(2,1)}) %all-gather.4.cloned.1.call-update) | async-done | bytes 8388624 | tf_op jit(solution)/shard_map/all_gather | solution.py:168
  91.6 4.8 fusion.192
  98.0 9.6 %while.52 = (s32[]{:T(128)}, bf16[4,256,4,64]{1,3,2,0:T(8,128)(2,1)S(1)}, bf16[4,256,4,64]{1,3,2,0:T(8,128)(2,1)}, bf16[4,256,4,64]{1,3,2,0:T(8,128)(2,1)S(1)}, ...) while((s32[]{:T(128)}, bf16[4,256,4,64]{1,3,2,0:T(8,128)(2,1)S(1)}, ...), condition=%wide.region_4.5_spmd.clone, body=%wide.region_1.4_spmd.clone.sunk | while | flops 103089664 | bytes 4272205 | solution.py:64
  111.5 97.0 %all-gather.6.cloned.1.call-done = bf16[2,1024,4096]{2,1,0:T(8,128)(2,1)} async-done(((bf16[2,32,4096]{2,1,0:T(8,128)(2,1)}), bf16[2,1024,4096]{2,1,0:T(8,128)(2,1)}) %all-gather.6.cloned.1.call-update) | async-done | bytes 16777232 | tf_op jit(solution)/shard_map/all_gather | solution.py:169
  208.6 8.6 multiply_convert_fusion.3
  221.8 4.6 fusion.195
  232.2 20.1 %while.53 = (s32[]{:T(128)}, bf16[4,256,4,64]{1,3,2,0:T(8,128)(2,1)}, bf16[4,256,4,64]{1,3,2,0:T(8,128)(2,1)}, bf16[4,256,4,64]{1,3,2,0:T(8,128)(2,1)}, bf16[4,2...) while((s32[]{:T(128)}, bf16[4,256,4,64]{1,3,2,0:T(8,128)(2,1)}, ...), condition=%wide.region_12.13_spmd.clone, body=%wide.region_9.12_spmd.clone.sunk | while | flops 103089664 | bytes 4272205 | solution.py:64
  252.3 2.6 fusion.308
  255.5 9.7 %multiply_convert_fusion.2 = (bf16[256,4096]{1,0:T(8,128)(2,1)}, f32[256,4096]{1,0:T(8,128)}) fusion(bf16[256,1024]{1,0:T(8,128)(2,1)S(1)} %fusion.264, bf16[2,1024,4096]{2,1,0:T(8,128)(2,1)} %all-gather.6.cloned.1.call-done), kind=kOutput, calls=%fused_computation.170 | convolution fusion | flops 2156920832 | bytes 15204352 | tf_op jit(solution)/shard_map/dot_general | solution.py:115
  265.2 4.1 fusion.309
  271.7 6.2 fusion.177
  277.9 4.3 multiply_reduce_fusion.5
  283.7 2.5 fusion.239
  289.8 36.0 %while.54 = (s32[]{:T(128)}, bf16[4,256,4,64]{1,3,2,0:T(8,128)(2,1)}, bf16[4,256,4,64]{1,3,2,0:T(8,128)(2,1)}, bf16[4,256,4,64]{1,3,2,0:T(8,128)(2,1)}, bf16[4,2...) while((s32[]{:T(128)}, ...), condition=%wide.region_25.26_spmd.clone, body=%wide.region_21.0_spmd.clone.sunk | while | flops 205718016 | bytes 17398996 | solution.py:94
  325.8 5.7 multiply_reduce_fusion.2
  333.9 7.3 fusion.170
  341.4 2.7 multiply_reduce_fusion.3
  345.4 9.0 convolution_convert_fusion.1
  355.6 9.0 convolution_convert_fusion
  365.2 2.6 fusion.242
  368.9 3.8 convolution_convert_fusion.3
  375.2 26.1 %while.55 = (s32[]{:T(128)}, bf16[4,256,4,64]{1,3,2,0:T(8,128)(2,1)}, bf16[4,256,4,64]{1,3,2,0:T(8,128)(2,1)}, bf16[4,256,4,64]{1,3,2,0:T(8,128)(2,1)}, bf16[4,2...) while((s32[]{:T(128)}, ...), condition=%wide.region_34.35_spmd.clone, body=%wide.region_30.0_spmd.clone.sunk | while | flops 205718016 | bytes 17398996 | solution.py:94
  401.4 8.2 convolution_convert_fusion.2
  409.6 7.6 pad_maximum_fusion
  418.4 5.9 fusion.230
  424.2 53.1 %reduce-scatter.13.cloned.1.call-done = f32[32,4]{1,0:T(8,128)} async-done(((f32[1024,4]{1,0:T(8,128)}), f32[32,4]{1,0:T(8,128)}) %reduce-scatter.13.cloned.1.call-update) | async-done | bytes 528
  479.3 145.0 %reduce-scatter.9.cloned.1.call-done = bf16[32,4096]{1,0:T(8,128)(2,1)} async-done(((bf16[1024,4096]{1,0:T(8,128)(2,1)}), bf16[32,4096]{1,0:T(8,128)(2,1)}) %reduce-scatter.9.cloned.1.call-update) | async-done | bytes 262160 | tf_op jit(solution)/shard_map/reduce_scatter | solution.py:175
  624.4 146.8 %reduce-scatter.11.cloned.1.call-done = bf16[32,4096]{1,0:T(8,128)(2,1)} async-done(((bf16[1024,4096]{1,0:T(8,128)(2,1)}), bf16[32,4096]{1,0:T(8,128)(2,1)}) %reduce-scatter.11.cloned.1.call-update) | async-done | bytes 262160 | tf_op jit(solution)/shard_map/reduce_scatter | solution.py:175
  771.1 3.2 fusion.276
  774.3 2.8 multiply_add_fusion
  777.1 141.0 %reduce-scatter.7.cloned.1.call-done = bf16[32,4096]{1,0:T(8,128)(2,1)} async-done(((bf16[1024,4096]{1,0:T(8,128)(2,1)}), bf16[32,4096]{1,0:T(8,128)(2,1)}) %reduce-scatter.7.cloned.1.call-update) | async-done | bytes 262160 | tf_op jit(solution)/shard_map/reduce_scatter | solution.py:175
  (327 shorter events, 136.1 us)
Async XLA Ops:
  7.2 84.5 %all-gather.4.cloned.1.call-start = ((), (), s32[]{:S(2)}) async-start(), calls=%async_computation.4 | async-start | bytes 8650752 | tf_op jit(solution)/shard_map/all_gather | solution.py:168
  9.0 199.6 %all-gather.6.cloned.1.call-start = ((), (), s32[]{:S(2)}) async-start(), calls=%async_computation.5 | async-start | bytes 17301504 | tf_op jit(solution)/shard_map/all_gather | solution.py:169
  11.2 466.2 %reduce-scatter.13.cloned.1.call-start = ((), (), s32[]{:S(2)}) async-start(), calls=%async_computation.9 | async-start | bytes 540672
  98.0 10.6 %copy-start.13 = (bf16[256,1024]{1,0:T(8,128)(2,1)S(1)}, bf16[256,1024]{1,0:T(8,128)(2,1)}, u32[]{:S(2)}) copy-start(bf16[256,1024]{1,0:T(8,128)(2,1)} %param.20) | copy-start | bytes 1572868
  107.6 109.6 %copy-start.7 = (bf16[4,256,4,64]{1,3,2,0:T(8,128)(2,1)}, bf16[4,256,4,64]{1,3,2,0:T(8,128)(2,1)S(1)}, u32[]{:S(2)}) copy-start(bf16[4,256,4,64]{1,3,2,0:T(8,128)(2,1)S(1)} %get-tuple-element.179) | copy-start | bytes 1572868
  111.5 105.7 %copy-start.26 = (bf16[256,1024]{1,0:T(8,128)(2,1)}, bf16[256,1024]{1,0:T(8,128)(2,1)S(1)}, u32[]{:S(2)}) copy-start(bf16[256,1024]{1,0:T(8,128)(2,1)S(1)} %fusion.262) | copy-start | bytes 1572868
  208.6 9.4 %copy-start.41 = (bf16[2,1024,4096]{2,1,0:T(8,128)(2,1)S(1)}, bf16[2,1024,4096]{2,1,0:T(8,128)(2,1)}, u32[]{:S(2)}) copy-start(bf16[2,1024,4096]{2,1,0:T(8,128)(2,1)} %all-gather.6.cloned.1.call-done) | copy-start | bytes 50331652
  254.9 10.2 %slice-start = ((s8[16777216]{0:T(1024)(128)(4,1)}), s8[4194304]{0:T(1024)(128)(4,1)S(1)}, s32[]{:S(2)}) async-start(s8[16777216]{0:T(1024)(128)(4,1)} %bitcast.440), calls=%async_computation.10 | async-start | bytes 8388608
  255.4 9.7 %copy-start.28 = (bf16[256,1024]{1,0:T(8,128)(2,1)}, bf16[256,1024]{1,0:T(8,128)(2,1)S(1)}, u32[]{:S(2)}) copy-start(bf16[256,1024]{1,0:T(8,128)(2,1)S(1)} %fusion.264) | copy-start | bytes 1572868
  255.4 9.7 %slice-start.1 = ((s8[16777216]{0:T(1024)(128)(4,1)}), s8[4194304]{0:T(1024)(128)(4,1)S(1)}, s32[]{:S(2)}) async-start(s8[16777216]{0:T(1024)(128)(4,1)} %bitcast.440), calls=%async_computation.11 | async-start | bytes 8388608
  255.5 9.7 %slice-start.2 = ((s8[16777216]{0:T(1024)(128)(4,1)}), s8[4194304]{0:T(1024)(128)(4,1)S(1)}, s32[]{:S(2)}) async-start(s8[16777216]{0:T(1024)(128)(4,1)} %bitcast.440), calls=%async_computation.12 | async-start | bytes 8388608
  255.5 9.7 %slice-start.3 = ((s8[16777216]{0:T(1024)(128)(4,1)}), s8[4194304]{0:T(1024)(128)(4,1)S(1)}, s32[]{:S(2)}) async-start(s8[16777216]{0:T(1024)(128)(4,1)} %bitcast.440), calls=%async_computation.13 | async-start | bytes 8388608
  271.7 6.2 copy-start.31
  283.7 6.1 copy-start.30
  331.6 9.7 %slice-start.4 = ((s8[16777216]{0:T(1024)(128)(4,1)}), s8[4194304]{0:T(1024)(128)(4,1)S(1)}, s32[]{:S(2)}) async-start(s8[16777216]{0:T(1024)(128)(4,1)} %bitcast.442), calls=%async_computation.14 | async-start | bytes 8388608
  333.9 7.3 slice-start.5
  333.9 7.3 slice-start.6
  333.9 7.5 slice-start.7
  345.3 279.1 %reduce-scatter.9.cloned.1.call-start = ((), (), s32[]{:S(2)}) async-start(), calls=%async_computation.7 | async-start | bytes 8650752 | tf_op jit(solution)/shard_map/reduce_scatter | solution.py:175
  354.4 416.7 %reduce-scatter.11.cloned.1.call-start = ((), (), s32[]{:S(2)}) async-start(), calls=%async_computation.8 | async-start | bytes 8650752 | tf_op jit(solution)/shard_map/reduce_scatter | solution.py:175
  364.6 553.6 %reduce-scatter.7.cloned.1.call-start = ((), (), s32[]{:S(2)}) async-start(), calls=%async_computation.6 | async-start | bytes 8650752 | tf_op jit(solution)/shard_map/reduce_scatter | solution.py:175
  368.8 6.4 copy-start.1
  368.8 6.4 copy-start.3
  418.4 59.8 %copy-start.38 = (f32[4,32]{1,0:T(4,128)S(1)}, f32[4,32]{1,0:T(4,128)}, u32[]{:S(2)}) copy-start(f32[4,32]{1,0:T(4,128)} %param.25) | copy-start | bytes 1540
  418.4 59.8 %copy-start.40 = (f32[4,32]{1,0:T(4,128)S(1)}, f32[4,32]{1,0:T(4,128)}, u32[]{:S(2)}) copy-start(f32[4,32]{1,0:T(4,128)} %param.28) | copy-start | bytes 1540
  418.4 60.4 %copy-start.39 = (f32[4,32]{1,0:T(4,128)S(1)}, f32[4,32]{1,0:T(4,128)}, u32[]{:S(2)}) copy-start(f32[4,32]{1,0:T(4,128)} %param.31) | copy-start | bytes 1540
  418.4 352.8 %copy-start.6 = (f32[2,32,4096]{2,1,0:T(8,128)S(1)}, f32[2,32,4096]{2,1,0:T(8,128)}, u32[]{:S(2)}) copy-start(f32[2,32,4096]{2,1,0:T(8,128)} %param.24) | copy-start | bytes 3145732
  478.1 299.0 %copy-start.36 = (f32[4,32]{1,0:T(4,128)}, f32[4,32]{1,0:T(4,128)S(1)}, u32[]{:S(2)}) copy-start(f32[4,32]{1,0:T(4,128)S(1)} %copy.128) | copy-start | bytes 1540
  478.7 298.4 %copy-start.37 = (f32[4,32]{1,0:T(4,128)}, f32[4,32]{1,0:T(4,128)S(1)}, u32[]{:S(2)}) copy-start(f32[4,32]{1,0:T(4,128)S(1)} %get-tuple-element.332) | copy-start | bytes 1540
  771.1 147.0 %copy-start.11 = (f32[32,4096]{1,0:T(8,128)S(1)}, f32[32,4096]{1,0:T(8,128)}, u32[]{:S(2)}) copy-start(f32[32,4096]{1,0:T(8,128)} %param.23) | copy-start | bytes 1572868
  774.3 147.1 %copy-start.5 = (f32[2,32,4096]{2,1,0:T(8,128)}, f32[2,32,4096]{2,1,0:T(8,128)S(1)}, u32[]{:S(2)}) copy-start(f32[2,32,4096]{2,1,0:T(8,128)S(1)} %get-tuple-element.335) | copy-start | bytes 3145732
  774.3 146.1 %copy-start.14 = (f32[32,4096]{1,0:T(8,128)S(1)}, f32[32,4096]{1,0:T(8,128)}, u32[]{:S(2)}) copy-start(f32[32,4096]{1,0:T(8,128)} %param.29) | copy-start | bytes 1572868
  (52 other events, 89.8 us)
Sparse Core Ops, SparseCore 0:
  11.5 80.1 all-gather.3
  95.1 113.4 all-gather.5
  345.4 131.8 reduce-scatter.12
  479.6 144.7 reduce-scatter.8
  626.6 144.4 reduce-scatter.10
  773.4 144.6 reduce-scatter.6

commit v2 on v1

--- a/solution.py
+++ b/solution.py
@@ -1,8 +1,11 @@
+import functools
 import math
 
 import jax
 import jax.numpy as jnp
 from jax import lax
+from jax.experimental import pallas as pl
+from jax.experimental.pallas import tpu as pltpu
 from jax.sharding import PartitionSpec as P
 
 HEAD_DIM = 64
@@ -155,26 +158,216 @@
     return (grad_rows, factors, jnp.stack([grad_gain1, grad_bias1, grad_gain2, grad_bias2]))
 
 
-def weight_sum(layer_pairs):
+def weight_sum(layer_pairs, picker):
     left = jnp.concatenate([pair[0] for pair in layer_pairs])
     right = jnp.concatenate([pair[1] for pair in layer_pairs])
-    return jnp.einsum("td,tf->df", left, right, preferred_element_type=jnp.float32).astype(
-        jnp.bfloat16
-    )
-
-
-def fetch_forward(pieces):
-    return (
-        lax.all_gather(pieces[0], ("dp", "fsdp"), axis=0, tiled=True),
-        lax.all_gather(pieces[1], ("dp", "fsdp"), axis=1, tiled=True),
-        lax.all_gather(pieces[2], ("dp", "fsdp"), axis=1, tiled=True),
-    )
-
-
-def owner_sum(term, dim):
-    return lax.psum_scatter(term, ("dp", "fsdp"), scatter_dimension=dim, tiled=True).astype(
-        jnp.float32
-    )
+    left = jnp.dot(left, picker, preferred_element_type=jnp.float32).astype(jnp.bfloat16)
+    return [
+        jnp.einsum("td,tf->df", part, right, preferred_element_type=jnp.float32).astype(jnp.bfloat16)
+        for part in jnp.split(left, 2, axis=1)
+    ]
+
+
+AXES = ("dp", "fsdp")
+NORM_COLS = 128
+
+
+class Route:
+    def __init__(self):
+        rows, cols = lax.axis_size("dp"), lax.axis_size("fsdp")
+        self.inner = cols // 4
+        self.ring_size = rows // 2 * self.inner
+        self.cols = cols
+        self.world = rows * cols
+        row, col = lax.axis_index("dp"), lax.axis_index("fsdp")
+        self.q = row // 2 * self.inner + col // 4
+        self.y, self.x, self.c = row % 2, col // 2 % 2, col % 2
+
+    def joint(self, q, y, x, c):
+        return (q // self.inner * 2 + y) * self.cols + q % self.inner * 4 + x * 2 + c
+
+    def move(self, array, step):
+        pairs = []
+        for q in range(self.ring_size):
+            for y in (0, 1):
+                for x in (0, 1):
+                    for c in (0, 1):
+                        to = step(q, y, x, c)
+                        pairs.append((self.joint(q, y, x, c), self.joint(*to)))
+        return lax.ppermute(array, AXES, pairs)
+
+    def ring(self, array):
+        return self.move(array, lambda q, y, x, c: ((q + 1) % self.ring_size, y, x, c))
+
+    def core(self, array):
+        return self.move(array, lambda q, y, x, c: (q, y, x, 1 - c))
+
+    def first(self, array):
+        return self.move(array, lambda q, y, x, c: (q, y ^ c, x ^ (1 - c), c))
+
+    def second(self, array):
+        return self.move(array, lambda q, y, x, c: (q, y ^ (1 - c), x ^ c, c))
+
+    def owner(self, back, first, second, core):
+        c = self.c ^ core
+        x = self.x ^ jnp.where(c == 0, first, second)
+        y = self.y ^ jnp.where(c == 0, second, first)
+        return self.joint((self.q + self.ring_size - back) % self.ring_size, y, x, c)
+
+
+def gather_ring_first(route, piece):
+    slots = [piece]
+    for _ in range(route.ring_size - 1):
+        slots.append(route.ring(slots[-1]))
+    base = jnp.concatenate(slots)
+    blocks = [(base, 0, 0), (route.first(base), 1, 0)]
+    blocks += [(route.second(block), first, 1) for block, first, _ in blocks]
+    arrays, owners = [], []
+    for core in (0, 1):
+        for block, first, second in blocks:
+            arrays.append(route.core(block) if core else block)
+            owners += [route.owner(i, first, second, core) for i in range(route.ring_size)]
+    return arrays, owners
+
+
+def gather_ring_middle(route, piece):
+    pair = jnp.concatenate([piece, route.first(piece)])
+    arrays, owners = [], []
+    for i in range(route.ring_size):
+        if i:
+            pair = route.ring(pair)
+        other = route.second(pair)
+        for core in (0, 1):
+            for second, block in ((0, pair), (1, other)):
+                arrays.append(route.core(block) if core else block)
+                owners += [route.owner(i, first, second, core) for first in (0, 1)]
+    return arrays, owners
+
+
+def place_kernel(owners_ref, *refs, widths):
+    count = len(refs) - len(widths) - 2
+    parts, outs, whole, sem = refs[:count], refs[count:-2], refs[-2], refs[-1]
+    shard = whole.shape[0] // owners_ref.shape[0]
+    copies = []
+    for part in parts:
+        for local in range(part.shape[0] // shard):
+            row = pl.multiple_of(owners_ref[len(copies)] * shard, shard)
+            copies.append(
+                pltpu.make_async_copy(
+                    part.at[pl.ds(local * shard, shard)],
+                    whole.at[pl.ds(row, shard)],
+                    sem.at[len(copies)],
+                )
+            )
+    for copy in copies:
+        copy.start()
+    for copy in copies:
+        copy.wait()
+    column = 0
+    copies = []
+    for out, width in zip(outs, widths):
+        copies.append(
+            pltpu.make_async_copy(whole.at[:, pl.ds(column, width)], out, sem.at[len(copies)])
+        )
+        column += width
+    for copy in copies:
+        copy.start()
+    for copy in copies:
+        copy.wait()
+
+
+def place_rows(arrays, owners, widths):
+    owners = jnp.stack(owners).astype(jnp.int32)
+    rows = sum(array.shape[0] for array in arrays)
+    anywhere = pl.BlockSpec(memory_space=pl.ANY)
+    kind = arrays[0].dtype
+    return pl.pallas_call(
+        functools.partial(place_kernel, widths=widths),
+        out_shape=[jax.ShapeDtypeStruct((rows, width), kind) for width in widths],
+        in_specs=[pl.BlockSpec(memory_space=pltpu.SMEM)] + [anywhere] * len(arrays),
+        out_specs=[anywhere] * len(widths),
+        scratch_shapes=[
+            pltpu.VMEM((rows, sum(widths)), kind),
+            pltpu.SemaphoreType.DMA((owners.size,)),
+        ],
+        cost_estimate=pl.CostEstimate(
+            flops=0, bytes_accessed=4 * rows * sum(widths), transcendentals=0
+        ),
+        compiler_params=pltpu.CompilerParams(vmem_limit_bytes=16 * 2**20),
+    )(owners, *arrays)
+
+
+def row_picker(owners, shard):
+    rows = (jnp.stack(owners)[:, None] * shard + jnp.arange(shard)[None, :]).reshape(1, -1)
+    return (jnp.arange(rows.size)[:, None] == rows).astype(jnp.bfloat16)
+
+
+def add_low(left, right):
+    return (left.astype(jnp.float32) + right.astype(jnp.float32)).astype(jnp.bfloat16)
+
+
+def owners_ring_last(route):
+    return [
+        route.owner(1 + j, first, second, core)
+        for core in (1, 0)
+        for second in (1, 0)
+        for first in (1, 0)
+        for j in range(route.ring_size)
+    ]
+
+
+def scatter_ring_last(route, send, keep):
+    for step in (route.core, route.second):
+        arrived = step(send)
+        half = keep.shape[0] // 2
+        send, keep = add_low(keep[:half], arrived[:half]), add_low(keep[half:], arrived[half:])
+    arrived = route.first(send)
+    pieces = [
+        add_low(a, b) for a, b in zip(cut(keep, route.ring_size), cut(arrived, route.ring_size))
+    ]
+    moving = pieces[0]
+    for piece in pieces[1:-1]:
+        moving = add_low(piece, route.ring(moving))
+    return pieces[-1].astype(jnp.float32) + route.ring(moving).astype(jnp.float32)
+
+
+def owners_ring_middle(route):
+    return [
+        route.owner(1 + j, first, second, core)
+        for core in (1, 0)
+        for second in (1, 0)
+        for j in range(route.ring_size)
+        for first in (1, 0)
+    ]
+
+
+def cut(array, count):
+    size = array.shape[0] // count
+    return [array[k * size : (k + 1) * size] for k in range(count)]
+
+
+def scatter_whole(route, upper, lower):
+    return lax.psum_scatter(
+        jnp.concatenate([upper, lower]), AXES, scatter_dimension=0, tiled=True
+    ).astype(jnp.float32)
+
+
+def scatter_ring_middle(route, send, keep):
+    arrived = route.core(send)
+    half = keep.shape[0] // 2
+    pieces = route.ring_size
+    sends = [
+        add_low(a, b) for a, b in zip(cut(keep[:half], pieces), cut(arrived[:half], pieces))
+    ]
+    keeps = [
+        add_low(a, b) for a, b in zip(cut(keep[half:], pieces), cut(arrived[half:], pieces))
+    ]
+    moving = None
+    for j in range(pieces):
+        local = add_low(keeps[j], route.second(sends[j]))
+        moving = local if moving is None else add_low(local, route.ring(moving))
+    shard = moving.shape[0] // 2
+    return moving[shard:].astype(jnp.float32) + route.first(moving[:shard]).astype(jnp.float32)
 
 
 def update(gradient, master, moment, average, step_rate):
@@ -205,12 +398,26 @@
     segment = jnp.sum((position[:, None] >= seq_ends[None, :]).astype(jnp.int32), axis=1)
     same_seq = segment[:, None] == segment[None, :]
     live_rows = (position < seq_ends[-1]).astype(jnp.float32)[:, None]
-    pieces = (
-        att_master.astype(jnp.bfloat16),
-        ffn_master.astype(jnp.bfloat16),
-        norm_master.astype(jnp.bfloat16),
-    )
-    weights = fetch_forward(pieces)
+    route = Route()
+    shard = att_master.shape[0]
+    norm_piece = jnp.pad(norm_master.T, ((0, 0), (0, NORM_COLS - norm_master.shape[0])))
+    att_piece = jnp.concatenate([att_master, norm_piece], axis=1).astype(jnp.bfloat16)
+    ffn_pieces = ffn_master.astype(jnp.bfloat16)
+    width = att_master.shape[1]
+    tiled = shard % 16 == 0
+    if tiled:
+        att_full, norm_full = place_rows(
+            *gather_ring_middle(route, att_piece), (width, NORM_COLS)
+        )
+        [up_full] = place_rows(*gather_ring_middle(route, ffn_pieces[0]), (width,))
+        [down_full] = place_rows(*gather_ring_first(route, ffn_pieces[1]), (width,))
+    else:
+        whole = [
+            lax.all_gather(piece, AXES, axis=0, tiled=True)
+            for piece in (att_piece, ffn_pieces[0], ffn_pieces[1])
+        ]
+        att_full, norm_full, up_full, down_full = whole[0][:, :width], whole[0][:, width:], *whole[1:]
+    weights = (att_full, (up_full, down_full), norm_full[:, : norm_master.shape[0]].T)
     norm_values = weights[2].astype(jnp.float32)
     stored = []
     current = tokens.astype(jnp.float32)
@@ -223,10 +430,27 @@
         grad_now, pairs, norm_part = layer_back(stored[depth], weights, same_seq, grad_now)
         factors.append(pairs)
         norm_term = norm_term + norm_part
-    down, up, proj, inproj = [weight_sum(pairs) for pairs in zip(*factors)]
-    ffn_total = jnp.stack([owner_sum(up, 0), owner_sum(down, 0)])
-    att_total = owner_sum(jnp.concatenate([inproj, proj], axis=1), 0)
-    totals = (att_total, ffn_total, owner_sum(norm_term, 1))
+    downs, ups, projs, inprojs = zip(*factors)
+    middle = row_picker(owners_ring_middle(route), shard)
+    last = row_picker(owners_ring_last(route), shard)
+    scatter_middle, scatter_last = scatter_ring_middle, scatter_ring_last
+    if not tiled:
+        middle = last = row_picker(list(range(route.world)), shard)
+        scatter_middle = scatter_last = scatter_whole
+    down_share = scatter_middle(route, *weight_sum(downs, middle))
+    up_share = scatter_middle(route, *weight_sum(ups, middle))
+    norm_rows = jnp.pad(norm_term.T, ((0, 0), (0, NORM_COLS - norm_term.shape[0])))
+    norm_rows = jnp.einsum(
+        "dr,dn->rn", last, norm_rows.astype(jnp.bfloat16), preferred_element_type=jnp.float32
+    ).astype(jnp.bfloat16)
+    att_parts = zip(weight_sum(inprojs, last), weight_sum(projs, last), jnp.split(norm_rows, 2))
+    att_halves = [jnp.concatenate(parts, axis=1) for parts in att_parts]
+    att_share = scatter_last(route, *att_halves)
+    totals = (
+        att_share[:, :width],
+        jnp.stack([up_share, down_share]),
+        att_share[:, width : width + norm_master.shape[0]].T,
+    )
     step_rate = 0.1 / math.sqrt(row_count * lax.axis_size(("dp", "fsdp")))
     att_out = update(totals[0], att_master, att_moment, att_average, step_rate)
     ffn_out = update(totals[1], ffn_master, ffn_moment, ffn_average, step_rate)

time: 933 us -> 585 us (0.63)
  waiting for transfers between devices: 614 us -> 188 us
  local copies, waits for them, and re-layouts: 34.3 us -> 79.5 us
  blocking collectives: 43.4 us -> 0 us
  starting transfers between devices: 0.25 us -> 40.8 us
  other arithmetic: 31.8 us -> 52.6 us
  Pallas kernels: 0 us -> 14.4 us
  between operations: 17.6 us -> 5.2 us
  matrix products: 185 us -> 196 us
    reduce_scatter x3 -> x0, waiting for transfers between devices: 433 us -> none  [owner_sum(): lax.psum_scatter(term, ('dp', 'fsdp'), scatter_dimension=dim, tiled=True)]
    ppermute x0 -> x66, waiting for transfers between devices: none -> 188 us  [move(): return lax.ppermute(array, AXES, pairs)]
    all_gather x2 -> x0, waiting for transfers between devices: 128 us -> none  [the longest x1 97 us: fetch_forward(): lax.all_gather(pieces[1], ('dp', 'fsdp'), axis=1, tiled=True)]
    unnamed x7 -> x0, waiting for transfers between devices: 53.2 us -> none
    all_gather x1 -> x0, blocking collectives: 43.4 us -> none  [fetch_forward(): lax.all_gather(pieces[2], ('dp', 'fsdp'), axis=1, tiled=True)]
    ppermute x0 -> x66, starting transfers between devices: none -> 40.8 us  [move(): return lax.ppermute(array, AXES, pairs)]
    unnamed x94 -> x204, local copies, waits for them, and re-layouts: 9.64 us -> 47.8 us
    dot_general x4 -> x13, matrix products: 30.1 us -> 60.8 us  [the longest x8 51.7 us: weight_sum(): jnp.einsum('td,tf->df', part, right, preferred_element_type=jnp.float32)]
  transfers between devices with their start and end apart: 6 -> 66, of which waited for: 6 -> 27; matrix products, arithmetic and copies ran while one was open for 11% -> 28% of each run, Pallas kernels for 0% -> 2%
where the time goes in v2:
time: 585 us; the launch traced here: 578 us
  matrix products  196 us (34%)
  waiting for transfers between devices  188 us (32%)
  local copies, waits for them, and re-layouts  79.5 us (14%)
  other arithmetic  52.6 us (9%)
  starting transfers between devices  40.8 us (7%)
  Pallas kernels  14.4 us (2%)
    ppermute x66, waiting for transfers between devices, move(): return lax.ppermute(array, AXES, pairs)  188 us
    dot_general x8, matrix products, weight_sum(): jnp.einsum('td,tf->df', part, right, preferred_element_type=jnp.float32)  51.7 us
    unnamed x204, local copies, waits for them, and re-layouts  47.8 us
    ppermute x66, starting transfers between devices, move(): return lax.ppermute(array, AXES, pairs)  40.8 us
    convert_element_type x15, other arithmetic, add_low(): (left.astype(jnp.float32) + right.astype(jnp.float32)).astype(jnp.bfloat16)  21.5 us
    dot_general x8, matrix products, one_group(): jnp.einsum('hqk,qhd->khd', softmax_rows.astype(jnp.bfloat16), grad_rows,...  18.4 us
    dot_general x8, matrix products, one_group(): jnp.einsum('hqk,khd->qhd', softmax_rows.astype(jnp.bfloat16), value_rows,...  18.3 us
    pallas_call x3, Pallas kernels, place_rows(): pl.pallas_call(functools.partial(place_kernel, widths=widths), out_shape=...  14.4 us
  transfers between devices with their start and end apart: 66, of which 27 were waited for; matrix products, arithmetic and copies ran while one was open for 28% of the time, Pallas kernels for 2%

profile of v2, /device:TPU:0, one launch (start us, length us, event | category | flops | bytes accessed | tf_op | source)
XLA Modules:
  0.0 578.3 jit_solution(11730960794026898623)
XLA Ops:
  14.8 9.7 %collective-permute-done.33 = bf16[32,4096]{1,0:T(8,128)(2,1)S(1)} collective-permute-done((bf16[32,4096]{1,0:T(8,128)(2,1)S(1)}, bf16[32,4096]{1,0:T(8,128)(2,1)S(1)}, u32[]{:S(2)}, u32[]{:S(2)}) %collective-permute-start.33) | collective-permute-done | bytes 262176 | tf_op jit(solution)/shard_map/ppermute | solution.py:197
  26.6 14.6 %collective-permute-done.34 = bf16[32,4096]{1,0:T(8,128)(2,1)S(1)} collective-permute-done((bf16[32,4096]{1,0:T(8,128)(2,1)S(1)}, bf16[32,4096]{1,0:T(8,128)(2,1)S(1)}, u32[]{:S(2)}, u32[]{:S(2)}) %collective-permute-start.34) | collective-permute-done | bytes 262176 | tf_op jit(solution)/shard_map/ppermute | solution.py:197
  45.5 7.4 %collective-permute-done.4.refs_4_ = bf16[64,4224]{1,0:T(8,128)(2,1)S(1)} collective-permute-done((bf16[64,4224]{1,0:T(8,128)(2,1)S(1)}, bf16[64,4224]{1,0:T(8,128)(2,1)S(1)}, u32[]{:S(2)}, u32[]{:S(2)}) %collective-permute-start.4) | collective-permute-done | bytes 540704 | tf_op jit(solution)/shard_map/ppermute | solution.py:197
  55.9 8.2 %collective-permute-done.24.refs_8_ = bf16[64,4096]{1,0:T(8,128)(2,1)S(1)} collective-permute-done((bf16[64,4096]{1,0:T(8,128)(2,1)S(1)}, bf16[64,4096]{1,0:T(8,128)(2,1)S(1)}, u32[]{:S(2)}, u32[]{:S(2)}) %collective-permute-start.24) | collective-permute-done | bytes 524320 | tf_op jit(solution)/shard_map/ppermute | solution.py:197
  69.0 5.0 collective-permute-done.8.refs_8_
  74.1 5.3 collective-permute-done.5.refs_5_
  83.1 8.4 %collective-permute-done.35.refs_1_ = bf16[128,4096]{1,0:T(8,128)(2,1)S(1)} collective-permute-done((bf16[128,4096]{1,0:T(8,128)(2,1)S(1)}, bf16[128,4096]{1,0:T(8,128)(2,1)S(1)}, u32[]{:S(2)}, u32[]{:S(2)}) %collective-permute-start.35) | collective-permute-done | bytes 1048608 | tf_op jit(solution)/shard_map/ppermute | solution.py:197
  145.7 4.9 shard_map.251
  155.9 25.6 %while.52 = (s32[]{:T(128)}, bf16[4,256,4,64]{1,3,2,0:T(8,128)(2,1)}, bf16[4,256,4,64]{1,3,2,0:T(8,128)(2,1)}, bf16[4,256,4,64]{1,3,2,0:T(8,128)(2,1)}, bf16[4,2...) while((s32[]{:T(128)}, bf16[4,256,4,64]{1,3,2,0:T(8,128)(2,1)}, ...), condition=%wide.region_4.5_spmd.clone, body=%wide.region_1.4_spmd.clone.sunk | while | flops 103089664 | bytes 4272205 | solution.py:67
  186.1 8.8 %multiply_convert_fusion.3 = (bf16[256,4096]{1,0:T(8,128)(2,1)S(1)}, f32[256,4096]{1,0:T(8,128)}) fusion(bf16[256,1024]{1,0:T(8,128)(2,1)S(1)} %fusion.248, bf16[1024,4096]{1,0:T(8,128)(2,1)} %copy-done), kind=kOutput, calls=%fused_computation.170 | convolution fusion | flops 2156920832 | bytes 15204352 | tf_op jit(solution)/shard_map/dot_general | solution.py:118
  194.9 5.6 shard_map.253
  210.3 12.3 %while.53 = (s32[]{:T(128)}, bf16[4,256,4,64]{1,3,2,0:T(8,128)(2,1)}, bf16[4,256,4,64]{1,3,2,0:T(8,128)(2,1)}, bf16[4,256,4,64]{1,3,2,0:T(8,128)(2,1)S(1)}, bf16...) while((s32[]{:T(128)}, bf16[4,256,4,64]{1,3,2,0:T(8,128)(2,1)}, ...), condition=%wide.region_12.13_spmd.clone, body=%wide.region_9.12_spmd.clone.sunk | while | flops 103089664 | bytes 4272205 | solution.py:67
  230.6 5.1 multiply_convert_fusion.2
  242.8 4.8 fusion.169
  258.0 26.1 %while.54 = (s32[]{:T(128)}, bf16[4,256,4,64]{1,3,2,0:T(8,128)(2,1)}, bf16[4,256,4,64]{1,3,2,0:T(8,128)(2,1)}, bf16[4,256,4,64]{1,3,2,0:T(8,128)(2,1)}, bf16[4,2...) while((s32[]{:T(128)}, ...), condition=%wide.region_25.26_spmd.clone, body=%wide.region_21.25_spmd.clone.sunk | while | flops 205718016 | bytes 17398996 | solution.py:97
  284.1 5.9 %multiply_reduce_fusion.2 = (f32[1024]{0:T(1024)S(1)}, f32[256]{0:T(256)S(1)}, f32[1024]{0:T(1024)S(1)}, f32[256,1024]{1,0:T(8,128)S(1)}) fusion(f32[256,1024]{1,0:T(8,128)S(1)} %get-tuple-element.484, f32[256]{0:T(256)S(1)} %fusion.263, f32[256]{0:T(256)S(1)} %broadcast_multiply_fusion.2, f32[1024]{0:T(1024)S(1)} %get-tuple-element.360, ...), kind=kOutput, calls=%fused_computation.285 | convolution fusion | flops 1617950464 | bytes 11026432 | tf_op jit(solution)/shard_map/te,de->td/dot_general | solution.py:149
  292.7 8.4 %fusion.162 = bf16[256,4096]{1,0:T(8,128)(2,1)S(1)} fusion(f32[256,4096]{1,0:T(8,128)S(1)} %copy-done.90, bf16[256,1024]{1,0:T(8,128)(2,1)S(1)} %add_convert_fusion.42, bf16[1024,4096]{1,0:T(8,128)(2,1)} %copy-done.1), kind=kOutput, calls=%fused_computation.152 | convolution fusion | flops 2168455168 | bytes 15204352 | tf_op jit(solution)/shard_map/dot_general | solution.py:136
  304.0 4.9 convolution_convert_fusion.2
  320.5 25.9 %while.55 = (s32[]{:T(128)}, bf16[4,256,4,64]{1,3,2,0:T(8,128)(2,1)}, bf16[4,256,4,64]{1,3,2,0:T(8,128)(2,1)}, bf16[4,256,4,64]{1,3,2,0:T(8,128)(2,1)}, bf16[4,2...) while((s32[]{:T(128)}, ...), condition=%wide.region_34.35_spmd.clone, body=%wide.region_30.34_spmd.clone.sunk | while | flops 205718016 | bytes 17398996 | solution.py:97
  349.9 15.5 %convolution_convert_fusion.4 = bf16[512,3072]{0,1:T(8,128)(2,1)S(1)} fusion(bf16[512,1024]{1,0:T(8,128)(2,1)S(1)} %copy-done.92, bf16[256,1024]{0,1:T(8,128)(2,1)S(1)} %bitcast.421, bf16[256,1024]{0,1:T(8,128)(2,1)S(1)} %bitcast.418, bf16[256,1024]{0,1:T(8,128)(2,1)S(1)} %bitcast.415, bf16[256,1024]{0,1:T(8,128)(2,1)S(1)} %bitcast.431, ...), kind=kOutput, calls=%fused_computation.140 | convolution fusion | flops 1631059968 | bytes 6815744 | tf_op jit(solution)/shard_map/td,tf->df/dot_general | solution.py:166
  367.9 4.6 convolution_convert_fusion.3
  377.0 15.6 %convolution_convert_fusion.5 = bf16[512,3072]{0,1:T(8,128)(2,1)S(1)} fusion(bf16[512,1024]{1,0:T(8,128)(2,1)S(1)} %copy-done.92, bf16[256,1024]{0,1:T(8,128)(2,1)S(1)} %bitcast.422, bf16[256,1024]{0,1:T(8,128)(2,1)S(1)} %bitcast.419, bf16[256,1024]{0,1:T(8,128)(2,1)S(1)} %bitcast.416, bf16[256,1024]{0,1:T(8,128)(2,1)S(1)} %bitcast.432, ...), kind=kOutput, calls=%fused_computation.141 | convolution fusion | flops 1631059968 | bytes 6815744 | tf_op jit(solution)/shard_map/td,tf->df/dot_general | solution.py:166
  410.8 19.7 %collective-permute-done.61 = bf16[64,4096]{1,0:T(8,128)(2,1)S(1)} collective-permute-done((bf16[64,4096]{1,0:T(8,128)(2,1)S(1)}, bf16[64,4096]{1,0:T(8,128)(2,1)S(1)}, u32[]{:S(2)}, u32[]{:S(2)}) %collective-permute-start.61) | collective-permute-done | bytes 524320 | tf_op jit(solution)/shard_map/ppermute | solution.py:197
  433.3 12.0 %collective-permute-done.53 = bf16[64,4096]{1,0:T(8,128)(2,1)S(1)} collective-permute-done((bf16[64,4096]{1,0:T(8,128)(2,1)S(1)}, bf16[64,4096]{1,0:T(8,128)(2,1)S(1)}, u32[]{:S(2)}, u32[]{:S(2)}) %collective-permute-start.53) | collective-permute-done | bytes 524320 | tf_op jit(solution)/shard_map/ppermute | solution.py:197
  448.2 11.0 %collective-permute-done.62 = bf16[64,4096]{1,0:T(8,128)(2,1)S(1)} collective-permute-done((bf16[64,4096]{1,0:T(8,128)(2,1)S(1)}, bf16[64,4096]{1,0:T(8,128)(2,1)S(1)}, u32[]{:S(2)}, u32[]{:S(2)}) %collective-permute-start.62) | collective-permute-done | bytes 524320 | tf_op jit(solution)/shard_map/ppermute | solution.py:197
  462.2 10.1 %collective-permute-done.54 = bf16[64,4096]{1,0:T(8,128)(2,1)S(1)} collective-permute-done((bf16[64,4096]{1,0:T(8,128)(2,1)S(1)}, bf16[64,4096]{1,0:T(8,128)(2,1)S(1)}, u32[]{:S(2)}, u32[]{:S(2)}) %collective-permute-start.54) | collective-permute-done | bytes 524320 | tf_op jit(solution)/shard_map/ppermute | solution.py:197
  473.9 15.0 %collective-permute-done.63 = bf16[64,4096]{1,0:T(8,128)(2,1)S(1)} collective-permute-done((bf16[64,4096]{1,0:T(8,128)(2,1)S(1)}, bf16[64,4096]{1,0:T(8,128)(2,1)S(1)}, u32[]{:S(2)}, u32[]{:S(2)}) %collective-permute-start.63) | collective-permute-done | bytes 524320 | tf_op jit(solution)/shard_map/ppermute | solution.py:197
  490.3 9.8 %collective-permute-done.55 = bf16[64,4096]{1,0:T(8,128)(2,1)S(1)} collective-permute-done((bf16[64,4096]{1,0:T(8,128)(2,1)S(1)}, bf16[64,4096]{1,0:T(8,128)(2,1)S(1)}, u32[]{:S(2)}, u32[]{:S(2)}) %collective-permute-start.55) | collective-permute-done | bytes 524320 | tf_op jit(solution)/shard_map/ppermute | solution.py:197
  511.0 8.5 %collective-permute-done.44 = bf16[128,4224]{0,1:T(8,128)(2,1)S(1)} collective-permute-done((bf16[128,4224]{0,1:T(8,128)(2,1)S(1)}, bf16[128,4224]{0,1:T(8,128)(2,1)S(1)}, u32[]{:S(2)}, u32[]{:S(2)}) %collective-permute-start.44) | collective-permute-done | bytes 1081376 | tf_op jit(solution)/shard_map/ppermute | solution.py:197
  524.3 6.0 %collective-permute-done.45 = bf16[32,4224]{1,0:T(8,128)(2,1)} collective-permute-done((bf16[32,4224]{1,0:T(8,128)(2,1)S(1)}, bf16[32,4224]{1,0:T(8,128)(2,1)}, u32[]{:S(2)}, u32[]{:S(2)}) %collective-permute-start.45) | collective-permute-done | bytes 270368 | tf_op jit(solution)/shard_map/ppermute | solution.py:197
  539.1 6.3 %collective-permute-done.46 = bf16[32,4224]{1,0:T(8,128)(2,1)S(1)} collective-permute-done((bf16[32,4224]{1,0:T(8,128)(2,1)S(1)}, bf16[32,4224]{1,0:T(8,128)(2,1)S(1)}, u32[]{:S(2)}, u32[]{:S(2)}) %collective-permute-start.46) | collective-permute-done | bytes 270368 | tf_op jit(solution)/shard_map/ppermute | solution.py:197
  552.0 5.6 collective-permute-done.47
  (606 shorter events, 325.3 us)
Async XLA Ops:
  13.4 27.9 %collective-permute-start.20 = (bf16[64,4096]{1,0:T(8,128)(2,1)S(1)}, bf16[64,4096]{1,0:T(8,128)(2,1)S(1)}, u32[]{:S(2)}, u32[]{:S(2)}) collective-permute-start(bf16[64,4096]{1,0:T(8,128)(2,1)S(1)} %pad_maximum_fusion.14.refs_0_), channel_id=1, source_target_pairs={{0,8},{1,9},{2,10},{3,11},{4,12},{5,13},{6,14},{7,15},{8,16},{9,17... | collective-permute-start | bytes 1572872 | tf_op jit(solution)/shard_map/ppermute | solution.py:197
  24.4 16.9 %collective-permute-start.34 = (bf16[32,4096]{1,0:T(8,128)(2,1)S(1)}, bf16[32,4096]{1,0:T(8,128)(2,1)S(1)}, u32[]{:S(2)}, u32[]{:S(2)}) collective-permute-start(bf16[32,4096]{1,0:T(8,128)(2,1)S(1)} %collective-permute-done.33), channel_id=1, source_target_pairs={{0,8},{1,9},{2,10},{3,11},{4,12},{5,13},{6,14},{7,15},{8,16},{9,17... | collective-permute-start | bytes 786440 | tf_op jit(solution)/shard_map/ppermute | solution.py:197
  24.5 28.4 %collective-permute-start.4 = (bf16[64,4224]{1,0:T(8,128)(2,1)S(1)}, bf16[64,4224]{1,0:T(8,128)(2,1)S(1)}, u32[]{:S(2)}, u32[]{:S(2)}) collective-permute-start(bf16[64,4224]{1,0:T(8,128)(2,1)S(1)} %pad_maximum_fusion.13.refs_0_), channel_id=1, source_target_pairs={{0,8},{1,9},{2,10},{3,11},{4,12},{5,13},{6,14},{7,15},{8,16},{9,17... | collective-permute-start | bytes 1622024 | tf_op jit(solution)/shard_map/ppermute | solution.py:197
  24.5 29.2 %collective-permute-start.1 = (bf16[64,4224]{1,0:T(8,128)(2,1)S(1)}, bf16[64,4224]{1,0:T(8,128)(2,1)S(1)}, u32[]{:S(2)}, u32[]{:S(2)}) collective-permute-start(bf16[64,4224]{1,0:T(8,128)(2,1)S(1)} %pad_maximum_fusion.13.refs_0_), channel_id=1, source_target_pairs={{0,4},{1,3},{2,6},{3,1},{4,0},{5,7},{6,2},{7,5},{8,12},{9,11},{10,... | collective-permute-start | bytes 1622024 | tf_op jit(solution)/shard_map/ppermute | solution.py:197
  41.8 22.3 %collective-permute-start.24 = (bf16[64,4096]{1,0:T(8,128)(2,1)S(1)}, bf16[64,4096]{1,0:T(8,128)(2,1)S(1)}, u32[]{:S(2)}, u32[]{:S(2)}) collective-permute-start(bf16[64,4096]{1,0:T(8,128)(2,1)S(1)} %collective-permute-done.20.refs_4_), channel_id=1, source_target_pairs={{0,8},{1,9},{2,10},{3,11},{4,12},{5,13},{6,14},{7,15},{8,16},{9,17... | collective-permute-start | bytes 1572872 | tf_op jit(solution)/shard_map/ppermute | solution.py:197
  44.0 21.4 %collective-permute-start.21 = (bf16[64,4096]{1,0:T(8,128)(2,1)S(1)}, bf16[64,4096]{1,0:T(8,128)(2,1)}, u32[]{:S(2)}, u32[]{:S(2)}) collective-permute-start(bf16[64,4096]{1,0:T(8,128)(2,1)S(1)} %collective-permute-done.20.refs_4_), channel_id=1, source_target_pairs={{0,4},{1,3},{2,6},{3,1},{4,0},{5,7},{6,2},{7,5},{8,12},{9,11},{10,... | collective-permute-start | bytes 1572872 | tf_op jit(solution)/shard_map/ppermute | solution.py:197
  55.8 18.3 %collective-permute-start.8 = (bf16[64,4224]{1,0:T(8,128)(2,1)S(1)}, bf16[64,4224]{1,0:T(8,128)(2,1)}, u32[]{:S(2)}, u32[]{:S(2)}) collective-permute-start(bf16[64,4224]{1,0:T(8,128)(2,1)S(1)} %collective-permute-done.4.refs_4_), channel_id=1, source_target_pairs={{0,8},{1,9},{2,10},{3,11},{4,12},{5,13},{6,14},{7,15},{8,16},{9,17... | collective-permute-start | bytes 1622024 | tf_op jit(solution)/shard_map/ppermute | solution.py:197
  65.4 26.1 %collective-permute-start.35 = (bf16[128,4096]{1,0:T(8,128)(2,1)S(1)}, bf16[128,4096]{1,0:T(8,128)(2,1)S(1)}, u32[]{:S(2)}, u32[]{:S(2)}) collective-permute-start(bf16[128,4096]{1,0:T(8,128)(2,1)S(1)} %pad_maximum_fusion.8.refs_0_), channel_id=1, source_target_pairs={{0,2},{1,5},{2,0},{3,7},{4,6},{5,1},{6,4},{7,3},{8,10},{9,13},{10,... | collective-permute-start | bytes 3145736 | tf_op jit(solution)/shard_map/ppermute | solution.py:197
  67.7 24.7 %collective-permute-start.36 = (bf16[128,4096]{1,0:T(8,128)(2,1)S(1)}, bf16[128,4096]{1,0:T(8,128)(2,1)}, u32[]{:S(2)}, u32[]{:S(2)}) collective-permute-start(bf16[128,4096]{1,0:T(8,128)(2,1)S(1)} %pad_maximum_fusion.8.refs_0_), channel_id=1, source_target_pairs={{0,4},{1,3},{2,6},{3,1},{4,0},{5,7},{6,2},{7,5},{8,12},{9,11},{10,... | collective-permute-start | bytes 3145736 | tf_op jit(solution)/shard_map/ppermute | solution.py:197
  80.2 17.7 %collective-permute-start.25 = (bf16[64,4096]{1,0:T(8,128)(2,1)S(1)}, bf16[64,4096]{1,0:T(8,128)(2,1)S(1)}, u32[]{:S(2)}, u32[]{:S(2)}) collective-permute-start(bf16[64,4096]{1,0:T(8,128)(2,1)S(1)} %collective-permute-done.24.refs_8_), channel_id=1, source_target_pairs={{0,4},{1,3},{2,6},{3,1},{4,0},{5,7},{6,2},{7,5},{8,12},{9,11},{10,... | collective-permute-start | bytes 1572872 | tf_op jit(solution)/shard_map/ppermute | solution.py:197
  82.3 17.1 %collective-permute-start.26 = (bf16[64,4096]{1,0:T(8,128)(2,1)S(1)}, bf16[64,4096]{1,0:T(8,128)(2,1)S(1)}, u32[]{:S(2)}, u32[]{:S(2)}) collective-permute-start(bf16[64,4096]{1,0:T(8,128)(2,1)S(1)} %collective-permute-done.24.refs_8_), channel_id=1, source_target_pairs={{0,1},{1,0},{2,3},{3,2},{4,5},{5,4},{6,7},{7,6},{8,9},{9,8},{10,11... | collective-permute-start | bytes 1572872 | tf_op jit(solution)/shard_map/ppermute | solution.py:197
  109.6 35.7 %collective-permute-start.37 = (bf16[128,4096]{1,0:T(8,128)(2,1)S(1)}, bf16[128,4096]{1,0:T(8,128)(2,1)}, u32[]{:S(2)}, u32[]{:S(2)}) collective-permute-start(bf16[128,4096]{1,0:T(8,128)(2,1)S(1)} %collective-permute-done.35.refs_1_), channel_id=1, source_target_pairs={{0,4},{1,3},{2,6},{3,1},{4,0},{5,7},{6,2},{7,5},{8,12},{9,11},{10,... | collective-permute-start | bytes 3145736 | tf_op jit(solution)/shard_map/ppermute | solution.py:197
  111.2 33.4 %collective-permute-start.7 = (bf16[64,4224]{1,0:T(8,128)(2,1)}, bf16[64,4224]{1,0:T(8,128)(2,1)}, u32[]{:S(2)}, u32[]{:S(2)}) collective-permute-start(bf16[64,4224]{1,0:T(8,128)(2,1)} %copy-done.9), channel_id=1, source_target_pairs={{0,1},{1,0},{2,3},{3,2},{4,5},{5,4},{6,7},{7,6},{8,9},{9,8},{10,11... | collective-permute-start | bytes 1622024 | tf_op jit(solution)/shard_map/ppermute | solution.py:197
  111.3 33.4 %collective-permute-start.14 = (bf16[64,4224]{1,0:T(8,128)(2,1)}, bf16[64,4224]{1,0:T(8,128)(2,1)}, u32[]{:S(2)}, u32[]{:S(2)}) collective-permute-start(bf16[64,4224]{1,0:T(8,128)(2,1)} %collective-permute-done.12.refs_12_), channel_id=1, source_target_pairs={{0,1},{1,0},{2,3},{3,2},{4,5},{5,4},{6,7},{7,6},{8,9},{9,8},{10,11... | collective-permute-start | bytes 1622024 | tf_op jit(solution)/shard_map/ppermute | solution.py:197
  115.2 29.9 %collective-permute-start.11 = (bf16[64,4224]{1,0:T(8,128)(2,1)}, bf16[64,4224]{1,0:T(8,128)(2,1)}, u32[]{:S(2)}, u32[]{:S(2)}) collective-permute-start(bf16[64,4224]{1,0:T(8,128)(2,1)} %collective-permute-done.9.refs_9_), channel_id=1, source_target_pairs={{0,1},{1,0},{2,3},{3,2},{4,5},{5,4},{6,7},{7,6},{8,9},{9,8},{10,11... | collective-permute-start | bytes 1622024 | tf_op jit(solution)/shard_map/ppermute | solution.py:197
  115.2 30.5 %collective-permute-start.15 = (bf16[64,4224]{1,0:T(8,128)(2,1)}, bf16[64,4224]{1,0:T(8,128)(2,1)}, u32[]{:S(2)}, u32[]{:S(2)}) collective-permute-start(bf16[64,4224]{1,0:T(8,128)(2,1)} %collective-permute-done.13.refs_13_), channel_id=1, source_target_pairs={{0,1},{1,0},{2,3},{3,2},{4,5},{5,4},{6,7},{7,6},{8,9},{9,8},{10,11... | collective-permute-start | bytes 1622024 | tf_op jit(solution)/shard_map/ppermute | solution.py:197
  144.7 50.2 %collective-permute-start.38 = (bf16[128,4096]{1,0:T(8,128)(2,1)S(1)}, bf16[128,4096]{1,0:T(8,128)(2,1)}, u32[]{:S(2)}, u32[]{:S(2)}) collective-permute-start(bf16[128,4096]{1,0:T(8,128)(2,1)S(1)} %pad_maximum_fusion.8.refs_0_), channel_id=1, source_target_pairs={{0,1},{1,0},{2,3},{3,2},{4,5},{5,4},{6,7},{7,6},{8,9},{9,8},{10,11... | collective-permute-start | bytes 3145736 | tf_op jit(solution)/shard_map/ppermute | solution.py:197
  144.7 50.2 %collective-permute-start.39 = (bf16[128,4096]{1,0:T(8,128)(2,1)S(1)}, bf16[128,4096]{1,0:T(8,128)(2,1)}, u32[]{:S(2)}, u32[]{:S(2)}) collective-permute-start(bf16[128,4096]{1,0:T(8,128)(2,1)S(1)} %collective-permute-done.35.refs_1_), channel_id=1, source_target_pairs={{0,1},{1,0},{2,3},{3,2},{4,5},{5,4},{6,7},{7,6},{8,9},{9,8},{10,11... | collective-permute-start | bytes 3145736 | tf_op jit(solution)/shard_map/ppermute | solution.py:197
  145.2 49.7 %collective-permute-start.40 = (bf16[128,4096]{1,0:T(8,128)(2,1)}, bf16[128,4096]{1,0:T(8,128)(2,1)}, u32[]{:S(2)}, u32[]{:S(2)}) collective-permute-start(bf16[128,4096]{1,0:T(8,128)(2,1)} %collective-permute-done.36.refs_2_), channel_id=1, source_target_pairs={{0,1},{1,0},{2,3},{3,2},{4,5},{5,4},{6,7},{7,6},{8,9},{9,8},{10,11... | collective-permute-start | bytes 3145736 | tf_op jit(solution)/shard_map/ppermute | solution.py:197
  145.3 49.7 %collective-permute-start.41 = (bf16[128,4096]{1,0:T(8,128)(2,1)}, bf16[128,4096]{1,0:T(8,128)(2,1)}, u32[]{:S(2)}, u32[]{:S(2)}) collective-permute-start(bf16[128,4096]{1,0:T(8,128)(2,1)} %collective-permute-done.37.refs_3_), channel_id=1, source_target_pairs={{0,1},{1,0},{2,3},{3,2},{4,5},{5,4},{6,7},{7,6},{8,9},{9,8},{10,11... | collective-permute-start | bytes 3145736 | tf_op jit(solution)/shard_map/ppermute | solution.py:197
  308.8 86.9 %collective-permute-start.48 = (bf16[512,4096]{1,0:T(8,128)(2,1)}, bf16[512,4096]{1,0:T(8,128)(2,1)}, u32[]{:S(2)}, u32[]{:S(2)}) collective-permute-start(bf16[512,4096]{1,0:T(8,128)(2,1)} %convolution_convert_fusion.2), channel_id=1, source_target_pairs={{0,1},{1,0},{2,3},{3,2},{4,5},{5,4},{6,7},{7,6},{8,9},{9,8},{10,11... | collective-permute-start | bytes 12582920 | tf_op jit(solution)/shard_map/ppermute | solution.py:197
  313.3 89.1 %collective-permute-start.57 = (bf16[512,4096]{1,0:T(8,128)(2,1)}, bf16[512,4096]{1,0:T(8,128)(2,1)}, u32[]{:S(2)}, u32[]{:S(2)}) collective-permute-start(bf16[512,4096]{1,0:T(8,128)(2,1)} %convolution_convert_fusion), channel_id=1, source_target_pairs={{0,1},{1,0},{2,3},{3,2},{4,5},{5,4},{6,7},{7,6},{8,9},{9,8},{10,11... | collective-permute-start | bytes 12582920 | tf_op jit(solution)/shard_map/ppermute | solution.py:197
  365.8 39.4 %collective-permute-start.42 = (bf16[512,4224]{0,1:T(8,128)(2,1)S(1)}, bf16[512,4224]{0,1:T(8,128)(2,1)S(1)}, u32[]{:S(2)}, u32[]{:S(2)}) collective-permute-start(bf16[512,4224]{0,1:T(8,128)(2,1)S(1)} %pad_maximum_fusion.1), channel_id=1, source_target_pairs={{0,1},{1,0},{2,3},{3,2},{4,5},{5,4},{6,7},{7,6},{8,9},{9,8},{10,11... | collective-permute-start | bytes 12976136 | tf_op jit(solution)/shard_map/ppermute | solution.py:197
  400.4 31.4 %collective-permute-start.51 = (bf16[64,4096]{1,0:T(8,128)(2,1)S(1)}, bf16[64,4096]{1,0:T(8,128)(2,1)S(1)}, u32[]{:S(2)}, u32[]{:S(2)}) collective-permute-start(bf16[64,4096]{1,0:T(8,128)(2,1)S(1)} %get-tuple-element.454), channel_id=1, source_target_pairs={{0,4},{1,3},{2,6},{3,1},{4,0},{5,7},{6,2},{7,5},{8,12},{9,11},{10,... | collective-permute-start | bytes 1572872 | tf_op jit(solution)/shard_map/ppermute | solution.py:197
  400.9 59.7 %collective-permute-start.50 = (bf16[64,4096]{1,0:T(8,128)(2,1)S(1)}, bf16[64,4096]{1,0:T(8,128)(2,1)S(1)}, u32[]{:S(2)}, u32[]{:S(2)}) collective-permute-start(bf16[64,4096]{1,0:T(8,128)(2,1)S(1)} %get-tuple-element.455), channel_id=1, source_target_pairs={{0,4},{1,3},{2,6},{3,1},{4,0},{5,7},{6,2},{7,5},{8,12},{9,11},{10,... | collective-permute-start | bytes 1572872 | tf_op jit(solution)/shard_map/ppermute | solution.py:197
  402.4 87.9 %collective-permute-start.49 = (bf16[64,4096]{1,0:T(8,128)(2,1)S(1)}, bf16[64,4096]{1,0:T(8,128)(2,1)S(1)}, u32[]{:S(2)}, u32[]{:S(2)}) collective-permute-start(bf16[64,4096]{1,0:T(8,128)(2,1)S(1)} %get-tuple-element.452), channel_id=1, source_target_pairs={{0,4},{1,3},{2,6},{3,1},{4,0},{5,7},{6,2},{7,5},{8,12},{9,11},{10,... | collective-permute-start | bytes 1572872 | tf_op jit(solution)/shard_map/ppermute | solution.py:197
  405.2 25.3 %collective-permute-start.61 = (bf16[64,4096]{1,0:T(8,128)(2,1)S(1)}, bf16[64,4096]{1,0:T(8,128)(2,1)S(1)}, u32[]{:S(2)}, u32[]{:S(2)}) collective-permute-start(bf16[64,4096]{1,0:T(8,128)(2,1)S(1)} %get-tuple-element.457), channel_id=1, source_target_pairs={{0,4},{1,3},{2,6},{3,1},{4,0},{5,7},{6,2},{7,5},{8,12},{9,11},{10,... | collective-permute-start | bytes 1572872 | tf_op jit(solution)/shard_map/ppermute | solution.py:197
  408.2 38.5 %collective-permute-start.60 = (bf16[64,4096]{1,0:T(8,128)(2,1)S(1)}, bf16[64,4096]{1,0:T(8,128)(2,1)S(1)}, u32[]{:S(2)}, u32[]{:S(2)}) collective-permute-start(bf16[64,4096]{1,0:T(8,128)(2,1)S(1)} %get-tuple-element.458), channel_id=1, source_target_pairs={{0,4},{1,3},{2,6},{3,1},{4,0},{5,7},{6,2},{7,5},{8,12},{9,11},{10,... | collective-permute-start | bytes 1572872 | tf_op jit(solution)/shard_map/ppermute | solution.py:197
  431.8 41.8 %collective-permute-start.59 = (bf16[64,4096]{1,0:T(8,128)(2,1)S(1)}, bf16[64,4096]{1,0:T(8,128)(2,1)S(1)}, u32[]{:S(2)}, u32[]{:S(2)}) collective-permute-start(bf16[64,4096]{1,0:T(8,128)(2,1)S(1)} %get-tuple-element.459), channel_id=1, source_target_pairs={{0,4},{1,3},{2,6},{3,1},{4,0},{5,7},{6,2},{7,5},{8,12},{9,11},{10,... | collective-permute-start | bytes 1572872 | tf_op jit(solution)/shard_map/ppermute | solution.py:197
  446.7 57.6 %collective-permute-start.58 = (bf16[64,4096]{1,0:T(8,128)(2,1)S(1)}, bf16[64,4096]{1,0:T(8,128)(2,1)S(1)}, u32[]{:S(2)}, u32[]{:S(2)}) collective-permute-start(bf16[64,4096]{1,0:T(8,128)(2,1)S(1)} %get-tuple-element.456), channel_id=1, source_target_pairs={{0,4},{1,3},{2,6},{3,1},{4,0},{5,7},{6,2},{7,5},{8,12},{9,11},{10,... | collective-permute-start | bytes 1572872 | tf_op jit(solution)/shard_map/ppermute | solution.py:197
  460.6 42.0 %collective-permute-start.43 = (bf16[256,4224]{0,1:T(8,128)(2,1)S(1)}, bf16[256,4224]{0,1:T(8,128)(2,1)S(1)}, u32[]{:S(2)}, u32[]{:S(2)}) collective-permute-start(bf16[256,4224]{0,1:T(8,128)(2,1)S(1)} %get-tuple-element.451), channel_id=1, source_target_pairs={{0,4},{1,3},{2,6},{3,1},{4,0},{5,7},{6,2},{7,5},{8,12},{9,11},{10,... | collective-permute-start | bytes 6488072 | tf_op jit(solution)/shard_map/ppermute | solution.py:197
  473.6 26.6 %collective-permute-start.55 = (bf16[64,4096]{1,0:T(8,128)(2,1)S(1)}, bf16[64,4096]{1,0:T(8,128)(2,1)S(1)}, u32[]{:S(2)}, u32[]{:S(2)}) collective-permute-start(bf16[64,4096]{1,0:T(8,128)(2,1)S(1)} %add_convert_fusion.26), channel_id=1, source_target_pairs={{0,8},{1,9},{2,10},{3,11},{4,12},{5,13},{6,14},{7,15},{8,16},{9,17... | collective-permute-start | bytes 1572872 | tf_op jit(solution)/shard_map/ppermute | solution.py:197
  (164 other events, 1093.8 us)

commit v3 on v2

--- a/solution.py
+++ b/solution.py
@@ -12,160 +12,494 @@
 LAYERS = 2
 
 
-head_group = 4
-
-
-def normalize(values_in, gain_row, bias_row):
-    centered = values_in - jnp.mean(values_in, axis=-1, keepdims=True)
+LOW = jnp.bfloat16
+SCALE = HEAD_DIM ** (-0.5)
+PAIR = 2 * HEAD_DIM
+TILE = 256
+FF_TILE = 512
+ROWS = 64
+GELU_RATE = math.sqrt(2.0 / math.pi)
+ANYWHERE = pl.BlockSpec(memory_space=pl.ANY)
+SCALARS = pl.BlockSpec(memory_space=pltpu.SMEM)
+VECTORS = pl.BlockSpec(memory_space=pltpu.VMEM)
+
+
+def product(left, right, left_dim=1, right_dim=0):
+    dims = (((left_dim,), (right_dim,)), ((), ()))
+    return lax.dot_general(left, right, dims, preferred_element_type=jnp.float32)
+
+
+def columns(index, width):
+    return pl.ds(pl.multiple_of(index * width, width), width)
+
+
+def column_copy(source, target, sem, index, width):
+    part = pl.ds(index * width, width)
+    return pltpu.make_async_copy(source.at[:, part], target.at[:, part], sem.at[index])
+
+
+def fill_mask(lengths_ref, mask_ref):
+    shape = mask_ref.shape
+    key_row = lax.broadcasted_iota(jnp.int32, shape, 0)
+    query_row = lax.broadcasted_iota(jnp.int32, shape, 1)
+    end = 0
+    key_segment = jnp.zeros(shape, jnp.int32)
+    query_segment = jnp.zeros(shape, jnp.int32)
+    for slot in range(lengths_ref.shape[1]):
+        end = end + lengths_ref[0, slot]
+        key_segment += (key_row >= end).astype(jnp.int32)
+        query_segment += (query_row >= end).astype(jnp.int32)
+    mask_ref[...] = jnp.where(key_segment == query_segment, 0.0, -1e30)
+
+
+def row_blocks(count, body):
+    def step(block, carry):
+        body(pl.ds(pl.multiple_of(block * ROWS, ROWS), ROWS))
+        return carry
+
+    lax.fori_loop(0, count // ROWS, step, 0)
+
+
+def normalize(values, gain, bias):
+    centered = values - jnp.mean(values, axis=-1, keepdims=True)
     spread = jnp.mean(centered * centered, axis=-1, keepdims=True)
-    return centered * lax.rsqrt(spread + 1e-05) * gain_row + bias_row
-
-
-def gelu_tanh(inner_value):
-    return jax.nn.gelu(inner_value, approximate=True)
-
-
-def split_heads(head_block):
-    return head_block.reshape(head_block.shape[0], -1, head_group, HEAD_DIM).transpose(1, 0, 2, 3)
-
-
-def merge_heads(head_block):
-    return head_block.transpose(1, 0, 2, 3).reshape(head_block.shape[1], -1)
-
-
-def softmax_of(query_rows, key_rows, same_seq):
-    scores = jnp.einsum(
-        "qhd,khd->hqk", query_rows, key_rows, preferred_element_type=jnp.float32
-    ) * HEAD_DIM ** (-0.5)
-    scores = jnp.where(same_seq[None], scores, -1e30)
-    row_peak = jnp.max(scores, axis=-1, keepdims=True)
-    weights = jnp.exp(scores - row_peak)
-    return weights / jnp.sum(weights, axis=-1, keepdims=True)
-
-
-def head_parts(qkv_rows):
-    model_width = qkv_rows.shape[1] // 3
-    return (
-        split_heads(qkv_rows[:, :model_width]),
-        split_heads(qkv_rows[:, model_width : 2 * model_width]),
-        split_heads(qkv_rows[:, 2 * model_width :]),
-    )
-
-
-def attend(qkv_rows, same_seq):
-
-    def one_group(group_item):
-        query_rows, key_rows, value_rows = group_item
-        softmax_rows = softmax_of(query_rows, key_rows, same_seq)
-        return jnp.einsum(
-            "hqk,khd->qhd",
-            softmax_rows.astype(jnp.bfloat16),
-            value_rows,
-            preferred_element_type=jnp.float32,
+    inverse = lax.rsqrt(spread + 1e-05)
+    unit = centered * inverse
+    return unit, inverse, unit * gain + bias
+
+
+def normalize_back(grad, unit, inverse, gain):
+    scaled = grad * gain
+    mean = jnp.mean(scaled, axis=-1, keepdims=True)
+    along = jnp.mean(scaled * unit, axis=-1, keepdims=True)
+    return inverse * (scaled - mean - unit * along)
+
+
+def half_lanes(rows, half):
+    lane = lax.broadcasted_iota(jnp.int32, (rows, PAIR), 1)
+    return (lane >= HEAD_DIM) == bool(half)
+
+
+def attend_forward_kernel(
+    lengths_ref,
+    rows_ref,
+    norm_ref,
+    weight_ref,
+    low_ref,
+    qkv_ref,
+    mixed_ref,
+    lse_ref,
+    hidden_ref,
+    unit_ref,
+    inverse_ref,
+    held_ref,
+    mask_ref,
+    sum_ref,
+    sem,
+):
+    count, width = rows_ref.shape
+    chunks = [column_copy(weight_ref, held_ref, sem, k, width) for k in range(4)]
+    for copy in chunks:
+        copy.start()
+    low_ref[...] = rows_ref[...].astype(LOW)
+    fill_mask(lengths_ref, mask_ref)
+    tiles = width // TILE
+    for k in range(3):
+        chunks[k].wait()
+
+        def project(tile, carry):
+            part = columns(k * tiles + tile, TILE)
+            qkv_ref[:, part] = product(low_ref[...], held_ref[:, part]).astype(LOW)
+            return carry
+
+        lax.fori_loop(0, tiles, project, 0)
+
+    def one_pair(pair, carry):
+        query = qkv_ref[:, columns(pair, PAIR)] * jnp.asarray(SCALE, LOW)
+        key = qkv_ref[:, columns(width // PAIR + pair, PAIR)]
+        value = qkv_ref[:, columns(2 * width // PAIR + pair, PAIR)]
+        halves, sums = [], []
+        for half in (0, 1):
+            own = jnp.where(half_lanes(count, half), query, jnp.zeros_like(query))
+            scores = product(key, own, 1, 1) + mask_ref[...]
+            peak = jnp.max(scores, axis=0, keepdims=True)
+            weights = jnp.exp(scores - peak)
+            total = jnp.sum(weights, axis=0, keepdims=True)
+            sums.append(peak + jnp.log(total))
+            mixed = product(value, weights.astype(LOW), 0, 0)
+            halves.append(mixed[half * HEAD_DIM : (half + 1) * HEAD_DIM] * (1.0 / total))
+        lse_ref[pair] = jnp.concatenate(sums, axis=0)
+        mixed_ref[:, columns(pair, PAIR)] = jnp.concatenate(halves, axis=0).T.astype(LOW)
+        return carry
+
+    lax.fori_loop(0, width // PAIR, one_pair, 0)
+    chunks[3].wait()
+
+    def project_out(tile, carry):
+        part = columns(tile, TILE)
+        branch = product(mixed_ref[...], held_ref[:, columns(3 * tiles + tile, TILE)])
+        sum_ref[:, part] = rows_ref[:, part].astype(jnp.float32) + branch
+        return carry
+
+    lax.fori_loop(0, tiles, project_out, 0)
+
+    def norm_rows(block):
+        unit, inverse, hidden = normalize(sum_ref[block, :], norm_ref[0:1], norm_ref[1:2])
+        hidden_ref[block, :] = hidden
+        unit_ref[block, :] = unit
+        inverse_ref[block, :] = jnp.broadcast_to(inverse, (ROWS, 128))
+
+    row_blocks(count, norm_rows)
+
+
+def attend_forward(lengths, rows, norm, weight):
+    count, width = rows.shape
+    shape = jax.ShapeDtypeStruct
+    return pl.pallas_call(
+        attend_forward_kernel,
+        out_shape=[
+            shape((count, width), LOW),
+            shape((count, 3 * width), LOW),
+            shape((count, width), LOW),
+            shape((width // PAIR, 2, count), jnp.float32),
+            shape((count, width), jnp.float32),
+            shape((count, width), jnp.float32),
+            shape((count, 128), jnp.float32),
+        ],
+        in_specs=[SCALARS, VECTORS, VECTORS, ANYWHERE],
+        out_specs=[VECTORS] * 7,
+        scratch_shapes=[
+            pltpu.VMEM(weight.shape, LOW),
+            pltpu.VMEM((count, count), jnp.float32),
+            pltpu.VMEM((count, width), jnp.float32),
+            pltpu.SemaphoreType.DMA((4,)),
+        ],
+        cost_estimate=pl.CostEstimate(
+            flops=2 * count * weight.size + 4 * count * count * width,
+            bytes_accessed=2 * weight.size + 20 * count * width,
+            transcendentals=count * count * width // HEAD_DIM,
+        ),
+        compiler_params=pltpu.CompilerParams(vmem_limit_bytes=32 * 2**20),
+    )(lengths, rows, norm, weight)
+
+
+def ffn_forward_kernel(
+    hidden_ref,
+    norm_ref,
+    up_ref,
+    down_ref,
+    low_ref,
+    active_ref,
+    slope_ref,
+    unit_ref,
+    inverse_ref,
+    out_ref,
+    held_up,
+    held_down,
+    sum_ref,
+    up_sem,
+    down_sem,
+):
+    count, _ = hidden_ref.shape
+    tiles = up_ref.shape[1] // FF_TILE
+    for tile in range(tiles):
+        column_copy(up_ref, held_up, up_sem, tile, FF_TILE).start()
+        column_copy(down_ref, held_down, down_sem, tile, FF_TILE).start()
+    low_ref[...] = hidden_ref[...].astype(LOW)
+    sum_ref[...] = hidden_ref[...]
+    for tile in range(tiles):
+        part = pl.ds(tile * FF_TILE, FF_TILE)
+        column_copy(up_ref, held_up, up_sem, tile, FF_TILE).wait()
+        inner = product(low_ref[...], held_up[:, part])
+        square = inner * inner
+        bend = jnp.tanh(GELU_RATE * inner * (1.0 + 0.044715 * square))
+        rise = 0.5 + 0.5 * bend
+        active = (inner * rise).astype(LOW)
+        active_ref[:, part] = active
+        slope = rise + (0.5 * GELU_RATE) * inner * (1.0 - bend * bend) * (
+            1.0 + 3 * 0.044715 * square
         )
-
-    return merge_heads(lax.map(one_group, head_parts(qkv_rows)))
-
-
-def attend_back(qkv_rows, grad_mixed, same_seq):
-    query_all, key_all, value_all = head_parts(qkv_rows)
-
-    def one_group(group_item):
-        query_rows, key_rows, value_rows, grad_rows = group_item
-        softmax_rows = softmax_of(query_rows, key_rows, same_seq)
-        grad_probs = jnp.einsum(
-            "qhd,khd->hqk", grad_rows, value_rows, preferred_element_type=jnp.float32
+        slope_ref[:, part] = slope.astype(LOW)
+        column_copy(down_ref, held_down, down_sem, tile, FF_TILE).wait()
+        sum_ref[...] += product(active, held_down[:, part], 1, 1)
+
+    def norm_rows(block):
+        unit, inverse, values = normalize(sum_ref[block, :], norm_ref[2:3], norm_ref[3:4])
+        out_ref[block, :] = values.astype(out_ref.dtype)
+        unit_ref[block, :] = unit
+        inverse_ref[block, :] = jnp.broadcast_to(inverse, (ROWS, 128))
+
+    row_blocks(count, norm_rows)
+
+
+def ffn_forward(hidden, norm, up, down, out_type):
+    count, width = hidden.shape
+    inner = up.shape[1]
+    tiles = inner // FF_TILE
+    shape = jax.ShapeDtypeStruct
+    return pl.pallas_call(
+        ffn_forward_kernel,
+        out_shape=[
+            shape((count, width), LOW),
+            shape((count, inner), LOW),
+            shape((count, inner), LOW),
+            shape((count, width), jnp.float32),
+            shape((count, 128), jnp.float32),
+            shape((count, width), out_type),
+        ],
+        in_specs=[VECTORS, VECTORS, ANYWHERE, ANYWHERE],
+        out_specs=[VECTORS] * 6,
+        scratch_shapes=[
+            pltpu.VMEM(up.shape, LOW),
+            pltpu.VMEM(down.shape, LOW),
+            pltpu.VMEM((count, width), jnp.float32),
+            pltpu.SemaphoreType.DMA((tiles,)),
+            pltpu.SemaphoreType.DMA((tiles,)),
+        ],
+        cost_estimate=pl.CostEstimate(
+            flops=4 * count * up.size,
+            bytes_accessed=4 * up.size + 4 * count * inner + 16 * count * width,
+            transcendentals=count * inner,
+        ),
+        compiler_params=pltpu.CompilerParams(vmem_limit_bytes=48 * 2**20),
+    )(hidden, norm, up, down)
+
+
+def ffn_backward_kernel(
+    grad_ref,
+    unit2_ref,
+    inverse2_ref,
+    slope_ref,
+    unit1_ref,
+    inverse1_ref,
+    norm_ref,
+    up_ref,
+    down_ref,
+    out_low_ref,
+    inner_low_ref,
+    first_ref,
+    first_low_ref,
+    norm_grad_ref,
+    held_up,
+    held_down,
+    sum_ref,
+    up_sem,
+    down_sem,
+):
+    count, _ = grad_ref.shape
+    tiles = up_ref.shape[1] // FF_TILE
+    for tile in range(tiles):
+        column_copy(down_ref, held_down, down_sem, tile, FF_TILE).start()
+        column_copy(up_ref, held_up, up_sem, tile, FF_TILE).start()
+    norm_grad_ref[...] = jnp.zeros_like(norm_grad_ref)
+
+    def second_norm(block):
+        grad, unit = grad_ref[block, :], unit2_ref[block, :]
+        norm_grad_ref[2:3] += jnp.sum(grad * unit, axis=0, keepdims=True)
+        norm_grad_ref[3:4] += jnp.sum(grad, axis=0, keepdims=True)
+        second = normalize_back(grad, unit, inverse2_ref[block, 0:1], norm_ref[2:3])
+        sum_ref[block, :] = second
+        out_low_ref[block, :] = second.astype(LOW)
+
+    row_blocks(count, second_norm)
+    for tile in range(tiles):
+        part = pl.ds(tile * FF_TILE, FF_TILE)
+        column_copy(down_ref, held_down, down_sem, tile, FF_TILE).wait()
+        active = product(out_low_ref[...], held_down[:, part])
+        inner = (active * slope_ref[:, part].astype(jnp.float32)).astype(LOW)
+        inner_low_ref[:, part] = inner
+        column_copy(up_ref, held_up, up_sem, tile, FF_TILE).wait()
+        sum_ref[...] += product(inner, held_up[:, part], 1, 1)
+
+    def first_norm(block):
+        grad, unit = sum_ref[block, :], unit1_ref[block, :]
+        norm_grad_ref[0:1] += jnp.sum(grad * unit, axis=0, keepdims=True)
+        norm_grad_ref[1:2] += jnp.sum(grad, axis=0, keepdims=True)
+        first = normalize_back(grad, unit, inverse1_ref[block, 0:1], norm_ref[0:1])
+        first_ref[block, :] = first
+        first_low_ref[block, :] = first.astype(LOW)
+
+    row_blocks(count, first_norm)
+
+
+def ffn_backward(grad, unit2, inverse2, slope, unit1, inverse1, norm, up, down):
+    count, width = grad.shape
+    inner = up.shape[1]
+    tiles = inner // FF_TILE
+    shape = jax.ShapeDtypeStruct
+    return pl.pallas_call(
+        ffn_backward_kernel,
+        out_shape=[
+            shape((count, width), LOW),
+            shape((count, inner), LOW),
+            shape((count, width), jnp.float32),
+            shape((count, width), LOW),
+            shape(norm.shape, jnp.float32),
+        ],
+        in_specs=[VECTORS] * 7 + [ANYWHERE] * 2,
+        out_specs=[VECTORS] * 5,
+        scratch_shapes=[
+            pltpu.VMEM(up.shape, LOW),
+            pltpu.VMEM(down.shape, LOW),
+            pltpu.VMEM((count, width), jnp.float32),
+            pltpu.SemaphoreType.DMA((tiles,)),
+            pltpu.SemaphoreType.DMA((tiles,)),
+        ],
+        cost_estimate=pl.CostEstimate(
+            flops=4 * count * up.size,
+            bytes_accessed=4 * up.size + 4 * count * inner + 20 * count * width,
+            transcendentals=0,
+        ),
+        compiler_params=pltpu.CompilerParams(vmem_limit_bytes=48 * 2**20),
+    )(grad, unit2, inverse2, slope, unit1, inverse1, norm, up, down)
+
+
+def attend_backward_kernel(
+    lengths_ref,
+    first_ref,
+    first_low_ref,
+    qkv_ref,
+    lse_ref,
+    weight_ref,
+    qkv_grad_ref,
+    rows_grad_ref,
+    held_ref,
+    mask_ref,
+    mixed_ref,
+    sem,
+):
+    count, width = first_ref.shape
+    chunks = [column_copy(weight_ref, held_ref, sem, k, width) for k in range(4)]
+    for copy in reversed(chunks):
+        copy.start()
+    fill_mask(lengths_ref, mask_ref)
+    chunks[3].wait()
+    tiles = width // TILE
+
+    def back_out(tile, carry):
+        part = columns(tile, TILE)
+        mixed_ref[:, part] = product(
+            first_low_ref[...], held_ref[part, pl.ds(3 * width, width)], 1, 1
+        ).astype(LOW)
+        return carry
+
+    lax.fori_loop(0, tiles, back_out, 0)
+
+    def one_pair(pair, carry):
+        query_part = columns(pair, PAIR)
+        key_part = columns(width // PAIR + pair, PAIR)
+        value_part = columns(2 * width // PAIR + pair, PAIR)
+        query = qkv_ref[:, query_part] * jnp.asarray(SCALE, LOW)
+        key = qkv_ref[:, key_part]
+        value = qkv_ref[:, value_part]
+        grad = mixed_ref[:, query_part]
+        lse = lse_ref[pair]
+        key_grads, value_grads, query_grads = [], [], []
+        for half in (0, 1):
+            lanes = half_lanes(count, half)
+            own_query = jnp.where(lanes, query, jnp.zeros_like(query))
+            own_grad = jnp.where(lanes, grad, jnp.zeros_like(grad))
+            scores = product(key, own_query, 1, 1) + mask_ref[...]
+            weights = jnp.exp(scores - lse[half : half + 1])
+            weight_grad = product(value, own_grad, 1, 1)
+            value_grads.append(product(weights.astype(LOW), grad))
+            along = jnp.sum(weights * weight_grad, axis=0, keepdims=True)
+            low = (weights * (weight_grad - along)).astype(LOW)
+            key_grads.append(product(low, query))
+            back = product(key, low, 0, 0)
+            query_grads.append(back[half * HEAD_DIM : (half + 1) * HEAD_DIM])
+        lanes = half_lanes(count, 1)
+        query_grad = jnp.concatenate(query_grads, axis=0).T * SCALE
+        qkv_grad_ref[:, query_part] = query_grad.astype(LOW)
+        qkv_grad_ref[:, key_part] = jnp.where(lanes, key_grads[1], key_grads[0]).astype(LOW)
+        qkv_grad_ref[:, value_part] = jnp.where(lanes, value_grads[1], value_grads[0]).astype(LOW)
+        return carry
+
+    lax.fori_loop(0, width // PAIR, one_pair, 0)
+    for k in range(3):
+        chunks[k].wait()
+
+    def back_in(tile, carry):
+        part = columns(tile, TILE)
+        rows_grad_ref[:, part] = first_ref[:, part] + product(
+            qkv_grad_ref[...], held_ref[part, pl.ds(0, 3 * width)], 1, 1
         )
-        grad_value = jnp.einsum(
-            "hqk,qhd->khd",
-            softmax_rows.astype(jnp.bfloat16),
-            grad_rows,
-            preferred_element_type=jnp.float32,
-        )
-        grad_scores = softmax_rows * (
-            grad_probs - jnp.sum(softmax_rows * grad_probs, axis=-1, keepdims=True)
-        )
-        grad_low = grad_scores.astype(jnp.bfloat16)
-        grad_query = jnp.einsum(
-            "hqk,khd->qhd", grad_low, key_rows, preferred_element_type=jnp.float32
-        ) * HEAD_DIM ** (-0.5)
-        grad_key = jnp.einsum(
-            "hqk,qhd->khd", grad_low, query_rows, preferred_element_type=jnp.float32
-        ) * HEAD_DIM ** (-0.5)
-        return (grad_query, grad_key, grad_value)
-
-    grad_query, grad_key, grad_value = lax.map(
-        one_group, (query_all, key_all, value_all, split_heads(grad_mixed))
-    )
-    return jnp.concatenate(
-        [merge_heads(grad_query), merge_heads(grad_key), merge_heads(grad_value)], axis=1
-    ).astype(jnp.bfloat16)
-
-
-def layer_states(rows_in, weights, same_seq):
-    att_full, ffn_full, norm_full = weights
-    model_width = att_full.shape[0]
-    norm_values = norm_full.astype(jnp.float32)
-    rows_low = rows_in.astype(jnp.bfloat16)
-    qkv_rows = jnp.dot(
-        rows_low, att_full[:, : 3 * model_width], preferred_element_type=jnp.float32
-    ).astype(jnp.bfloat16)
-    mixed_rows = attend(qkv_rows, same_seq).astype(jnp.bfloat16)
-    branch = jnp.dot(mixed_rows, att_full[:, 3 * model_width :], preferred_element_type=jnp.float32)
-    first_sum = rows_in + branch
-    hidden = normalize(first_sum, norm_values[0], norm_values[1])
-    hidden_low = hidden.astype(jnp.bfloat16)
-    inner_rows = jnp.dot(hidden_low, ffn_full[0], preferred_element_type=jnp.float32)
-    active = gelu_tanh(inner_rows).astype(jnp.bfloat16)
-    second = hidden + jnp.einsum(
-        "tf,df->td", active, ffn_full[1], preferred_element_type=jnp.float32
-    )
-    return (rows_low, qkv_rows, mixed_rows, first_sum, hidden_low, inner_rows, active, second)
-
-
-def layer_back(states, weights, same_seq, grad_out):
-    att_full, ffn_full, norm_full = weights
-    model_width = att_full.shape[0]
-    norm_values = norm_full.astype(jnp.float32)
-    rows_low, qkv_rows, mixed_rows, first_sum, hidden_low, inner_rows, active, second = (
-        states
-    )
-    second_value, second_back = jax.vjp(normalize, second, norm_values[2], norm_values[3])
-    grad_second, grad_gain2, grad_bias2 = second_back(grad_out)
-    grad_ffn_out = grad_second.astype(jnp.bfloat16)
-    grad_active = jnp.dot(grad_ffn_out, ffn_full[1], preferred_element_type=jnp.float32)
-    gelu_value, gelu_back = jax.vjp(gelu_tanh, inner_rows)
-    grad_inner = gelu_back(grad_active)[0].astype(jnp.bfloat16)
-    grad_hidden = grad_second + jnp.einsum(
-        "tf,df->td", grad_inner, ffn_full[0], preferred_element_type=jnp.float32
-    )
-    first_value, first_back = jax.vjp(normalize, first_sum, norm_values[0], norm_values[1])
-    grad_first, grad_gain1, grad_bias1 = first_back(grad_hidden)
-    grad_branch = grad_first.astype(jnp.bfloat16)
-    grad_mixed = jnp.einsum(
-        "te,de->td", grad_branch, att_full[:, 3 * model_width :], preferred_element_type=jnp.float32
-    ).astype(jnp.bfloat16)
-    grad_qkv = attend_back(qkv_rows, grad_mixed, same_seq)
-    grad_rows = grad_first + jnp.einsum(
-        "te,de->td", grad_qkv, att_full[:, : 3 * model_width], preferred_element_type=jnp.float32
-    )
-    factors = (
-        (grad_ffn_out, active),
-        (hidden_low, grad_inner),
-        (mixed_rows, grad_branch),
-        (rows_low, grad_qkv),
-    )
-    return (grad_rows, factors, jnp.stack([grad_gain1, grad_bias1, grad_gain2, grad_bias2]))
+        return carry
+
+    lax.fori_loop(0, tiles, back_in, 0)
+
+
+def attend_backward(lengths, first, first_low, qkv, lse, weight):
+    count, width = first.shape
+    shape = jax.ShapeDtypeStruct
+    return pl.pallas_call(
+        attend_backward_kernel,
+        out_shape=[shape((count, 3 * width), LOW), shape((count, width), jnp.float32)],
+        in_specs=[SCALARS] + [VECTORS] * 4 + [ANYWHERE],
+        out_specs=[VECTORS] * 2,
+        scratch_shapes=[
+            pltpu.VMEM(weight.shape, LOW),
+            pltpu.VMEM((count, count), jnp.float32),
+            pltpu.VMEM((count, width), LOW),
+            pltpu.SemaphoreType.DMA((4,)),
+        ],
+        cost_estimate=pl.CostEstimate(
+            flops=2 * count * weight.size + 10 * count * count * width,
+            bytes_accessed=2 * weight.size + 24 * count * width,
+            transcendentals=count * count * width // HEAD_DIM,
+        ),
+        compiler_params=pltpu.CompilerParams(vmem_limit_bytes=32 * 2**20),
+    )(lengths, first, first_low, qkv, lse, weight)
+
+
+def weight_sum_kernel(picker_ref, left_a, left_b, right_a, right_b, send_ref, keep_ref, turned):
+    count = left_a.shape[0]
+    half = send_ref.shape[0]
+
+    @pl.when(pl.program_id(0) == 0)
+    def _():
+        for layer, left in enumerate((left_a, left_b)):
+            turned[:, layer * count : (layer + 1) * count] = product(
+                picker_ref[...], left[...], 1, 1
+            ).astype(LOW)
+
+    right = jnp.concatenate([right_a[...], right_b[...]], axis=0)
+    for block in range(2 * half // TILE):
+        rows = slice(block * TILE, (block + 1) * TILE)
+        total = product(turned[rows], right).astype(LOW)
+        if block * TILE < half:
+            send_ref[rows] = total
+        else:
+            keep_ref[block * TILE - half : (block + 1) * TILE - half] = total
 
 
 def weight_sum(layer_pairs, picker):
-    left = jnp.concatenate([pair[0] for pair in layer_pairs])
-    right = jnp.concatenate([pair[1] for pair in layer_pairs])
-    left = jnp.dot(left, picker, preferred_element_type=jnp.float32).astype(jnp.bfloat16)
-    return [
-        jnp.einsum("td,tf->df", part, right, preferred_element_type=jnp.float32).astype(jnp.bfloat16)
-        for part in jnp.split(left, 2, axis=1)
-    ]
+    (left_a, right_a), (left_b, right_b) = layer_pairs
+    count, rows = left_a.shape
+    wide = right_a.shape[1]
+    whole = pl.BlockSpec((count, rows), lambda tile: (0, 0))
+    right = pl.BlockSpec((count, FF_TILE), lambda tile: (0, tile))
+    out = pl.BlockSpec((rows // 2, FF_TILE), lambda tile: (0, tile))
+    return pl.pallas_call(
+        weight_sum_kernel,
+        grid=(wide // FF_TILE,),
+        out_shape=[jax.ShapeDtypeStruct((rows // 2, wide), LOW)] * 2,
+        in_specs=[
+            pl.BlockSpec((rows, rows), lambda tile: (0, 0)),
+            whole,
+            whole,
+            right,
+            right,
+        ],
+        out_specs=[out, out],
+        scratch_shapes=[pltpu.VMEM((rows, 2 * count), LOW)],
+        cost_estimate=pl.CostEstimate(
+            flops=4 * count * rows * (wide + rows),
+            bytes_accessed=2 * rows * (wide + rows) + 4 * count * (wide + rows),
+            transcendentals=0,
+        ),
+        compiler_params=pltpu.CompilerParams(vmem_limit_bytes=32 * 2**20),
+    )(picker, left_a, left_b, right_a, right_b)
 
 
 AXES = ("dp", "fsdp")
@@ -298,8 +632,8 @@
 
 
 def row_picker(owners, shard):
-    rows = (jnp.stack(owners)[:, None] * shard + jnp.arange(shard)[None, :]).reshape(1, -1)
-    return (jnp.arange(rows.size)[:, None] == rows).astype(jnp.bfloat16)
+    rows = (jnp.stack(owners)[:, None] * shard + jnp.arange(shard)[None, :]).reshape(-1, 1)
+    return (rows == jnp.arange(rows.size)[None, :]).astype(jnp.bfloat16)
 
 
 def add_low(left, right):
@@ -393,11 +727,7 @@
 ):
     row_count = tokens.shape[0]
     lengths = [seq_lengths[0, slot] for slot in range(seq_lengths.shape[1])]
-    seq_ends = jnp.stack([sum(lengths[: slot + 1]) for slot in range(len(lengths))])
-    position = jnp.arange(row_count, dtype=jnp.int32)
-    segment = jnp.sum((position[:, None] >= seq_ends[None, :]).astype(jnp.int32), axis=1)
-    same_seq = segment[:, None] == segment[None, :]
-    live_rows = (position < seq_ends[-1]).astype(jnp.float32)[:, None]
+    live_rows = (jnp.arange(row_count) < sum(lengths)).astype(jnp.float32)[:, None]
     route = Route()
     shard = att_master.shape[0]
     norm_piece = jnp.pad(norm_master.T, ((0, 0), (0, NORM_COLS - norm_master.shape[0])))
@@ -417,20 +747,39 @@
             for piece in (att_piece, ffn_pieces[0], ffn_pieces[1])
         ]
         att_full, norm_full, up_full, down_full = whole[0][:, :width], whole[0][:, width:], *whole[1:]
-    weights = (att_full, (up_full, down_full), norm_full[:, : norm_master.shape[0]].T)
-    norm_values = weights[2].astype(jnp.float32)
+    norm_values = norm_full[:, : norm_master.shape[0]].T.astype(jnp.float32)
     stored = []
-    current = tokens.astype(jnp.float32)
+    current = tokens
     for depth in range(LAYERS):
-        stored.append(layer_states(current, weights, same_seq))
-        current = normalize(stored[depth][7], norm_values[2], norm_values[3])
+        low, qkv, mixed, lse, hidden, unit1, inverse1 = attend_forward(
+            seq_lengths, current, norm_values, att_full
+        )
+        hidden_low, active, slope, unit2, inverse2, current = ffn_forward(
+            hidden,
+            norm_values,
+            up_full,
+            down_full,
+            jnp.bfloat16 if depth == LAYERS - 1 else jnp.float32,
+        )
+        stored.append(
+            (low, qkv, mixed, lse, unit1, inverse1, hidden_low, active, slope, unit2, inverse2)
+        )
     grad_now = cotangent.astype(jnp.float32) * live_rows
-    factors, norm_term = [], 0.0
+    downs, ups, projs, inprojs = [], [], [], []
+    norm_term = 0.0
     for depth in reversed(range(LAYERS)):
-        grad_now, pairs, norm_part = layer_back(stored[depth], weights, same_seq, grad_now)
-        factors.append(pairs)
+        low, qkv, mixed, lse, unit1, inverse1, hidden_low, active, slope, unit2, inverse2 = stored[
+            depth
+        ]
+        out_low, inner_low, first, first_low, norm_part = ffn_backward(
+            grad_now, unit2, inverse2, slope, unit1, inverse1, norm_values, up_full, down_full
+        )
+        qkv_low, grad_now = attend_backward(seq_lengths, first, first_low, qkv, lse, att_full)
         norm_term = norm_term + norm_part
-    downs, ups, projs, inprojs = zip(*factors)
+        downs.append((out_low, active))
+        ups.append((hidden_low, inner_low))
+        projs.append((mixed, first_low))
+        inprojs.append((low, qkv_low))
     middle = row_picker(owners_ring_middle(route), shard)
     last = row_picker(owners_ring_last(route), shard)
     scatter_middle, scatter_last = scatter_ring_middle, scatter_ring_last
@@ -441,7 +790,7 @@
     up_share = scatter_middle(route, *weight_sum(ups, middle))
     norm_rows = jnp.pad(norm_term.T, ((0, 0), (0, NORM_COLS - norm_term.shape[0])))
     norm_rows = jnp.einsum(
-        "dr,dn->rn", last, norm_rows.astype(jnp.bfloat16), preferred_element_type=jnp.float32
+        "rd,dn->rn", last, norm_rows.astype(jnp.bfloat16), preferred_element_type=jnp.float32
     ).astype(jnp.bfloat16)
     att_parts = zip(weight_sum(inprojs, last), weight_sum(projs, last), jnp.split(norm_rows, 2))
     att_halves = [jnp.concatenate(parts, axis=1) for parts in att_parts]
@@ -456,7 +805,7 @@
     ffn_out = update(totals[1], ffn_master, ffn_moment, ffn_average, step_rate)
     norm_out = update(totals[2], norm_master, norm_moment, norm_average, step_rate)
     return (
-        current.astype(jnp.bfloat16),
+        current,
         grad_now,
         att_out[0],
         att_out[1],

time: 585 us -> 506 us (0.86)
  matrix products: 196 us -> 0.83 us
  Pallas kernels: 14.4 us -> 147 us
  waiting for transfers between devices: 188 us -> 216 us
  local copies, waits for them, and re-layouts: 79.5 us -> 58.3 us
  other arithmetic: 52.6 us -> 36.9 us
    dot_general x77 -> x1, matrix products: 184 us -> 0.83 us  [shards(): jnp.einsum('rd,dn->rn', last, norm_rows.astype(jnp.bfloat16), preferred_e...]
    pallas_call x0 -> x12, Pallas kernels: none -> 132 us  [the longest x2 30.4 us: attend_forward(): pl.pallas_call(attend_forward_kernel, out_shape=[shape((count, width), LO...]
    ppermute x66, waiting for transfers between devices: 188 us -> 216 us  [move(): return lax.ppermute(array, AXES, pairs)]
    sub x16 -> x0, matrix products: 12.3 us -> none  [softmax_of(): weights = jnp.exp(scores - row_peak)]
    while x64 -> x0, local copies, waits for them, and re-layouts: 11 us -> none
    unnamed x204 -> x182, local copies, waits for them, and re-layouts: 47.8 us -> 56.6 us
    another operation x9 -> x1, local copies, waits for them, and re-layouts: 6.9 us -> 0.1 us
  transfers between devices with their start and end apart: 66 -> 66, of which waited for: 27 -> 23; matrix products, arithmetic and copies ran while one was open for 28% -> 7% of each run, Pallas kernels for 2% -> 11%
where the time goes in v3:
time: 506 us; the launch traced here: 500 us
  waiting for transfers between devices  216 us (43%)
  Pallas kernels  147 us (29%)
  local copies, waits for them, and re-layouts  58.3 us (12%)
  other arithmetic  36.9 us (7%)
  starting transfers between devices  36.8 us (7%)
    ppermute x66, waiting for transfers between devices, move(): return lax.ppermute(array, AXES, pairs)  216 us
    unnamed x182, local copies, waits for them, and re-layouts  56.6 us
    ppermute x66, starting transfers between devices, move(): return lax.ppermute(array, AXES, pairs)  36.8 us
    pallas_call x2, Pallas kernels, attend_forward(): pl.pallas_call(attend_forward_kernel, out_shape=[shape((count, width), LO...  30.4 us
    pallas_call x2, Pallas kernels, attend_backward(): pl.pallas_call(attend_backward_kernel, out_shape=[shape((count, 3 * width...  28.1 us
    pallas_call x4, Pallas kernels, weight_sum(): pl.pallas_call(weight_sum_kernel, grid=(wide // FF_TILE,), out_shape=[jax...  25.9 us
    pallas_call x2, Pallas kernels, ffn_forward(): pl.pallas_call(ffn_forward_kernel, out_shape=[shape((count, width), LOW),...  24.6 us
    pallas_call x2, Pallas kernels, ffn_backward(): pl.pallas_call(ffn_backward_kernel, out_shape=[shape((count, width), LOW)...  23 us
  transfers between devices with their start and end apart: 66, of which 23 were waited for; matrix products, arithmetic and copies ran while one was open for 7% of the time, Pallas kernels for 11%

profile of v3, /device:TPU:0, one launch (start us, length us, event | category | flops | bytes accessed | tf_op | source)
XLA Modules:
  0.0 500.2 jit_solution(1694235845920307937)
XLA Ops:
  16.3 8.1 %collective-permute-done.33 = bf16[32,4096]{1,0:T(8,128)(2,1)S(1)} collective-permute-done((bf16[32,4096]{1,0:T(8,128)(2,1)S(1)}, bf16[32,4096]{1,0:T(8,128)(2,1)S(1)}, u32[]{:S(2)}, u32[]{:S(2)}) %collective-permute-start.33) | collective-permute-done | bytes 262176 | tf_op jit(solution)/shard_map/ppermute | solution.py:531
  24.6 16.7 %collective-permute-done.34 = bf16[32,4096]{1,0:T(8,128)(2,1)S(1)} collective-permute-done((bf16[32,4096]{1,0:T(8,128)(2,1)S(1)}, bf16[32,4096]{1,0:T(8,128)(2,1)S(1)}, u32[]{:S(2)}, u32[]{:S(2)}) %collective-permute-start.34) | collective-permute-done | bytes 262176 | tf_op jit(solution)/shard_map/ppermute | solution.py:531
  44.2 8.7 %collective-permute-done.4.refs_4_ = bf16[64,4224]{1,0:T(8,128)(2,1)S(1)} collective-permute-done((bf16[64,4224]{1,0:T(8,128)(2,1)S(1)}, bf16[64,4224]{1,0:T(8,128)(2,1)S(1)}, u32[]{:S(2)}, u32[]{:S(2)}) %collective-permute-start.4) | collective-permute-done | bytes 540704 | tf_op jit(solution)/shard_map/ppermute | solution.py:531
  56.9 7.3 %collective-permute-done.24.refs_8_ = bf16[64,4096]{1,0:T(8,128)(2,1)} collective-permute-done((bf16[64,4096]{1,0:T(8,128)(2,1)S(1)}, bf16[64,4096]{1,0:T(8,128)(2,1)}, u32[]{:S(2)}, u32[]{:S(2)}) %collective-permute-start.24) | collective-permute-done | bytes 524320 | tf_op jit(solution)/shard_map/ppermute | solution.py:531
  69.1 5.0 collective-permute-done.8.refs_8_
  74.1 17.6 %collective-permute-done.5.refs_5_ = bf16[64,4224]{1,0:T(8,128)(2,1)S(1)} collective-permute-done((bf16[64,4224]{1,0:T(8,128)(2,1)S(1)}, bf16[64,4224]{1,0:T(8,128)(2,1)S(1)}, u32[]{:S(2)}, u32[]{:S(2)}) %collective-permute-start.5) | collective-permute-done | bytes 540704 | tf_op jit(solution)/shard_map/ppermute | solution.py:531
  95.3 13.2 %collective-permute-done.28.refs_12_ = bf16[64,4096]{1,0:T(8,128)(2,1)} collective-permute-done((bf16[64,4096]{1,0:T(8,128)(2,1)}, bf16[64,4096]{1,0:T(8,128)(2,1)}, u32[]{:S(2)}, u32[]{:S(2)}) %collective-permute-start.28) | collective-permute-done | bytes 524320 | tf_op jit(solution)/shard_map/ppermute | solution.py:531
  111.3 8.5 %collective-permute-done.12.refs_12_ = bf16[64,4224]{1,0:T(8,128)(2,1)} collective-permute-done((bf16[64,4224]{1,0:T(8,128)(2,1)}, bf16[64,4224]{1,0:T(8,128)(2,1)}, u32[]{:S(2)}, u32[]{:S(2)}) %collective-permute-start.12) | collective-permute-done | bytes 540704 | tf_op jit(solution)/shard_map/ppermute | solution.py:531
  129.6 11.3 %collective-permute-done.13.refs_13_ = bf16[64,4224]{1,0:T(8,128)(2,1)} collective-permute-done((bf16[64,4224]{1,0:T(8,128)(2,1)}, bf16[64,4224]{1,0:T(8,128)(2,1)}, u32[]{:S(2)}, u32[]{:S(2)}) %collective-permute-start.13) | collective-permute-done | bytes 540704 | tf_op jit(solution)/shard_map/ppermute | solution.py:531
  158.6 4.7 shard_map.251
  171.4 15.1 %shard_map.252 = (bf16[256,1024]{1,0:T(8,128)(2,1)S(1)}, bf16[256,3072]{1,0:T(8,128)(2,1)S(1)}, bf16[256,1024]{1,0:T(8,128)(2,1)S(1)}, f32[8,2,256]{2,1,0:T(2,12...) custom-call(s32[1,4]{1,0:T(1,128)S(1)} %copy-done.45, ...), custom_call_target="tpu_custom_call" | custom-call | flops 2415919104 | bytes 13631488 | tf_op jit(solution)/shard_map/pallas_call | solution.py:158
  188.2 5.8 %shard_map.254.down_ref = bf16[1024,4096]{1,0:T(8,128)(2,1)S(1)} custom-call(s32[32]{0:T(128)S(1)} %stack.127.owners_ref, bf16[128,4096]{1,0:T(8,128)(2,1)S(1)} %pad_maximum_fusion.2.refs_0_, bf16[128,4096]{1,0:T(8,128)(2,1)} %collective-permute-done.35.refs_1_, bf16[128,4096]{1,0:T(8,128)(2,1)} %collective-permute-done.36.refs_2_, ...), custom_call_target="tpu_custom_call" | custom-call | bytes 16777216 | tf_op jit(solution)/shard_map/pallas_call | solution.py:618
  197.3 12.2 %shard_map.255 = (bf16[256,1024]{1,0:T(8,128)(2,1)S(1)}, bf16[256,4096]{1,0:T(8,128)(2,1)S(1)}, bf16[256,4096]{1,0:T(8,128)(2,1)}, f32[256,1024]{1,0:T(8,128)S(1...) custom-call(f32[256,1024]{1,0:T(8,128)S(1)} %get-tuple-element.69.hidden_ref, ...), custom_call_target="tpu_custom_call" | custom-call | flops 4294967296 | bytes 25165824 | tf_op jit(solution)/shard_map/pallas_call | solution.py:240
  211.7 15.3 %shard_map.256 = (bf16[256,1024]{1,0:T(8,128)(2,1)S(1)}, bf16[256,3072]{1,0:T(8,128)(2,1)S(1)}, bf16[256,1024]{1,0:T(8,128)(2,1)S(1)}, f32[8,2,256]{2,1,0:T(2,12...) custom-call(s32[1,4]{1,0:T(1,128)S(1)} %copy-done.45, ...), custom_call_target="tpu_custom_call" | custom-call | flops 2415919104 | bytes 13631488 | tf_op jit(solution)/shard_map/pallas_call | solution.py:158
  228.9 12.4 %shard_map.257 = (bf16[256,1024]{1,0:T(8,128)(2,1)S(1)}, bf16[256,4096]{1,0:T(8,128)(2,1)S(1)}, bf16[256,4096]{1,0:T(8,128)(2,1)}, f32[256,1024]{1,0:T(8,128)S(1...) custom-call(f32[256,1024]{1,0:T(8,128)S(1)} %get-tuple-element.71.hidden_ref, ...), custom_call_target="tpu_custom_call" | custom-call | flops 4294967296 | bytes 25165824 | tf_op jit(solution)/shard_map/pallas_call | solution.py:240
  247.3 11.4 %shard_map.258 = (bf16[256,1024]{1,0:T(8,128)(2,1)S(1)}, bf16[256,4096]{1,0:T(8,128)(2,1)}, f32[256,1024]{1,0:T(8,128)S(1)}, bf16[256,1024]{1,0:T(8,128)(2,1)S(1)}, f32[4,1024]{1,0:T(4,128)S(1)}) custom-call(f32[256,1024]{1,0:T(8,128)S(1)} %convert_multiply_fusion.grad_ref, f32[256,1024]{1,0:T(8,128)S(1)} %copy-done.20, f32[256,128]{1,0:T(8,128)S(1)} %copy-done.44, ...), custom_call_target="tpu_custom_call" | custom-call | flops 4294967296 | bytes 26214400 | tf_op jit(solution)/shard_map/pallas_call | solution.py:330
  260.9 13.7 %shard_map.259 = (bf16[256,3072]{1,0:T(8,128)(2,1)S(1)}, f32[256,1024]{1,0:T(8,128)S(1)}) custom-call(s32[1,4]{1,0:T(1,128)S(1)} %copy-done.45, f32[256,1024]{1,0:T(8,128)S(1)} %get-tuple-element.78.first_ref, bf16[256,1024]{1,0:T(8,128)(2,1)S(1)} %get-tuple-element.79.first_low_ref.right_a, bf16[256,3072]{1,0:T(8,128)(2,1)S(1)} %copy-done.13, ...), custom_call_target="tpu_custom_call" | custom-call | flops 2818572288 | bytes 14680064 | tf_op jit(solution)/shard_map/pallas_call | solution.py:435
  275.8 11.6 %shard_map.260 = (bf16[256,1024]{1,0:T(8,128)(2,1)S(1)}, bf16[256,4096]{1,0:T(8,128)(2,1)}, f32[256,1024]{1,0:T(8,128)S(1)}, bf16[256,1024]{1,0:T(8,128)(2,1)S(1)}, f32[4,1024]{1,0:T(4,128)S(1)}) custom-call(f32[256,1024]{1,0:T(8,128)S(1)} %get-tuple-element.82.grad_ref, f32[256,1024]{1,0:T(8,128)S(1)} %copy-done.17, ...), custom_call_target="tpu_custom_call" | custom-call | flops 4294967296 | bytes 26214400 | tf_op jit(solution)/shard_map/pallas_call | solution.py:330
  292.6 8.2 %shard_map.264 = (bf16[512,4096]{1,0:T(8,128)(2,1)}, bf16[512,4096]{1,0:T(8,128)(2,1)S(1)}) custom-call(bf16[1024,1024]{1,0:T(8,128)(2,1)S(1)} %copy-done.8, bf16[256,1024]{1,0:T(8,128)(2,1)S(1)} %copy-done.68, bf16[256,1024]{1,0:T(8,128)(2,1)S(1)} %copy-done.64, bf16[256,4096]{1,0:T(8,128)(2,1)S(1)} %copy-done.54, bf16[256,4096]{1,0:T(8,128)(2,1)S(1)} %copy-done.55), custom_call_target="tpu_custom_call" | custom-call | flops 5368709120 | bytes 15728640 | tf_op jit(solution)/shard_map/pallas_call | solution.py:483
  304.9 8.2 %shard_map.265 = (bf16[512,4096]{1,0:T(8,128)(2,1)}, bf16[512,4096]{1,0:T(8,128)(2,1)S(1)}) custom-call(bf16[1024,1024]{1,0:T(8,128)(2,1)S(1)} %copy-done.8, bf16[256,1024]{1,0:T(8,128)(2,1)S(1)} %copy-done.66, bf16[256,1024]{1,0:T(8,128)(2,1)S(1)} %get-tuple-element.112.left_b, bf16[256,4096]{1,0:T(8,128)(2,1)S(1)} %copy-done.53, ...), custom_call_target="tpu_custom_call" | custom-call | flops 5368709120 | bytes 15728640 | tf_op jit(solution)/shard_map/pallas_call | solution.py:483
  316.0 14.4 %shard_map.261 = (bf16[256,3072]{1,0:T(8,128)(2,1)S(1)}, f32[256,1024]{1,0:T(8,128)}) custom-call(s32[1,4]{1,0:T(1,128)S(1)} %copy-done.45, f32[256,1024]{1,0:T(8,128)S(1)} %get-tuple-element.88.first_ref, bf16[256,1024]{1,0:T(8,128)(2,1)S(1)} %get-tuple-element.89.first_low_ref.right_b, bf16[256,3072]{1,0:T(8,128)(2,1)S(1)} %copy-done.11, ...), custom_call_target="tpu_custom_call" | custom-call | flops 2818572288 | bytes 14680064 | tf_op jit(solution)/shard_map/pallas_call | solution.py:435
  330.6 6.5 %shard_map.262 = (bf16[512,3072]{1,0:T(8,128)(2,1)S(1)}, bf16[512,3072]{1,0:T(8,128)(2,1)S(1)}) custom-call(bf16[1024,1024]{1,0:T(8,128)(2,1)S(1)} %copy-done.9, bf16[256,1024]{1,0:T(8,128)(2,1)S(1)} %copy-done.62, bf16[256,1024]{1,0:T(8,128)(2,1)S(1)} %copy-done.72, bf16[256,3072]{1,0:T(8,128)(2,1)S(1)} %copy-done.57, ...), custom_call_target="tpu_custom_call" | custom-call | flops 4294967296 | bytes 12582912 | tf_op jit(solution)/shard_map/pallas_call | solution.py:483
  360.9 19.1 %collective-permute-done.61 = bf16[64,4096]{1,0:T(8,128)(2,1)S(1)} collective-permute-done((bf16[64,4096]{1,0:T(8,128)(2,1)S(1)}, bf16[64,4096]{1,0:T(8,128)(2,1)S(1)}, u32[]{:S(2)}, u32[]{:S(2)}) %collective-permute-start.61) | collective-permute-done | bytes 524320 | tf_op jit(solution)/shard_map/ppermute | solution.py:531
  382.3 12.5 %collective-permute-done.53 = bf16[64,4096]{1,0:T(8,128)(2,1)S(1)} collective-permute-done((bf16[64,4096]{1,0:T(8,128)(2,1)S(1)}, bf16[64,4096]{1,0:T(8,128)(2,1)S(1)}, u32[]{:S(2)}, u32[]{:S(2)}) %collective-permute-start.53) | collective-permute-done | bytes 524320 | tf_op jit(solution)/shard_map/ppermute | solution.py:531
  397.2 11.5 %collective-permute-done.62 = bf16[64,4096]{1,0:T(8,128)(2,1)S(1)} collective-permute-done((bf16[64,4096]{1,0:T(8,128)(2,1)S(1)}, bf16[64,4096]{1,0:T(8,128)(2,1)S(1)}, u32[]{:S(2)}, u32[]{:S(2)}) %collective-permute-start.62) | collective-permute-done | bytes 524320 | tf_op jit(solution)/shard_map/ppermute | solution.py:531
  411.1 10.6 %collective-permute-done.54 = bf16[64,4096]{1,0:T(8,128)(2,1)S(1)} collective-permute-done((bf16[64,4096]{1,0:T(8,128)(2,1)S(1)}, bf16[64,4096]{1,0:T(8,128)(2,1)S(1)}, u32[]{:S(2)}, u32[]{:S(2)}) %collective-permute-start.54) | collective-permute-done | bytes 524320 | tf_op jit(solution)/shard_map/ppermute | solution.py:531
  423.1 15.3 %collective-permute-done.63 = bf16[64,4096]{1,0:T(8,128)(2,1)S(1)} collective-permute-done((bf16[64,4096]{1,0:T(8,128)(2,1)S(1)}, bf16[64,4096]{1,0:T(8,128)(2,1)S(1)}, u32[]{:S(2)}, u32[]{:S(2)}) %collective-permute-start.63) | collective-permute-done | bytes 524320 | tf_op jit(solution)/shard_map/ppermute | solution.py:531
  439.8 9.8 %collective-permute-done.55 = bf16[64,4096]{1,0:T(8,128)(2,1)S(1)} collective-permute-done((bf16[64,4096]{1,0:T(8,128)(2,1)S(1)}, bf16[64,4096]{1,0:T(8,128)(2,1)S(1)}, u32[]{:S(2)}, u32[]{:S(2)}) %collective-permute-start.55) | collective-permute-done | bytes 524320 | tf_op jit(solution)/shard_map/ppermute | solution.py:531
  459.2 9.8 %collective-permute-done.44 = bf16[128,4224]{1,0:T(8,128)(2,1)S(1)} collective-permute-done((bf16[128,4224]{1,0:T(8,128)(2,1)S(1)}, bf16[128,4224]{1,0:T(8,128)(2,1)S(1)}, u32[]{:S(2)}, u32[]{:S(2)}) %collective-permute-start.44) | collective-permute-done | bytes 1081376 | tf_op jit(solution)/shard_map/ppermute | solution.py:531
  471.9 5.5 %collective-permute-done.45 = bf16[32,4224]{1,0:T(8,128)(2,1)S(1)} collective-permute-done((bf16[32,4224]{1,0:T(8,128)(2,1)S(1)}, bf16[32,4224]{1,0:T(8,128)(2,1)S(1)}, u32[]{:S(2)}, u32[]{:S(2)}) %collective-permute-start.45) | collective-permute-done | bytes 270368 | tf_op jit(solution)/shard_map/ppermute | solution.py:531
  479.3 6.5 %collective-permute-done.46 = bf16[32,4224]{1,0:T(8,128)(2,1)S(1)} collective-permute-done((bf16[32,4224]{1,0:T(8,128)(2,1)S(1)}, bf16[32,4224]{1,0:T(8,128)(2,1)S(1)}, u32[]{:S(2)}, u32[]{:S(2)}) %collective-permute-start.46) | collective-permute-done | bytes 270368 | tf_op jit(solution)/shard_map/ppermute | solution.py:531
  487.2 7.1 %collective-permute-done.47 = bf16[32,4224]{1,0:T(8,128)(2,1)S(1)} collective-permute-done((bf16[32,4224]{1,0:T(8,128)(2,1)S(1)}, bf16[32,4224]{1,0:T(8,128)(2,1)S(1)}, u32[]{:S(2)}, u32[]{:S(2)}) %collective-permute-start.47) | collective-permute-done | bytes 270368 | tf_op jit(solution)/shard_map/ppermute | solution.py:531
  (361 shorter events, 151.6 us)
Async XLA Ops:
  13.5 29.4 %collective-permute-start.20 = (bf16[64,4096]{1,0:T(8,128)(2,1)S(1)}, bf16[64,4096]{1,0:T(8,128)(2,1)S(1)}, u32[]{:S(2)}, u32[]{:S(2)}) collective-permute-start(bf16[64,4096]{1,0:T(8,128)(2,1)S(1)} %pad_maximum_fusion.5.refs_0_), channel_id=1, source_target_pairs={{0,8},{1,9},{2,10},{3,11},{4,12},{5,13},{6,14},{7,15},{8,16},{9,17... | collective-permute-start | bytes 1572872 | tf_op jit(solution)/shard_map/ppermute | solution.py:531
  14.8 28.0 %collective-permute-start.17 = (bf16[64,4096]{1,0:T(8,128)(2,1)S(1)}, bf16[64,4096]{1,0:T(8,128)(2,1)S(1)}, u32[]{:S(2)}, u32[]{:S(2)}) collective-permute-start(bf16[64,4096]{1,0:T(8,128)(2,1)S(1)} %pad_maximum_fusion.5.refs_0_), channel_id=1, source_target_pairs={{0,4},{1,3},{2,6},{3,1},{4,0},{5,7},{6,2},{7,5},{8,12},{9,11},{10,... | collective-permute-start | bytes 1572872 | tf_op jit(solution)/shard_map/ppermute | solution.py:531
  16.3 26.6 %collective-permute-start.18 = (bf16[64,4096]{1,0:T(8,128)(2,1)S(1)}, bf16[64,4096]{1,0:T(8,128)(2,1)S(1)}, u32[]{:S(2)}, u32[]{:S(2)}) collective-permute-start(bf16[64,4096]{1,0:T(8,128)(2,1)S(1)} %pad_maximum_fusion.5.refs_0_), channel_id=1, source_target_pairs={{0,1},{1,0},{2,3},{3,2},{4,5},{5,4},{6,7},{7,6},{8,9},{9,8},{10,11... | collective-permute-start | bytes 1572872 | tf_op jit(solution)/shard_map/ppermute | solution.py:531
  24.5 28.4 %collective-permute-start.4 = (bf16[64,4224]{1,0:T(8,128)(2,1)S(1)}, bf16[64,4224]{1,0:T(8,128)(2,1)S(1)}, u32[]{:S(2)}, u32[]{:S(2)}) collective-permute-start(bf16[64,4224]{1,0:T(8,128)(2,1)S(1)} %pad_maximum_fusion.4.refs_0_), channel_id=1, source_target_pairs={{0,8},{1,9},{2,10},{3,11},{4,12},{5,13},{6,14},{7,15},{8,16},{9,17... | collective-permute-start | bytes 1622024 | tf_op jit(solution)/shard_map/ppermute | solution.py:531
  42.8 21.4 %collective-permute-start.24 = (bf16[64,4096]{1,0:T(8,128)(2,1)S(1)}, bf16[64,4096]{1,0:T(8,128)(2,1)}, u32[]{:S(2)}, u32[]{:S(2)}) collective-permute-start(bf16[64,4096]{1,0:T(8,128)(2,1)S(1)} %collective-permute-done.20.refs_4_), channel_id=1, source_target_pairs={{0,8},{1,9},{2,10},{3,11},{4,12},{5,13},{6,14},{7,15},{8,16},{9,17... | collective-permute-start | bytes 1572872 | tf_op jit(solution)/shard_map/ppermute | solution.py:531
  43.7 21.8 %collective-permute-start.21 = (bf16[64,4096]{1,0:T(8,128)(2,1)S(1)}, bf16[64,4096]{1,0:T(8,128)(2,1)}, u32[]{:S(2)}, u32[]{:S(2)}) collective-permute-start(bf16[64,4096]{1,0:T(8,128)(2,1)S(1)} %collective-permute-done.20.refs_4_), channel_id=1, source_target_pairs={{0,4},{1,3},{2,6},{3,1},{4,0},{5,7},{6,2},{7,5},{8,12},{9,11},{10,... | collective-permute-start | bytes 1572872 | tf_op jit(solution)/shard_map/ppermute | solution.py:531
  55.8 18.3 %collective-permute-start.8 = (bf16[64,4224]{1,0:T(8,128)(2,1)S(1)}, bf16[64,4224]{1,0:T(8,128)(2,1)}, u32[]{:S(2)}, u32[]{:S(2)}) collective-permute-start(bf16[64,4224]{1,0:T(8,128)(2,1)S(1)} %collective-permute-done.4.refs_4_), channel_id=1, source_target_pairs={{0,8},{1,9},{2,10},{3,11},{4,12},{5,13},{6,14},{7,15},{8,16},{9,17... | collective-permute-start | bytes 1622024 | tf_op jit(solution)/shard_map/ppermute | solution.py:531
  64.2 30.2 %collective-permute-start.35 = (bf16[128,4096]{1,0:T(8,128)(2,1)S(1)}, bf16[128,4096]{1,0:T(8,128)(2,1)}, u32[]{:S(2)}, u32[]{:S(2)}) collective-permute-start(bf16[128,4096]{1,0:T(8,128)(2,1)S(1)} %pad_maximum_fusion.2.refs_0_), channel_id=1, source_target_pairs={{0,2},{1,5},{2,0},{3,7},{4,6},{5,1},{6,4},{7,3},{8,10},{9,13},{10,... | collective-permute-start | bytes 3145736 | tf_op jit(solution)/shard_map/ppermute | solution.py:531
  65.5 29.7 %collective-permute-start.36 = (bf16[128,4096]{1,0:T(8,128)(2,1)S(1)}, bf16[128,4096]{1,0:T(8,128)(2,1)}, u32[]{:S(2)}, u32[]{:S(2)}) collective-permute-start(bf16[128,4096]{1,0:T(8,128)(2,1)S(1)} %pad_maximum_fusion.2.refs_0_), channel_id=1, source_target_pairs={{0,4},{1,3},{2,6},{3,1},{4,0},{5,7},{6,2},{7,5},{8,12},{9,11},{10,... | collective-permute-start | bytes 3145736 | tf_op jit(solution)/shard_map/ppermute | solution.py:531
  67.8 23.9 %collective-permute-start.5 = (bf16[64,4224]{1,0:T(8,128)(2,1)S(1)}, bf16[64,4224]{1,0:T(8,128)(2,1)S(1)}, u32[]{:S(2)}, u32[]{:S(2)}) collective-permute-start(bf16[64,4224]{1,0:T(8,128)(2,1)S(1)} %collective-permute-done.4.refs_4_), channel_id=1, source_target_pairs={{0,4},{1,3},{2,6},{3,1},{4,0},{5,7},{6,2},{7,5},{8,12},{9,11},{10,... | collective-permute-start | bytes 1622024 | tf_op jit(solution)/shard_map/ppermute | solution.py:531
  69.1 22.6 %collective-permute-start.6 = (bf16[64,4224]{1,0:T(8,128)(2,1)S(1)}, bf16[64,4224]{1,0:T(8,128)(2,1)S(1)}, u32[]{:S(2)}, u32[]{:S(2)}) collective-permute-start(bf16[64,4224]{1,0:T(8,128)(2,1)S(1)} %collective-permute-done.4.refs_4_), channel_id=1, source_target_pairs={{0,1},{1,0},{2,3},{3,2},{4,5},{5,4},{6,7},{7,6},{8,9},{9,8},{10,11... | collective-permute-start | bytes 1622024 | tf_op jit(solution)/shard_map/ppermute | solution.py:531
  74.1 19.5 %collective-permute-start.3 = (bf16[64,4224]{1,0:T(8,128)(2,1)S(1)}, bf16[64,4224]{1,0:T(8,128)(2,1)S(1)}, u32[]{:S(2)}, u32[]{:S(2)}) collective-permute-start(bf16[64,4224]{1,0:T(8,128)(2,1)S(1)} %collective-permute-done.1.refs_1_), channel_id=1, source_target_pairs={{0,1},{1,0},{2,3},{3,2},{4,5},{5,4},{6,7},{7,6},{8,9},{9,8},{10,11... | collective-permute-start | bytes 1622024 | tf_op jit(solution)/shard_map/ppermute | solution.py:531
  94.4 25.4 %collective-permute-start.12 = (bf16[64,4224]{1,0:T(8,128)(2,1)}, bf16[64,4224]{1,0:T(8,128)(2,1)}, u32[]{:S(2)}, u32[]{:S(2)}) collective-permute-start(bf16[64,4224]{1,0:T(8,128)(2,1)} %collective-permute-done.8.refs_8_), channel_id=1, source_target_pairs={{0,8},{1,9},{2,10},{3,11},{4,12},{5,13},{6,14},{7,15},{8,16},{9,17... | collective-permute-start | bytes 1622024 | tf_op jit(solution)/shard_map/ppermute | solution.py:531
  119.9 21.6 %collective-permute-start.37 = (bf16[128,4096]{1,0:T(8,128)(2,1)}, bf16[128,4096]{1,0:T(8,128)(2,1)}, u32[]{:S(2)}, u32[]{:S(2)}) collective-permute-start(bf16[128,4096]{1,0:T(8,128)(2,1)} %collective-permute-done.35.refs_1_), channel_id=1, source_target_pairs={{0,4},{1,3},{2,6},{3,1},{4,0},{5,7},{6,2},{7,5},{8,12},{9,11},{10,... | collective-permute-start | bytes 3145736 | tf_op jit(solution)/shard_map/ppermute | solution.py:531
  121.6 19.3 %collective-permute-start.13 = (bf16[64,4224]{1,0:T(8,128)(2,1)}, bf16[64,4224]{1,0:T(8,128)(2,1)}, u32[]{:S(2)}, u32[]{:S(2)}) collective-permute-start(bf16[64,4224]{1,0:T(8,128)(2,1)} %collective-permute-done.12.refs_12_), channel_id=1, source_target_pairs={{0,4},{1,3},{2,6},{3,1},{4,0},{5,7},{6,2},{7,5},{8,12},{9,11},{10,... | collective-permute-start | bytes 1622024 | tf_op jit(solution)/shard_map/ppermute | solution.py:531
  123.8 17.1 %collective-permute-start.14 = (bf16[64,4224]{1,0:T(8,128)(2,1)}, bf16[64,4224]{1,0:T(8,128)(2,1)}, u32[]{:S(2)}, u32[]{:S(2)}) collective-permute-start(bf16[64,4224]{1,0:T(8,128)(2,1)} %collective-permute-done.12.refs_12_), channel_id=1, source_target_pairs={{0,1},{1,0},{2,3},{3,2},{4,5},{5,4},{6,7},{7,6},{8,9},{9,8},{10,11... | collective-permute-start | bytes 1622024 | tf_op jit(solution)/shard_map/ppermute | solution.py:531
  123.8 17.6 %collective-permute-start.11 = (bf16[64,4224]{1,0:T(8,128)(2,1)}, bf16[64,4224]{1,0:T(8,128)(2,1)}, u32[]{:S(2)}, u32[]{:S(2)}) collective-permute-start(bf16[64,4224]{1,0:T(8,128)(2,1)} %collective-permute-done.9.refs_9_), channel_id=1, source_target_pairs={{0,1},{1,0},{2,3},{3,2},{4,5},{5,4},{6,7},{7,6},{8,9},{9,8},{10,11... | collective-permute-start | bytes 1622024 | tf_op jit(solution)/shard_map/ppermute | solution.py:531
  140.9 47.2 %collective-permute-start.38 = (bf16[128,4096]{1,0:T(8,128)(2,1)S(1)}, bf16[128,4096]{1,0:T(8,128)(2,1)}, u32[]{:S(2)}, u32[]{:S(2)}) collective-permute-start(bf16[128,4096]{1,0:T(8,128)(2,1)S(1)} %pad_maximum_fusion.2.refs_0_), channel_id=1, source_target_pairs={{0,1},{1,0},{2,3},{3,2},{4,5},{5,4},{6,7},{7,6},{8,9},{9,8},{10,11... | collective-permute-start | bytes 3145736 | tf_op jit(solution)/shard_map/ppermute | solution.py:531
  140.9 47.2 %collective-permute-start.39 = (bf16[128,4096]{1,0:T(8,128)(2,1)}, bf16[128,4096]{1,0:T(8,128)(2,1)}, u32[]{:S(2)}, u32[]{:S(2)}) collective-permute-start(bf16[128,4096]{1,0:T(8,128)(2,1)} %collective-permute-done.35.refs_1_), channel_id=1, source_target_pairs={{0,1},{1,0},{2,3},{3,2},{4,5},{5,4},{6,7},{7,6},{8,9},{9,8},{10,11... | collective-permute-start | bytes 3145736 | tf_op jit(solution)/shard_map/ppermute | solution.py:531
  141.4 46.7 %collective-permute-start.40 = (bf16[128,4096]{1,0:T(8,128)(2,1)}, bf16[128,4096]{1,0:T(8,128)(2,1)}, u32[]{:S(2)}, u32[]{:S(2)}) collective-permute-start(bf16[128,4096]{1,0:T(8,128)(2,1)} %collective-permute-done.36.refs_2_), channel_id=1, source_target_pairs={{0,1},{1,0},{2,3},{3,2},{4,5},{5,4},{6,7},{7,6},{8,9},{9,8},{10,11... | collective-permute-start | bytes 3145736 | tf_op jit(solution)/shard_map/ppermute | solution.py:531
  141.5 46.6 %collective-permute-start.41 = (bf16[128,4096]{1,0:T(8,128)(2,1)}, bf16[128,4096]{1,0:T(8,128)(2,1)}, u32[]{:S(2)}, u32[]{:S(2)}) collective-permute-start(bf16[128,4096]{1,0:T(8,128)(2,1)} %collective-permute-done.37.refs_3_), channel_id=1, source_target_pairs={{0,1},{1,0},{2,3},{3,2},{4,5},{5,4},{6,7},{7,6},{8,9},{9,8},{10,11... | collective-permute-start | bytes 3145736 | tf_op jit(solution)/shard_map/ppermute | solution.py:531
  302.9 41.9 %collective-permute-start.48 = (bf16[512,4096]{1,0:T(8,128)(2,1)}, bf16[512,4096]{1,0:T(8,128)(2,1)}, u32[]{:S(2)}, u32[]{:S(2)}) collective-permute-start(bf16[512,4096]{1,0:T(8,128)(2,1)} %get-tuple-element.110), channel_id=1, source_target_pairs={{0,1},{1,0},{2,3},{3,2},{4,5},{5,4},{6,7},{7,6},{8,9},{9,8},{10,11... | collective-permute-start | bytes 12582920 | tf_op jit(solution)/shard_map/ppermute | solution.py:531
  315.0 36.3 %collective-permute-start.57 = (bf16[512,4096]{1,0:T(8,128)(2,1)}, bf16[512,4096]{1,0:T(8,128)(2,1)}, u32[]{:S(2)}, u32[]{:S(2)}) collective-permute-start(bf16[512,4096]{1,0:T(8,128)(2,1)} %get-tuple-element.116), channel_id=1, source_target_pairs={{0,1},{1,0},{2,3},{3,2},{4,5},{5,4},{6,7},{7,6},{8,9},{9,8},{10,11... | collective-permute-start | bytes 12582920 | tf_op jit(solution)/shard_map/ppermute | solution.py:531
  349.3 31.9 %collective-permute-start.51 = (bf16[64,4096]{1,0:T(8,128)(2,1)S(1)}, bf16[64,4096]{1,0:T(8,128)(2,1)S(1)}, u32[]{:S(2)}, u32[]{:S(2)}) collective-permute-start(bf16[64,4096]{1,0:T(8,128)(2,1)S(1)} %get-tuple-element.166), channel_id=1, source_target_pairs={{0,4},{1,3},{2,6},{3,1},{4,0},{5,7},{6,2},{7,5},{8,12},{9,11},{10,... | collective-permute-start | bytes 1572872 | tf_op jit(solution)/shard_map/ppermute | solution.py:531
  350.3 59.7 %collective-permute-start.50 = (bf16[64,4096]{1,0:T(8,128)(2,1)S(1)}, bf16[64,4096]{1,0:T(8,128)(2,1)S(1)}, u32[]{:S(2)}, u32[]{:S(2)}) collective-permute-start(bf16[64,4096]{1,0:T(8,128)(2,1)S(1)} %get-tuple-element.167), channel_id=1, source_target_pairs={{0,4},{1,3},{2,6},{3,1},{4,0},{5,7},{6,2},{7,5},{8,12},{9,11},{10,... | collective-permute-start | bytes 1572872 | tf_op jit(solution)/shard_map/ppermute | solution.py:531
  351.3 88.4 %collective-permute-start.49 = (bf16[64,4096]{1,0:T(8,128)(2,1)S(1)}, bf16[64,4096]{1,0:T(8,128)(2,1)S(1)}, u32[]{:S(2)}, u32[]{:S(2)}) collective-permute-start(bf16[64,4096]{1,0:T(8,128)(2,1)S(1)} %get-tuple-element.164), channel_id=1, source_target_pairs={{0,4},{1,3},{2,6},{3,1},{4,0},{5,7},{6,2},{7,5},{8,12},{9,11},{10,... | collective-permute-start | bytes 1572872 | tf_op jit(solution)/shard_map/ppermute | solution.py:531
  354.7 25.3 %collective-permute-start.61 = (bf16[64,4096]{1,0:T(8,128)(2,1)S(1)}, bf16[64,4096]{1,0:T(8,128)(2,1)S(1)}, u32[]{:S(2)}, u32[]{:S(2)}) collective-permute-start(bf16[64,4096]{1,0:T(8,128)(2,1)S(1)} %get-tuple-element.169), channel_id=1, source_target_pairs={{0,4},{1,3},{2,6},{3,1},{4,0},{5,7},{6,2},{7,5},{8,12},{9,11},{10,... | collective-permute-start | bytes 1572872 | tf_op jit(solution)/shard_map/ppermute | solution.py:531
  358.5 37.6 %collective-permute-start.60 = (bf16[64,4096]{1,0:T(8,128)(2,1)S(1)}, bf16[64,4096]{1,0:T(8,128)(2,1)S(1)}, u32[]{:S(2)}, u32[]{:S(2)}) collective-permute-start(bf16[64,4096]{1,0:T(8,128)(2,1)S(1)} %get-tuple-element.170), channel_id=1, source_target_pairs={{0,4},{1,3},{2,6},{3,1},{4,0},{5,7},{6,2},{7,5},{8,12},{9,11},{10,... | collective-permute-start | bytes 1572872 | tf_op jit(solution)/shard_map/ppermute | solution.py:531
  381.2 41.8 %collective-permute-start.59 = (bf16[64,4096]{1,0:T(8,128)(2,1)S(1)}, bf16[64,4096]{1,0:T(8,128)(2,1)S(1)}, u32[]{:S(2)}, u32[]{:S(2)}) collective-permute-start(bf16[64,4096]{1,0:T(8,128)(2,1)S(1)} %get-tuple-element.171), channel_id=1, source_target_pairs={{0,4},{1,3},{2,6},{3,1},{4,0},{5,7},{6,2},{7,5},{8,12},{9,11},{10,... | collective-permute-start | bytes 1572872 | tf_op jit(solution)/shard_map/ppermute | solution.py:531
  396.1 57.6 %collective-permute-start.58 = (bf16[64,4096]{1,0:T(8,128)(2,1)S(1)}, bf16[64,4096]{1,0:T(8,128)(2,1)S(1)}, u32[]{:S(2)}, u32[]{:S(2)}) collective-permute-start(bf16[64,4096]{1,0:T(8,128)(2,1)S(1)} %get-tuple-element.168), channel_id=1, source_target_pairs={{0,4},{1,3},{2,6},{3,1},{4,0},{5,7},{6,2},{7,5},{8,12},{9,11},{10,... | collective-permute-start | bytes 1572872 | tf_op jit(solution)/shard_map/ppermute | solution.py:531
  410.1 42.4 %collective-permute-start.43 = (bf16[256,4224]{1,0:T(8,128)(2,1)S(1)}, bf16[256,4224]{1,0:T(8,128)(2,1)S(1)}, u32[]{:S(2)}, u32[]{:S(2)}) collective-permute-start(bf16[256,4224]{1,0:T(8,128)(2,1)S(1)} %get-tuple-element.163), channel_id=1, source_target_pairs={{0,4},{1,3},{2,6},{3,1},{4,0},{5,7},{6,2},{7,5},{8,12},{9,11},{10,... | collective-permute-start | bytes 6488072 | tf_op jit(solution)/shard_map/ppermute | solution.py:531
  423.1 26.6 %collective-permute-start.55 = (bf16[64,4096]{1,0:T(8,128)(2,1)S(1)}, bf16[64,4096]{1,0:T(8,128)(2,1)S(1)}, u32[]{:S(2)}, u32[]{:S(2)}) collective-permute-start(bf16[64,4096]{1,0:T(8,128)(2,1)S(1)} %add_convert_fusion.20), channel_id=1, source_target_pairs={{0,8},{1,9},{2,10},{3,11},{4,12},{5,13},{6,14},{7,15},{8,16},{9,17... | collective-permute-start | bytes 1572872 | tf_op jit(solution)/shard_map/ppermute | solution.py:531
  (122 other events, 1315.5 us)

commit v4 on v1

v4 whole, which is shorter than its diff:
```python
import functools
import math
import types

import jax
import jax.numpy as jnp
from jax import lax
from jax.experimental import pallas as pl
from jax.experimental.pallas import tpu as pltpu
from jax.sharding import PartitionSpec as P

HEAD_DIM = 64


LOW = jnp.bfloat16
SCALE = HEAD_DIM ** (-0.5)
PAIR = 2 * HEAD_DIM
TILE = 512
FF_TILE = 1024
ROWS = 32
NORM_COLS = 128
GELU_RATE = math.sqrt(2.0 / math.pi)
ANYWHERE = pl.BlockSpec(memory_space=pl.ANY)
IN_HBM = pl.BlockSpec(memory_space=pltpu.HBM)
SCALARS = pl.BlockSpec(memory_space=pltpu.SMEM)
VECTORS = pl.BlockSpec(memory_space=pltpu.VMEM)


def launch(body, given, made, scratch, products, moved, limit):
    names, specs, arrays = [], [], []
    for name, (spec, value) in given.items():
        group = value if isinstance(value, list) else [value]
        names += [(name, isinstance(value, list))] * len(group)
        specs += [spec] * len(group)
        arrays += group
    names += [(name, False) for name in (*made, *scratch)]

    def kernel(*refs):
        held = {}
        for (name, grouped), ref in zip(names, refs):
            if grouped:
                held.setdefault(name, []).append(ref)
            else:
                held[name] = ref
        body(types.SimpleNamespace(**held))

    outs = pl.pallas_call(
        kernel,
        out_shape=[jax.ShapeDtypeStruct(shape, kind) for _, shape, kind in made.values()],
        in_specs=specs,
        out_specs=[spec for spec, _, _ in made.values()],
        scratch_shapes=list(scratch.values()),
        cost_estimate=pl.CostEstimate(
            flops=2 * products, bytes_accessed=moved, transcendentals=0
        ),
        compiler_params=pltpu.CompilerParams(vmem_limit_bytes=limit * 2**20),
    )(*arrays)
    return types.SimpleNamespace(**dict(zip(made, outs)))


class Copies:
    def __init__(self, sem):
        self.sem, self.used, self.open = sem, 0, []

    def start(self, source, target, keep=True):
        copy = pltpu.make_async_copy(source, target, self.sem.at[self.used])
        self.used += 1
        copy.start()
        if keep:
            self.open.append(copy)
        return copy

    def rows(self, parts, owners_ref, target):
        if len(parts) == 1:
            return [self.start(parts[0], target, False)]
        shard = target.shape[0] // owners_ref.shape[0]
        copies = []
        for part in parts:
            for local in range(part.shape[0] // shard):
                row = pl.multiple_of(owners_ref[len(copies)] * shard, shard)
                source = part.at[pl.ds(local * shard, shard)]
                copies.append(self.start(source, target.at[pl.ds(row, shard)], False))
        return copies

    def finish(self):
        for copy in self.open:
            copy.wait()


def wait_all(copies):
    for copy in copies:
        copy.wait()


def product(left, right, left_dim=1, right_dim=0):
    dims = (((left_dim,), (right_dim,)), ((), ()))
    return lax.dot_general(left, right, dims, preferred_element_type=jnp.float32)


def tiles(total, size):
    return [slice(start, start + size) for start in range(0, total, size)]


def fill_mask(lengths_ref, mask_ref):
    shape = mask_ref.shape
    key_row = lax.broadcasted_iota(jnp.int32, shape, 0)
    query_row = lax.broadcasted_iota(jnp.int32, shape, 1)
    end = 0
    key_segment = jnp.zeros(shape, jnp.int32)
    query_segment = jnp.zeros(shape, jnp.int32)
    for slot in range(lengths_ref.shape[1]):
        end = end + lengths_ref[0, slot]
        key_segment += (key_row >= end).astype(jnp.int32)
        query_segment += (query_row >= end).astype(jnp.int32)
    mask_ref[...] = jnp.where(key_segment == query_segment, 0.0, -1e30)


def normalize(values, gain, bias):
    centered = values - jnp.mean(values, axis=-1, keepdims=True)
    spread = jnp.mean(centered * centered, axis=-1, keepdims=True)
    inverse = lax.rsqrt(spread + 1e-05)
    unit = centered * inverse
    return unit, inverse, unit * gain + bias


def normalize_back(grad, unit, inverse, gain):
    scaled = grad * gain
    mean = jnp.mean(scaled, axis=-1, keepdims=True)
    along = jnp.mean(scaled * unit, axis=-1, keepdims=True)
    return inverse * (scaled - mean - unit * along)


def half_lanes(rows, half):
    lane = lax.broadcasted_iota(jnp.int32, (rows, PAIR), 1)
    return (lane >= HEAD_DIM) == bool(half)


def add_norm_grad(norm_grad, row, grad, unit):
    norm_grad[row : row + 1] += jnp.sum(grad * unit, axis=0, keepdims=True)
    norm_grad[row + 1 : row + 2] += jnp.sum(grad, axis=0, keepdims=True)


def attend_forward(rows, low, att, att_ready, mask, qkv, mixed, lse, total, norm, hidden, unit, inverse):
    count, width = low.shape
    att_ready()
    for part in tiles(3 * width, TILE):
        qkv[:, part] = product(low[...], att[:, part]).astype(LOW)
    for pair, part in enumerate(tiles(width, PAIR)):
        query = qkv[:, part] * jnp.asarray(SCALE, LOW)
        key = qkv[:, slice(width + part.start, width + part.stop)]
        value = qkv[:, slice(2 * width + part.start, 2 * width + part.stop)]
        halves, sums = [], []
        for half in (0, 1):
            own = jnp.where(half_lanes(count, half), query, jnp.zeros_like(query))
            scores = product(key, own, 1, 1) + mask[...]
            peak = jnp.max(scores, axis=0, keepdims=True)
            weights = jnp.exp(scores - peak)
            sum_all = jnp.sum(weights, axis=0, keepdims=True)
            sums.append(peak + jnp.log(sum_all))
            out = product(value, weights.astype(LOW), 0, 0)
            halves.append(out[half * HEAD_DIM : (half + 1) * HEAD_DIM] * (1.0 / sum_all))
        lse[pair] = jnp.concatenate(sums, axis=0)
        mixed[:, part] = jnp.concatenate(halves, axis=0).T.astype(LOW)
    for part in tiles(width, TILE):
        out = slice(3 * width + part.start, 3 * width + part.stop)
        total[:, part] = rows[:, part].astype(jnp.float32) + product(mixed[...], att[:, out])
    for block in tiles(count, ROWS):
        unit[block], inverse[block], hidden[block] = normalize(total[block], norm[0:1], norm[1:2])


def ffn_forward(hidden, low, up, down, up_ready, down_ready, active, slope, total):
    low[...] = hidden[...].astype(LOW)
    total[...] = hidden[...]
    up_ready()
    for part in tiles(active.shape[1], FF_TILE):
        inner = product(low[...], up[:, part])
        square = inner * inner
        bend = jnp.tanh(GELU_RATE * inner * (1.0 + 0.044715 * square))
        rise = 0.5 + 0.5 * bend
        act = (inner * rise).astype(LOW)
        active[:, part] = act
        slope[:, part] = (
            rise
            + (0.5 * GELU_RATE) * inner * (1.0 - bend * bend) * (1.0 + 3 * 0.044715 * square)
        ).astype(LOW)
        if part.start == 0:
            down_ready()
        total[...] += product(act, down[:, part], 1, 1)


def ffn_backward(second, out_low, slope, up, down, unit, inverse, norm, inner_low, total, first, first_low, norm_grad, ready=None):
    count, _ = second.shape
    total[...] = second[...]
    for index, part in enumerate(tiles(slope.shape[1], FF_TILE)):
        if ready:
            ready(index)
        act = product(out_low[...], down[:, part])
        inner = (act * slope[:, part].astype(jnp.float32)).astype(LOW)
        inner_low[:, part] = inner
        total[...] += product(inner, up[:, part], 1, 1)
    for block in tiles(count, ROWS):
        grad, unit_rows = total[block], unit[block]
        add_norm_grad(norm_grad, 0, grad, unit_rows)
        out = normalize_back(grad, unit_rows, inverse[block], norm[0:1])
        first[block] = out
        first_low[block] = out.astype(LOW)


def attend_backward(first, first_low, qkv, lse, mask, att, mixed_grad, qkv_grad, rows_grad, ready=None):
    count, width = first.shape
    if ready:
        ready(3)
    for part in tiles(width, TILE):
        mixed_grad[:, part] = product(
            first_low[...], att[part, 3 * width : 4 * width], 1, 1
        ).astype(LOW)
    for pair, part in enumerate(tiles(width, PAIR)):
        key_part = slice(width + part.start, width + part.stop)
        value_part = slice(2 * width + part.start, 2 * width + part.stop)
        query = qkv[:, part] * jnp.asarray(SCALE, LOW)
        key, value, grad = qkv[:, key_part], qkv[:, value_part], mixed_grad[:, part]
        sums = lse[pair]
        key_grads, value_grads, query_grads = [], [], []
        for half in (0, 1):
            lanes = half_lanes(count, half)
            own_query = jnp.where(lanes, query, jnp.zeros_like(query))
            own_grad = jnp.where(lanes, grad, jnp.zeros_like(grad))
            weights = jnp.exp(product(key, own_query, 1, 1) + mask[...] - sums[half : half + 1])
            weight_grad = product(value, own_grad, 1, 1)
            value_grads.append(product(weights.astype(LOW), grad))
            along = jnp.sum(weights * weight_grad, axis=0, keepdims=True)
            low = (weights * (weight_grad - along)).astype(LOW)
            key_grads.append(product(low, query))
            back = product(key, low, 0, 0)
            query_grads.append(back[half * HEAD_DIM : (half + 1) * HEAD_DIM])
        lanes = half_lanes(count, 1)
        qkv_grad[:, part] = (jnp.concatenate(query_grads, axis=0).T * SCALE).astype(LOW)
        qkv_grad[:, key_part] = jnp.where(lanes, key_grads[1], key_grads[0]).astype(LOW)
        qkv_grad[:, value_part] = jnp.where(lanes, value_grads[1], value_grads[0]).astype(LOW)
    if ready:
        for chunk in range(3):
            ready(chunk)
    for part in tiles(width, TILE):
        rows_grad[:, part] = first[:, part] + product(qkv_grad[...], att[part, : 3 * width], 1, 1)


def weight_sum(picker, lefts, rights, turned, whole, copies, send, keep):
    count = lefts[0].shape[0]
    half = send.shape[0]
    for layer, left in enumerate(lefts):
        turned[:, layer * count : (layer + 1) * count] = product(
            picker[...], left[...], 1, 1
        ).astype(LOW)
    for part in tiles(rights[0].shape[1], TILE):
        right = jnp.concatenate([ref[:, part] for ref in rights], axis=0)
        whole[:, part] = product(turned[...], right).astype(LOW)
        columns = pl.ds(part.start, TILE)
        copies.start(whole.at[pl.ds(0, half), columns], send.at[:, columns])
        copies.start(whole.at[pl.ds(half, half), columns], keep.at[:, columns])


def first_attention(lengths, owners, tokens, parts):
    count, width = tokens.shape
    wide = parts[0].shape[1]

    def body(r):
        copies = Copies(r.sem)
        rows = copies.rows(r.parts, r.owners, r.held)
        fill_mask(r.lengths, r.mask)
        r.low[...] = r.tokens[...]

        def ready():
            wait_all(rows)
            copies.start(r.held.at[:, pl.ds(0, 4 * width)], r.att)
            r.turned[...] = r.held[:, 4 * width :].astype(jnp.float32).T
            r.norm[...] = r.turned[0:4]

        attend_forward(
            r.tokens,
            r.low,
            r.held,
            ready,
            r.mask,
            r.qkv,
            r.mixed,
            r.lse,
            r.total,
            r.norm,
            r.hidden,
            r.unit,
            r.inverse,
        )
        copies.finish()

    size = (count, width)
    return launch(
        body,
        {
            "lengths": (SCALARS, lengths),
            "owners": (SCALARS, owners),
            "tokens": (VECTORS, tokens),
            "parts": (IN_HBM, parts),
        },
        {
            "att": (IN_HBM, (width, 4 * width), LOW),
            "norm": (VECTORS, (4, width), jnp.float32),
            "qkv": (VECTORS, (count, 3 * width), LOW),
            "mixed": (VECTORS, size, LOW),
            "lse": (VECTORS, (width // PAIR, 2, count), jnp.float32),
            "hidden": (VECTORS, size, jnp.float32),
            "unit": (VECTORS, size, jnp.float32),
            "inverse": (VECTORS, (count, 1), jnp.float32),
        },
        {
            "held": pltpu.VMEM((width, wide), LOW),
            "low": pltpu.VMEM(size, LOW),
            "mask": pltpu.VMEM((count, count), jnp.float32),
            "total": pltpu.VMEM(size, jnp.float32),
            "turned": pltpu.VMEM((NORM_COLS, width), jnp.float32),
            "sem": pltpu.SemaphoreType.DMA((owners.size + 1,)),
        },
        4 * count * width * width + 2 * count * count * width,
        16 * width * width + 20 * count * width,
        40,
    )


def middle_layers(lengths, norm, hidden, cotangent, att, up_parts, up_owners, down_parts, down_owners, picker):
    count, width = hidden.shape
    inner = up_parts[0].shape[1]
    size, f32 = (count, width), jnp.float32
    results = {
        "hidden_low1": (size, LOW),
        "active1": ((count, inner), LOW),
        "slope1": ((count, inner), LOW),
        "low2": (size, LOW),
        "mixed2": (size, LOW),
        "hidden_low2": (size, LOW),
        "layer_output": (size, LOW),
        "inner_low2": ((count, inner), LOW),
        "first_low2": (size, LOW),
        "qkv_grad2": ((count, 3 * width), LOW),
        "second1": (size, f32),
        "out_low1": (size, LOW),
        "norm_grad": (norm.shape, f32),
    }

    def body(r):
        copies = Copies(r.sem)
        up_rows = copies.rows(r.up_parts, r.up_owners, r.held_up)
        down_rows = copies.rows(r.down_parts, r.down_owners, r.held_down)
        att_copy = copies.start(r.att, r.held_att, False)
        picker_copy = copies.start(r.picker, r.held_picker, False)
        fill_mask(r.lengths, r.mask)
        kept = []

        def up_ready():
            wait_all(up_rows)
            kept.append(copies.start(r.held_up, r.up_full, False))

        def down_ready():
            wait_all(down_rows)
            copies.start(r.held_down, r.down_full)

        def give(name):
            copies.start(getattr(r, "own_" + name), getattr(r, name))

        ffn_forward(
            r.hidden,
            r.own_hidden_low1,
            r.held_up,
            r.held_down,
            up_ready,
            down_ready,
            r.own_active1,
            r.own_slope1,
            r.total,
        )
        for name in ("hidden_low1", "active1", "slope1"):
            give(name)
        for block in tiles(count, ROWS):
            r.unit2[block], r.inverse2[block], rows = normalize(
                r.total[block], r.norm[2:3], r.norm[3:4]
            )
            r.rows[block] = rows
            r.own_low2[block] = rows.astype(LOW)
        give("low2")
        attend_forward(
            r.rows,
            r.own_low2,
            r.held_att,
            att_copy.wait,
            r.mask,
            r.qkv,
            r.own_mixed2,
            r.lse,
            r.total,
            r.norm,
            r.hidden2,
            r.unit1,
            r.inverse1,
        )
        give("mixed2")
        ffn_forward(
            r.hidden2,
            r.own_hidden_low2,
            r.held_up,
            r.held_down,
            lambda: None,
            lambda: None,
            r.active2,
            r.slope2,
            r.total,
        )
        give("hidden_low2")
        r.own_norm_grad[...] = jnp.zeros_like(r.own_norm_grad)
        live = 0
        for slot in range(r.lengths.shape[1]):
            live = live + r.lengths[0, slot]
        for block in tiles(count, ROWS):
            unit, inverse, rows = normalize(r.total[block], r.norm[2:3], r.norm[3:4])
            r.own_layer_output[block] = rows.astype(LOW)
            position = block.start + lax.broadcasted_iota(jnp.int32, unit.shape, 0)
            grad = jnp.where(position < live, r.cotangent[block].astype(f32), 0.0)
            add_norm_grad(r.own_norm_grad, 2, grad, unit)
            second = normalize_back(grad, unit, inverse, r.norm[2:3])
            r.rows[block] = second
            r.out_low2[block] = second.astype(LOW)
        give("layer_output")
        ffn_backward(
            r.rows,
            r.out_low2,
            r.slope2,
            r.held_up,
            r.held_down,
            r.unit1,
            r.inverse1,
            r.norm,
            r.own_inner_low2,
            r.total,
            r.rows,
            r.own_first_low2,
            r.own_norm_grad,
        )
        for name in ("inner_low2", "first_low2"):
            give(name)
        attend_backward(
            r.rows,
            r.own_first_low2,
            r.qkv,
            r.lse,
            r.mask,
            r.held_att,
            r.mixed_grad,
            r.own_qkv_grad2,
            r.total,
        )
        give("qkv_grad2")
        for block in tiles(count, ROWS):
            grad, unit = r.total[block], r.unit2[block]
            add_norm_grad(r.own_norm_grad, 2, grad, unit)
            second = normalize_back(grad, unit, r.inverse2[block], r.norm[2:3])
            r.own_second1[block] = second
            r.own_out_low1[block] = second.astype(LOW)
        for name in ("second1", "out_low1", "norm_grad"):
            give(name)
        picker_copy.wait()
        wait_all(kept)
        weight_sum(
            r.held_picker,
            (r.out_low2, r.own_out_low1),
            (r.active2, r.own_active1),
            r.turned,
            r.held_up,
            copies,
            r.send,
            r.keep,
        )
        copies.finish()

    made = {name: (IN_HBM, shape, kind) for name, (shape, kind) in results.items()}
    for name in ("up_full", "down_full"):
        made[name] = (IN_HBM, (width, inner), LOW)
    for name in ("send", "keep"):
        made[name] = (IN_HBM, (width // 2, inner), LOW)
    scratch = {"own_" + name: pltpu.VMEM(shape, kind) for name, (shape, kind) in results.items()}
    scratch |= {
        "held_up": pltpu.VMEM((width, inner), LOW),
        "held_down": pltpu.VMEM((width, inner), LOW),
        "held_att": pltpu.VMEM((width, 4 * width), LOW),
        "held_picker": pltpu.VMEM((width, width), LOW),
        "turned": pltpu.VMEM((width, 2 * count), LOW),
        "mask": pltpu.VMEM((count, count), f32),
        "qkv": pltpu.VMEM((count, 3 * width), LOW),
        "lse": pltpu.VMEM((width // PAIR, 2, count), f32),
        "active2": pltpu.VMEM((count, inner), LOW),
        "slope2": pltpu.VMEM((count, inner), LOW),
        "out_low2": pltpu.VMEM(size, LOW),
        "mixed_grad": pltpu.VMEM(size, LOW),
        "inverse1": pltpu.VMEM((count, 1), f32),
        "inverse2": pltpu.VMEM((count, 1), f32),
    }
    for name in ("total", "rows", "hidden2", "unit1", "unit2"):
        scratch[name] = pltpu.VMEM(size, f32)
    loads = len(up_parts) + len(down_parts) + 2 * up_owners.size
    scratch["sem"] = pltpu.SemaphoreType.DMA((loads + len(results) + 4 + 2 * (inner // TILE),))
    return launch(
        body,
        {
            "lengths": (SCALARS, lengths),
            "up_owners": (SCALARS, up_owners),
            "down_owners": (SCALARS, down_owners),
            "norm": (VECTORS, norm),
            "hidden": (VECTORS, hidden),
            "cotangent": (VECTORS, cotangent),
            "att": (IN_HBM, att),
            "picker": (IN_HBM, picker),
            "up_parts": (IN_HBM, up_parts),
            "down_parts": (IN_HBM, down_parts),
        },
        made,
        scratch,
        count * width * (8 * inner + 8 * width) + 7 * count * count * width,
        12 * width * inner,
        60,
    )


def first_ffn_backward(m, norm, unit, inverse, mixed, picker_up, picker_out):
    count, width = mixed.shape
    inner = m.slope1.shape[1]
    size, f32 = (count, width), jnp.float32
    late = {
        "picker_up": picker_up,
        "hidden_low2": m.hidden_low2,
        "hidden_low1": m.hidden_low1,
        "inner_low2": m.inner_low2,
        "picker_out": picker_out,
        "mixed2": m.mixed2,
        "mixed1": mixed,
        "first_low2": m.first_low2,
    }

    def body(r):
        copies = Copies(r.sem)
        parts = [pl.ds(part.start, FF_TILE) for part in tiles(inner, FF_TILE)]
        weights = [
            (
                copies.start(r.down.at[:, part], r.held_down.at[:, part], False),
                copies.start(r.up.at[:, part], r.held_up.at[:, part], False),
            )
            for part in parts
        ]
        loads = [copies.start(getattr(r, n), getattr(r, "own_" + n), False) for n in late]
        r.norm_grad[...] = jnp.zeros_like(r.norm_grad)
        ffn_backward(
            r.second,
            r.out_low,
            r.slope,
            r.held_up,
            r.held_down,
            r.unit,
            r.inverse,
            r.norm,
            r.inner_low,
            r.total,
            r.first,
            r.first_low,
            r.norm_grad,
            lambda index: wait_all(weights[index]),
        )
        wait_all(loads)
        weight_sum(
            r.own_picker_up,
            (r.own_hidden_low2, r.own_hidden_low1),
            (r.own_inner_low2, r.inner_low),
            r.turned,
            r.held_up,
            copies,
            r.send_up,
            r.keep_up,
        )
        weight_sum(
            r.own_picker_out,
            (r.own_mixed2, r.own_mixed1),
            (r.own_first_low2, r.first_low),
            r.turned,
            r.held_down,
            copies,
            r.send_out,
            r.keep_out,
        )
        copies.finish()

    given = {
        "second": (VECTORS, m.second1),
        "out_low": (VECTORS, m.out_low1),
        "slope": (VECTORS, m.slope1),
        "unit": (VECTORS, unit),
        "inverse": (VECTORS, inverse),
        "norm": (VECTORS, norm),
        "up": (IN_HBM, m.up_full),
        "down": (IN_HBM, m.down_full),
    }
    given |= {name: (IN_HBM, value) for name, value in late.items()}
    scratch = {"own_" + name: pltpu.VMEM(value.shape, LOW) for name, value in late.items()}
    scratch |= {
        "held_up": pltpu.VMEM((width, inner), LOW),
        "held_down": pltpu.VMEM((width, inner), LOW),
        "turned": pltpu.VMEM((width, 2 * count), LOW),
        "inner_low": pltpu.VMEM((count, inner), LOW),
        "total": pltpu.VMEM(size, f32),
        "sem": pltpu.SemaphoreType.DMA(
            (2 * (inner // FF_TILE) + len(late) + 2 * (inner + width) // TILE,)
        ),
    }
    return launch(
        body,
        given,
        {
            "first": (VECTORS, size, f32),
            "first_low": (VECTORS, size, LOW),
            "norm_grad": (VECTORS, norm.shape, f32),
            "send_up": (IN_HBM, (width // 2, inner), LOW),
            "keep_up": (IN_HBM, (width // 2, inner), LOW),
            "send_out": (IN_HBM, (width // 2, width), LOW),
            "keep_out": (IN_HBM, (width // 2, width), LOW),
        },
        scratch,
        count * width * (4 * inner + 2 * width),
        8 * width * inner,
        60,
    )


def first_attention_backward(lengths, first, first_low, qkv, lse, att, tokens, low2, qkv_grad2, norm_grads, picker):
    count, width = first.shape
    size, f32 = (count, width), jnp.float32
    late = {"picker": picker, "low2": low2, "tokens": tokens, "qkv_grad2": qkv_grad2}
    wide = 3 * width + NORM_COLS

    def body(r):
        copies = Copies(r.sem)
        chunks = [None] * 4
        for chunk in (3, 0, 1, 2):
            part = pl.ds(chunk * width, width)
            chunks[chunk] = copies.start(r.att.at[:, part], r.held.at[:, part], False)
        loads = [copies.start(getattr(r, n), getattr(r, "own_" + n), False) for n in late]
        fill_mask(r.lengths, r.mask)
        attend_backward(
            r.first,
            r.first_low,
            r.qkv,
            r.lse,
            r.mask,
            r.held,
            r.mixed_grad,
            r.qkv_grad,
            r.input_grad,
            lambda chunk: chunks[chunk].wait(),
        )
        wait_all(loads)
        r.norm_rows[...] = jnp.zeros_like(r.norm_rows)
        r.norm_rows[0:4] = (r.norm_a[...] + r.norm_b[...]).astype(LOW)
        extra = product(r.own_picker[...], r.norm_rows[...], 1, 1).astype(LOW)
        half = width // 2
        r.extra[...] = extra
        columns = pl.ds(3 * width, NORM_COLS)
        copies.start(r.extra.at[pl.ds(0, half)], r.send.at[:, columns])
        copies.start(r.extra.at[pl.ds(half, half)], r.keep.at[:, columns])
        weight_sum(
            r.own_picker,
            (r.own_low2, r.own_tokens),
            (r.own_qkv_grad2, r.qkv_grad),
            r.turned,
            r.whole,
            copies,
            r.send,
            r.keep,
        )
        copies.finish()

    given = {
        "lengths": (SCALARS, lengths),
        "first": (VECTORS, first),
        "first_low": (VECTORS, first_low),
        "qkv": (VECTORS, qkv),
        "lse": (VECTORS, lse),
        "norm_a": (VECTORS, norm_grads[0]),
        "norm_b": (VECTORS, norm_grads[1]),
        "att": (IN_HBM, att),
    }
    given |= {name: (IN_HBM, value) for name, value in late.items()}
    scratch = {"own_" + name: pltpu.VMEM(value.shape, LOW) for name, value in late.items()}
    scratch |= {
        "held": pltpu.VMEM((width, 4 * width), LOW),
        "mask": pltpu.VMEM((count, count), f32),
        "mixed_grad": pltpu.VMEM(size, LOW),
        "qkv_grad": pltpu.VMEM((count, 3 * width), LOW),
        "turned": pltpu.VMEM((width, 2 * count), LOW),
        "whole": pltpu.VMEM((width, 3 * width), LOW),
        "norm_rows": pltpu.VMEM((NORM_COLS, width), LOW),
        "extra": pltpu.VMEM((width, NORM_COLS), LOW),
        "sem": pltpu.SemaphoreType.DMA((4 + len(late) + 2 + 2 * (3 * width // TILE),)),
    }
    return launch(
        body,
        given,
        {
            "input_grad": (VECTORS, size, f32),
            "send": (IN_HBM, (width // 2, wide), LOW),
            "keep": (IN_HBM, (width // 2, wide), LOW),
        },
        scratch,
        count * width * 10 * width + 5 * count * count * width,
        16 * width * width,
        60,
    )


AXES = ("dp", "fsdp")


class Route:
    def __init__(self):
        rows, cols = lax.axis_size("dp"), lax.axis_size("fsdp")
        self.inner = cols // 4
        self.ring_size = rows // 2 * self.inner
        self.cols = cols
        self.world = rows * cols
        row, col = lax.axis_index("dp"), lax.axis_index("fsdp")
        self.q = row // 2 * self.inner + col // 4
        self.y, self.x, self.c = row % 2, col // 2 % 2, col % 2

    def joint(self, q, y, x, c):
        return (q // self.inner * 2 + y) * self.cols + q % self.inner * 4 + x * 2 + c

    def move(self, array, step):
        pairs = []
        for q in range(self.ring_size):
            for y in (0, 1):
                for x in (0, 1):
                    for c in (0, 1):
                        to = step(q, y, x, c)
                        pairs.append((self.joint(q, y, x, c), self.joint(*to)))
        return lax.ppermute(array, AXES, pairs)

    def ring(self, array):
        return self.move(array, lambda q, y, x, c: ((q + 1) % self.ring_size, y, x, c))

    def core(self, array):
        return self.move(array, lambda q, y, x, c: (q, y, x, 1 - c))

    def first(self, array):
        return self.move(array, lambda q, y, x, c: (q, y ^ c, x ^ (1 - c), c))

    def second(self, array):
        return self.move(array, lambda q, y, x, c: (q, y ^ (1 - c), x ^ c, c))

    def owner(self, back, first, second, core):
        c = self.c ^ core
        x = self.x ^ jnp.where(c == 0, first, second)
        y = self.y ^ jnp.where(c == 0, second, first)
        return self.joint((self.q + self.ring_size - back) % self.ring_size, y, x, c)


def after(value, *earlier):
    return lax.optimization_barrier((value, earlier))[0]


class RingFirst:
    def __init__(self, route, piece):
        self.route, self.slots = route, [piece]

    def step(self, *earlier):
        self.slots.append(self.route.ring(after(self.slots[-1], *earlier)))

    def finish(self):
        route = self.route
        base = jnp.concatenate(self.slots)
        blocks = [(base, 0, 0), (route.first(base), 1, 0)]
        blocks += [(route.second(block), first, 1) for block, first, _ in blocks]
        arrays, owners = [], []
        for core in (0, 1):
            for block, first, second in blocks:
                arrays.append(route.core(block) if core else block)
                owners += [route.owner(i, first, second, core) for i in range(route.ring_size)]
        return arrays, owners


class RingMiddle:
    def __init__(self, route, piece):
        self.route = route
        self.pairs = [jnp.concatenate([piece, route.first(piece)])]

    def step(self, *earlier):
        self.pairs.append(self.route.ring(after(self.pairs[-1], *earlier)))

    def finish(self):
        route = self.route
        arrays, owners = [], []
        for i, pair in enumerate(self.pairs):
            other = route.second(pair)
            for core in (0, 1):
                for second, block in ((0, pair), (1, other)):
                    arrays.append(route.core(block) if core else block)
                    owners += [route.owner(i, first, second, core) for first in (0, 1)]
        return arrays, owners


def row_picker(owners, shard):
    rows = (jnp.stack(owners)[:, None] * shard + jnp.arange(shard)[None, :]).reshape(-1, 1)
    return (rows == jnp.arange(rows.size)[None, :]).astype(jnp.bfloat16)


def add_low(left, right):
    return (left.astype(jnp.float32) + right.astype(jnp.float32)).astype(jnp.bfloat16)


def owners_ring_last(route):
    return [
        route.owner(1 + j, first, second, core)
        for core in (1, 0)
        for second in (1, 0)
        for first in (1, 0)
        for j in range(route.ring_size)
    ]


def owners_ring_middle(route):
    return [
        route.owner(1 + j, first, second, core)
        for core in (1, 0)
        for second in (1, 0)
        for j in range(route.ring_size)
        for first in (1, 0)
    ]


def cut(array, count):
    size = array.shape[0] // count
    return [array[k * size : (k + 1) * size] for k in range(count)]


class SumWhole:
    def __init__(self, route, upper, lower):
        self.term = jnp.concatenate([upper, lower])

    def spread(self, *earlier):
        return ()

    def step(self, *earlier):
        return ()

    def finish(self):
        return lax.psum_scatter(self.term, AXES, scatter_dimension=0, tiled=True).astype(
            jnp.float32
        )


class SumRingLast:
    def __init__(self, route, send, keep):
        self.route, self.keep = route, keep
        self.arrived = route.core(send)

    def fold(self, *earlier):
        half = self.keep.shape[0] // 2
        keep, arrived = after((self.keep, self.arrived), *earlier)
        send = add_low(keep[:half], arrived[:half])
        self.keep = add_low(keep[half:], arrived[half:])
        return send

    def finish(self):
        self.arrived = self.route.second(self.sent)
        self.arrived = self.route.first(self.fold())
        count = self.route.ring_size
        pieces = [add_low(a, b) for a, b in zip(cut(self.keep, count), cut(self.arrived, count))]
        moving = pieces[0]
        for piece in pieces[1:-1]:
            moving = add_low(piece, self.route.ring(moving))
        return pieces[-1].astype(jnp.float32) + self.route.ring(moving).astype(jnp.float32)

    def spread(self, *earlier):
        self.sent = self.fold(*earlier)
        return self.sent


class SumRingMiddle:
    def __init__(self, route, send, keep):
        self.route, self.keep = route, keep
        self.arrived = route.core(send)

    def spread(self, *earlier):
        half, count = self.keep.shape[0] // 2, self.route.ring_size
        keep, arrived = after((self.keep, self.arrived), *earlier)
        sends = [add_low(a, b) for a, b in zip(cut(keep[:half], count), cut(arrived[:half], count))]
        self.keeps = [
            add_low(a, b) for a, b in zip(cut(keep[half:], count), cut(arrived[half:], count))
        ]
        self.others = [self.route.second(send) for send in sends]
        self.moving = None
        self.done = 0
        return sends

    def step(self, *earlier):
        local = add_low(after(self.keeps[self.done], *earlier), self.others[self.done])
        self.moving = local if self.moving is None else add_low(local, self.route.ring(self.moving))
        self.done += 1
        return self.moving

    def finish(self):
        while self.done < len(self.keeps):
            self.step()
        shard = self.moving.shape[0] // 2
        other = self.route.first(self.moving[:shard])
        return self.moving[shard:].astype(jnp.float32) + other.astype(jnp.float32)


def update(gradient, master, moment, average, step_rate):
    moment_new = 0.9 * moment + gradient
    master_new = master - step_rate * (gradient + 0.9 * moment_new)
    average_new = 0.8 * average + 0.2 * master_new
    return (gradient, moment_new, master_new, average_new, master_new.astype(jnp.bfloat16))


def shards(
    tokens,
    cotangent,
    seq_lengths,
    att_master,
    ffn_master,
    norm_master,
    att_moment,
    ffn_moment,
    norm_moment,
    att_average,
    ffn_average,
    norm_average,
):
    row_count = tokens.shape[0]
    route = Route()
    shard = att_master.shape[0]
    norm_piece = jnp.pad(norm_master.T, ((0, 0), (0, NORM_COLS - norm_master.shape[0])))
    att_piece = jnp.concatenate([att_master, norm_piece], axis=1).astype(jnp.bfloat16)
    ffn_pieces = ffn_master.astype(jnp.bfloat16)
    width = att_master.shape[1]
    tiled = shard % 16 == 0
    if tiled:
        middle = row_picker(owners_ring_middle(route), shard)
        last = row_picker(owners_ring_last(route), shard)
        down = RingFirst(route, ffn_pieces[1])
        down.step()
        att = RingMiddle(route, att_piece)
        up = RingMiddle(route, ffn_pieces[0])
        att.step()
        for _ in range(route.ring_size - 2):
            down.step()
            att.step()
            up.step(down.slots[-1])
        up.step()
        att, down, up = att.finish(), down.finish(), up.finish()
        sum_middle, sum_last = SumRingMiddle, SumRingLast
    else:
        middle = last = row_picker(list(range(route.world)), shard)
        att, down, up = [
            ([lax.all_gather(piece, AXES, axis=0, tiled=True)], [0])
            for piece in (att_piece, ffn_pieces[1], ffn_pieces[0])
        ]
        sum_middle = sum_last = SumWhole
    (att_parts, att_owners), (down_parts, down_owners), (up_parts, up_owners) = [
        (parts, jnp.stack(owners).astype(jnp.int32) if tiled else jnp.zeros(1, jnp.int32))
        for parts, owners in (att, down, up)
    ]
    f = first_attention(seq_lengths, att_owners, tokens, att_parts)
    m = middle_layers(
        seq_lengths,
        f.norm,
        f.hidden,
        cotangent,
        f.att,
        up_parts,
        up_owners,
        down_parts,
        down_owners,
        middle,
    )
    down_sum = sum_middle(route, m.send, m.keep)
    b = first_ffn_backward(m, f.norm, f.unit, f.inverse, f.mixed, middle, last)
    up_sum = sum_middle(route, b.send_up, b.keep_up)
    out_sum = sum_last(route, b.send_out, b.keep_out)
    sends = down_sum.spread(b.first_low)
    a = first_attention_backward(
        seq_lengths,
        after(b.first, sends),
        b.first_low,
        f.qkv,
        f.lse,
        f.att,
        tokens,
        m.low2,
        m.qkv_grad2,
        (m.norm_grad, b.norm_grad),
        last,
    )
    in_sum = sum_last(route, a.send, a.keep)
    sends = up_sum.spread(a.input_grad)
    moving = down_sum.step(sends)
    sends = out_sum.spread(moving)
    sends = in_sum.spread(sends)
    down_share, up_share = down_sum.finish(), up_sum.finish()
    proj_share, inproj_share = out_sum.finish(), in_sum.finish()
    wide = 3 * width // 4
    totals = (
        jnp.concatenate([inproj_share[:, :wide], proj_share], axis=1),
        jnp.stack([up_share, down_share]),
        inproj_share[:, wide : wide + norm_master.shape[0]].T,
    )
    step_rate = 0.1 / math.sqrt(row_count * lax.axis_size(("dp", "fsdp")))
    att_out = update(totals[0], att_master, att_moment, att_average, step_rate)
    ffn_out = update(totals[1], ffn_master, ffn_moment, ffn_average, step_rate)
    norm_out = update(totals[2], norm_master, norm_moment, norm_average, step_rate)
    return (
        m.layer_output,
        a.input_grad,
        att_out[0],
        att_out[1],
        att_out[2],
        att_out[3],
        att_out[4],
        ffn_out[0],
        ffn_out[1],
        ffn_out[2],
        ffn_out[3],
        ffn_out[4],
        norm_out[0],
        norm_out[1],
        norm_out[2],
        norm_out[3],
        norm_out[4],
    )


def solution(mesh):
    return jax.shard_map(
        shards,
        mesh=mesh,
        in_specs=(
            P(("dp", "fsdp"), None),
            P(("dp", "fsdp"), None),
            P(("dp", "fsdp"), None),
            P(("dp", "fsdp"), None),
            P(None, ("dp", "fsdp"), None),
            P(None, ("dp", "fsdp")),
            P(("dp", "fsdp"), None),
            P(None, ("dp", "fsdp"), None),
            P(None, ("dp", "fsdp")),
            P(("dp", "fsdp"), None),
            P(None, ("dp", "fsdp"), None),
            P(None, ("dp", "fsdp")),
        ),
        out_specs=(
            P(("dp", "fsdp"), None),
            P(("dp", "fsdp"), None),
            P(("dp", "fsdp"), None),
            P(("dp", "fsdp"), None),
            P(("dp", "fsdp"), None),
            P(("dp", "fsdp"), None),
            P(("dp", "fsdp"), None),
            P(None, ("dp", "fsdp"), None),
            P(None, ("dp", "fsdp"), None),
            P(None, ("dp", "fsdp"), None),
            P(None, ("dp", "fsdp"), None),
            P(None, ("dp", "fsdp"), None),
            P(None, ("dp", "fsdp")),
            P(None, ("dp", "fsdp")),
            P(None, ("dp", "fsdp")),
            P(None, ("dp", "fsdp")),
            P(None, ("dp", "fsdp")),
        ),
        check_vma=False,
    )
```

time: 933 us -> 449 us (0.48)
  waiting for transfers between devices: 614 us -> 231 us
  matrix products: 185 us -> 0 us
  Pallas kernels: 0 us -> 102 us
  starting transfers between devices: 0.25 us -> 50.5 us
  blocking collectives: 43.4 us -> 0 us
  between operations: 17.6 us -> 2.07 us
    reduce_scatter x3 -> x0, waiting for transfers between devices: 433 us -> none  [owner_sum(): lax.psum_scatter(term, ('dp', 'fsdp'), scatter_dimension=dim, tiled=True)]
    ppermute x0 -> x72, waiting for transfers between devices: none -> 231 us  [move(): return lax.ppermute(array, AXES, pairs)]
    dot_general x68 -> x0, matrix products: 168 us -> none  [the longest x4 30.1 us: weight_sum(): jnp.einsum('td,tf->df', left, right, preferred_element_type=jnp.float32)]
    all_gather x2 -> x0, waiting for transfers between devices: 128 us -> none  [the longest x1 97 us: fetch_forward(): lax.all_gather(pieces[1], ('dp', 'fsdp'), axis=1, tiled=True)]
    pallas_call x0 -> x4, Pallas kernels: none -> 102 us  [launch(): pl.pallas_call(kernel, out_shape=[jax.ShapeDtypeStruct(shape, kind) for _...]
    unnamed x7 -> x0, waiting for transfers between devices: 53.2 us -> none
    ppermute x0 -> x72, starting transfers between devices: none -> 50.5 us  [move(): return lax.ppermute(array, AXES, pairs)]
    all_gather x1 -> x0, blocking collectives: 43.4 us -> none  [fetch_forward(): lax.all_gather(pieces[2], ('dp', 'fsdp'), axis=1, tiled=True)]
  transfers between devices with their start and end apart: 6 -> 72, of which waited for: 6 -> 26; matrix products, arithmetic and copies ran while one was open for 11% -> 6% of each run, Pallas kernels for 0% -> 12%
where the time goes in v4:
time: 449 us; the launch traced here: 443 us
  waiting for transfers between devices  231 us (51%)
  Pallas kernels  102 us (23%)
  starting transfers between devices  50.5 us (11%)
  other arithmetic  32.7 us (7%)
  local copies, waits for them, and re-layouts  25.1 us (6%)
    ppermute x72, waiting for transfers between devices, move(): return lax.ppermute(array, AXES, pairs)  231 us
    pallas_call x4, Pallas kernels, launch(): pl.pallas_call(kernel, out_shape=[jax.ShapeDtypeStruct(shape, kind) for _...  102 us
    ppermute x72, starting transfers between devices, move(): return lax.ppermute(array, AXES, pairs)  50.5 us
    unnamed x122, local copies, waits for them, and re-layouts  23.5 us
    convert_element_type x20, other arithmetic, add_low(): (left.astype(jnp.float32) + right.astype(jnp.float32)).astype(jnp.bfloat16)  19.7 us
  transfers between devices with their start and end apart: 72, of which 26 were waited for; matrix products, arithmetic and copies ran while one was open for 6% of the time, Pallas kernels for 12%

profile of v4, /device:TPU:0, one launch (start us, length us, event | category | flops | bytes accessed | tf_op | source)
XLA Modules:
  0.0 443.2 jit_solution(2473483800658551564)
XLA Ops:
  7.4 7.3 %collective-permute-done.20 = bf16[32,4096]{1,0:T(8,128)(2,1)S(1)} collective-permute-done((bf16[32,4096]{1,0:T(8,128)(2,1)S(1)}, bf16[32,4096]{1,0:T(8,128)(2,1)S(1)}, u32[]{:S(2)}, u32[]{:S(2)}) %collective-permute-start.20) | collective-permute-done | bytes 262176 | tf_op jit(solution)/shard_map/ppermute | solution.py:746
  16.7 9.0 %collective-permute-done.21 = bf16[32,4096]{1,0:T(8,128)(2,1)S(1)} collective-permute-done((bf16[32,4096]{1,0:T(8,128)(2,1)S(1)}, bf16[32,4096]{1,0:T(8,128)(2,1)S(1)}, u32[]{:S(2)}, u32[]{:S(2)}) %collective-permute-start.21) | collective-permute-done | bytes 262176 | tf_op jit(solution)/shard_map/ppermute | solution.py:746
  25.8 17.2 %collective-permute-done.26 = bf16[32,4096]{1,0:T(8,128)(2,1)S(1)} collective-permute-done((bf16[32,4096]{1,0:T(8,128)(2,1)S(1)}, bf16[32,4096]{1,0:T(8,128)(2,1)S(1)}, u32[]{:S(2)}, u32[]{:S(2)}) %collective-permute-start.26) | collective-permute-done | bytes 262176 | tf_op jit(solution)/shard_map/ppermute | solution.py:746
  44.0 10.2 %collective-permute-done.22.refs_12_ = bf16[64,4096]{1,0:T(8,128)(2,1)S(1)} collective-permute-done((bf16[64,4096]{1,0:T(8,128)(2,1)S(1)}, bf16[64,4096]{1,0:T(8,128)(2,1)S(1)}, u32[]{:S(2)}, u32[]{:S(2)}) %collective-permute-start.22) | collective-permute-done | bytes 524320 | tf_op jit(solution)/shard_map/ppermute | solution.py:746
  56.7 9.1 %collective-permute-done.8.refs_11_ = bf16[64,4224]{1,0:T(8,128)(2,1)S(1)} collective-permute-done((bf16[64,4224]{1,0:T(8,128)(2,1)S(1)}, bf16[64,4224]{1,0:T(8,128)(2,1)S(1)}, u32[]{:S(2)}, u32[]{:S(2)}) %collective-permute-start.8) | collective-permute-done | bytes 540704 | tf_op jit(solution)/shard_map/ppermute | solution.py:746
  70.8 3.9 collective-permute-done.27.refs_16_
  74.7 17.3 %collective-permute-done.23.refs_13_ = bf16[64,4096]{1,0:T(8,128)(2,1)S(1)} collective-permute-done((bf16[64,4096]{1,0:T(8,128)(2,1)S(1)}, bf16[64,4096]{1,0:T(8,128)(2,1)S(1)}, u32[]{:S(2)}, u32[]{:S(2)}) %collective-permute-start.23) | collective-permute-done | bytes 524320 | tf_op jit(solution)/shard_map/ppermute | solution.py:746
  92.5 3.4 collective-permute-start.10
  96.0 11.8 %collective-permute-done.12.refs_15_ = bf16[64,4224]{1,0:T(8,128)(2,1)S(1)} collective-permute-done((bf16[64,4224]{1,0:T(8,128)(2,1)S(1)}, bf16[64,4224]{1,0:T(8,128)(2,1)S(1)}, u32[]{:S(2)}, u32[]{:S(2)}) %collective-permute-start.12) | collective-permute-done | bytes 540704 | tf_op jit(solution)/shard_map/ppermute | solution.py:746
  107.8 3.3 collective-permute-start.29
  115.1 4.0 collective-permute-done.31.refs_20_
  125.8 8.3 %collective-permute-done.13.refs_16_ = bf16[64,4224]{1,0:T(8,128)(2,1)} collective-permute-done((bf16[64,4224]{1,0:T(8,128)(2,1)S(1)}, bf16[64,4224]{1,0:T(8,128)(2,1)}, u32[]{:S(2)}, u32[]{:S(2)}) %collective-permute-start.13) | collective-permute-done | bytes 540704 | tf_op jit(solution)/shard_map/ppermute | solution.py:746
  151.3 10.5 %shard_map.251 = (bf16[1024,4096]{1,0:T(8,128)(2,1)}, f32[4,1024]{1,0:T(4,128)S(1)}, bf16[256,3072]{1,0:T(8,128)(2,1)S(1)}, bf16[256,1024]{1,0:T(8,128)(2,1)S(1)...) custom-call(s32[1,4]{1,0:T(1,128)S(1)} %copy-done.18, ...), custom_call_target="tpu_custom_call" | custom-call | flops 2415919104 | bytes 22020096 | tf_op jit(solution)/shard_map/pallas_call | solution.py:47
  167.7 50.9 %shard_map.252 = (bf16[256,1024]{1,0:T(8,128)(2,1)}, bf16[256,4096]{1,0:T(8,128)(2,1)}, bf16[256,4096]{1,0:T(8,128)(2,1)}, bf16[256,1024]{1,0:T(8,128)(2,1)}, bf...) custom-call(s32[1,4]{1,0:T(1,128)} %refs_0_.5, ...), custom_call_target="tpu_custom_call" | custom-call | flops 22414360576 | bytes 50331648 | tf_op jit(solution)/shard_map/pallas_call | solution.py:47
  220.9 21.2 %shard_map.253 = (f32[256,1024]{1,0:T(8,128)}, bf16[256,1024]{1,0:T(8,128)(2,1)}, f32[4,1024]{1,0:T(4,128)}, bf16[512,4096]{1,0:T(8,128)(2,1)}, bf16[512,4096]{1...) custom-call(f32[256,1024]{1,0:T(8,128)} %get-tuple-element.73.refs_0_, ...), custom_call_target="tpu_custom_call" | custom-call | flops 9663676416 | bytes 33554432 | tf_op jit(solution)/shard_map/pallas_call | solution.py:47
  242.7 5.1 %add_convert_fusion.12 = (bf16[64,4096]{1,0:T(8,128)(2,1)S(1)}, bf16[64,4096]{1,0:T(8,128)(2,1)S(1)}, bf16[64,4096]{1,0:T(8,128)(2,1)S(1)}, bf16[64,4096]{1,0:T(...) fusion(bf16[512,4096]{1,0:T(8,128)(2,1)} %collective-permute-do, ...), kind=kLoop, calls=%fused_computation.21 | loop fusion | flops 8388608 | bytes 12582912 | tf_op jit(solution)/shard_map/convert_element_type | solution.py:817
  249.6 19.3 %shard_map.254 = (f32[256,1024]{1,0:T(8,128)}, bf16[512,3200]{1,0:T(8,128)(2,1)}, bf16[512,3200]{1,0:T(8,128)(2,1)}) custom-call(s32[1,4]{1,0:T(1,128)} %refs_0_.5, f32[256,1024]{1,0:T(8,128)} %get-tuple-element.92.refs_1_, bf16[256,1024]{1,0:T(8,128)(2,1)} %get-tuple-element.89.refs_2_, bf16[256,3072]{1,0:T(8,128)(2,1)} %copy-done.19, ...), custom_call_target="tpu_custom_call" | custom-call | flops 6039797760 | bytes 16777216 | tf_op jit(solution)/shard_map/pallas_call | solution.py:47
  269.0 5.1 %add_convert_fusion.23 = (bf16[64,4096]{1,0:T(8,128)(2,1)S(1)}, bf16[64,4096]{1,0:T(8,128)(2,1)S(1)}, bf16[64,4096]{1,0:T(8,128)(2,1)S(1)}, bf16[64,4096]{1,0:T(...) fusion(bf16[512,4096]{1,0:T(8,128)(2,1)} %collective-permute-do, ...), kind=kLoop, calls=%fused_computation.32 | loop fusion | flops 8388608 | bytes 12582912 | tf_op jit(solution)/shard_map/convert_element_type | solution.py:817
  280.1 6.9 %collective-permute-done.52 = bf16[256,1024]{1,0:T(8,128)(2,1)S(1)} collective-permute-done((bf16[256,1024]{1,0:T(8,128)(2,1)S(1)}, bf16[256,1024]{1,0:T(8,128)(2,1)S(1)}, u32[]{:S(2)}, u32[]{:S(2)}) %collective-permute-start.52) | collective-permute-done | bytes 524320 | tf_op jit(solution)/shard_map/ppermute | solution.py:746
  289.3 4.6 %collective-permute-done.60 = bf16[64,4096]{1,0:T(8,128)(2,1)S(1)} collective-permute-done((bf16[64,4096]{1,0:T(8,128)(2,1)S(1)}, bf16[64,4096]{1,0:T(8,128)(2,1)S(1)}, u32[]{:S(2)}, u32[]{:S(2)}) %collective-permute-start.60) | collective-permute-done | bytes 524320 | tf_op jit(solution)/shard_map/ppermute | solution.py:746
  299.7 11.5 %collective-permute-done.54 = bf16[32,1024]{1,0:T(8,128)(2,1)} collective-permute-done((bf16[32,1024]{1,0:T(8,128)(2,1)S(1)}, bf16[32,1024]{1,0:T(8,128)(2,1)}, u32[]{:S(2)}, u32[]{:S(2)}) %collective-permute-start.54) | collective-permute-done | bytes 65568 | tf_op jit(solution)/shard_map/ppermute | solution.py:746
  315.7 15.5 %collective-permute-done.55 = bf16[32,1024]{1,0:T(8,128)(2,1)S(1)} collective-permute-done((bf16[32,1024]{1,0:T(8,128)(2,1)S(1)}, bf16[32,1024]{1,0:T(8,128)(2,1)S(1)}, u32[]{:S(2)}, u32[]{:S(2)}) %collective-permute-start.55) | collective-permute-done | bytes 65568 | tf_op jit(solution)/shard_map/ppermute | solution.py:746
  331.7 17.3 %collective-permute-done.56 = bf16[32,1024]{1,0:T(8,128)(2,1)S(1)} collective-permute-done((bf16[32,1024]{1,0:T(8,128)(2,1)S(1)}, bf16[32,1024]{1,0:T(8,128)(2,1)S(1)}, u32[]{:S(2)}, u32[]{:S(2)}) %collective-permute-start.56) | collective-permute-done | bytes 65568 | tf_op jit(solution)/shard_map/ppermute | solution.py:746
  351.9 6.2 %collective-permute-done.66 = bf16[64,4096]{1,0:T(8,128)(2,1)S(1)} collective-permute-done((bf16[64,4096]{1,0:T(8,128)(2,1)S(1)}, bf16[64,4096]{1,0:T(8,128)(2,1)S(1)}, u32[]{:S(2)}, u32[]{:S(2)}) %collective-permute-start.66) | collective-permute-done | bytes 524320 | tf_op jit(solution)/shard_map/ppermute | solution.py:746
  358.1 10.3 %collective-permute-done.69 = bf16[64,4096]{1,0:T(8,128)(2,1)S(1)} collective-permute-done((bf16[64,4096]{1,0:T(8,128)(2,1)S(1)}, bf16[64,4096]{1,0:T(8,128)(2,1)S(1)}, u32[]{:S(2)}, u32[]{:S(2)}) %collective-permute-start.69) | collective-permute-done | bytes 524320 | tf_op jit(solution)/shard_map/ppermute | solution.py:746
  369.6 10.0 %collective-permute-done.63 = bf16[64,4096]{1,0:T(8,128)(2,1)S(1)} collective-permute-done((bf16[64,4096]{1,0:T(8,128)(2,1)S(1)}, bf16[64,4096]{1,0:T(8,128)(2,1)S(1)}, u32[]{:S(2)}, u32[]{:S(2)}) %collective-permute-start.63) | collective-permute-done | bytes 524320 | tf_op jit(solution)/shard_map/ppermute | solution.py:746
  381.6 7.4 %collective-permute-done.70 = bf16[64,4096]{1,0:T(8,128)(2,1)S(1)} collective-permute-done((bf16[64,4096]{1,0:T(8,128)(2,1)S(1)}, bf16[64,4096]{1,0:T(8,128)(2,1)S(1)}, u32[]{:S(2)}, u32[]{:S(2)}) %collective-permute-start.70) | collective-permute-done | bytes 524320 | tf_op jit(solution)/shard_map/ppermute | solution.py:746
  391.0 5.5 %collective-permute-done.47 = bf16[256,3200]{1,0:T(8,128)(2,1)S(1)} collective-permute-done((bf16[256,3200]{1,0:T(8,128)(2,1)S(1)}, bf16[256,3200]{1,0:T(8,128)(2,1)S(1)}, u32[]{:S(2)}, u32[]{:S(2)}) %collective-permute-start.47) | collective-permute-done | bytes 1638432 | tf_op jit(solution)/shard_map/ppermute | solution.py:746
  399.0 10.4 %collective-permute-done.48 = bf16[128,3200]{1,0:T(8,128)(2,1)S(1)} collective-permute-done((bf16[128,3200]{1,0:T(8,128)(2,1)S(1)}, bf16[128,3200]{1,0:T(8,128)(2,1)S(1)}, u32[]{:S(2)}, u32[]{:S(2)}) %collective-permute-start.48) | collective-permute-done | bytes 819232 | tf_op jit(solution)/shard_map/ppermute | solution.py:746
  409.6 11.4 %collective-permute-done.49 = bf16[32,3200]{1,0:T(8,128)(2,1)S(1)} collective-permute-done((bf16[32,3200]{1,0:T(8,128)(2,1)S(1)}, bf16[32,3200]{1,0:T(8,128)(2,1)S(1)}, u32[]{:S(2)}, u32[]{:S(2)}) %collective-permute-start.49) | collective-permute-done | bytes 204832 | tf_op jit(solution)/shard_map/ppermute | solution.py:746
  422.9 5.8 %collective-permute-done.50 = bf16[32,3200]{1,0:T(8,128)(2,1)S(1)} collective-permute-done((bf16[32,3200]{1,0:T(8,128)(2,1)S(1)}, bf16[32,3200]{1,0:T(8,128)(2,1)S(1)}, u32[]{:S(2)}, u32[]{:S(2)}) %collective-permute-start.50) | collective-permute-done | bytes 204832 | tf_op jit(solution)/shard_map/ppermute | solution.py:746
  430.0 6.4 %collective-permute-done.51 = bf16[32,3200]{1,0:T(8,128)(2,1)S(1)} collective-permute-done((bf16[32,3200]{1,0:T(8,128)(2,1)S(1)}, bf16[32,3200]{1,0:T(8,128)(2,1)S(1)}, u32[]{:S(2)}, u32[]{:S(2)}) %collective-permute-start.51) | collective-permute-done | bytes 204832 | tf_op jit(solution)/shard_map/ppermute | solution.py:746
  (298 shorter events, 95.1 us)
Async XLA Ops:
  14.8 28.7 %collective-permute-start.17 = (bf16[64,4096]{1,0:T(8,128)(2,1)S(1)}, bf16[64,4096]{1,0:T(8,128)(2,1)S(1)}, u32[]{:S(2)}, u32[]{:S(2)}) collective-permute-start(bf16[64,4096]{1,0:T(8,128)(2,1)S(1)} %pad_maximum_fusion.3.refs_8_), channel_id=1, source_target_pairs={{0,4},{1,3},{2,6},{3,1},{4,0},{5,7},{6,2},{7,5},{8,12},{9,11},{10,... | collective-permute-start | bytes 1572872 | tf_op jit(solution)/shard_map/ppermute | solution.py:746
  15.4 28.1 %collective-permute-start.4 = (bf16[64,4224]{1,0:T(8,128)(2,1)S(1)}, bf16[64,4224]{1,0:T(8,128)(2,1)S(1)}, u32[]{:S(2)}, u32[]{:S(2)}) collective-permute-start(bf16[64,4224]{1,0:T(8,128)(2,1)S(1)} %pad_maximum_fusion.2.refs_3_), channel_id=1, source_target_pairs={{0,8},{1,9},{2,10},{3,11},{4,12},{5,13},{6,14},{7,15},{8,16},{9,17... | collective-permute-start | bytes 1622024 | tf_op jit(solution)/shard_map/ppermute | solution.py:746
  25.8 28.4 %collective-permute-start.22 = (bf16[64,4096]{1,0:T(8,128)(2,1)S(1)}, bf16[64,4096]{1,0:T(8,128)(2,1)S(1)}, u32[]{:S(2)}, u32[]{:S(2)}) collective-permute-start(bf16[64,4096]{1,0:T(8,128)(2,1)S(1)} %pad_maximum_fusion.3.refs_8_), channel_id=1, source_target_pairs={{0,8},{1,9},{2,10},{3,11},{4,12},{5,13},{6,14},{7,15},{8,16},{9,17... | collective-permute-start | bytes 1572872 | tf_op jit(solution)/shard_map/ppermute | solution.py:746
  44.0 21.8 %collective-permute-start.8 = (bf16[64,4224]{1,0:T(8,128)(2,1)S(1)}, bf16[64,4224]{1,0:T(8,128)(2,1)S(1)}, u32[]{:S(2)}, u32[]{:S(2)}) collective-permute-start(bf16[64,4224]{1,0:T(8,128)(2,1)S(1)} %collective-permute-done.4.refs_7_), channel_id=1, source_target_pairs={{0,8},{1,9},{2,10},{3,11},{4,12},{5,13},{6,14},{7,15},{8,16},{9,17... | collective-permute-start | bytes 1622024 | tf_op jit(solution)/shard_map/ppermute | solution.py:746
  55.6 19.1 %collective-permute-start.27 = (bf16[64,4096]{1,0:T(8,128)(2,1)S(1)}, bf16[64,4096]{1,0:T(8,128)(2,1)S(1)}, u32[]{:S(2)}, u32[]{:S(2)}) collective-permute-start(bf16[64,4096]{1,0:T(8,128)(2,1)S(1)} %collective-permute-done.22.refs_12_), channel_id=1, source_target_pairs={{0,8},{1,9},{2,10},{3,11},{4,12},{5,13},{6,14},{7,15},{8,16},{9,17... | collective-permute-start | bytes 1572872 | tf_op jit(solution)/shard_map/ppermute | solution.py:746
  65.8 26.7 %collective-permute-start.35 = (bf16[128,4096]{1,0:T(8,128)(2,1)S(1)}, bf16[128,4096]{1,0:T(8,128)(2,1)}, u32[]{:S(2)}, u32[]{:S(2)}) collective-permute-start(bf16[128,4096]{1,0:T(8,128)(2,1)S(1)} %pad_maximum_fusion.refs_24_), channel_id=1, source_target_pairs={{0,2},{1,5},{2,0},{3,7},{4,6},{5,1},{6,4},{7,3},{8,10},{9,13},{10,... | collective-permute-start | bytes 3145736 | tf_op jit(solution)/shard_map/ppermute | solution.py:746
  67.2 28.7 %collective-permute-start.36 = (bf16[128,4096]{1,0:T(8,128)(2,1)S(1)}, bf16[128,4096]{1,0:T(8,128)(2,1)}, u32[]{:S(2)}, u32[]{:S(2)}) collective-permute-start(bf16[128,4096]{1,0:T(8,128)(2,1)S(1)} %pad_maximum_fusion.refs_24_), channel_id=1, source_target_pairs={{0,4},{1,3},{2,6},{3,1},{4,0},{5,7},{6,2},{7,5},{8,12},{9,11},{10,... | collective-permute-start | bytes 3145736 | tf_op jit(solution)/shard_map/ppermute | solution.py:746
  68.2 23.8 %collective-permute-start.23 = (bf16[64,4096]{1,0:T(8,128)(2,1)S(1)}, bf16[64,4096]{1,0:T(8,128)(2,1)S(1)}, u32[]{:S(2)}, u32[]{:S(2)}) collective-permute-start(bf16[64,4096]{1,0:T(8,128)(2,1)S(1)} %collective-permute-done.22.refs_12_), channel_id=1, source_target_pairs={{0,4},{1,3},{2,6},{3,1},{4,0},{5,7},{6,2},{7,5},{8,12},{9,11},{10,... | collective-permute-start | bytes 1572872 | tf_op jit(solution)/shard_map/ppermute | solution.py:746
  70.8 25.2 %collective-permute-start.38 = (bf16[128,4096]{1,0:T(8,128)(2,1)S(1)}, bf16[128,4096]{1,0:T(8,128)(2,1)S(1)}, u32[]{:S(2)}, u32[]{:S(2)}) collective-permute-start(bf16[128,4096]{1,0:T(8,128)(2,1)S(1)} %pad_maximum_fusion.refs_24_), channel_id=1, source_target_pairs={{0,1},{1,0},{2,3},{3,2},{4,5},{5,4},{6,7},{7,6},{8,9},{9,8},{10,11... | collective-permute-start | bytes 3145736 | tf_op jit(solution)/shard_map/ppermute | solution.py:746
  96.0 23.2 %collective-permute-start.31 = (bf16[64,4096]{1,0:T(8,128)(2,1)S(1)}, bf16[64,4096]{1,0:T(8,128)(2,1)}, u32[]{:S(2)}, u32[]{:S(2)}) collective-permute-start(bf16[64,4096]{1,0:T(8,128)(2,1)S(1)} %collective-permute-done.27.refs_16_), channel_id=1, source_target_pairs={{0,8},{1,9},{2,10},{3,11},{4,12},{5,13},{6,14},{7,15},{8,16},{9,17... | collective-permute-start | bytes 1572872 | tf_op jit(solution)/shard_map/ppermute | solution.py:746
  112.7 28.3 %collective-permute-start.37 = (bf16[128,4096]{1,0:T(8,128)(2,1)}, bf16[128,4096]{1,0:T(8,128)(2,1)}, u32[]{:S(2)}, u32[]{:S(2)}) collective-permute-start(bf16[128,4096]{1,0:T(8,128)(2,1)} %collective-permute-done.35.refs_25_), channel_id=1, source_target_pairs={{0,4},{1,3},{2,6},{3,1},{4,0},{5,7},{6,2},{7,5},{8,12},{9,11},{10,... | collective-permute-start | bytes 3145736 | tf_op jit(solution)/shard_map/ppermute | solution.py:746
  137.3 30.3 %collective-permute-start.39 = (bf16[128,4096]{1,0:T(8,128)(2,1)}, bf16[128,4096]{1,0:T(8,128)(2,1)}, u32[]{:S(2)}, u32[]{:S(2)}) collective-permute-start(bf16[128,4096]{1,0:T(8,128)(2,1)} %collective-permute-done.35.refs_25_), channel_id=1, source_target_pairs={{0,1},{1,0},{2,3},{3,2},{4,5},{5,4},{6,7},{7,6},{8,9},{9,8},{10,11... | collective-permute-start | bytes 3145736 | tf_op jit(solution)/shard_map/ppermute | solution.py:746
  139.7 28.0 %collective-permute-start.40 = (bf16[128,4096]{1,0:T(8,128)(2,1)}, bf16[128,4096]{1,0:T(8,128)(2,1)}, u32[]{:S(2)}, u32[]{:S(2)}) collective-permute-start(bf16[128,4096]{1,0:T(8,128)(2,1)} %collective-permute-done.36.refs_26_), channel_id=1, source_target_pairs={{0,1},{1,0},{2,3},{3,2},{4,5},{5,4},{6,7},{7,6},{8,9},{9,8},{10,11... | collective-permute-start | bytes 3145736 | tf_op jit(solution)/shard_map/ppermute | solution.py:746
  141.0 26.7 %collective-permute-start.41 = (bf16[128,4096]{1,0:T(8,128)(2,1)}, bf16[128,4096]{1,0:T(8,128)(2,1)}, u32[]{:S(2)}, u32[]{:S(2)}) collective-permute-start(bf16[128,4096]{1,0:T(8,128)(2,1)} %collective-permute-done.37.refs_27_), channel_id=1, source_target_pairs={{0,1},{1,0},{2,3},{3,2},{4,5},{5,4},{6,7},{7,6},{8,9},{9,8},{10,11... | collective-permute-start | bytes 3145736 | tf_op jit(solution)/shard_map/ppermute | solution.py:746
  141.6 26.0 %collective-permute-start.30 = (bf16[64,4096]{1,0:T(8,128)(2,1)}, bf16[64,4096]{1,0:T(8,128)(2,1)}, u32[]{:S(2)}, u32[]{:S(2)}) collective-permute-start(bf16[64,4096]{1,0:T(8,128)(2,1)} %copy-done.54), channel_id=1, source_target_pairs={{0,1},{1,0},{2,3},{3,2},{4,5},{5,4},{6,7},{7,6},{8,9},{9,8},{10,11... | collective-permute-start | bytes 1572872 | tf_op jit(solution)/shard_map/ppermute | solution.py:746
  142.1 25.5 %collective-permute-start.34 = (bf16[64,4096]{1,0:T(8,128)(2,1)}, bf16[64,4096]{1,0:T(8,128)(2,1)}, u32[]{:S(2)}, u32[]{:S(2)}) collective-permute-start(bf16[64,4096]{1,0:T(8,128)(2,1)} %copy-done.57), channel_id=1, source_target_pairs={{0,1},{1,0},{2,3},{3,2},{4,5},{5,4},{6,7},{7,6},{8,9},{9,8},{10,11... | collective-permute-start | bytes 1572872 | tf_op jit(solution)/shard_map/ppermute | solution.py:746
  218.5 24.2 %collective-permute-start.42 = (bf16[512,4096]{1,0:T(8,128)(2,1)}, bf16[512,4096]{1,0:T(8,128)(2,1)}, u32[]{:S(2)}, u32[]{:S(2)}) collective-permute-start(bf16[512,4096]{1,0:T(8,128)(2,1)} %get-tuple-element.88), channel_id=1, source_target_pairs={{0,1},{1,0},{2,3},{3,2},{4,5},{5,4},{6,7},{7,6},{8,9},{9,8},{10,11... | collective-permute-start | bytes 12582920 | tf_op jit(solution)/shard_map/ppermute | solution.py:746
  242.1 26.9 %collective-permute-start.45 = (bf16[512,4096]{1,0:T(8,128)(2,1)}, bf16[512,4096]{1,0:T(8,128)(2,1)}, u32[]{:S(2)}, u32[]{:S(2)}) collective-permute-start(bf16[512,4096]{1,0:T(8,128)(2,1)} %get-tuple-element.105), channel_id=1, source_target_pairs={{0,1},{1,0},{2,3},{3,2},{4,5},{5,4},{6,7},{7,6},{8,9},{9,8},{10,11... | collective-permute-start | bytes 12582920 | tf_op jit(solution)/shard_map/ppermute | solution.py:746
  242.2 34.0 %collective-permute-start.44 = (bf16[512,1024]{1,0:T(8,128)(2,1)}, bf16[512,1024]{1,0:T(8,128)(2,1)}, u32[]{:S(2)}, u32[]{:S(2)}) collective-permute-start(bf16[512,1024]{1,0:T(8,128)(2,1)} %get-tuple-element.103), channel_id=1, source_target_pairs={{0,1},{1,0},{2,3},{3,2},{4,5},{5,4},{6,7},{7,6},{8,9},{9,8},{10,11... | collective-permute-start | bytes 3145736 | tf_op jit(solution)/shard_map/ppermute | solution.py:746
  247.8 26.4 %collective-permute-start.46 = (bf16[64,4096]{1,0:T(8,128)(2,1)}, bf16[64,4096]{1,0:T(8,128)(2,1)}, u32[]{:S(2)}, u32[]{:S(2)}) collective-permute-start(bf16[64,4096]{1,0:T(8,128)(2,1)} %get-tuple-element.177), channel_id=1, source_target_pairs={{0,4},{1,3},{2,6},{3,1},{4,0},{5,7},{6,2},{7,5},{8,12},{9,11},{10,... | collective-permute-start | bytes 1572872 | tf_op jit(solution)/shard_map/ppermute | solution.py:746
  279.8 34.3 %collective-permute-start.59 = (bf16[64,4096]{1,0:T(8,128)(2,1)}, bf16[64,4096]{1,0:T(8,128)(2,1)}, u32[]{:S(2)}, u32[]{:S(2)}) collective-permute-start(bf16[64,4096]{1,0:T(8,128)(2,1)} %get-tuple-element.168), channel_id=1, source_target_pairs={{0,4},{1,3},{2,6},{3,1},{4,0},{5,7},{6,2},{7,5},{8,12},{9,11},{10,... | collective-permute-start | bytes 1572872 | tf_op jit(solution)/shard_map/ppermute | solution.py:746
  294.9 19.3 %collective-permute-start.61 = (bf16[64,4096]{1,0:T(8,128)(2,1)}, bf16[64,4096]{1,0:T(8,128)(2,1)}, u32[]{:S(2)}, u32[]{:S(2)}) collective-permute-start(bf16[64,4096]{1,0:T(8,128)(2,1)} %add_convert_fusion.16), channel_id=1, source_target_pairs={{0,8},{1,9},{2,10},{3,11},{4,12},{5,13},{6,14},{7,15},{8,16},{9,17... | collective-permute-start | bytes 1572872 | tf_op jit(solution)/shard_map/ppermute | solution.py:746
  297.6 52.0 %collective-permute-start.58 = (bf16[64,4096]{1,0:T(8,128)(2,1)}, bf16[64,4096]{1,0:T(8,128)(2,1)S(1)}, u32[]{:S(2)}, u32[]{:S(2)}) collective-permute-start(bf16[64,4096]{1,0:T(8,128)(2,1)} %get-tuple-element.167), channel_id=1, source_target_pairs={{0,4},{1,3},{2,6},{3,1},{4,0},{5,7},{6,2},{7,5},{8,12},{9,11},{10,... | collective-permute-start | bytes 1572872 | tf_op jit(solution)/shard_map/ppermute | solution.py:746
  299.7 69.9 %collective-permute-start.57 = (bf16[64,4096]{1,0:T(8,128)(2,1)}, bf16[64,4096]{1,0:T(8,128)(2,1)S(1)}, u32[]{:S(2)}, u32[]{:S(2)}) collective-permute-start(bf16[64,4096]{1,0:T(8,128)(2,1)} %get-tuple-element.166), channel_id=1, source_target_pairs={{0,4},{1,3},{2,6},{3,1},{4,0},{5,7},{6,2},{7,5},{8,12},{9,11},{10,... | collective-permute-start | bytes 1572872 | tf_op jit(solution)/shard_map/ppermute | solution.py:746
  311.2 20.1 %collective-permute-start.67 = (bf16[64,4096]{1,0:T(8,128)(2,1)}, bf16[64,4096]{1,0:T(8,128)(2,1)S(1)}, u32[]{:S(2)}, u32[]{:S(2)}) collective-permute-start(bf16[64,4096]{1,0:T(8,128)(2,1)} %get-tuple-element.176), channel_id=1, source_target_pairs={{0,4},{1,3},{2,6},{3,1},{4,0},{5,7},{6,2},{7,5},{8,12},{9,11},{10,... | collective-permute-start | bytes 1572872 | tf_op jit(solution)/shard_map/ppermute | solution.py:746
  331.3 37.4 %collective-permute-start.43 = (bf16[512,3200]{1,0:T(8,128)(2,1)}, bf16[512,3200]{1,0:T(8,128)(2,1)S(1)}, u32[]{:S(2)}, u32[]{:S(2)}) collective-permute-start(bf16[512,3200]{1,0:T(8,128)(2,1)} %get-tuple-element.101), channel_id=1, source_target_pairs={{0,1},{1,0},{2,3},{3,2},{4,5},{5,4},{6,7},{7,6},{8,9},{9,8},{10,11... | collective-permute-start | bytes 9830408 | tf_op jit(solution)/shard_map/ppermute | solution.py:746
  331.3 20.4 %collective-permute-start.62 = (bf16[64,4096]{1,0:T(8,128)(2,1)S(1)}, bf16[64,4096]{1,0:T(8,128)(2,1)S(1)}, u32[]{:S(2)}, u32[]{:S(2)}) collective-permute-start(bf16[64,4096]{1,0:T(8,128)(2,1)S(1)} %add_convert_fusion.15), channel_id=1, source_target_pairs={{0,8},{1,9},{2,10},{3,11},{4,12},{5,13},{6,14},{7,15},{8,16},{9,17... | collective-permute-start | bytes 1572872 | tf_op jit(solution)/shard_map/ppermute | solution.py:746
  349.7 32.0 %collective-permute-start.65 = (bf16[64,4096]{1,0:T(8,128)(2,1)S(1)}, bf16[64,4096]{1,0:T(8,128)(2,1)S(1)}, u32[]{:S(2)}, u32[]{:S(2)}) collective-permute-start(bf16[64,4096]{1,0:T(8,128)(2,1)S(1)} %copy-done.37), channel_id=1, source_target_pairs={{0,4},{1,3},{2,6},{3,1},{4,0},{5,7},{6,2},{7,5},{8,12},{9,11},{10,... | collective-permute-start | bytes 1572872 | tf_op jit(solution)/shard_map/ppermute | solution.py:746
  358.1 21.5 %collective-permute-start.63 = (bf16[64,4096]{1,0:T(8,128)(2,1)S(1)}, bf16[64,4096]{1,0:T(8,128)(2,1)S(1)}, u32[]{:S(2)}, u32[]{:S(2)}) collective-permute-start(bf16[64,4096]{1,0:T(8,128)(2,1)S(1)} %add_convert_fusion.14), channel_id=1, source_target_pairs={{0,8},{1,9},{2,10},{3,11},{4,12},{5,13},{6,14},{7,15},{8,16},{9,17... | collective-permute-start | bytes 1572872 | tf_op jit(solution)/shard_map/ppermute | solution.py:746
  368.6 20.5 %collective-permute-start.70 = (bf16[64,4096]{1,0:T(8,128)(2,1)S(1)}, bf16[64,4096]{1,0:T(8,128)(2,1)S(1)}, u32[]{:S(2)}, u32[]{:S(2)}) collective-permute-start(bf16[64,4096]{1,0:T(8,128)(2,1)S(1)} %add_convert_fusion.5), channel_id=1, source_target_pairs={{0,8},{1,9},{2,10},{3,11},{4,12},{5,13},{6,14},{7,15},{8,16},{9,17... | collective-permute-start | bytes 1572872 | tf_op jit(solution)/shard_map/ppermute | solution.py:746
  369.4 27.1 %collective-permute-start.47 = (bf16[256,3200]{1,0:T(8,128)(2,1)S(1)}, bf16[256,3200]{1,0:T(8,128)(2,1)S(1)}, u32[]{:S(2)}, u32[]{:S(2)}) collective-permute-start(bf16[256,3200]{1,0:T(8,128)(2,1)S(1)} %get-tuple-element.178), channel_id=1, source_target_pairs={{0,4},{1,3},{2,6},{3,1},{4,0},{5,7},{6,2},{7,5},{8,12},{9,11},{10,... | collective-permute-start | bytes 4915208 | tf_op jit(solution)/shard_map/ppermute | solution.py:746
  389.3 20.2 %collective-permute-start.71 = (bf16[32,4096]{1,0:T(8,128)(2,1)S(1)}, bf16[32,4096]{1,0:T(8,128)(2,1)S(1)}, u32[]{:S(2)}, u32[]{:S(2)}) collective-permute-start(bf16[32,4096]{1,0:T(8,128)(2,1)S(1)} %slice.350), channel_id=1, source_target_pairs={{0,2},{1,5},{2,0},{3,7},{4,6},{5,1},{6,4},{7,3},{8,10},{9,13},{10,... | collective-permute-start | bytes 786440 | tf_op jit(solution)/shard_map/ppermute | solution.py:746
  (98 other events, 1448.8 us)

commit v5 on v4

v5 whole, which is shorter than its diff:
```python
import functools
import math
import types

import jax
import jax.numpy as jnp
from jax import lax
from jax.experimental import pallas as pl
from jax.experimental.pallas import tpu as pltpu
from jax.sharding import PartitionSpec as P

HEAD_DIM = 64


LOW = jnp.bfloat16
SCALE = HEAD_DIM ** (-0.5)
PAIR = 2 * HEAD_DIM
TILE = 512
FF_TILE = 1024
ROWS = 32
NORM_COLS = 128
GELU_RATE = math.sqrt(2.0 / math.pi)
ANYWHERE = pl.BlockSpec(memory_space=pl.ANY)
IN_HBM = pl.BlockSpec(memory_space=pltpu.HBM)
SCALARS = pl.BlockSpec(memory_space=pltpu.SMEM)
VECTORS = pl.BlockSpec(memory_space=pltpu.VMEM)


def launch(body, given, made, scratch, own, products, moved, limit):
    names, specs, arrays = [], [], []
    for name, (spec, value) in given.items():
        group = value if isinstance(value, list) else [value]
        names += [(0, name, isinstance(value, list))] * len(group)
        specs += [spec] * len(group)
        arrays += group
    names += [(0, name, False) for name in (*made, *scratch)]
    names += [(1, name, False) for name in own]

    def kernel(*refs):
        held = ({}, {})
        for (which, name, grouped), ref in zip(names, refs):
            if grouped:
                held[which].setdefault(name, []).append(ref)
            else:
                held[which][name] = ref
        body(*(types.SimpleNamespace(**group) for group in held))

    outs = pl.pallas_call(
        kernel,
        out_shape=[jax.ShapeDtypeStruct(shape, kind) for _, shape, kind in made.values()],
        in_specs=specs,
        out_specs=[spec for spec, _, _ in made.values()],
        scratch_shapes=[*scratch.values(), *own.values()],
        cost_estimate=pl.CostEstimate(
            flops=16 * products, bytes_accessed=moved, transcendentals=0
        ),
        compiler_params=pltpu.CompilerParams(vmem_limit_bytes=limit * 2**20),
    )(*arrays)
    return types.SimpleNamespace(**dict(zip(made, outs)))


class Copies:
    def __init__(self, sem):
        self.sem, self.used, self.open = sem, 0, []

    def start(self, source, target, keep=True):
        copy = pltpu.make_async_copy(source, target, self.sem.at[self.used])
        self.used += 1
        copy.start()
        if keep:
            self.open.append(copy)
        return copy

    def rows(self, parts, owners_ref, target):
        if len(parts) == 1:
            return [self.start(parts[0], target, False)]
        shard = target.shape[0] // owners_ref.shape[0]
        copies = []
        for part in parts:
            for local in range(part.shape[0] // shard):
                row = pl.multiple_of(owners_ref[len(copies)] * shard, shard)
                source = part.at[pl.ds(local * shard, shard)]
                copies.append(self.start(source, target.at[pl.ds(row, shard)], False))
        return copies

    def finish(self):
        for copy in self.open:
            copy.wait()


def wait_all(copies):
    for copy in copies:
        copy.wait()


def product(left, right, left_dim=1, right_dim=0):
    dims = (((left_dim,), (right_dim,)), ((), ()))
    return lax.dot_general(left, right, dims, preferred_element_type=jnp.float32)


def tiles(total, size):
    return [slice(start, start + size) for start in range(0, total, size)]


def fill_mask(lengths_ref, mask_ref):
    shape = mask_ref.shape
    key_row = lax.broadcasted_iota(jnp.int32, shape, 0)
    query_row = lax.broadcasted_iota(jnp.int32, shape, 1)
    end = 0
    key_segment = jnp.zeros(shape, jnp.int32)
    query_segment = jnp.zeros(shape, jnp.int32)
    for slot in range(lengths_ref.shape[1]):
        end = end + lengths_ref[0, slot]
        key_segment += (key_row >= end).astype(jnp.int32)
        query_segment += (query_row >= end).astype(jnp.int32)
    mask_ref[...] = jnp.where(key_segment == query_segment, 0.0, -1e30)


def normalize(values, gain, bias):
    centered = values - jnp.mean(values, axis=-1, keepdims=True)
    spread = jnp.mean(centered * centered, axis=-1, keepdims=True)
    inverse = lax.rsqrt(spread + 1e-05)
    unit = centered * inverse
    return unit, inverse, unit * gain + bias


def normalize_back(grad, unit, inverse, gain):
    scaled = grad * gain
    mean = jnp.mean(scaled, axis=-1, keepdims=True)
    along = jnp.mean(scaled * unit, axis=-1, keepdims=True)
    return inverse * (scaled - mean - unit * along)


def half_lanes(rows, half):
    lane = lax.broadcasted_iota(jnp.int32, (rows, PAIR), 1)
    return (lane >= HEAD_DIM) == bool(half)


def add_norm_grad(norm_grad, row, grad, unit):
    norm_grad[row : row + 1] += jnp.sum(grad * unit, axis=0, keepdims=True)
    norm_grad[row + 1 : row + 2] += jnp.sum(grad, axis=0, keepdims=True)


def attend_forward(rows, low, att, att_ready, mask, qkv, mixed, lse, total, norm, hidden, unit, inverse):
    count, width = low.shape
    att_ready()
    for part in tiles(3 * width, TILE):
        qkv[:, part] = product(low[...], att[:, part]).astype(LOW)
    for pair, part in enumerate(tiles(width, PAIR)):
        query = qkv[:, part] * jnp.asarray(SCALE, LOW)
        key = qkv[:, slice(width + part.start, width + part.stop)]
        value = qkv[:, slice(2 * width + part.start, 2 * width + part.stop)]
        halves, sums = [], []
        for half in (0, 1):
            own = jnp.where(half_lanes(count, half), query, jnp.zeros_like(query))
            scores = product(key, own, 1, 1) + mask[...]
            peak = jnp.max(scores, axis=0, keepdims=True)
            weights = jnp.exp(scores - peak)
            sum_all = jnp.sum(weights, axis=0, keepdims=True)
            sums.append(peak + jnp.log(sum_all))
            out = product(value, weights.astype(LOW), 0, 0)
            halves.append(out[half * HEAD_DIM : (half + 1) * HEAD_DIM] * (1.0 / sum_all))
        lse[pair] = jnp.concatenate(sums, axis=0)
        mixed[:, part] = jnp.concatenate(halves, axis=0).T.astype(LOW)
    for part in tiles(width, TILE):
        out = slice(3 * width + part.start, 3 * width + part.stop)
        total[:, part] = rows[:, part].astype(jnp.float32) + product(mixed[...], att[:, out])
    for block in tiles(count, ROWS):
        unit[block], inverse[block], hidden[block] = normalize(total[block], norm[0:1], norm[1:2])


def ffn_forward(hidden, low, up, down, up_ready, down_ready, active, slope, total):
    low[...] = hidden[...].astype(LOW)
    total[...] = hidden[...]
    up_ready()
    for part in tiles(active.shape[1], FF_TILE):
        inner = product(low[...], up[:, part])
        square = inner * inner
        bend = jnp.tanh(GELU_RATE * inner * (1.0 + 0.044715 * square))
        rise = 0.5 + 0.5 * bend
        act = (inner * rise).astype(LOW)
        active[:, part] = act
        slope[:, part] = (
            rise
            + (0.5 * GELU_RATE) * inner * (1.0 - bend * bend) * (1.0 + 3 * 0.044715 * square)
        ).astype(LOW)
        if part.start == 0:
            down_ready()
        total[...] += product(act, down[:, part], 1, 1)


def ffn_backward(second, out_low, slope, up, down, unit, inverse, norm, inner_low, total, first, first_low, norm_grad, ready=None, norm_ready=None):
    count, _ = second.shape
    total[...] = second[...]
    for index, part in enumerate(tiles(slope.shape[1], FF_TILE)):
        if ready:
            ready(index)
        act = product(out_low[...], down[:, part])
        inner = (act * slope[:, part].astype(jnp.float32)).astype(LOW)
        inner_low[:, part] = inner
        total[...] += product(inner, up[:, part], 1, 1)
    if norm_ready:
        norm_ready()
    for block in tiles(count, ROWS):
        grad, unit_rows = total[block], unit[block]
        add_norm_grad(norm_grad, 0, grad, unit_rows)
        out = normalize_back(grad, unit_rows, inverse[block], norm[0:1])
        first[block] = out
        first_low[block] = out.astype(LOW)


def attend_backward(first, first_low, qkv, lse, mask, att, mixed_grad, qkv_grad, rows_grad, ready=None):
    count, width = first.shape
    if ready:
        ready(3)
    for part in tiles(width, TILE):
        mixed_grad[:, part] = product(
            first_low[...], att[part, 3 * width : 4 * width], 1, 1
        ).astype(LOW)
    for pair, part in enumerate(tiles(width, PAIR)):
        key_part = slice(width + part.start, width + part.stop)
        value_part = slice(2 * width + part.start, 2 * width + part.stop)
        query = qkv[:, part] * jnp.asarray(SCALE, LOW)
        key, value, grad = qkv[:, key_part], qkv[:, value_part], mixed_grad[:, part]
        sums = lse[pair]
        key_grads, value_grads, query_grads = [], [], []
        for half in (0, 1):
            lanes = half_lanes(count, half)
            own_query = jnp.where(lanes, query, jnp.zeros_like(query))
            own_grad = jnp.where(lanes, grad, jnp.zeros_like(grad))
            weights = jnp.exp(product(key, own_query, 1, 1) + mask[...] - sums[half : half + 1])
            weight_grad = product(value, own_grad, 1, 1)
            value_grads.append(product(weights.astype(LOW), grad))
            along = jnp.sum(weights * weight_grad, axis=0, keepdims=True)
            low = (weights * (weight_grad - along)).astype(LOW)
            key_grads.append(product(low, query))
            back = product(key, low, 0, 0)
            query_grads.append(back[half * HEAD_DIM : (half + 1) * HEAD_DIM])
        lanes = half_lanes(count, 1)
        qkv_grad[:, part] = (jnp.concatenate(query_grads, axis=0).T * SCALE).astype(LOW)
        qkv_grad[:, key_part] = jnp.where(lanes, key_grads[1], key_grads[0]).astype(LOW)
        qkv_grad[:, value_part] = jnp.where(lanes, value_grads[1], value_grads[0]).astype(LOW)
    if ready:
        for chunk in range(3):
            ready(chunk)
    for part in tiles(width, TILE):
        rows_grad[:, part] = first[:, part] + product(qkv_grad[...], att[part, : 3 * width], 1, 1)


def weight_sum(picker, lefts, rights, turned, whole, copies, send, keep, offset=0, ready=None):
    count = lefts[0].shape[0]
    half = send.shape[0]
    for layer, left in enumerate(lefts):
        turned[:, layer * count : (layer + 1) * count] = product(
            picker[...], left[...], 1, 1
        ).astype(LOW)
    for index, part in enumerate(tiles(rights[0].shape[1], TILE)):
        if ready:
            ready(index)
        right = jnp.concatenate([ref[:, part] for ref in rights], axis=0)
        start = offset + part.start
        whole[:, start : start + TILE] = product(turned[...], right).astype(LOW)
        columns = pl.ds(start, TILE)
        copies.start(whole.at[pl.ds(0, half), columns], send.at[:, columns])
        copies.start(whole.at[pl.ds(half, half), columns], keep.at[:, columns])


def both_layers(lengths, tokens, cotangent, att_parts, att_owners, up_parts, up_owners, down_parts, down_owners, picker):
    count, width = tokens.shape
    inner = up_parts[0].shape[1]
    wide = att_parts[0].shape[1]
    size, f32 = (count, width), jnp.float32
    results = dict(
        qkv1=((count, 3 * width), LOW),
        mixed1=(size, LOW),
        lse1=((width // PAIR, 2, count), f32),
        unit_first=(size, f32),
        inverse_first=((count, 1), f32),
        norm=((4, width), f32),
        hidden_low1=(size, LOW),
        active1=((count, inner), LOW),
        slope1=((count, inner), LOW),
        low2=(size, LOW),
        mixed2=(size, LOW),
        hidden_low2=(size, LOW),
        layer_output=(size, LOW),
        inner_low2=((count, inner), LOW),
        first_low2=(size, LOW),
        qkv_grad2=((count, 3 * width), LOW),
        second1=(size, f32),
        out_low1=(size, LOW),
        norm_grad=((4, width), f32),
    )

    def body(r, own):
        copies = Copies(r.sem)
        att_rows = copies.rows(r.att_parts, r.att_owners, r.held_att)
        up_rows = copies.rows(r.up_parts, r.up_owners, r.held_up)
        down_rows = copies.rows(r.down_parts, r.down_owners, r.held_down)
        picker_copy = copies.start(r.picker, r.held_picker, False)
        fill_mask(r.lengths, r.mask)
        kept = []

        def up_ready():
            wait_all(up_rows)
            kept.append(copies.start(r.held_up, r.up_full, False))

        def down_ready():
            wait_all(down_rows)
            copies.start(r.held_down, r.down_full)

        def give(name):
            copies.start(getattr(own, name), getattr(r, name))

        def att_ready():
            wait_all(att_rows)
            copies.start(r.held_att.at[:, pl.ds(0, 4 * width)], r.att_full)
            turned = r.held_att[:, 4 * width :].astype(f32).T
            own.norm[...] = turned[0:4]

        attend_forward(
            r.tokens,
            r.tokens,
            r.held_att,
            att_ready,
            r.mask,
            own.qkv1,
            own.mixed1,
            own.lse1,
            r.total,
            own.norm,
            r.hidden2,
            own.unit_first,
            own.inverse_first,
        )
        for name in ("norm", "qkv1", "mixed1", "lse1", "unit_first", "inverse_first"):
            give(name)
        ffn_forward(
            r.hidden2,
            own.hidden_low1,
            r.held_up,
            r.held_down,
            up_ready,
            down_ready,
            own.active1,
            own.slope1,
            r.total,
        )
        for name in ("hidden_low1", "active1", "slope1"):
            give(name)
        for block in tiles(count, ROWS):
            r.unit2[block], r.inverse2[block], rows = normalize(
                r.total[block], own.norm[2:3], own.norm[3:4]
            )
            r.rows[block] = rows
            own.low2[block] = rows.astype(LOW)
        give("low2")
        attend_forward(
            r.rows,
            own.low2,
            r.held_att,
            lambda: None,
            r.mask,
            r.qkv,
            own.mixed2,
            r.lse,
            r.total,
            own.norm,
            r.hidden2,
            r.unit1,
            r.inverse1,
        )
        give("mixed2")
        ffn_forward(
            r.hidden2,
            own.hidden_low2,
            r.held_up,
            r.held_down,
            lambda: None,
            lambda: None,
            r.active2,
            own.inner_low2,
            r.total,
        )
        give("hidden_low2")
        own.norm_grad[...] = jnp.zeros_like(own.norm_grad)
        live = 0
        for slot in range(r.lengths.shape[1]):
            live = live + r.lengths[0, slot]
        for block in tiles(count, ROWS):
            unit, inverse, rows = normalize(r.total[block], own.norm[2:3], own.norm[3:4])
            own.layer_output[block] = rows.astype(LOW)
            position = block.start + lax.broadcasted_iota(jnp.int32, unit.shape, 0)
            grad = jnp.where(position < live, r.cotangent[block].astype(f32), 0.0)
            add_norm_grad(own.norm_grad, 2, grad, unit)
            second = normalize_back(grad, unit, inverse, own.norm[2:3])
            r.rows[block] = second
            r.out_low2[block] = second.astype(LOW)
        give("layer_output")
        ffn_backward(
            r.rows,
            r.out_low2,
            own.inner_low2,
            r.held_up,
            r.held_down,
            r.unit1,
            r.inverse1,
            own.norm,
            own.inner_low2,
            r.total,
            r.rows,
            own.first_low2,
            own.norm_grad,
        )
        for name in ("inner_low2", "first_low2"):
            give(name)
        attend_backward(
            r.rows,
            own.first_low2,
            r.qkv,
            r.lse,
            r.mask,
            r.held_att,
            r.mixed_grad,
            own.qkv_grad2,
            r.total,
        )
        give("qkv_grad2")
        for block in tiles(count, ROWS):
            grad, unit = r.total[block], r.unit2[block]
            add_norm_grad(own.norm_grad, 2, grad, unit)
            second = normalize_back(grad, unit, r.inverse2[block], own.norm[2:3])
            own.second1[block] = second
            own.out_low1[block] = second.astype(LOW)
        for name in ("second1", "out_low1", "norm_grad"):
            give(name)
        picker_copy.wait()
        wait_all(kept)
        weight_sum(
            r.held_picker,
            (r.out_low2, own.out_low1),
            (r.active2, own.active1),
            r.turned,
            r.held_up,
            copies,
            r.send,
            r.keep,
        )
        copies.finish()

    made = {name: (IN_HBM, shape, kind) for name, (shape, kind) in results.items()}
    made |= dict(
        att_full=(IN_HBM, (width, 4 * width), LOW),
        up_full=(IN_HBM, (width, inner), LOW),
        down_full=(IN_HBM, (width, inner), LOW),
        send=(IN_HBM, (width // 2, inner), LOW),
        keep=(IN_HBM, (width // 2, inner), LOW),
    )
    own = {name: pltpu.VMEM(shape, kind) for name, (shape, kind) in results.items()}
    rows_f32 = pltpu.VMEM(size, f32)
    scratch = dict(
        held_up=pltpu.VMEM((width, inner), LOW),
        held_down=pltpu.VMEM((width, inner), LOW),
        held_att=pltpu.VMEM((width, wide), LOW),
        held_picker=pltpu.VMEM((width, width), LOW),
        turned=pltpu.VMEM((width, 2 * count), LOW),
        mask=pltpu.VMEM((count, count), f32),
        qkv=pltpu.VMEM((count, 3 * width), LOW),
        lse=pltpu.VMEM((width // PAIR, 2, count), f32),
        active2=pltpu.VMEM((count, inner), LOW),
        out_low2=pltpu.VMEM(size, LOW),
        mixed_grad=pltpu.VMEM(size, LOW),
        inverse1=pltpu.VMEM((count, 1), f32),
        inverse2=pltpu.VMEM((count, 1), f32),
        total=rows_f32,
        rows=rows_f32,
        hidden2=rows_f32,
        unit1=rows_f32,
        unit2=rows_f32,
    )
    loads = 3 * up_owners.size
    copies = loads + len(results) + 5 + 2 * (inner // TILE)
    scratch |= dict(sem=pltpu.SemaphoreType.DMA((copies,)))
    return launch(
        body,
        dict(
            lengths=(SCALARS, lengths),
            up_owners=(SCALARS, up_owners),
            down_owners=(SCALARS, down_owners),
            att_owners=(SCALARS, att_owners),
            tokens=(VECTORS, tokens),
            cotangent=(VECTORS, cotangent),
            att_parts=(IN_HBM, att_parts),
            picker=(IN_HBM, picker),
            up_parts=(IN_HBM, up_parts),
            down_parts=(IN_HBM, down_parts),
        ),
        made,
        scratch,
        own,
        count * width * (8 * inner + 12 * width) + 9 * count * count * width,
        12 * width * inner,
        60,
    )


def first_ffn_backward(m, norm, unit, inverse):
    count, width = m.second1.shape
    inner = m.slope1.shape[1]
    size, f32 = (count, width), jnp.float32

    def body(r, own):
        copies = Copies(r.sem)
        slope = copies.start(r.slope, own.slope, False)
        weights = []
        for part in tiles(inner, FF_TILE):
            part = pl.ds(part.start, FF_TILE)
            pair = ((r.down, own.down), (r.up, own.up))
            weights.append([copies.start(a.at[:, part], b.at[:, part], False) for a, b in pair])
        unit_copy = copies.start(r.unit, own.unit, False)
        r.norm_grad[...] = jnp.zeros_like(r.norm_grad)

        def ready(index):
            if index == 0:
                slope.wait()
            wait_all(weights[index])

        def norm_ready():
            unit_copy.wait()
            copies.start(own.inner_low, r.inner_low)

        ffn_backward(
            r.second,
            r.out_low,
            own.slope,
            own.up,
            own.down,
            own.unit,
            r.inverse,
            r.norm,
            own.inner_low,
            r.total,
            r.first,
            r.first_low,
            r.norm_grad,
            ready,
            norm_ready,
        )
        copies.finish()

    return launch(
        body,
        dict(
            second=(VECTORS, m.second1),
            out_low=(VECTORS, m.out_low1),
            inverse=(VECTORS, inverse),
            norm=(VECTORS, norm),
            slope=(IN_HBM, m.slope1),
            unit=(IN_HBM, unit),
            up=(IN_HBM, m.up_full),
            down=(IN_HBM, m.down_full),
        ),
        dict(
            first=(VECTORS, size, f32),
            first_low=(VECTORS, size, LOW),
            norm_grad=(VECTORS, norm.shape, f32),
            inner_low=(IN_HBM, (count, inner), LOW),
        ),
        dict(
            total=pltpu.VMEM(size, f32),
            sem=pltpu.SemaphoreType.DMA((2 * (inner // FF_TILE) + 3,)),
        ),
        dict(
            up=pltpu.VMEM((width, inner), LOW),
            down=pltpu.VMEM((width, inner), LOW),
            slope=pltpu.VMEM((count, inner), LOW),
            inner_low=pltpu.VMEM((count, inner), LOW),
            unit=pltpu.VMEM(size, f32),
        ),
        count * width * 4 * inner,
        4 * width * inner,
        60,
    )


def up_and_out_gradients(lefts_up, rights_up, lefts_out, rights_out, picker):
    count, width = lefts_up[0].shape
    inner = rights_up[0].shape[1]
    late = dict(right_up=rights_up, left_out=lefts_out, right_out=rights_out)

    def body(r, own):
        copies = Copies(r.sem)
        parts = [
            [
                [
                    copies.start(ref.at[:, pl.ds(part.start, TILE)], to.at[:, pl.ds(part.start, TILE)], False)
                    for ref, to in zip(r.right_up, (own.up_a, own.up_b))
                ]
                for part in tiles(inner, TILE)
            ]
        ][0]
        loads = [
            copies.start(ref, to, False)
            for ref, to in zip(
                (*r.left_out, *r.right_out), (own.left_a, own.left_b, own.out_a, own.out_b)
            )
        ]
        weight_sum(
            r.picker,
            r.left_up,
            (own.up_a, own.up_b),
            r.turned,
            r.whole,
            copies,
            r.send,
            r.keep,
            0,
            lambda index: wait_all(parts[index]),
        )
        wait_all(loads)
        weight_sum(
            r.picker,
            (own.left_a, own.left_b),
            (own.out_a, own.out_b),
            r.turned,
            r.whole,
            copies,
            r.send,
            r.keep,
            inner,
        )
        copies.finish()

    given = dict(picker=(VECTORS, picker), left_up=(VECTORS, list(lefts_up)))
    given |= {name: (IN_HBM, list(pair)) for name, pair in late.items()}
    low = pltpu.VMEM((count, width), LOW)
    return launch(
        body,
        given,
        dict(
            send=(IN_HBM, (width // 2, inner + width), LOW),
            keep=(IN_HBM, (width // 2, inner + width), LOW),
        ),
        dict(
            whole=pltpu.VMEM((width, inner + width), LOW),
            turned=pltpu.VMEM((width, 2 * count), LOW),
            sem=pltpu.SemaphoreType.DMA((4 + 2 * (inner // TILE) + 2 * (inner + width) // TILE,)),
        ),
        dict(
            up_a=pltpu.VMEM((count, inner), LOW),
            up_b=pltpu.VMEM((count, inner), LOW),
            left_a=low,
            left_b=low,
            out_a=low,
            out_b=low,
        ),
        count * width * 2 * (inner + 3 * width),
        4 * width * inner,
        60,
    )


def first_attention_backward(lengths, first, first_low, qkv, lse, att, tokens, low2, qkv_grad2, norm_grads, picker):
    count, width = first.shape
    size, f32 = (count, width), jnp.float32
    late = dict(picker=picker, low2=low2, tokens=tokens, qkv_grad2=qkv_grad2)
    wide = 3 * width + NORM_COLS

    def body(r, own):
        copies = Copies(r.sem)
        chunks = [None] * 4
        for chunk in (3, 0, 1, 2):
            part = pl.ds(chunk * width, width)
            chunks[chunk] = copies.start(r.att.at[:, part], r.held.at[:, part], False)
        loads = [copies.start(getattr(r, n), getattr(own, n), False) for n in late]
        fill_mask(r.lengths, r.mask)
        attend_backward(
            r.first,
            r.first_low,
            r.qkv,
            r.lse,
            r.mask,
            r.held,
            r.mixed_grad,
            r.qkv_grad,
            r.input_grad,
            lambda chunk: chunks[chunk].wait(),
        )
        wait_all(loads)
        r.norm_rows[...] = jnp.zeros_like(r.norm_rows)
        r.norm_rows[0:4] = (r.norm_a[...] + r.norm_b[...]).astype(LOW)
        extra = product(own.picker[...], r.norm_rows[...], 1, 1).astype(LOW)
        half = width // 2
        r.extra[...] = extra
        columns = pl.ds(3 * width, NORM_COLS)
        copies.start(r.extra.at[pl.ds(0, half)], r.send.at[:, columns])
        copies.start(r.extra.at[pl.ds(half, half)], r.keep.at[:, columns])
        weight_sum(
            own.picker,
            (own.low2, own.tokens),
            (own.qkv_grad2, r.qkv_grad),
            r.turned,
            r.whole,
            copies,
            r.send,
            r.keep,
        )
        copies.finish()

    given = dict(
        lengths=(SCALARS, lengths),
        first=(VECTORS, first),
        first_low=(VECTORS, first_low),
        qkv=(VECTORS, qkv),
        lse=(VECTORS, lse),
        norm_a=(VECTORS, norm_grads[0]),
        norm_b=(VECTORS, norm_grads[1]),
        att=(IN_HBM, att),
    )
    given |= {name: (IN_HBM, value) for name, value in late.items()}
    own = {name: pltpu.VMEM(value.shape, LOW) for name, value in late.items()}
    scratch = dict(
        held=pltpu.VMEM((width, 4 * width), LOW),
        mask=pltpu.VMEM((count, count), f32),
        mixed_grad=pltpu.VMEM(size, LOW),
        qkv_grad=pltpu.VMEM((count, 3 * width), LOW),
        turned=pltpu.VMEM((width, 2 * count), LOW),
        whole=pltpu.VMEM((width, 3 * width), LOW),
        norm_rows=pltpu.VMEM((NORM_COLS, width), LOW),
        extra=pltpu.VMEM((width, NORM_COLS), LOW),
        sem=pltpu.SemaphoreType.DMA((4 + len(late) + 2 + 2 * (3 * width // TILE),)),
    )
    return launch(
        body,
        given,
        dict(
            input_grad=(VECTORS, size, f32),
            send=(IN_HBM, (width // 2, wide), LOW),
            keep=(IN_HBM, (width // 2, wide), LOW),
        ),
        scratch,
        own,
        count * width * 10 * width + 5 * count * count * width,
        16 * width * width,
        60,
    )


AXES = ("dp", "fsdp")


class Route:
    def __init__(self):
        rows, cols = lax.axis_size("dp"), lax.axis_size("fsdp")
        self.inner = cols // 4
        self.ring_size = rows // 2 * self.inner
        self.cols = cols
        self.world = rows * cols
        row, col = lax.axis_index("dp"), lax.axis_index("fsdp")
        self.q = row // 2 * self.inner + col // 4
        self.y, self.x, self.c = row % 2, col // 2 % 2, col % 2

    def joint(self, q, y, x, c):
        return (q // self.inner * 2 + y) * self.cols + q % self.inner * 4 + x * 2 + c

    def move(self, array, step):
        pairs = []
        for q in range(self.ring_size):
            for y in (0, 1):
                for x in (0, 1):
                    for c in (0, 1):
                        to = step(q, y, x, c)
                        pairs.append((self.joint(q, y, x, c), self.joint(*to)))
        return lax.ppermute(array, AXES, pairs)

    def ring(self, array, hops=1):
        return self.move(array, lambda q, y, x, c: ((q + hops) % self.ring_size, y, x, c))

    def core(self, array):
        return self.move(array, lambda q, y, x, c: (q, y, x, 1 - c))

    def first(self, array):
        return self.move(array, lambda q, y, x, c: (q, y ^ c, x ^ (1 - c), c))

    def second(self, array):
        return self.move(array, lambda q, y, x, c: (q, y ^ (1 - c), x ^ c, c))

    def owner(self, back, first, second, core):
        c = self.c ^ core
        x = self.x ^ jnp.where(c == 0, first, second)
        y = self.y ^ jnp.where(c == 0, second, first)
        return self.joint((self.q + self.ring_size - back) % self.ring_size, y, x, c)


def after(value, *earlier):
    return lax.optimization_barrier((value, earlier))[0]


def gather_all(route, att, up, down):
    last = route.ring_size - 1
    pairs = [[jnp.concatenate([piece, route.first(piece)])] for piece in (att, up)]
    chains = (*pairs, [down])
    others = ([], [])
    turns = [2] + [which for _ in range(last - 1) for which in (0, 2)] + [1, 0] + [1] * (last - 1)
    arrived = [(), ()]
    for turn, which in enumerate(turns):
        here = after(chains[which][-1], arrived[turn])
        chains[which].append(route.ring(here))
        arrived.append(chains[which][-1])
        if which < 2:
            others[which].append(route.second(here))
    base = jnp.concatenate(chains[2])
    first, both = route.first(base), route.second(base)
    crossed = route.second(after(first, pairs[1][1]))
    others[0].append(route.second(after(pairs[0][last], first)))
    others[1].append(route.second(pairs[1][last]))
    arrays, owners = [[], [], []], [[], [], []]

    def add(which, block, second, blocks, when):
        for core in (0, 1):
            arrays[which].append(route.core(after(block, when)) if core else block)
            owners[which] += [route.owner(back, flip, second, core) for back, flip in blocks]

    for which, chain in enumerate(pairs):
        for k in range(last + 1):
            blocks = [(k, 0), (k, 1)]
            add(which, chain[k], 0, blocks, ())
            add(which, others[which][k], 1, blocks, pairs[1][min(k + 1 + which, last)])
    rows = range(last + 1)
    add(2, base, 0, [(k, 0) for k in rows], pairs[0][last])
    add(2, first, 0, [(k, 1) for k in rows], pairs[1][max(last - 1, 0)])
    add(2, both, 1, [(k, 0) for k in rows], pairs[1][last])
    add(2, crossed, 1, [(k, 1) for k in rows], pairs[1][last])
    return arrays, owners


def row_picker(owners, shard):
    rows = (jnp.stack(owners)[:, None] * shard + jnp.arange(shard)[None, :]).reshape(-1, 1)
    return (rows == jnp.arange(rows.size)[None, :]).astype(jnp.bfloat16)


def add_all(*terms):
    total = terms[0].astype(jnp.float32)
    for term in terms[1:]:
        total = total + term.astype(jnp.float32)
    return total


def add_low(*terms):
    return add_all(*terms).astype(jnp.bfloat16)


def owners_ring_last(route):
    return [
        route.owner(1 + j, first, second, core)
        for core in (1, 0)
        for second in (1, 0)
        for first in (1, 0)
        for j in range(route.ring_size)
    ]


def owners_ring_middle(route):
    return [
        route.owner(1 + j, first, second, core)
        for core in (1, 0)
        for second in (1, 0)
        for j in range(route.ring_size)
        for first in (1, 0)
    ]


def cut(array, count):
    size = array.shape[0] // count
    return [array[k * size : (k + 1) * size] for k in range(count)]


class SumWhole:
    def __init__(self, route, upper, lower):
        self.term = jnp.concatenate([upper, lower])

    def steps(self):
        return iter(())

    def total(self):
        return lax.psum_scatter(self.term, AXES, scatter_dimension=0, tiled=True).astype(
            jnp.float32
        )


class SumRingMiddle:
    def __init__(self, route, send, keep):
        self.route, self.terms = route, (keep, route.core(send))
        self.result = None

    def steps(self):
        route, terms = self.route, self.terms
        count = route.ring_size
        half = terms[0].shape[0] // 2
        block = half // count
        earlier = yield
        near = after(terms, earlier)
        sends = [add_low(*(part[: half // 2] for part in near))]
        sends.append(add_low(*(part[half // 2 : half] for part in near)))
        others = [route.second(send) for send in sends]
        earlier = yield sends
        moving = None
        for j in range(count):
            arrived = [] if moving is None else [route.ring(moving)]
            near, far, arrived = after((terms, others if j else others[:1], arrived), earlier)
            start = half + j * block
            local = [part[start : start + block] for part in near]
            offset = j * block % (half // 2)
            local.append(far[2 * j // count][offset : offset + block])
            local += arrived
            if j < count - 1:
                moving = add_low(*local)
                earlier = yield moving
        shard = block // 2
        turned = add_low(*(part[:shard] for part in local))
        rest = add_all(*(part[shard:] for part in local))
        earlier = yield (turned, rest)
        self.result = rest + after(route.first(turned), earlier).astype(jnp.float32)
        yield self.result

    def total(self):
        return self.result


class SumRingLast:
    def __init__(self, route, send, keep):
        self.route, self.terms = route, [keep, route.core(send)]
        self.result = None

    def steps(self):
        route, terms = self.route, self.terms
        earlier = yield
        start, total = 0, terms[0].shape[0]
        for step in (route.second, route.first):
            half = (total - start) // 2
            near = after(terms, earlier)
            send = add_low(*self.part(near, start, half))
            start += half
            terms = terms + [step(send)]
            earlier = yield send
        block = (total - start) // route.ring_size
        moving = None
        for j in range(route.ring_size):
            arrived = [] if moving is None else [route.ring(moving)]
            near, arrived = after((terms, arrived), earlier)
            local = self.part(near, start + j * block, block) + arrived
            if j < route.ring_size - 1:
                moving = add_low(*local)
                earlier = yield moving
        self.result = add_all(*local)
        yield self.result

    @staticmethod
    def part(terms, start, size):
        total = terms[0].shape[0]
        skips = [start - (total - term.shape[0]) for term in terms]
        return [term[skip : skip + size] for term, skip in zip(terms, skips)]

    def total(self):
        return self.result


def advance(chain, earlier):
    try:
        return chain.send(earlier)
    except StopIteration:
        return None


def update(gradient, master, moment, average, step_rate):
    moment_new = 0.9 * moment + gradient
    master_new = master - step_rate * (gradient + 0.9 * moment_new)
    average_new = 0.8 * average + 0.2 * master_new
    return (gradient, moment_new, master_new, average_new, master_new.astype(jnp.bfloat16))


def shards(
    tokens,
    cotangent,
    seq_lengths,
    att_master,
    ffn_master,
    norm_master,
    att_moment,
    ffn_moment,
    norm_moment,
    att_average,
    ffn_average,
    norm_average,
):
    row_count = tokens.shape[0]
    route = Route()
    shard = att_master.shape[0]
    norm_piece = jnp.pad(norm_master.T, ((0, 0), (0, NORM_COLS - norm_master.shape[0])))
    att_piece = jnp.concatenate([att_master, norm_piece], axis=1).astype(jnp.bfloat16)
    ffn_pieces = ffn_master.astype(jnp.bfloat16)
    width = att_master.shape[1]
    tiled = shard % 16 == 0
    if tiled:
        middle = row_picker(owners_ring_middle(route), shard)
        last = row_picker(owners_ring_last(route), shard)
        arrays, owners = gather_all(route, att_piece, *ffn_pieces)
        middle, last = lax.optimization_barrier((middle, last))
        sum_middle, sum_last = SumRingMiddle, SumRingLast
    else:
        middle = last = row_picker(list(range(route.world)), shard)
        pieces = (att_piece, *ffn_pieces)
        arrays = [[lax.all_gather(piece, AXES, axis=0, tiled=True)] for piece in pieces]
        owners = [[0]] * 3
        sum_middle = sum_last = SumWhole
    owned = [
        jnp.stack(rows).astype(jnp.int32) if tiled else jnp.zeros(1, jnp.int32) for rows in owners
    ]
    m = both_layers(
        seq_lengths,
        tokens,
        cotangent,
        arrays[0],
        owned[0],
        arrays[1],
        owned[1],
        arrays[2],
        owned[2],
        middle,
    )
    down_sum = sum_middle(route, m.send, m.keep)
    down_steps = down_sum.steps()
    next(down_steps, None)
    b = first_ffn_backward(m, m.norm, m.unit_first, m.inverse_first)
    sends = down_steps.send(b.norm_grad) if tiled else ()
    c = up_and_out_gradients(
        after((m.hidden_low2, m.hidden_low1), sends),
        (m.inner_low2, b.inner_low),
        (m.mixed2, m.mixed1),
        (m.first_low2, b.first_low),
        middle,
    )
    up_sum = sum_middle(route, c.send, c.keep)
    sends = down_steps.send(c.send) if tiled else ()
    a = first_attention_backward(
        seq_lengths,
        after(b.first, sends),
        b.first_low,
        m.qkv1,
        m.lse1,
        m.att_full,
        tokens,
        m.low2,
        m.qkv_grad2,
        (m.norm_grad, b.norm_grad),
        last,
    )
    in_sum = sum_last(route, a.send, a.keep)
    if tiled:
        up_steps, in_steps = up_sum.steps(), in_sum.steps()
        next(up_steps)
        next(in_steps)
        order = [down_steps, up_steps, down_steps, up_steps, in_steps, down_steps, up_steps]
        order += [in_steps, down_steps, up_steps, in_steps, up_steps, in_steps, up_steps, in_steps]
        earlier = a.input_grad
        for chain in order:
            earlier = chain.send(earlier)
        for chain in (down_steps, up_steps, in_steps):
            for earlier in iter(functools.partial(advance, chain, earlier), None):
                pass
    down_share, up_share, inproj_share = down_sum.total(), up_sum.total(), in_sum.total()
    inner = ffn_master.shape[2]
    proj_share = up_share[:, inner:]
    up_share = up_share[:, :inner]
    wide = 3 * width // 4
    totals = (
        jnp.concatenate([inproj_share[:, :wide], proj_share], axis=1),
        jnp.stack([up_share, down_share]),
        inproj_share[:, wide : wide + norm_master.shape[0]].T,
    )
    step_rate = 0.1 / math.sqrt(row_count * lax.axis_size(("dp", "fsdp")))
    att_out = update(totals[0], att_master, att_moment, att_average, step_rate)
    ffn_out = update(totals[1], ffn_master, ffn_moment, ffn_average, step_rate)
    norm_out = update(totals[2], norm_master, norm_moment, norm_average, step_rate)
    return (
        m.layer_output,
        a.input_grad,
        att_out[0],
        att_out[1],
        att_out[2],
        att_out[3],
        att_out[4],
        ffn_out[0],
        ffn_out[1],
        ffn_out[2],
        ffn_out[3],
        ffn_out[4],
        norm_out[0],
        norm_out[1],
        norm_out[2],
        norm_out[3],
        norm_out[4],
    )


def solution(mesh):
    return jax.shard_map(
        shards,
        mesh=mesh,
        in_specs=(
            P(("dp", "fsdp"), None),
            P(("dp", "fsdp"), None),
            P(("dp", "fsdp"), None),
            P(("dp", "fsdp"), None),
            P(None, ("dp", "fsdp"), None),
            P(None, ("dp", "fsdp")),
            P(("dp", "fsdp"), None),
            P(None, ("dp", "fsdp"), None),
            P(None, ("dp", "fsdp")),
            P(("dp", "fsdp"), None),
            P(None, ("dp", "fsdp"), None),
            P(None, ("dp", "fsdp")),
        ),
        out_specs=(
            P(("dp", "fsdp"), None),
            P(("dp", "fsdp"), None),
            P(("dp", "fsdp"), None),
            P(("dp", "fsdp"), None),
            P(("dp", "fsdp"), None),
            P(("dp", "fsdp"), None),
            P(("dp", "fsdp"), None),
            P(None, ("dp", "fsdp"), None),
            P(None, ("dp", "fsdp"), None),
            P(None, ("dp", "fsdp"), None),
            P(None, ("dp", "fsdp"), None),
            P(None, ("dp", "fsdp"), None),
            P(None, ("dp", "fsdp")),
            P(None, ("dp", "fsdp")),
            P(None, ("dp", "fsdp")),
            P(None, ("dp", "fsdp")),
            P(None, ("dp", "fsdp")),
        ),
        check_vma=False,
    )
```

time: 449 us -> 360 us (0.80)
  waiting for transfers between devices: 231 us -> 171 us
  local copies, waits for them, and re-layouts: 25.1 us -> 6.83 us
  starting transfers between devices: 50.5 us -> 38.7 us
  other arithmetic: 32.7 us -> 38.9 us
    ppermute x72 -> x62, waiting for transfers between devices: 231 us -> 171 us  [move(): return lax.ppermute(array, AXES, pairs)]
    unnamed x122 -> x88, local copies, waits for them, and re-layouts: 23.5 us -> 4.69 us
    ppermute x72 -> x62, starting transfers between devices: 50.5 us -> 38.7 us  [move(): return lax.ppermute(array, AXES, pairs)]
    convert_element_type x20 -> x14, other arithmetic: 19.7 us -> 24.9 us  [add_low(): return add_all(*terms).astype(jnp.bfloat16)]
  transfers between devices with their start and end apart: 72 -> 62, of which waited for: 26 -> 25; matrix products, arithmetic and copies ran while one was open for 6% -> 9% of each run, Pallas kernels for 12% -> 12%
where the time goes in v5:
time: 360 us; the launch traced here: 355 us
  waiting for transfers between devices  171 us (48%)
  Pallas kernels  97.6 us (27%)
  other arithmetic  38.9 us (11%)
  starting transfers between devices  38.7 us (11%)
  local copies, waits for them, and re-layouts  6.83 us (2%)
    ppermute x62, waiting for transfers between devices, move(): return lax.ppermute(array, AXES, pairs)  171 us
    pallas_call x4, Pallas kernels, launch(): pl.pallas_call(kernel, out_shape=[jax.ShapeDtypeStruct(shape, kind) for _...  97.6 us
    ppermute x62, starting transfers between devices, move(): return lax.ppermute(array, AXES, pairs)  38.7 us
    convert_element_type x14, other arithmetic, add_low(): return add_all(*terms).astype(jnp.bfloat16)  24.9 us
  transfers between devices with their start and end apart: 62, of which 25 were waited for; matrix products, arithmetic and copies ran while one was open for 9% of the time, Pallas kernels for 12%

profile of v5, /device:TPU:0, one launch (start us, length us, event | category | flops | bytes accessed | tf_op | source)
XLA Modules:
  0.0 354.9 jit_solution(16139633916478802740)
XLA Ops:
  2.6 3.0 collective-permute-start
  9.1 7.5 %collective-permute-done.13 = bf16[32,4096]{1,0:T(8,128)(2,1)S(1)} collective-permute-done((bf16[32,4096]{1,0:T(8,128)(2,1)S(1)}, bf16[32,4096]{1,0:T(8,128)(2,1)S(1)}, u32[]{:S(2)}, u32[]{:S(2)}) %collective-permute-start.13) | collective-permute-done | bytes 262176 | tf_op jit(solution)/shard_map/ppermute | solution.py:774
  18.5 9.1 %collective-permute-done.14 = bf16[32,4096]{1,0:T(8,128)(2,1)S(1)} collective-permute-done((bf16[32,4096]{1,0:T(8,128)(2,1)S(1)}, bf16[32,4096]{1,0:T(8,128)(2,1)S(1)}, u32[]{:S(2)}, u32[]{:S(2)}) %collective-permute-start.14) | collective-permute-done | bytes 262176 | tf_op jit(solution)/shard_map/ppermute | solution.py:774
  28.3 11.0 %collective-permute-done.4.refs_10_ = bf16[64,4224]{1,0:T(8,128)(2,1)S(1)} collective-permute-done((bf16[64,4224]{1,0:T(8,128)(2,1)S(1)}, bf16[64,4224]{1,0:T(8,128)(2,1)S(1)}, u32[]{:S(2)}, u32[]{:S(2)}) %collective-permute-start.4) | collective-permute-done | bytes 540704 | tf_op jit(solution)/shard_map/ppermute | solution.py:774
  39.2 5.6 %collective-permute-done.15 = bf16[32,4096]{1,0:T(8,128)(2,1)S(1)} collective-permute-done((bf16[32,4096]{1,0:T(8,128)(2,1)S(1)}, bf16[32,4096]{1,0:T(8,128)(2,1)S(1)}, u32[]{:S(2)}, u32[]{:S(2)}) %collective-permute-start.15) | collective-permute-done | bytes 262176 | tf_op jit(solution)/shard_map/ppermute | solution.py:774
  48.5 5.7 %collective-permute-done.5.refs_14_ = bf16[64,4224]{1,0:T(8,128)(2,1)S(1)} collective-permute-done((bf16[64,4224]{1,0:T(8,128)(2,1)S(1)}, bf16[64,4224]{1,0:T(8,128)(2,1)S(1)}, u32[]{:S(2)}, u32[]{:S(2)}) %collective-permute-start.5) | collective-permute-done | bytes 540704 | tf_op jit(solution)/shard_map/ppermute | solution.py:774
  54.2 6.0 %collective-permute-done.9.refs_12_ = bf16[64,4224]{1,0:T(8,128)(2,1)} collective-permute-done((bf16[64,4224]{1,0:T(8,128)(2,1)S(1)}, bf16[64,4224]{1,0:T(8,128)(2,1)}, u32[]{:S(2)}, u32[]{:S(2)}) %collective-permute-start.9) | collective-permute-done | bytes 540704 | tf_op jit(solution)/shard_map/ppermute | solution.py:774
  60.6 10.5 %collective-permute-done.21.refs_41_ = bf16[128,4096]{1,0:T(8,128)(2,1)S(1)} collective-permute-done((bf16[128,4096]{1,0:T(8,128)(2,1)S(1)}, bf16[128,4096]{1,0:T(8,128)(2,1)S(1)}, u32[]{:S(2)}, u32[]{:S(2)}) %collective-permute-start.21) | collective-permute-done | bytes 1048608 | tf_op jit(solution)/shard_map/ppermute | solution.py:774
  71.7 5.3 %collective-permute-done.25.refs_25_ = bf16[64,4096]{1,0:T(8,128)(2,1)S(1)} collective-permute-done((bf16[64,4096]{1,0:T(8,128)(2,1)S(1)}, bf16[64,4096]{1,0:T(8,128)(2,1)S(1)}, u32[]{:S(2)}, u32[]{:S(2)}) %collective-permute-start.25) | collective-permute-done | bytes 524320 | tf_op jit(solution)/shard_map/ppermute | solution.py:774
  77.3 5.0 %collective-permute-done.17.refs_18_ = bf16[64,4224]{1,0:T(8,128)(2,1)S(1)} collective-permute-done((bf16[64,4224]{1,0:T(8,128)(2,1)S(1)}, bf16[64,4224]{1,0:T(8,128)(2,1)S(1)}, u32[]{:S(2)}, u32[]{:S(2)}) %collective-permute-start.17) | collective-permute-done | bytes 540704 | tf_op jit(solution)/shard_map/ppermute | solution.py:774
  86.9 6.2 %collective-permute-done.10.refs_31_ = bf16[64,4096]{1,0:T(8,128)(2,1)S(1)} collective-permute-done((bf16[64,4096]{1,0:T(8,128)(2,1)S(1)}, bf16[64,4096]{1,0:T(8,128)(2,1)S(1)}, u32[]{:S(2)}, u32[]{:S(2)}) %collective-permute-start.10) | collective-permute-done | bytes 524320 | tf_op jit(solution)/shard_map/ppermute | solution.py:774
  96.5 11.6 %collective-permute-done.18.refs_35_ = bf16[64,4096]{1,0:T(8,128)(2,1)} collective-permute-done((bf16[64,4096]{1,0:T(8,128)(2,1)S(1)}, bf16[64,4096]{1,0:T(8,128)(2,1)}, u32[]{:S(2)}, u32[]{:S(2)}) %collective-permute-start.18) | collective-permute-done | bytes 524320 | tf_op jit(solution)/shard_map/ppermute | solution.py:774
  109.8 3.9 %collective-permute-done.31.refs_33_ = bf16[64,4096]{1,0:T(8,128)(2,1)} collective-permute-done((bf16[64,4096]{1,0:T(8,128)(2,1)S(1)}, bf16[64,4096]{1,0:T(8,128)(2,1)}, u32[]{:S(2)}, u32[]{:S(2)}) %collective-permute-start.31) | collective-permute-done | bytes 524320 | tf_op jit(solution)/shard_map/ppermute | solution.py:774
  118.2 5.3 %collective-permute-done.34.refs_37_ = bf16[64,4096]{1,0:T(8,128)(2,1)} collective-permute-done((bf16[64,4096]{1,0:T(8,128)(2,1)}, bf16[64,4096]{1,0:T(8,128)(2,1)}, u32[]{:S(2)}, u32[]{:S(2)}) %collective-permute-start.34) | collective-permute-done | bytes 524320 | tf_op jit(solution)/shard_map/ppermute | solution.py:774
  127.9 2.8 fusion
  130.9 53.6 %shard_map.251 = (bf16[256,3072]{1,0:T(8,128)(2,1)}, bf16[256,1024]{1,0:T(8,128)(2,1)}, f32[8,2,256]{2,1,0:T(2,128)}, f32[256,1024]{1,0:T(8,128)}, f32[256,1]{1,...) custom-call(s32[1,4]{1,0:T(1,128)} %refs_0_.3, ...), custom_call_target="tpu_custom_call" | custom-call | flops 198642237440 | bytes 50331648 | tf_op jit(solution)/shard_map/pallas_call | solution.py:48
  184.7 11.8 %shard_map.252 = (f32[256,1024]{1,0:T(8,128)}, bf16[256,1024]{1,0:T(8,128)(2,1)}, f32[4,1024]{1,0:T(4,128)}, bf16[256,4096]{1,0:T(8,128)(2,1)}) custom-call(f32[256,1024]{1,0:T(8,128)} %get-tuple-element.158.refs_0_, bf16[256,1024]{1,0:T(8,128)(2,1)} %get-tuple-element.159.refs_1_, f32[256,1]{1,0:T(8,128)} %get-tuple-element.160.refs_2_, ...), custom_call_target="tpu_custom_call" | custom-call | flops 68719476736 | bytes 16777216 | tf_op jit(solution)/shard_map/pallas_call | solution.py:48
  196.5 3.9 %add_convert_fusion.3 = (bf16[128,4096]{1,0:T(8,128)(2,1)}, bf16[128,4096]{1,0:T(8,128)(2,1)S(1)}) fusion(bf16[512,4096]{1,0:T(8,128)(2,1)} %collective-permute-done.42, bf16[512,4096]{1,0:T(8,128)(2,1)} %get-tuple-element.213), kind=kLoop, calls=%fused_computation.7 | loop fusion | flops 4194304 | bytes 6291456 | tf_op jit(solution)/shard_map/convert_element_type | solution.py:850
  202.5 12.8 %shard_map.253 = (bf16[512,5120]{1,0:T(8,128)(2,1)}, bf16[512,5120]{1,0:T(8,128)(2,1)}) custom-call(bf16[1024,1024]{1,0:T(8,128)(2,1)} %get-tuple-element.147.refs_22_.refs_0_, bf16[256,1024]{1,0:T(8,128)(2,1)} %get-tuple-element.174.refs_1_, bf16[256,1024]{1,0:T(8,128)(2,1)} %get-tuple-element.175.refs_2_, bf16[256,4096]{1,0:T(8,128)(2,1)} %get-tuple-element.176.refs_3_, ...), custom_call_target="tpu_custom_call" | custom-call | flops 60129542144 | bytes 16777216 | tf_op jit(solution)/shard_map/pallas_call | solution.py:48
  215.9 2.6 add_convert_fusion.11
  218.5 19.4 %shard_map.254 = (f32[256,1024]{1,0:T(8,128)}, bf16[512,3200]{1,0:T(8,128)(2,1)}, bf16[512,3200]{1,0:T(8,128)(2,1)}) custom-call(s32[1,4]{1,0:T(1,128)} %refs_0_.3, f32[256,1024]{1,0:T(8,128)} %get-tuple-element.186.refs_1_, bf16[256,1024]{1,0:T(8,128)(2,1)} %get-tuple-element.181.refs_8_.refs_2_, bf16[256,3072]{1,0:T(8,128)(2,1)} %get-tuple-element.187.refs_3_, ...), custom_call_target="tpu_custom_call" | custom-call | flops 48318382080 | bytes 16777216 | tf_op jit(solution)/shard_map/pallas_call | solution.py:48
  238.0 2.6 add_convert_fusion.10
  240.8 5.1 %add_convert_fusion.1 = (bf16[128,5120]{1,0:T(8,128)(2,1)}, bf16[128,5120]{1,0:T(8,128)(2,1)}) fusion(bf16[512,5120]{1,0:T(8,128)(2,1)} %collective-permute-done.45, bf16[512,5120]{1,0:T(8,128)(2,1)} %get-tuple-element.233), kind=kLoop, calls=%fused_computation.5 | loop fusion | flops 5242880 | bytes 7864320 | tf_op jit(solution)/shard_map/convert_element_type | solution.py:850
  248.1 9.4 %collective-permute-done.49 = bf16[64,4096]{1,0:T(8,128)(2,1)} collective-permute-done((bf16[64,4096]{1,0:T(8,128)(2,1)}, bf16[64,4096]{1,0:T(8,128)(2,1)}, u32[]{:S(2)}, u32[]{:S(2)}) %collective-permute-start.49) | collective-permute-done | bytes 524320 | tf_op jit(solution)/shard_map/ppermute | solution.py:774
  259.3 4.5 %collective-permute-done.48 = bf16[128,5120]{1,0:T(8,128)(2,1)} collective-permute-done((bf16[128,5120]{1,0:T(8,128)(2,1)}, bf16[128,5120]{1,0:T(8,128)(2,1)}, u32[]{:S(2)}, u32[]{:S(2)}) %collective-permute-start.48) | collective-permute-done | bytes 1310752 | tf_op jit(solution)/shard_map/ppermute | solution.py:774
  267.3 8.6 %collective-permute-done.53 = bf16[64,4096]{1,0:T(8,128)(2,1)S(1)} collective-permute-done((bf16[64,4096]{1,0:T(8,128)(2,1)S(1)}, bf16[64,4096]{1,0:T(8,128)(2,1)S(1)}, u32[]{:S(2)}, u32[]{:S(2)}) %collective-permute-start.53) | collective-permute-done | bytes 524320 | tf_op jit(solution)/shard_map/ppermute | solution.py:774
  279.5 9.3 %collective-permute-done.52 = bf16[64,5120]{1,0:T(8,128)(2,1)S(1)} collective-permute-done((bf16[64,5120]{1,0:T(8,128)(2,1)S(1)}, bf16[64,5120]{1,0:T(8,128)(2,1)S(1)}, u32[]{:S(2)}, u32[]{:S(2)}) %collective-permute-start.52) | collective-permute-done | bytes 655392 | tf_op jit(solution)/shard_map/ppermute | solution.py:774
  290.7 7.4 %collective-permute-done.50 = bf16[256,3200]{1,0:T(8,128)(2,1)S(1)} collective-permute-done((bf16[256,3200]{1,0:T(8,128)(2,1)S(1)}, bf16[256,3200]{1,0:T(8,128)(2,1)S(1)}, u32[]{:S(2)}, u32[]{:S(2)}) %collective-permute-start.50) | collective-permute-done | bytes 1638432 | tf_op jit(solution)/shard_map/ppermute | solution.py:774
  300.9 7.3 %collective-permute-done.55 = bf16[64,5120]{1,0:T(8,128)(2,1)S(1)} collective-permute-done((bf16[64,5120]{1,0:T(8,128)(2,1)S(1)}, bf16[64,5120]{1,0:T(8,128)(2,1)S(1)}, u32[]{:S(2)}, u32[]{:S(2)}) %collective-permute-start.55) | collective-permute-done | bytes 655392 | tf_op jit(solution)/shard_map/ppermute | solution.py:774
  311.7 16.9 %collective-permute-done.58 = bf16[64,5120]{1,0:T(8,128)(2,1)S(1)} collective-permute-done((bf16[64,5120]{1,0:T(8,128)(2,1)S(1)}, bf16[64,5120]{1,0:T(8,128)(2,1)S(1)}, u32[]{:S(2)}, u32[]{:S(2)}) %collective-permute-start.58) | collective-permute-done | bytes 655392 | tf_op jit(solution)/shard_map/ppermute | solution.py:774
  331.2 6.2 %collective-permute-done.60 = bf16[32,5120]{1,0:T(8,128)(2,1)S(1)} collective-permute-done((bf16[32,5120]{1,0:T(8,128)(2,1)S(1)}, bf16[32,5120]{1,0:T(8,128)(2,1)S(1)}, u32[]{:S(2)}, u32[]{:S(2)}) %collective-permute-start.60) | collective-permute-done | bytes 327712 | tf_op jit(solution)/shard_map/ppermute | solution.py:774
  341.8 6.3 %collective-permute-done.61 = bf16[32,3200]{1,0:T(8,128)(2,1)S(1)} collective-permute-done((bf16[32,3200]{1,0:T(8,128)(2,1)S(1)}, bf16[32,3200]{1,0:T(8,128)(2,1)S(1)}, u32[]{:S(2)}, u32[]{:S(2)}) %collective-permute-start.61) | collective-permute-done | bytes 204832 | tf_op jit(solution)/shard_map/ppermute | solution.py:774
  (238 shorter events, 67.0 us)
Async XLA Ops:
  8.5 19.1 %collective-permute-start.3 = (bf16[32,4096]{1,0:T(8,128)(2,1)S(1)}, bf16[32,4096]{1,0:T(8,128)(2,1)S(1)}, u32[]{:S(2)}, u32[]{:S(2)}) collective-permute-start(bf16[32,4096]{1,0:T(8,128)(2,1)S(1)} %get-tuple-element.307), channel_id=1, source_target_pairs={{0,2},{1,5},{2,0},{3,7},{4,6},{5,1},{6,4},{7,3},{8,10},{9,13},{10,... | collective-permute-start | bytes 786440 | tf_op jit(solution)/shard_map/ppermute | solution.py:774
  16.7 22.6 %collective-permute-start.4 = (bf16[64,4224]{1,0:T(8,128)(2,1)S(1)}, bf16[64,4224]{1,0:T(8,128)(2,1)S(1)}, u32[]{:S(2)}, u32[]{:S(2)}) collective-permute-start(bf16[64,4224]{1,0:T(8,128)(2,1)S(1)} %pad_maximum_fusion.2.refs_6_), channel_id=1, source_target_pairs={{0,8},{1,9},{2,10},{3,11},{4,12},{5,13},{6,14},{7,15},{8,16},{9,17... | collective-permute-start | bytes 1622024 | tf_op jit(solution)/shard_map/ppermute | solution.py:774
  18.0 29.0 %collective-permute-start.2 = (bf16[64,4224]{1,0:T(8,128)(2,1)S(1)}, bf16[64,4224]{1,0:T(8,128)(2,1)S(1)}, u32[]{:S(2)}, u32[]{:S(2)}) collective-permute-start(bf16[64,4224]{1,0:T(8,128)(2,1)S(1)} %pad_maximum_fusion.2.refs_6_), channel_id=1, source_target_pairs={{0,4},{1,3},{2,6},{3,1},{4,0},{5,7},{6,2},{7,5},{8,12},{9,11},{10,... | collective-permute-start | bytes 1622024 | tf_op jit(solution)/shard_map/ppermute | solution.py:774
  27.6 17.2 %collective-permute-start.15 = (bf16[32,4096]{1,0:T(8,128)(2,1)S(1)}, bf16[32,4096]{1,0:T(8,128)(2,1)S(1)}, u32[]{:S(2)}, u32[]{:S(2)}) collective-permute-start(bf16[32,4096]{1,0:T(8,128)(2,1)S(1)} %collective-permute-done.14), channel_id=1, source_target_pairs={{0,8},{1,9},{2,10},{3,11},{4,12},{5,13},{6,14},{7,15},{8,16},{9,17... | collective-permute-start | bytes 786440 | tf_op jit(solution)/shard_map/ppermute | solution.py:774
  27.7 18.7 %collective-permute-start.24 = (bf16[64,4096]{1,0:T(8,128)(2,1)S(1)}, bf16[64,4096]{1,0:T(8,128)(2,1)S(1)}, u32[]{:S(2)}, u32[]{:S(2)}) collective-permute-start(bf16[64,4096]{1,0:T(8,128)(2,1)S(1)} %pad_maximum_fusion.3.refs_23_), channel_id=1, source_target_pairs={{0,1},{1,0},{2,3},{3,2},{4,5},{5,4},{6,7},{7,6},{8,9},{9,8},{10,11... | collective-permute-start | bytes 1572872 | tf_op jit(solution)/shard_map/ppermute | solution.py:774
  27.8 26.4 %collective-permute-start.1 = (bf16[64,4224]{1,0:T(8,128)(2,1)S(1)}, bf16[64,4224]{1,0:T(8,128)(2,1)S(1)}, u32[]{:S(2)}, u32[]{:S(2)}) collective-permute-start(bf16[64,4224]{1,0:T(8,128)(2,1)S(1)} %pad_maximum_fusion.2.refs_6_), channel_id=1, source_target_pairs={{0,1},{1,0},{2,3},{3,2},{4,5},{5,4},{6,7},{7,6},{8,9},{9,8},{10,11... | collective-permute-start | bytes 1622024 | tf_op jit(solution)/shard_map/ppermute | solution.py:774
  44.9 26.2 %collective-permute-start.21 = (bf16[128,4096]{1,0:T(8,128)(2,1)S(1)}, bf16[128,4096]{1,0:T(8,128)(2,1)S(1)}, u32[]{:S(2)}, u32[]{:S(2)}) collective-permute-start(bf16[128,4096]{1,0:T(8,128)(2,1)S(1)} %pad_maximum_fusion.refs_39_), channel_id=1, source_target_pairs={{0,2},{1,5},{2,0},{3,7},{4,6},{5,1},{6,4},{7,3},{8,10},{9,13},{10,... | collective-permute-start | bytes 3145736 | tf_op jit(solution)/shard_map/ppermute | solution.py:774
  47.0 24.6 %collective-permute-start.38 = (bf16[128,4096]{1,0:T(8,128)(2,1)S(1)}, bf16[128,4096]{1,0:T(8,128)(2,1)S(1)}, u32[]{:S(2)}, u32[]{:S(2)}) collective-permute-start(bf16[128,4096]{1,0:T(8,128)(2,1)S(1)} %pad_maximum_fusion.refs_39_), channel_id=1, source_target_pairs={{0,4},{1,3},{2,6},{3,1},{4,0},{5,7},{6,2},{7,5},{8,12},{9,11},{10,... | collective-permute-start | bytes 3145736 | tf_op jit(solution)/shard_map/ppermute | solution.py:774
  54.2 17.5 %collective-permute-start.6 = (bf16[64,4096]{1,0:T(8,128)(2,1)S(1)}, bf16[64,4096]{1,0:T(8,128)(2,1)S(1)}, u32[]{:S(2)}, u32[]{:S(2)}) collective-permute-start(bf16[64,4096]{1,0:T(8,128)(2,1)S(1)} %pad_maximum_fusion.3.refs_23_), channel_id=1, source_target_pairs={{0,8},{1,9},{2,10},{3,11},{4,12},{5,13},{6,14},{7,15},{8,16},{9,17... | collective-permute-start | bytes 1572872 | tf_op jit(solution)/shard_map/ppermute | solution.py:774
  60.3 16.7 %collective-permute-start.25 = (bf16[64,4096]{1,0:T(8,128)(2,1)S(1)}, bf16[64,4096]{1,0:T(8,128)(2,1)S(1)}, u32[]{:S(2)}, u32[]{:S(2)}) collective-permute-start(bf16[64,4096]{1,0:T(8,128)(2,1)S(1)} %pad_maximum_fusion.3.refs_23_), channel_id=1, source_target_pairs={{0,4},{1,3},{2,6},{3,1},{4,0},{5,7},{6,2},{7,5},{8,12},{9,11},{10,... | collective-permute-start | bytes 1572872 | tf_op jit(solution)/shard_map/ppermute | solution.py:774
  60.6 21.8 %collective-permute-start.17 = (bf16[64,4224]{1,0:T(8,128)(2,1)S(1)}, bf16[64,4224]{1,0:T(8,128)(2,1)S(1)}, u32[]{:S(2)}, u32[]{:S(2)}) collective-permute-start(bf16[64,4224]{1,0:T(8,128)(2,1)S(1)} %collective-permute-done.5.refs_14_), channel_id=1, source_target_pairs={{0,8},{1,9},{2,10},{3,11},{4,12},{5,13},{6,14},{7,15},{8,16},{9,17... | collective-permute-start | bytes 1622024 | tf_op jit(solution)/shard_map/ppermute | solution.py:774
  71.7 21.5 %collective-permute-start.10 = (bf16[64,4096]{1,0:T(8,128)(2,1)S(1)}, bf16[64,4096]{1,0:T(8,128)(2,1)S(1)}, u32[]{:S(2)}, u32[]{:S(2)}) collective-permute-start(bf16[64,4096]{1,0:T(8,128)(2,1)S(1)} %collective-permute-done.6.refs_27_), channel_id=1, source_target_pairs={{0,8},{1,9},{2,10},{3,11},{4,12},{5,13},{6,14},{7,15},{8,16},{9,17... | collective-permute-start | bytes 1572872 | tf_op jit(solution)/shard_map/ppermute | solution.py:774
  77.0 16.1 %collective-permute-start.28 = (bf16[64,4096]{1,0:T(8,128)(2,1)S(1)}, bf16[64,4096]{1,0:T(8,128)(2,1)S(1)}, u32[]{:S(2)}, u32[]{:S(2)}) collective-permute-start(bf16[64,4096]{1,0:T(8,128)(2,1)S(1)} %collective-permute-done.6.refs_27_), channel_id=1, source_target_pairs={{0,4},{1,3},{2,6},{3,1},{4,0},{5,7},{6,2},{7,5},{8,12},{9,11},{10,... | collective-permute-start | bytes 1572872 | tf_op jit(solution)/shard_map/ppermute | solution.py:774
  93.1 20.9 %collective-permute-start.40 = (bf16[128,4096]{1,0:T(8,128)(2,1)S(1)}, bf16[128,4096]{1,0:T(8,128)(2,1)S(1)}, u32[]{:S(2)}, u32[]{:S(2)}) collective-permute-start(bf16[128,4096]{1,0:T(8,128)(2,1)S(1)} %collective-permute-done.21.refs_41_), channel_id=1, source_target_pairs={{0,4},{1,3},{2,6},{3,1},{4,0},{5,7},{6,2},{7,5},{8,12},{9,11},{10,... | collective-permute-start | bytes 3145736 | tf_op jit(solution)/shard_map/ppermute | solution.py:774
  93.3 20.4 %collective-permute-start.31 = (bf16[64,4096]{1,0:T(8,128)(2,1)S(1)}, bf16[64,4096]{1,0:T(8,128)(2,1)}, u32[]{:S(2)}, u32[]{:S(2)}) collective-permute-start(bf16[64,4096]{1,0:T(8,128)(2,1)S(1)} %collective-permute-done.10.refs_31_), channel_id=1, source_target_pairs={{0,4},{1,3},{2,6},{3,1},{4,0},{5,7},{6,2},{7,5},{8,12},{9,11},{10,... | collective-permute-start | bytes 1572872 | tf_op jit(solution)/shard_map/ppermute | solution.py:774
  95.3 22.3 %collective-permute-start.36 = (bf16[128,4096]{1,0:T(8,128)(2,1)S(1)}, bf16[128,4096]{1,0:T(8,128)(2,1)}, u32[]{:S(2)}, u32[]{:S(2)}) collective-permute-start(bf16[128,4096]{1,0:T(8,128)(2,1)S(1)} %pad_maximum_fusion.refs_39_), channel_id=1, source_target_pairs={{0,1},{1,0},{2,3},{3,2},{4,5},{5,4},{6,7},{7,6},{8,9},{9,8},{10,11... | collective-permute-start | bytes 3145736 | tf_op jit(solution)/shard_map/ppermute | solution.py:774
  96.4 18.6 %collective-permute-start.26 = (bf16[64,4096]{1,0:T(8,128)(2,1)S(1)}, bf16[64,4096]{1,0:T(8,128)(2,1)S(1)}, u32[]{:S(2)}, u32[]{:S(2)}) collective-permute-start(bf16[64,4096]{1,0:T(8,128)(2,1)S(1)} %collective-permute-done.25.refs_25_), channel_id=1, source_target_pairs={{0,1},{1,0},{2,3},{3,2},{4,5},{5,4},{6,7},{7,6},{8,9},{9,8},{10,11... | collective-permute-start | bytes 1572872 | tf_op jit(solution)/shard_map/ppermute | solution.py:774
  200.4 15.5 %collective-permute-start.43 = (bf16[128,4096]{1,0:T(8,128)(2,1)S(1)}, bf16[128,4096]{1,0:T(8,128)(2,1)S(1)}, u32[]{:S(2)}, u32[]{:S(2)}) collective-permute-start(bf16[128,4096]{1,0:T(8,128)(2,1)S(1)} %get-tuple-element.305), channel_id=1, source_target_pairs={{0,4},{1,3},{2,6},{3,1},{4,0},{5,7},{6,2},{7,5},{8,12},{9,11},{10,... | collective-permute-start | bytes 3145736 | tf_op jit(solution)/shard_map/ppermute | solution.py:774
  201.4 36.5 %collective-permute-start.46 = (bf16[128,4096]{1,0:T(8,128)(2,1)}, bf16[128,4096]{1,0:T(8,128)(2,1)}, u32[]{:S(2)}, u32[]{:S(2)}) collective-permute-start(bf16[128,4096]{1,0:T(8,128)(2,1)} %get-tuple-element.304), channel_id=1, source_target_pairs={{0,4},{1,3},{2,6},{3,1},{4,0},{5,7},{6,2},{7,5},{8,12},{9,11},{10,... | collective-permute-start | bytes 3145736 | tf_op jit(solution)/shard_map/ppermute | solution.py:774
  215.3 25.5 %collective-permute-start.45 = (bf16[512,5120]{1,0:T(8,128)(2,1)}, bf16[512,5120]{1,0:T(8,128)(2,1)}, u32[]{:S(2)}, u32[]{:S(2)}) collective-permute-start(bf16[512,5120]{1,0:T(8,128)(2,1)} %get-tuple-element.182), channel_id=1, source_target_pairs={{0,1},{1,0},{2,3},{3,2},{4,5},{5,4},{6,7},{7,6},{8,9},{9,8},{10,11... | collective-permute-start | bytes 15728648 | tf_op jit(solution)/shard_map/ppermute | solution.py:774
  218.5 19.5 %collective-permute-start.47 = (bf16[64,4096]{1,0:T(8,128)(2,1)}, bf16[64,4096]{1,0:T(8,128)(2,1)}, u32[]{:S(2)}, u32[]{:S(2)}) collective-permute-start(bf16[64,4096]{1,0:T(8,128)(2,1)} %add_convert_fusion.11), channel_id=1, source_target_pairs={{0,8},{1,9},{2,10},{3,11},{4,12},{5,13},{6,14},{7,15},{8,16},{9,17... | collective-permute-start | bytes 1572872 | tf_op jit(solution)/shard_map/ppermute | solution.py:774
  237.9 28.3 %collective-permute-start.44 = (bf16[512,3200]{1,0:T(8,128)(2,1)}, bf16[512,3200]{1,0:T(8,128)(2,1)S(1)}, u32[]{:S(2)}, u32[]{:S(2)}) collective-permute-start(bf16[512,3200]{1,0:T(8,128)(2,1)} %get-tuple-element.196), channel_id=1, source_target_pairs={{0,1},{1,0},{2,3},{3,2},{4,5},{5,4},{6,7},{7,6},{8,9},{9,8},{10,11... | collective-permute-start | bytes 9830408 | tf_op jit(solution)/shard_map/ppermute | solution.py:774
  240.5 16.9 %collective-permute-start.49 = (bf16[64,4096]{1,0:T(8,128)(2,1)}, bf16[64,4096]{1,0:T(8,128)(2,1)}, u32[]{:S(2)}, u32[]{:S(2)}) collective-permute-start(bf16[64,4096]{1,0:T(8,128)(2,1)} %add_convert_fusion.10), channel_id=1, source_target_pairs={{0,8},{1,9},{2,10},{3,11},{4,12},{5,13},{6,14},{7,15},{8,16},{9,17... | collective-permute-start | bytes 1572872 | tf_op jit(solution)/shard_map/ppermute | solution.py:774
  245.9 17.9 %collective-permute-start.48 = (bf16[128,5120]{1,0:T(8,128)(2,1)}, bf16[128,5120]{1,0:T(8,128)(2,1)}, u32[]{:S(2)}, u32[]{:S(2)}) collective-permute-start(bf16[128,5120]{1,0:T(8,128)(2,1)} %get-tuple-element.301), channel_id=1, source_target_pairs={{0,4},{1,3},{2,6},{3,1},{4,0},{5,7},{6,2},{7,5},{8,12},{9,11},{10,... | collective-permute-start | bytes 3932168 | tf_op jit(solution)/shard_map/ppermute | solution.py:774
  246.9 32.6 %collective-permute-start.51 = (bf16[128,5120]{1,0:T(8,128)(2,1)}, bf16[128,5120]{1,0:T(8,128)(2,1)S(1)}, u32[]{:S(2)}, u32[]{:S(2)}) collective-permute-start(bf16[128,5120]{1,0:T(8,128)(2,1)} %get-tuple-element.300), channel_id=1, source_target_pairs={{0,4},{1,3},{2,6},{3,1},{4,0},{5,7},{6,2},{7,5},{8,12},{9,11},{10,... | collective-permute-start | bytes 3932168 | tf_op jit(solution)/shard_map/ppermute | solution.py:774
  259.2 16.6 %collective-permute-start.53 = (bf16[64,4096]{1,0:T(8,128)(2,1)S(1)}, bf16[64,4096]{1,0:T(8,128)(2,1)S(1)}, u32[]{:S(2)}, u32[]{:S(2)}) collective-permute-start(bf16[64,4096]{1,0:T(8,128)(2,1)S(1)} %add_convert_fusion.9), channel_id=1, source_target_pairs={{0,8},{1,9},{2,10},{3,11},{4,12},{5,13},{6,14},{7,15},{8,16},{9,17... | collective-permute-start | bytes 1572872 | tf_op jit(solution)/shard_map/ppermute | solution.py:774
  265.5 23.3 %collective-permute-start.52 = (bf16[64,5120]{1,0:T(8,128)(2,1)S(1)}, bf16[64,5120]{1,0:T(8,128)(2,1)S(1)}, u32[]{:S(2)}, u32[]{:S(2)}) collective-permute-start(bf16[64,5120]{1,0:T(8,128)(2,1)S(1)} %add_convert_fusion.8), channel_id=1, source_target_pairs={{0,8},{1,9},{2,10},{3,11},{4,12},{5,13},{6,14},{7,15},{8,16},{9,17... | collective-permute-start | bytes 1966088 | tf_op jit(solution)/shard_map/ppermute | solution.py:774
  266.6 31.5 %collective-permute-start.50 = (bf16[256,3200]{1,0:T(8,128)(2,1)S(1)}, bf16[256,3200]{1,0:T(8,128)(2,1)S(1)}, u32[]{:S(2)}, u32[]{:S(2)}) collective-permute-start(bf16[256,3200]{1,0:T(8,128)(2,1)S(1)} %add_convert_fusion), channel_id=1, source_target_pairs={{0,4},{1,3},{2,6},{3,1},{4,0},{5,7},{6,2},{7,5},{8,12},{9,11},{10,... | collective-permute-start | bytes 4915208 | tf_op jit(solution)/shard_map/ppermute | solution.py:774
  277.5 23.4 %collective-permute-start.56 = (bf16[32,4096]{1,0:T(8,128)(2,1)S(1)}, bf16[32,4096]{1,0:T(8,128)(2,1)S(1)}, u32[]{:S(2)}, u32[]{:S(2)}) collective-permute-start(bf16[32,4096]{1,0:T(8,128)(2,1)S(1)} %get-tuple-element.303), channel_id=1, source_target_pairs={{0,2},{1,5},{2,0},{3,7},{4,6},{5,1},{6,4},{7,3},{8,10},{9,13},{10,... | collective-permute-start | bytes 786440 | tf_op jit(solution)/shard_map/ppermute | solution.py:774
  290.7 17.5 %collective-permute-start.55 = (bf16[64,5120]{1,0:T(8,128)(2,1)S(1)}, bf16[64,5120]{1,0:T(8,128)(2,1)S(1)}, u32[]{:S(2)}, u32[]{:S(2)}) collective-permute-start(bf16[64,5120]{1,0:T(8,128)(2,1)S(1)} %add_convert_fusion.7), channel_id=1, source_target_pairs={{0,8},{1,9},{2,10},{3,11},{4,12},{5,13},{6,14},{7,15},{8,16},{9,17... | collective-permute-start | bytes 1966088 | tf_op jit(solution)/shard_map/ppermute | solution.py:774
  309.8 18.8 %collective-permute-start.58 = (bf16[64,5120]{1,0:T(8,128)(2,1)S(1)}, bf16[64,5120]{1,0:T(8,128)(2,1)S(1)}, u32[]{:S(2)}, u32[]{:S(2)}) collective-permute-start(bf16[64,5120]{1,0:T(8,128)(2,1)S(1)} %add_convert_fusion.6), channel_id=1, source_target_pairs={{0,8},{1,9},{2,10},{3,11},{4,12},{5,13},{6,14},{7,15},{8,16},{9,17... | collective-permute-start | bytes 1966088 | tf_op jit(solution)/shard_map/ppermute | solution.py:774
  311.3 19.7 %collective-permute-start.57 = (bf16[32,3200]{1,0:T(8,128)(2,1)S(1)}, bf16[32,3200]{1,0:T(8,128)(2,1)S(1)}, u32[]{:S(2)}, u32[]{:S(2)}) collective-permute-start(bf16[32,3200]{1,0:T(8,128)(2,1)S(1)} %add_convert_fusion.16), channel_id=1, source_target_pairs={{0,8},{1,9},{2,10},{3,11},{4,12},{5,13},{6,14},{7,15},{8,16},{9,17... | collective-permute-start | bytes 614408 | tf_op jit(solution)/shard_map/ppermute | solution.py:774
  (72 other events, 1687.1 us)

commit v6 on v5

--- a/solution.py
+++ b/solution.py
@@ -274,12 +274,10 @@
         qkv1=((count, 3 * width), LOW),
         mixed1=(size, LOW),
         lse1=((width // PAIR, 2, count), f32),
-        unit_first=(size, f32),
-        inverse_first=((count, 1), f32),
-        norm=((4, width), f32),
         hidden_low1=(size, LOW),
         active1=((count, inner), LOW),
-        slope1=((count, inner), LOW),
+        inner_low1=((count, inner), LOW),
+        first_low1=(size, LOW),
         low2=(size, LOW),
         mixed2=(size, LOW),
         hidden_low2=(size, LOW),
@@ -287,8 +285,6 @@
         inner_low2=((count, inner), LOW),
         first_low2=(size, LOW),
         qkv_grad2=((count, 3 * width), LOW),
-        second1=(size, f32),
-        out_low1=(size, LOW),
         norm_grad=((4, width), f32),
     )
 
@@ -299,15 +295,12 @@
         down_rows = copies.rows(r.down_parts, r.down_owners, r.held_down)
         picker_copy = copies.start(r.picker, r.held_picker, False)
         fill_mask(r.lengths, r.mask)
-        kept = []
 
         def up_ready():
             wait_all(up_rows)
-            kept.append(copies.start(r.held_up, r.up_full, False))
 
         def down_ready():
             wait_all(down_rows)
-            copies.start(r.held_down, r.down_full)
 
         def give(name):
             copies.start(getattr(own, name), getattr(r, name))
@@ -316,7 +309,7 @@
             wait_all(att_rows)
             copies.start(r.held_att.at[:, pl.ds(0, 4 * width)], r.att_full)
             turned = r.held_att[:, 4 * width :].astype(f32).T
-            own.norm[...] = turned[0:4]
+            r.norm[...] = turned[0:4]
 
         attend_forward(
             r.tokens,
@@ -328,12 +321,12 @@
             own.mixed1,
             own.lse1,
             r.total,
-            own.norm,
+            r.norm,
             r.hidden2,
-            own.unit_first,
-            own.inverse_first,
-        )
-        for name in ("norm", "qkv1", "mixed1", "lse1", "unit_first", "inverse_first"):
+            r.unit_first,
+            r.inverse_first,
+        )
+        for name in ("qkv1", "mixed1", "lse1"):
             give(name)
         ffn_forward(
             r.hidden2,
@@ -343,14 +336,14 @@
             up_ready,
             down_ready,
             own.active1,
-            own.slope1,
+            own.inner_low1,
             r.total,
         )
-        for name in ("hidden_low1", "active1", "slope1"):
+        for name in ("hidden_low1", "active1"):
             give(name)
         for block in tiles(count, ROWS):
             r.unit2[block], r.inverse2[block], rows = normalize(
-                r.total[block], own.norm[2:3], own.norm[3:4]
+                r.total[block], r.norm[2:3], r.norm[3:4]
             )
             r.rows[block] = rows
             own.low2[block] = rows.astype(LOW)
@@ -365,7 +358,7 @@
             own.mixed2,
             r.lse,
             r.total,
-            own.norm,
+            r.norm,
             r.hidden2,
             r.unit1,
             r.inverse1,
@@ -388,12 +381,12 @@
         for slot in range(r.lengths.shape[1]):
             live = live + r.lengths[0, slot]
         for block in tiles(count, ROWS):
-            unit, inverse, rows = normalize(r.total[block], own.norm[2:3], own.norm[3:4])
+            unit, inverse, rows = normalize(r.total[block], r.norm[2:3], r.norm[3:4])
             own.layer_output[block] = rows.astype(LOW)
             position = block.start + lax.broadcasted_iota(jnp.int32, unit.shape, 0)
             grad = jnp.where(position < live, r.cotangent[block].astype(f32), 0.0)
             add_norm_grad(own.norm_grad, 2, grad, unit)
-            second = normalize_back(grad, unit, inverse, own.norm[2:3])
+            second = normalize_back(grad, unit, inverse, r.norm[2:3])
             r.rows[block] = second
             r.out_low2[block] = second.astype(LOW)
         give("layer_output")
@@ -405,7 +398,7 @@
             r.held_down,
             r.unit1,
             r.inverse1,
-            own.norm,
+            r.norm,
             own.inner_low2,
             r.total,
             r.rows,
@@ -429,16 +422,31 @@
         for block in tiles(count, ROWS):
             grad, unit = r.total[block], r.unit2[block]
             add_norm_grad(own.norm_grad, 2, grad, unit)
-            second = normalize_back(grad, unit, r.inverse2[block], own.norm[2:3])
-            own.second1[block] = second
-            own.out_low1[block] = second.astype(LOW)
-        for name in ("second1", "out_low1", "norm_grad"):
+            second = normalize_back(grad, unit, r.inverse2[block], r.norm[2:3])
+            r.rows[block] = second
+            r.out_low1[block] = second.astype(LOW)
+        ffn_backward(
+            r.rows,
+            r.out_low1,
+            own.inner_low1,
+            r.held_up,
+            r.held_down,
+            r.unit_first,
+            r.inverse_first,
+            r.norm,
+            own.inner_low1,
+            r.total,
+            r.rows,
+            own.first_low1,
+            own.norm_grad,
+        )
+        copies.start(r.rows, r.first1)
+        for name in ("inner_low1", "first_low1", "norm_grad"):
             give(name)
         picker_copy.wait()
-        wait_all(kept)
         weight_sum(
             r.held_picker,
-            (r.out_low2, own.out_low1),
+            (r.out_low2, r.out_low1),
             (r.active2, own.active1),
             r.turned,
             r.held_up,
@@ -451,8 +459,7 @@
     made = {name: (IN_HBM, shape, kind) for name, (shape, kind) in results.items()}
     made |= dict(
         att_full=(IN_HBM, (width, 4 * width), LOW),
-        up_full=(IN_HBM, (width, inner), LOW),
-        down_full=(IN_HBM, (width, inner), LOW),
+        first1=(IN_HBM, size, f32),
         send=(IN_HBM, (width // 2, inner), LOW),
         keep=(IN_HBM, (width // 2, inner), LOW),
     )
@@ -468,10 +475,14 @@
         qkv=pltpu.VMEM((count, 3 * width), LOW),
         lse=pltpu.VMEM((width // PAIR, 2, count), f32),
         active2=pltpu.VMEM((count, inner), LOW),
+        out_low1=pltpu.VMEM(size, LOW),
         out_low2=pltpu.VMEM(size, LOW),
+        unit_first=rows_f32,
+        inverse_first=pltpu.VMEM((count, 1), f32),
         mixed_grad=pltpu.VMEM(size, LOW),
         inverse1=pltpu.VMEM((count, 1), f32),
         inverse2=pltpu.VMEM((count, 1), f32),
+        norm=pltpu.VMEM((4, width), f32),
         total=rows_f32,
         rows=rows_f32,
         hidden2=rows_f32,
@@ -498,117 +509,27 @@
         made,
         scratch,
         own,
-        count * width * (8 * inner + 12 * width) + 9 * count * count * width,
+        count * width * (10 * inner + 12 * width) + 9 * count * count * width,
         12 * width * inner,
         60,
     )
 
 
-def first_ffn_backward(m, norm, unit, inverse):
-    count, width = m.second1.shape
-    inner = m.slope1.shape[1]
-    size, f32 = (count, width), jnp.float32
+def up_gradient(lefts, rights, picker):
+    count, width = lefts[0].shape
+    inner = rights[0].shape[1]
 
     def body(r, own):
         copies = Copies(r.sem)
-        slope = copies.start(r.slope, own.slope, False)
-        weights = []
-        for part in tiles(inner, FF_TILE):
-            part = pl.ds(part.start, FF_TILE)
-            pair = ((r.down, own.down), (r.up, own.up))
-            weights.append([copies.start(a.at[:, part], b.at[:, part], False) for a, b in pair])
-        unit_copy = copies.start(r.unit, own.unit, False)
-        r.norm_grad[...] = jnp.zeros_like(r.norm_grad)
-
-        def ready(index):
-            if index == 0:
-                slope.wait()
-            wait_all(weights[index])
-
-        def norm_ready():
-            unit_copy.wait()
-            copies.start(own.inner_low, r.inner_low)
-
-        ffn_backward(
-            r.second,
-            r.out_low,
-            own.slope,
-            own.up,
-            own.down,
-            own.unit,
-            r.inverse,
-            r.norm,
-            own.inner_low,
-            r.total,
-            r.first,
-            r.first_low,
-            r.norm_grad,
-            ready,
-            norm_ready,
-        )
-        copies.finish()
-
-    return launch(
-        body,
-        dict(
-            second=(VECTORS, m.second1),
-            out_low=(VECTORS, m.out_low1),
-            inverse=(VECTORS, inverse),
-            norm=(VECTORS, norm),
-            slope=(IN_HBM, m.slope1),
-            unit=(IN_HBM, unit),
-            up=(IN_HBM, m.up_full),
-            down=(IN_HBM, m.down_full),
-        ),
-        dict(
-            first=(VECTORS, size, f32),
-            first_low=(VECTORS, size, LOW),
-            norm_grad=(VECTORS, norm.shape, f32),
-            inner_low=(IN_HBM, (count, inner), LOW),
-        ),
-        dict(
-            total=pltpu.VMEM(size, f32),
-            sem=pltpu.SemaphoreType.DMA((2 * (inner // FF_TILE) + 3,)),
-        ),
-        dict(
-            up=pltpu.VMEM((width, inner), LOW),
-            down=pltpu.VMEM((width, inner), LOW),
-            slope=pltpu.VMEM((count, inner), LOW),
-            inner_low=pltpu.VMEM((count, inner), LOW),
-            unit=pltpu.VMEM(size, f32),
-        ),
-        count * width * 4 * inner,
-        4 * width * inner,
-        60,
-    )
-
-
-def up_and_out_gradients(lefts_up, rights_up, lefts_out, rights_out, picker):
-    count, width = lefts_up[0].shape
-    inner = rights_up[0].shape[1]
-    late = dict(right_up=rights_up, left_out=lefts_out, right_out=rights_out)
-
-    def body(r, own):
-        copies = Copies(r.sem)
-        parts = [
-            [
-                [
-                    copies.start(ref.at[:, pl.ds(part.start, TILE)], to.at[:, pl.ds(part.start, TILE)], False)
-                    for ref, to in zip(r.right_up, (own.up_a, own.up_b))
-                ]
-                for part in tiles(inner, TILE)
-            ]
-        ][0]
-        loads = [
-            copies.start(ref, to, False)
-            for ref, to in zip(
-                (*r.left_out, *r.right_out), (own.left_a, own.left_b, own.out_a, own.out_b)
-            )
-        ]
+        parts = []
+        for part in tiles(inner, TILE):
+            part = pl.ds(part.start, TILE)
+            pair = zip(r.rights, (own.right_a, own.right_b))
+            parts.append([copies.start(a.at[:, part], b.at[:, part], False) for a, b in pair])
         weight_sum(
             r.picker,
-            r.left_up,
-            (own.up_a, own.up_b),
+            r.lefts,
+            (own.right_a, own.right_b),
             r.turned,
             r.whole,
             copies,
@@ -617,54 +538,45 @@
             0,
             lambda index: wait_all(parts[index]),
         )
-        wait_all(loads)
-        weight_sum(
-            r.picker,
-            (own.left_a, own.left_b),
-            (own.out_a, own.out_b),
-            r.turned,
-            r.whole,
-            copies,
-            r.send,
-            r.keep,
-            inner,
-        )
         copies.finish()
 
-    given = dict(picker=(VECTORS, picker), left_up=(VECTORS, list(lefts_up)))
-    given |= {name: (IN_HBM, list(pair)) for name, pair in late.items()}
-    low = pltpu.VMEM((count, width), LOW)
+    right = pltpu.VMEM((count, inner), LOW)
     return launch(
         body,
-        given,
         dict(
-            send=(IN_HBM, (width // 2, inner + width), LOW),
-            keep=(IN_HBM, (width // 2, inner + width), LOW),
+            picker=(VECTORS, picker),
+            lefts=(VECTORS, list(lefts)),
+            rights=(IN_HBM, list(rights)),
         ),
         dict(
-            whole=pltpu.VMEM((width, inner + width), LOW),
-            turned=pltpu.VMEM((width, 2 * count), LOW),
-            sem=pltpu.SemaphoreType.DMA((4 + 2 * (inner // TILE) + 2 * (inner + width) // TILE,)),
+            send=(IN_HBM, (width // 2, inner), LOW),
+            keep=(IN_HBM, (width // 2, inner), LOW),
         ),
         dict(
-            up_a=pltpu.VMEM((count, inner), LOW),
-            up_b=pltpu.VMEM((count, inner), LOW),
-            left_a=low,
-            left_b=low,
-            out_a=low,
-            out_b=low,
+            whole=pltpu.VMEM((width, inner), LOW),
+            turned=pltpu.VMEM((width, 2 * count), LOW),
+            sem=pltpu.SemaphoreType.DMA((4 * (inner // TILE),)),
         ),
-        count * width * 2 * (inner + 3 * width),
+        dict(right_a=right, right_b=right),
+        count * width * 2 * (inner + width),
         4 * width * inner,
         60,
     )
 
 
-def first_attention_backward(lengths, first, first_low, qkv, lse, att, tokens, low2, qkv_grad2, norm_grads, picker):
+def first_attention_backward(lengths, first, first_low, qkv, lse, att, tokens, low2, qkv_grad2, mixed, first_low2, norm_grad, picker):
     count, width = first.shape
     size, f32 = (count, width), jnp.float32
-    late = dict(picker=picker, low2=low2, tokens=tokens, qkv_grad2=qkv_grad2)
-    wide = 3 * width + NORM_COLS
+    late = dict(
+        picker=picker,
+        low2=low2,
+        tokens=tokens,
+        qkv_grad2=qkv_grad2,
+        mixed1=mixed[0],
+        mixed2=mixed[1],
+        first_low2=first_low2,
+    )
+    wide = 4 * width + NORM_COLS
 
     def body(r, own):
         copies = Copies(r.sem)
@@ -687,14 +599,6 @@
             lambda chunk: chunks[chunk].wait(),
         )
         wait_all(loads)
-        r.norm_rows[...] = jnp.zeros_like(r.norm_rows)
-        r.norm_rows[0:4] = (r.norm_a[...] + r.norm_b[...]).astype(LOW)
-        extra = product(own.picker[...], r.norm_rows[...], 1, 1).astype(LOW)
-        half = width // 2
-        r.extra[...] = extra
-        columns = pl.ds(3 * width, NORM_COLS)
-        copies.start(r.extra.at[pl.ds(0, half)], r.send.at[:, columns])
-        copies.start(r.extra.at[pl.ds(half, half)], r.keep.at[:, columns])
         weight_sum(
             own.picker,
             (own.low2, own.tokens),
@@ -705,6 +609,25 @@
             r.send,
             r.keep,
         )
+        weight_sum(
+            own.picker,
+            (own.mixed2, own.mixed1),
+            (own.first_low2, r.first_low),
+            r.turned,
+            r.whole,
+            copies,
+            r.send,
+            r.keep,
+            3 * width,
+        )
+        r.norm_rows[...] = jnp.zeros_like(r.norm_rows)
+        r.norm_rows[0:4] = r.norm_grad[...].astype(LOW)
+        extra = product(own.picker[...], r.norm_rows[...], 1, 1).astype(LOW)
+        half = width // 2
+        r.extra[...] = extra
+        columns = pl.ds(4 * width, NORM_COLS)
+        copies.start(r.extra.at[pl.ds(0, half)], r.send.at[:, columns])
+        copies.start(r.extra.at[pl.ds(half, half)], r.keep.at[:, columns])
         copies.finish()
 
     given = dict(
@@ -713,8 +636,7 @@
         first_low=(VECTORS, first_low),
         qkv=(VECTORS, qkv),
         lse=(VECTORS, lse),
-        norm_a=(VECTORS, norm_grads[0]),
-        norm_b=(VECTORS, norm_grads[1]),
+        norm_grad=(VECTORS, norm_grad),
         att=(IN_HBM, att),
     )
     given |= {name: (IN_HBM, value) for name, value in late.items()}
@@ -725,10 +647,10 @@
         mixed_grad=pltpu.VMEM(size, LOW),
         qkv_grad=pltpu.VMEM((count, 3 * width), LOW),
         turned=pltpu.VMEM((width, 2 * count), LOW),
-        whole=pltpu.VMEM((width, 3 * width), LOW),
+        whole=pltpu.VMEM((width, 4 * width), LOW),
         norm_rows=pltpu.VMEM((NORM_COLS, width), LOW),
         extra=pltpu.VMEM((width, NORM_COLS), LOW),
-        sem=pltpu.SemaphoreType.DMA((4 + len(late) + 2 + 2 * (3 * width // TILE),)),
+        sem=pltpu.SemaphoreType.DMA((4 + len(late) + 2 + 2 * (4 * width // TILE),)),
     )
     return launch(
         body,
@@ -740,7 +662,7 @@
         ),
         scratch,
         own,
-        count * width * 10 * width + 5 * count * count * width,
+        count * width * 14 * width + 5 * count * count * width,
         16 * width * width,
         60,
     )
@@ -796,24 +718,33 @@
     return lax.optimization_barrier((value, earlier))[0]
 
 
-def gather_all(route, att, up, down):
+def gather_all(route, att, up, down, besides):
     last = route.ring_size - 1
     pairs = [[jnp.concatenate([piece, route.first(piece)])] for piece in (att, up)]
     chains = (*pairs, [down])
-    others = ([], [])
+    others = [[route.second(chain[0])] for chain in pairs]
     turns = [2] + [which for _ in range(last - 1) for which in (0, 2)] + [1, 0] + [1] * (last - 1)
     arrived = [(), ()]
+    first = crossed = ()
     for turn, which in enumerate(turns):
-        here = after(chains[which][-1], arrived[turn])
+        early = ()
+        if turn == 3:
+            early = others[1][0]
+        if turn == len(turns) - 1:
+            early = crossed
+        before = arrived[turn - 1] if which == 1 and len(chains[1]) == 1 and turn else arrived[turn]
+        here = after(chains[which][-1], (before, early))
         chains[which].append(route.ring(here))
         arrived.append(chains[which][-1])
-        if which < 2:
+        if which < 2 and len(chains[which]) > 2:
             others[which].append(route.second(here))
-    base = jnp.concatenate(chains[2])
-    first, both = route.first(base), route.second(base)
-    crossed = route.second(after(first, pairs[1][1]))
+        if which == 2 and len(chains[2]) > last:
+            base = jnp.concatenate(chains[2])
+            first = route.first(base)
+            both = route.second(after(base, others[0][1]))
+            crossed = route.second(after(first, others[0][1]))
     others[0].append(route.second(after(pairs[0][last], first)))
-    others[1].append(route.second(pairs[1][last]))
+    others[1].append(route.second(after(pairs[1][last], others[0][last])))
     arrays, owners = [[], [], []], [[], [], []]
 
     def add(which, block, second, blocks, when):
@@ -827,7 +758,7 @@
             add(which, chain[k], 0, blocks, ())
             add(which, others[which][k], 1, blocks, pairs[1][min(k + 1 + which, last)])
     rows = range(last + 1)
-    add(2, base, 0, [(k, 0) for k in rows], pairs[0][last])
+    add(2, base, 0, [(k, 0) for k in rows], (pairs[0][last], besides))
     add(2, first, 0, [(k, 1) for k in rows], pairs[1][max(last - 1, 0)])
     add(2, both, 1, [(k, 0) for k in rows], pairs[1][last])
     add(2, crossed, 1, [(k, 1) for k in rows], pairs[1][last])
@@ -876,7 +807,7 @@
 
 
 class SumWhole:
-    def __init__(self, route, upper, lower):
+    def __init__(self, route, upper, lower, eager=False):
         self.term = jnp.concatenate([upper, lower])
 
     def steps(self):
@@ -889,8 +820,8 @@
 
 
 class SumRingMiddle:
-    def __init__(self, route, send, keep):
-        self.route, self.terms = route, (keep, route.core(send))
+    def __init__(self, route, send, keep, eager=False):
+        self.route, self.terms, self.eager = route, (keep, route.core(send)), eager
         self.result = None
 
     def steps(self):
@@ -899,15 +830,16 @@
         half = terms[0].shape[0] // 2
         block = half // count
         earlier = yield
-        near = after(terms, earlier)
-        sends = [add_low(*(part[: half // 2] for part in near))]
-        sends.append(add_low(*(part[half // 2 : half] for part in near)))
-        others = [route.second(send) for send in sends]
-        earlier = yield sends
+        others = []
+        for cut in (slice(0, half // 2), slice(half // 2, half)):
+            send = add_low(*(part[cut] for part in after(terms, earlier)))
+            others.append(route.second(send))
+            earlier = yield send
         moving = None
         for j in range(count):
             arrived = [] if moving is None else [route.ring(moving)]
-            near, far, arrived = after((terms, others if j else others[:1], arrived), earlier)
+            due = 2 if j and self.eager else 2 * j // count + 1
+            near, far, arrived = after((terms, others[:due], arrived), earlier)
             start = half + j * block
             local = [part[start : start + block] for part in near]
             offset = j * block % (half // 2)
@@ -1004,8 +936,7 @@
     if tiled:
         middle = row_picker(owners_ring_middle(route), shard)
         last = row_picker(owners_ring_last(route), shard)
-        arrays, owners = gather_all(route, att_piece, *ffn_pieces)
-        middle, last = lax.optimization_barrier((middle, last))
+        arrays, owners = gather_all(route, att_piece, *ffn_pieces, (middle, last))
         sum_middle, sum_last = SumRingMiddle, SumRingLast
     else:
         middle = last = row_picker(list(range(route.world)), shard)
@@ -1028,60 +959,63 @@
         owned[2],
         middle,
     )
-    down_sum = sum_middle(route, m.send, m.keep)
+    down_sum = sum_middle(route, m.send, m.keep, True)
     down_steps = down_sum.steps()
     next(down_steps, None)
-    b = first_ffn_backward(m, m.norm, m.unit_first, m.inverse_first)
-    sends = down_steps.send(b.norm_grad) if tiled else ()
-    c = up_and_out_gradients(
-        after((m.hidden_low2, m.hidden_low1), sends),
-        (m.inner_low2, b.inner_low),
-        (m.mixed2, m.mixed1),
-        (m.first_low2, b.first_low),
-        middle,
-    )
+    c = up_gradient((m.hidden_low2, m.hidden_low1), (m.inner_low2, m.inner_low1), middle)
     up_sum = sum_middle(route, c.send, c.keep)
     sends = down_steps.send(c.send) if tiled else ()
+    sends = down_steps.send(sends) if tiled else ()
     a = first_attention_backward(
         seq_lengths,
-        after(b.first, sends),
-        b.first_low,
+        after(m.first1, sends),
+        m.first_low1,
         m.qkv1,
         m.lse1,
         m.att_full,
         tokens,
         m.low2,
         m.qkv_grad2,
-        (m.norm_grad, b.norm_grad),
+        (m.mixed1, m.mixed2),
+        m.first_low2,
+        m.norm_grad,
         last,
     )
     in_sum = sum_last(route, a.send, a.keep)
+    step_rate = 0.1 / math.sqrt(row_count * lax.axis_size(AXES))
+
+    def ffn_update():
+        shares = jnp.stack([up_sum.total(), down_sum.total()])
+        return update(shares, ffn_master, ffn_moment, ffn_average, step_rate)
+
     if tiled:
         up_steps, in_steps = up_sum.steps(), in_sum.steps()
         next(up_steps)
         next(in_steps)
-        order = [down_steps, up_steps, down_steps, up_steps, in_steps, down_steps, up_steps]
-        order += [in_steps, down_steps, up_steps, in_steps, up_steps, in_steps, up_steps, in_steps]
+        order = [down_steps, up_steps, up_steps, down_steps, up_steps, in_steps, down_steps]
+        order += [up_steps, in_steps, down_steps, up_steps, in_steps, down_steps, up_steps]
+        order += [in_steps, up_steps, in_steps]
         earlier = a.input_grad
         for chain in order:
             earlier = chain.send(earlier)
-        for chain in (down_steps, up_steps, in_steps):
+        for chain in (down_steps, up_steps):
             for earlier in iter(functools.partial(advance, chain, earlier), None):
                 pass
-    down_share, up_share, inproj_share = down_sum.total(), up_sum.total(), in_sum.total()
-    inner = ffn_master.shape[2]
-    proj_share = up_share[:, inner:]
-    up_share = up_share[:, :inner]
-    wide = 3 * width // 4
-    totals = (
-        jnp.concatenate([inproj_share[:, :wide], proj_share], axis=1),
-        jnp.stack([up_share, down_share]),
-        inproj_share[:, wide : wide + norm_master.shape[0]].T,
-    )
-    step_rate = 0.1 / math.sqrt(row_count * lax.axis_size(("dp", "fsdp")))
-    att_out = update(totals[0], att_master, att_moment, att_average, step_rate)
-    ffn_out = update(totals[1], ffn_master, ffn_moment, ffn_average, step_rate)
-    norm_out = update(totals[2], norm_master, norm_moment, norm_average, step_rate)
+        ffn_out = ffn_update()
+        earlier = (earlier, ffn_out)
+        for earlier in iter(functools.partial(advance, in_steps, earlier), None):
+            pass
+    else:
+        ffn_out = ffn_update()
+    att_total = in_sum.total()
+    norm_total = lax.dot_general(
+        jnp.eye(norm_master.shape[0], NORM_COLS, dtype=jnp.float32),
+        att_total[:, width:],
+        (((1,), (1,)), ((), ())),
+        precision=lax.Precision.HIGHEST,
+    )
+    att_out = update(att_total[:, :width], att_master, att_moment, att_average, step_rate)
+    norm_out = update(norm_total, norm_master, norm_moment, norm_average, step_rate)
     return (
         m.layer_output,
         a.input_grad,

time: 360 us -> 342 us (0.950)
  starting transfers between devices: 38.7 us -> 30.3 us
  Pallas kernels: 97.6 us -> 89.4 us
  other arithmetic: 38.9 us -> 30.8 us
  waiting for transfers between devices: 171 us -> 176 us
    ppermute x62, starting transfers between devices: 38.7 us -> 30.3 us  [move(): return lax.ppermute(array, AXES, pairs)]
    pallas_call x4 -> x3, Pallas kernels: 97.6 us -> 89.4 us  [launch(): pl.pallas_call(kernel, out_shape=[jax.ShapeDtypeStruct(shape, kind) for _...]
    convert_element_type x14 -> x15, other arithmetic: 24.9 us -> 17.1 us  [add_low(): return add_all(*terms).astype(jnp.bfloat16)]
    ppermute x62, waiting for transfers between devices: 171 us -> 176 us  [move(): return lax.ppermute(array, AXES, pairs)]
  transfers between devices with their start and end apart: 62 -> 62, of which waited for: 25 -> 24; matrix products, arithmetic and copies ran while one was open for 9% -> 8% of each run, Pallas kernels for 12% -> 9%
where the time goes in v6:
time: 342 us; the launch traced here: 338 us
  waiting for transfers between devices  176 us (51%)
  Pallas kernels  89.4 us (26%)
  other arithmetic  30.8 us (9%)
  starting transfers between devices  30.3 us (9%)
  local copies, waits for them, and re-layouts  8.34 us (2%)
    ppermute x62, waiting for transfers between devices, move(): return lax.ppermute(array, AXES, pairs)  176 us
    pallas_call x3, Pallas kernels, launch(): pl.pallas_call(kernel, out_shape=[jax.ShapeDtypeStruct(shape, kind) for _...  89.4 us
    ppermute x62, starting transfers between devices, move(): return lax.ppermute(array, AXES, pairs)  30.3 us
    convert_element_type x15, other arithmetic, add_low(): return add_all(*terms).astype(jnp.bfloat16)  17.1 us
  transfers between devices with their start and end apart: 62, of which 24 were waited for; matrix products, arithmetic and copies ran while one was open for 8% of the time, Pallas kernels for 9%

profile of v6, /device:TPU:0, one launch (start us, length us, event | category | flops | bytes accessed | tf_op | source)
XLA Modules:
  0.0 337.9 jit_solution(8170479760977711378)
XLA Ops:
  2.1 3.1 collective-permute-start.4
  7.4 6.0 %collective-permute-done.4 = bf16[32,4096]{1,0:T(8,128)(2,1)S(1)} collective-permute-done((bf16[32,4096]{1,0:T(8,128)(2,1)S(1)}, bf16[32,4096]{1,0:T(8,128)(2,1)S(1)}, u32[]{:S(2)}, u32[]{:S(2)}) %collective-permute-start.4) | collective-permute-done | bytes 262176 | tf_op jit(solution)/shard_map/ppermute | solution.py:696
  15.1 7.6 %collective-permute-done.5 = bf16[32,4096]{1,0:T(8,128)(2,1)S(1)} collective-permute-done((bf16[32,4096]{1,0:T(8,128)(2,1)S(1)}, bf16[32,4096]{1,0:T(8,128)(2,1)S(1)}, u32[]{:S(2)}, u32[]{:S(2)}) %collective-permute-start.5) | collective-permute-done | bytes 262176 | tf_op jit(solution)/shard_map/ppermute | solution.py:696
  22.9 10.9 %collective-permute-done.16 = bf16[32,4096]{1,0:T(8,128)(2,1)S(1)} collective-permute-done((bf16[32,4096]{1,0:T(8,128)(2,1)S(1)}, bf16[32,4096]{1,0:T(8,128)(2,1)S(1)}, u32[]{:S(2)}, u32[]{:S(2)}) %collective-permute-start.16) | collective-permute-done | bytes 262176 | tf_op jit(solution)/shard_map/ppermute | solution.py:696
  35.7 9.4 %collective-permute-done.8.refs_10_ = bf16[64,4224]{1,0:T(8,128)(2,1)S(1)} collective-permute-done((bf16[64,4224]{1,0:T(8,128)(2,1)S(1)}, bf16[64,4224]{1,0:T(8,128)(2,1)S(1)}, u32[]{:S(2)}, u32[]{:S(2)}) %collective-permute-start.8) | collective-permute-done | bytes 540704 | tf_op jit(solution)/shard_map/ppermute | solution.py:696
  48.0 8.5 %collective-permute-done.6.refs_27_ = bf16[64,4096]{1,0:T(8,128)(2,1)} collective-permute-done((bf16[64,4096]{1,0:T(8,128)(2,1)S(1)}, bf16[64,4096]{1,0:T(8,128)(2,1)}, u32[]{:S(2)}, u32[]{:S(2)}) %collective-permute-start.6) | collective-permute-done | bytes 524320 | tf_op jit(solution)/shard_map/ppermute | solution.py:696
  57.1 11.0 %collective-permute-done.14.refs_14_ = bf16[64,4224]{1,0:T(8,128)(2,1)} collective-permute-done((bf16[64,4224]{1,0:T(8,128)(2,1)S(1)}, bf16[64,4224]{1,0:T(8,128)(2,1)}, u32[]{:S(2)}, u32[]{:S(2)}) %collective-permute-start.14) | collective-permute-done | bytes 540704 | tf_op jit(solution)/shard_map/ppermute | solution.py:696
  69.8 9.5 %collective-permute-done.12.refs_31_ = bf16[64,4096]{1,0:T(8,128)(2,1)} collective-permute-done((bf16[64,4096]{1,0:T(8,128)(2,1)}, bf16[64,4096]{1,0:T(8,128)(2,1)}, u32[]{:S(2)}, u32[]{:S(2)}) %collective-permute-start.12) | collective-permute-done | bytes 524320 | tf_op jit(solution)/shard_map/ppermute | solution.py:696
  80.2 8.3 %collective-permute-done.18.refs_18_ = bf16[64,4224]{1,0:T(8,128)(2,1)} collective-permute-done((bf16[64,4224]{1,0:T(8,128)(2,1)}, bf16[64,4224]{1,0:T(8,128)(2,1)}, u32[]{:S(2)}, u32[]{:S(2)}) %collective-permute-start.18) | collective-permute-done | bytes 540704 | tf_op jit(solution)/shard_map/ppermute | solution.py:696
  90.3 1.8 fusion.refs_22_.refs_0_
  93.3 1.7 fusion.1.refs_7_
  95.7 3.3 collective-permute-done.24.refs_20_
  100.0 9.0 %collective-permute-done.21.refs_35_ = bf16[64,4096]{1,0:T(8,128)(2,1)S(1)} collective-permute-done((bf16[64,4096]{1,0:T(8,128)(2,1)}, bf16[64,4096]{1,0:T(8,128)(2,1)S(1)}, u32[]{:S(2)}, u32[]{:S(2)}) %collective-permute-start.21) | collective-permute-done | bytes 524320 | tf_op jit(solution)/shard_map/ppermute | solution.py:696
  109.0 6.7 %collective-permute-done.32.refs_33_ = bf16[64,4096]{1,0:T(8,128)(2,1)S(1)} collective-permute-done((bf16[64,4096]{1,0:T(8,128)(2,1)}, bf16[64,4096]{1,0:T(8,128)(2,1)S(1)}, u32[]{:S(2)}, u32[]{:S(2)}) %collective-permute-start.32) | collective-permute-done | bytes 524320 | tf_op jit(solution)/shard_map/ppermute | solution.py:696
  119.9 5.6 %collective-permute-done.35.refs_37_ = bf16[64,4096]{1,0:T(8,128)(2,1)} collective-permute-done((bf16[64,4096]{1,0:T(8,128)(2,1)S(1)}, bf16[64,4096]{1,0:T(8,128)(2,1)}, u32[]{:S(2)}, u32[]{:S(2)}) %collective-permute-start.35) | collective-permute-done | bytes 524320 | tf_op jit(solution)/shard_map/ppermute | solution.py:696
  130.8 58.1 %shard_map.251 = (bf16[256,3072]{1,0:T(8,128)(2,1)}, bf16[256,1024]{1,0:T(8,128)(2,1)}, f32[8,2,256]{2,1,0:T(2,128)}, bf16[256,1024]{1,0:T(8,128)(2,1)}, bf16[25...) custom-call(s32[1,4]{1,0:T(1,128)} %refs_0_.3, ...), custom_call_target="tpu_custom_call" | custom-call | flops 233001975808 | bytes 50331648 | tf_op jit(solution)/shard_map/pallas_call | solution.py:48
  189.3 10.4 %shard_map.252 = (bf16[512,4096]{1,0:T(8,128)(2,1)}, bf16[512,4096]{1,0:T(8,128)(2,1)}) custom-call(bf16[1024,1024]{1,0:T(8,128)(2,1)} %fusion.refs_22_.refs_0_, bf16[256,1024]{1,0:T(8,128)(2,1)} %get-tuple-element.155.refs_1_, bf16[256,1024]{1,0:T(8,128)(2,1)} %get-tuple-element.156.refs_2_, bf16[256,4096]{1,0:T(8,128)(2,1)} %get-tuple-element.157.refs_3_, ...), custom_call_target="tpu_custom_call" | custom-call | flops 42949672960 | bytes 16777216 | tf_op jit(solution)/shard_map/pallas_call | solution.py:48
  199.9 1.8 add_convert_fusion.5
  202.8 1.8 add_convert_fusion.4
  205.7 20.9 %shard_map.253 = (f32[256,1024]{1,0:T(8,128)}, bf16[512,4224]{1,0:T(8,128)(2,1)}, bf16[512,4224]{1,0:T(8,128)(2,1)}) custom-call(s32[1,4]{1,0:T(1,128)} %refs_0_.3, f32[256,1024]{1,0:T(8,128)} %get-tuple-element.164.refs_1_, bf16[256,1024]{1,0:T(8,128)(2,1)} %get-tuple-element.165.refs_2_, bf16[256,3072]{1,0:T(8,128)(2,1)} %get-tuple-element.166.refs_3_, ...), custom_call_target="tpu_custom_call" | custom-call | flops 65498251264 | bytes 16777216 | tf_op jit(solution)/shard_map/pallas_call | solution.py:48
  226.7 1.7 add_convert_fusion.11
  228.5 1.9 add_convert_fusion.3
  233.0 11.5 %collective-permute-done.48 = bf16[64,4096]{1,0:T(8,128)(2,1)S(1)} collective-permute-done((bf16[64,4096]{1,0:T(8,128)(2,1)S(1)}, bf16[64,4096]{1,0:T(8,128)(2,1)S(1)}, u32[]{:S(2)}, u32[]{:S(2)}) %collective-permute-start.48) | collective-permute-done | bytes 524320 | tf_op jit(solution)/shard_map/ppermute | solution.py:696
  250.1 12.7 %collective-permute-done.51 = bf16[64,4096]{1,0:T(8,128)(2,1)S(1)} collective-permute-done((bf16[64,4096]{1,0:T(8,128)(2,1)S(1)}, bf16[64,4096]{1,0:T(8,128)(2,1)S(1)}, u32[]{:S(2)}, u32[]{:S(2)}) %collective-permute-start.51) | collective-permute-done | bytes 524320 | tf_op jit(solution)/shard_map/ppermute | solution.py:696
  264.4 9.7 %collective-permute-done.50 = bf16[64,4096]{1,0:T(8,128)(2,1)S(1)} collective-permute-done((bf16[64,4096]{1,0:T(8,128)(2,1)S(1)}, bf16[64,4096]{1,0:T(8,128)(2,1)S(1)}, u32[]{:S(2)}, u32[]{:S(2)}) %collective-permute-start.50) | collective-permute-done | bytes 524320 | tf_op jit(solution)/shard_map/ppermute | solution.py:696
  277.0 8.3 %collective-permute-done.55 = bf16[64,4096]{1,0:T(8,128)(2,1)S(1)} collective-permute-done((bf16[64,4096]{1,0:T(8,128)(2,1)S(1)}, bf16[64,4096]{1,0:T(8,128)(2,1)S(1)}, u32[]{:S(2)}, u32[]{:S(2)}) %collective-permute-start.55) | collective-permute-done | bytes 524320 | tf_op jit(solution)/shard_map/ppermute | solution.py:696
  287.8 7.4 %collective-permute-done.53 = bf16[128,4096]{1,0:T(8,128)(2,1)S(1)} collective-permute-done((bf16[128,4096]{1,0:T(8,128)(2,1)S(1)}, bf16[128,4096]{1,0:T(8,128)(2,1)S(1)}, u32[]{:S(2)}, u32[]{:S(2)}) %collective-permute-start.53) | collective-permute-done | bytes 1048608 | tf_op jit(solution)/shard_map/ppermute | solution.py:696
  299.2 14.3 %collective-permute-done.57 = bf16[64,4096]{1,0:T(8,128)(2,1)S(1)} collective-permute-done((bf16[64,4096]{1,0:T(8,128)(2,1)S(1)}, bf16[64,4096]{1,0:T(8,128)(2,1)S(1)}, u32[]{:S(2)}, u32[]{:S(2)}) %collective-permute-start.57) | collective-permute-done | bytes 524320 | tf_op jit(solution)/shard_map/ppermute | solution.py:696
  317.1 4.2 %collective-permute-done.60 = bf16[32,4096]{1,0:T(8,128)(2,1)S(1)} collective-permute-done((bf16[32,4096]{1,0:T(8,128)(2,1)S(1)}, bf16[32,4096]{1,0:T(8,128)(2,1)S(1)}, u32[]{:S(2)}, u32[]{:S(2)}) %collective-permute-start.60) | collective-permute-done | bytes 262176 | tf_op jit(solution)/shard_map/ppermute | solution.py:696
  321.4 1.7 fusion.6
  323.1 2.2 collective-permute-done.59
  326.8 7.0 %collective-permute-done.61 = bf16[32,4224]{1,0:T(8,128)(2,1)S(1)} collective-permute-done((bf16[32,4224]{1,0:T(8,128)(2,1)S(1)}, bf16[32,4224]{1,0:T(8,128)(2,1)S(1)}, u32[]{:S(2)}, u32[]{:S(2)}) %collective-permute-start.61) | collective-permute-done | bytes 270368 | tf_op jit(solution)/shard_map/ppermute | solution.py:696
  (226 shorter events, 57.6 us)
Async XLA Ops:
  6.8 15.9 %collective-permute-start = (bf16[32,4224]{1,0:T(8,128)(2,1)S(1)}, bf16[32,4224]{1,0:T(8,128)(2,1)S(1)}, u32[]{:S(2)}, u32[]{:S(2)}) collective-permute-start(bf16[32,4224]{1,0:T(8,128)(2,1)S(1)} %pad_maximum_fusion.4), channel_id=1, source_target_pairs={{0,2},{1,5},{2,0},{3,7},{4,6},{5,1},{6,4},{7,3},{8,10},{9,13},{10,... | collective-permute-start | bytes 811016 | tf_op jit(solution)/shard_map/ppermute | solution.py:696
  13.5 22.2 %collective-permute-start.10 = (bf16[64,4096]{1,0:T(8,128)(2,1)S(1)}, bf16[64,4096]{1,0:T(8,128)(2,1)S(1)}, u32[]{:S(2)}, u32[]{:S(2)}) collective-permute-start(bf16[64,4096]{1,0:T(8,128)(2,1)S(1)} %pad_maximum_fusion.3.refs_23_), channel_id=1, source_target_pairs={{0,4},{1,3},{2,6},{3,1},{4,0},{5,7},{6,2},{7,5},{8,12},{9,11},{10,... | collective-permute-start | bytes 1572872 | tf_op jit(solution)/shard_map/ppermute | solution.py:696
  22.8 22.4 %collective-permute-start.8 = (bf16[64,4224]{1,0:T(8,128)(2,1)S(1)}, bf16[64,4224]{1,0:T(8,128)(2,1)S(1)}, u32[]{:S(2)}, u32[]{:S(2)}) collective-permute-start(bf16[64,4224]{1,0:T(8,128)(2,1)S(1)} %pad_maximum_fusion.2.refs_6_), channel_id=1, source_target_pairs={{0,8},{1,9},{2,10},{3,11},{4,12},{5,13},{6,14},{7,15},{8,16},{9,17... | collective-permute-start | bytes 1622024 | tf_op jit(solution)/shard_map/ppermute | solution.py:696
  33.9 23.2 %collective-permute-start.19 = (bf16[128,4096]{1,0:T(8,128)(2,1)S(1)}, bf16[128,4096]{1,0:T(8,128)(2,1)S(1)}, u32[]{:S(2)}, u32[]{:S(2)}) collective-permute-start(bf16[128,4096]{1,0:T(8,128)(2,1)S(1)} %pad_maximum_fusion.refs_39_), channel_id=1, source_target_pairs={{0,2},{1,5},{2,0},{3,7},{4,6},{5,1},{6,4},{7,3},{8,10},{9,13},{10,... | collective-permute-start | bytes 3145736 | tf_op jit(solution)/shard_map/ppermute | solution.py:696
  35.7 20.8 %collective-permute-start.6 = (bf16[64,4096]{1,0:T(8,128)(2,1)S(1)}, bf16[64,4096]{1,0:T(8,128)(2,1)}, u32[]{:S(2)}, u32[]{:S(2)}) collective-permute-start(bf16[64,4096]{1,0:T(8,128)(2,1)S(1)} %pad_maximum_fusion.3.refs_23_), channel_id=1, source_target_pairs={{0,8},{1,9},{2,10},{3,11},{4,12},{5,13},{6,14},{7,15},{8,16},{9,17... | collective-permute-start | bytes 1572872 | tf_op jit(solution)/shard_map/ppermute | solution.py:696
  45.7 22.4 %collective-permute-start.14 = (bf16[64,4224]{1,0:T(8,128)(2,1)S(1)}, bf16[64,4224]{1,0:T(8,128)(2,1)}, u32[]{:S(2)}, u32[]{:S(2)}) collective-permute-start(bf16[64,4224]{1,0:T(8,128)(2,1)S(1)} %collective-permute-done.8.refs_10_), channel_id=1, source_target_pairs={{0,8},{1,9},{2,10},{3,11},{4,12},{5,13},{6,14},{7,15},{8,16},{9,17... | collective-permute-start | bytes 1622024 | tf_op jit(solution)/shard_map/ppermute | solution.py:696
  46.5 22.1 %collective-permute-start.2 = (bf16[64,4224]{1,0:T(8,128)(2,1)S(1)}, bf16[64,4224]{1,0:T(8,128)(2,1)S(1)}, u32[]{:S(2)}, u32[]{:S(2)}) collective-permute-start(bf16[64,4224]{1,0:T(8,128)(2,1)S(1)} %pad_maximum_fusion.2.refs_6_), channel_id=1, source_target_pairs={{0,4},{1,3},{2,6},{3,1},{4,0},{5,7},{6,2},{7,5},{8,12},{9,11},{10,... | collective-permute-start | bytes 1622024 | tf_op jit(solution)/shard_map/ppermute | solution.py:696
  56.5 13.2 %collective-permute-start.29 = (bf16[64,4096]{1,0:T(8,128)(2,1)}, bf16[64,4096]{1,0:T(8,128)(2,1)}, u32[]{:S(2)}, u32[]{:S(2)}) collective-permute-start(bf16[64,4096]{1,0:T(8,128)(2,1)} %collective-permute-done.6.refs_27_), channel_id=1, source_target_pairs={{0,4},{1,3},{2,6},{3,1},{4,0},{5,7},{6,2},{7,5},{8,12},{9,11},{10,... | collective-permute-start | bytes 1572872 | tf_op jit(solution)/shard_map/ppermute | solution.py:696
  57.1 22.2 %collective-permute-start.12 = (bf16[64,4096]{1,0:T(8,128)(2,1)}, bf16[64,4096]{1,0:T(8,128)(2,1)}, u32[]{:S(2)}, u32[]{:S(2)}) collective-permute-start(bf16[64,4096]{1,0:T(8,128)(2,1)} %collective-permute-done.6.refs_27_), channel_id=1, source_target_pairs={{0,8},{1,9},{2,10},{3,11},{4,12},{5,13},{6,14},{7,15},{8,16},{9,17... | collective-permute-start | bytes 1572872 | tf_op jit(solution)/shard_map/ppermute | solution.py:696
  68.1 21.2 %collective-permute-start.20 = (bf16[128,4096]{1,0:T(8,128)(2,1)S(1)}, bf16[128,4096]{1,0:T(8,128)(2,1)}, u32[]{:S(2)}, u32[]{:S(2)}) collective-permute-start(bf16[128,4096]{1,0:T(8,128)(2,1)S(1)} %collective-permute-done.19.refs_41_), channel_id=1, source_target_pairs={{0,4},{1,3},{2,6},{3,1},{4,0},{5,7},{6,2},{7,5},{8,12},{9,11},{10,... | collective-permute-start | bytes 3145736 | tf_op jit(solution)/shard_map/ppermute | solution.py:696
  68.6 19.8 %collective-permute-start.18 = (bf16[64,4224]{1,0:T(8,128)(2,1)}, bf16[64,4224]{1,0:T(8,128)(2,1)}, u32[]{:S(2)}, u32[]{:S(2)}) collective-permute-start(bf16[64,4224]{1,0:T(8,128)(2,1)} %collective-permute-done.14.refs_14_), channel_id=1, source_target_pairs={{0,8},{1,9},{2,10},{3,11},{4,12},{5,13},{6,14},{7,15},{8,16},{9,17... | collective-permute-start | bytes 1622024 | tf_op jit(solution)/shard_map/ppermute | solution.py:696
  69.8 18.9 %collective-permute-start.7 = (bf16[64,4224]{1,0:T(8,128)(2,1)}, bf16[64,4224]{1,0:T(8,128)(2,1)}, u32[]{:S(2)}, u32[]{:S(2)}) collective-permute-start(bf16[64,4224]{1,0:T(8,128)(2,1)} %copy-done.27), channel_id=1, source_target_pairs={{0,1},{1,0},{2,3},{3,2},{4,5},{5,4},{6,7},{7,6},{8,9},{9,8},{10,11... | collective-permute-start | bytes 1622024 | tf_op jit(solution)/shard_map/ppermute | solution.py:696
  92.1 23.6 %collective-permute-start.39 = (bf16[128,4096]{1,0:T(8,128)(2,1)S(1)}, bf16[128,4096]{1,0:T(8,128)(2,1)S(1)}, u32[]{:S(2)}, u32[]{:S(2)}) collective-permute-start(bf16[128,4096]{1,0:T(8,128)(2,1)S(1)} %pad_maximum_fusion.refs_39_), channel_id=1, source_target_pairs={{0,4},{1,3},{2,6},{3,1},{4,0},{5,7},{6,2},{7,5},{8,12},{9,11},{10,... | collective-permute-start | bytes 3145736 | tf_op jit(solution)/shard_map/ppermute | solution.py:696
  93.2 15.9 %collective-permute-start.21 = (bf16[64,4096]{1,0:T(8,128)(2,1)}, bf16[64,4096]{1,0:T(8,128)(2,1)S(1)}, u32[]{:S(2)}, u32[]{:S(2)}) collective-permute-start(bf16[64,4096]{1,0:T(8,128)(2,1)} %collective-permute-done.12.refs_31_), channel_id=1, source_target_pairs={{0,8},{1,9},{2,10},{3,11},{4,12},{5,13},{6,14},{7,15},{8,16},{9,17... | collective-permute-start | bytes 1572872 | tf_op jit(solution)/shard_map/ppermute | solution.py:696
  95.1 22.2 %collective-permute-start.38 = (bf16[128,4096]{1,0:T(8,128)(2,1)S(1)}, bf16[128,4096]{1,0:T(8,128)(2,1)S(1)}, u32[]{:S(2)}, u32[]{:S(2)}) collective-permute-start(bf16[128,4096]{1,0:T(8,128)(2,1)S(1)} %collective-permute-done.19.refs_41_), channel_id=1, source_target_pairs={{0,1},{1,0},{2,3},{3,2},{4,5},{5,4},{6,7},{7,6},{8,9},{9,8},{10,11... | collective-permute-start | bytes 3145736 | tf_op jit(solution)/shard_map/ppermute | solution.py:696
  95.2 22.1 %collective-permute-start.37 = (bf16[128,4096]{1,0:T(8,128)(2,1)S(1)}, bf16[128,4096]{1,0:T(8,128)(2,1)S(1)}, u32[]{:S(2)}, u32[]{:S(2)}) collective-permute-start(bf16[128,4096]{1,0:T(8,128)(2,1)S(1)} %pad_maximum_fusion.refs_39_), channel_id=1, source_target_pairs={{0,1},{1,0},{2,3},{3,2},{4,5},{5,4},{6,7},{7,6},{8,9},{9,8},{10,11... | collective-permute-start | bytes 3145736 | tf_op jit(solution)/shard_map/ppermute | solution.py:696
  99.0 16.7 %collective-permute-start.32 = (bf16[64,4096]{1,0:T(8,128)(2,1)}, bf16[64,4096]{1,0:T(8,128)(2,1)S(1)}, u32[]{:S(2)}, u32[]{:S(2)}) collective-permute-start(bf16[64,4096]{1,0:T(8,128)(2,1)} %collective-permute-done.12.refs_31_), channel_id=1, source_target_pairs={{0,4},{1,3},{2,6},{3,1},{4,0},{5,7},{6,2},{7,5},{8,12},{9,11},{10,... | collective-permute-start | bytes 1572872 | tf_op jit(solution)/shard_map/ppermute | solution.py:696
  199.7 28.8 %collective-permute-start.44 = (bf16[512,4096]{1,0:T(8,128)(2,1)}, bf16[512,4096]{1,0:T(8,128)(2,1)}, u32[]{:S(2)}, u32[]{:S(2)}) collective-permute-start(bf16[512,4096]{1,0:T(8,128)(2,1)} %get-tuple-element.159), channel_id=1, source_target_pairs={{0,1},{1,0},{2,3},{3,2},{4,5},{5,4},{6,7},{7,6},{8,9},{9,8},{10,11... | collective-permute-start | bytes 12582920 | tf_op jit(solution)/shard_map/ppermute | solution.py:696
  201.7 25.0 %collective-permute-start.45 = (bf16[128,4096]{1,0:T(8,128)(2,1)S(1)}, bf16[128,4096]{1,0:T(8,128)(2,1)}, u32[]{:S(2)}, u32[]{:S(2)}) collective-permute-start(bf16[128,4096]{1,0:T(8,128)(2,1)S(1)} %add_convert_fusion.5), channel_id=1, source_target_pairs={{0,4},{1,3},{2,6},{3,1},{4,0},{5,7},{6,2},{7,5},{8,12},{9,11},{10,... | collective-permute-start | bytes 3145736 | tf_op jit(solution)/shard_map/ppermute | solution.py:696
  204.6 28.4 %collective-permute-start.47 = (bf16[128,4096]{1,0:T(8,128)(2,1)S(1)}, bf16[128,4096]{1,0:T(8,128)(2,1)S(1)}, u32[]{:S(2)}, u32[]{:S(2)}) collective-permute-start(bf16[128,4096]{1,0:T(8,128)(2,1)S(1)} %add_convert_fusion.4), channel_id=1, source_target_pairs={{0,4},{1,3},{2,6},{3,1},{4,0},{5,7},{6,2},{7,5},{8,12},{9,11},{10,... | collective-permute-start | bytes 3145736 | tf_op jit(solution)/shard_map/ppermute | solution.py:696
  226.6 20.9 %collective-permute-start.43 = (bf16[512,4224]{1,0:T(8,128)(2,1)}, bf16[512,4224]{1,0:T(8,128)(2,1)S(1)}, u32[]{:S(2)}, u32[]{:S(2)}) collective-permute-start(bf16[512,4224]{1,0:T(8,128)(2,1)} %get-tuple-element.177), channel_id=1, source_target_pairs={{0,1},{1,0},{2,3},{3,2},{4,5},{5,4},{6,7},{7,6},{8,9},{9,8},{10,11... | collective-permute-start | bytes 12976136 | tf_op jit(solution)/shard_map/ppermute | solution.py:696
  228.4 16.2 %collective-permute-start.48 = (bf16[64,4096]{1,0:T(8,128)(2,1)S(1)}, bf16[64,4096]{1,0:T(8,128)(2,1)S(1)}, u32[]{:S(2)}, u32[]{:S(2)}) collective-permute-start(bf16[64,4096]{1,0:T(8,128)(2,1)S(1)} %add_convert_fusion.11), channel_id=1, source_target_pairs={{0,8},{1,9},{2,10},{3,11},{4,12},{5,13},{6,14},{7,15},{8,16},{9,17... | collective-permute-start | bytes 1572872 | tf_op jit(solution)/shard_map/ppermute | solution.py:696
  230.4 15.8 %collective-permute-start.46 = (bf16[128,4096]{1,0:T(8,128)(2,1)S(1)}, bf16[128,4096]{1,0:T(8,128)(2,1)S(1)}, u32[]{:S(2)}, u32[]{:S(2)}) collective-permute-start(bf16[128,4096]{1,0:T(8,128)(2,1)S(1)} %add_convert_fusion.3), channel_id=1, source_target_pairs={{0,4},{1,3},{2,6},{3,1},{4,0},{5,7},{6,2},{7,5},{8,12},{9,11},{10,... | collective-permute-start | bytes 3145736 | tf_op jit(solution)/shard_map/ppermute | solution.py:696
  246.2 16.7 %collective-permute-start.51 = (bf16[64,4096]{1,0:T(8,128)(2,1)S(1)}, bf16[64,4096]{1,0:T(8,128)(2,1)S(1)}, u32[]{:S(2)}, u32[]{:S(2)}) collective-permute-start(bf16[64,4096]{1,0:T(8,128)(2,1)S(1)} %add_convert_fusion.10), channel_id=1, source_target_pairs={{0,8},{1,9},{2,10},{3,11},{4,12},{5,13},{6,14},{7,15},{8,16},{9,17... | collective-permute-start | bytes 1572872 | tf_op jit(solution)/shard_map/ppermute | solution.py:696
  248.0 27.4 %collective-permute-start.49 = (bf16[256,4224]{1,0:T(8,128)(2,1)S(1)}, bf16[256,4224]{1,0:T(8,128)(2,1)S(1)}, u32[]{:S(2)}, u32[]{:S(2)}) collective-permute-start(bf16[256,4224]{1,0:T(8,128)(2,1)S(1)} %add_convert_fusion), channel_id=1, source_target_pairs={{0,4},{1,3},{2,6},{3,1},{4,0},{5,7},{6,2},{7,5},{8,12},{9,11},{10,... | collective-permute-start | bytes 6488072 | tf_op jit(solution)/shard_map/ppermute | solution.py:696
  249.1 46.1 %collective-permute-start.53 = (bf16[128,4096]{1,0:T(8,128)(2,1)S(1)}, bf16[128,4096]{1,0:T(8,128)(2,1)S(1)}, u32[]{:S(2)}, u32[]{:S(2)}) collective-permute-start(bf16[128,4096]{1,0:T(8,128)(2,1)S(1)} %add_convert_fusion.2), channel_id=1, source_target_pairs={{0,4},{1,3},{2,6},{3,1},{4,0},{5,7},{6,2},{7,5},{8,12},{9,11},{10,... | collective-permute-start | bytes 3145736 | tf_op jit(solution)/shard_map/ppermute | solution.py:696
  250.1 24.0 %collective-permute-start.50 = (bf16[64,4096]{1,0:T(8,128)(2,1)S(1)}, bf16[64,4096]{1,0:T(8,128)(2,1)S(1)}, u32[]{:S(2)}, u32[]{:S(2)}) collective-permute-start(bf16[64,4096]{1,0:T(8,128)(2,1)S(1)} %add_convert_fusion.9), channel_id=1, source_target_pairs={{0,8},{1,9},{2,10},{3,11},{4,12},{5,13},{6,14},{7,15},{8,16},{9,17... | collective-permute-start | bytes 1572872 | tf_op jit(solution)/shard_map/ppermute | solution.py:696
  264.3 21.0 %collective-permute-start.55 = (bf16[64,4096]{1,0:T(8,128)(2,1)S(1)}, bf16[64,4096]{1,0:T(8,128)(2,1)S(1)}, u32[]{:S(2)}, u32[]{:S(2)}) collective-permute-start(bf16[64,4096]{1,0:T(8,128)(2,1)S(1)} %add_convert_fusion.8), channel_id=1, source_target_pairs={{0,8},{1,9},{2,10},{3,11},{4,12},{5,13},{6,14},{7,15},{8,16},{9,17... | collective-permute-start | bytes 1572872 | tf_op jit(solution)/shard_map/ppermute | solution.py:696
  275.4 19.9 %collective-permute-start.54 = (bf16[64,4096]{1,0:T(8,128)(2,1)S(1)}, bf16[64,4096]{1,0:T(8,128)(2,1)S(1)}, u32[]{:S(2)}, u32[]{:S(2)}) collective-permute-start(bf16[64,4096]{1,0:T(8,128)(2,1)S(1)} %add_convert_fusion.7), channel_id=1, source_target_pairs={{0,8},{1,9},{2,10},{3,11},{4,12},{5,13},{6,14},{7,15},{8,16},{9,17... | collective-permute-start | bytes 1572872 | tf_op jit(solution)/shard_map/ppermute | solution.py:696
  276.0 20.7 %collective-permute-start.52 = (bf16[128,4224]{1,0:T(8,128)(2,1)S(1)}, bf16[128,4224]{1,0:T(8,128)(2,1)S(1)}, u32[]{:S(2)}, u32[]{:S(2)}) collective-permute-start(bf16[128,4224]{1,0:T(8,128)(2,1)S(1)} %add_convert_fusion.1), channel_id=1, source_target_pairs={{0,2},{1,5},{2,0},{3,7},{4,6},{5,1},{6,4},{7,3},{8,10},{9,13},{10,... | collective-permute-start | bytes 3244040 | tf_op jit(solution)/shard_map/ppermute | solution.py:696
  296.6 17.0 %collective-permute-start.57 = (bf16[64,4096]{1,0:T(8,128)(2,1)S(1)}, bf16[64,4096]{1,0:T(8,128)(2,1)S(1)}, u32[]{:S(2)}, u32[]{:S(2)}) collective-permute-start(bf16[64,4096]{1,0:T(8,128)(2,1)S(1)} %add_convert_fusion.6), channel_id=1, source_target_pairs={{0,8},{1,9},{2,10},{3,11},{4,12},{5,13},{6,14},{7,15},{8,16},{9,17... | collective-permute-start | bytes 1572872 | tf_op jit(solution)/shard_map/ppermute | solution.py:696
  296.8 20.0 %collective-permute-start.56 = (bf16[32,4224]{1,0:T(8,128)(2,1)S(1)}, bf16[32,4224]{1,0:T(8,128)(2,1)S(1)}, u32[]{:S(2)}, u32[]{:S(2)}) collective-permute-start(bf16[32,4224]{1,0:T(8,128)(2,1)S(1)} %add_convert_fusion.14), channel_id=1, source_target_pairs={{0,8},{1,9},{2,10},{3,11},{4,12},{5,13},{6,14},{7,15},{8,16},{9,17... | collective-permute-start | bytes 811016 | tf_op jit(solution)/shard_map/ppermute | solution.py:696
  (71 other events, 816.6 us)

commit v7 on v6

--- a/solution.py
+++ b/solution.py
@@ -568,6 +568,8 @@
     count, width = first.shape
     size, f32 = (count, width), jnp.float32
     late = dict(
+        first_low=first_low,
+        qkv=qkv,
         picker=picker,
         low2=low2,
         tokens=tokens,
@@ -581,24 +583,35 @@
     def body(r, own):
         copies = Copies(r.sem)
         chunks = [None] * 4
+        loads = []
         for chunk in (3, 0, 1, 2):
             part = pl.ds(chunk * width, width)
             chunks[chunk] = copies.start(r.att.at[:, part], r.held.at[:, part], False)
-        loads = [copies.start(getattr(r, n), getattr(own, n), False) for n in late]
+            if chunk == 3:
+                loads = [copies.start(getattr(r, n), getattr(own, n), False) for n in late]
+        first_copy = copies.start(r.first, r.total, False)
         fill_mask(r.lengths, r.mask)
+        def ready(chunk):
+            chunks[chunk].wait()
+            if chunk == 3:
+                wait_all(loads[:2])
+            if chunk == 0:
+                first_copy.wait()
+
         attend_backward(
-            r.first,
-            r.first_low,
-            r.qkv,
+            r.total,
+            own.first_low,
+            own.qkv,
             r.lse,
             r.mask,
             r.held,
             r.mixed_grad,
             r.qkv_grad,
-            r.input_grad,
-            lambda chunk: chunks[chunk].wait(),
-        )
-        wait_all(loads)
+            r.total,
+            ready,
+        )
+        copies.start(r.total, r.input_grad)
+        wait_all(loads[2:])
         weight_sum(
             own.picker,
             (own.low2, own.tokens),
@@ -612,7 +625,7 @@
         weight_sum(
             own.picker,
             (own.mixed2, own.mixed1),
-            (own.first_low2, r.first_low),
+            (own.first_low2, own.first_low),
             r.turned,
             r.whole,
             copies,
@@ -632,9 +645,7 @@
 
     given = dict(
         lengths=(SCALARS, lengths),
-        first=(VECTORS, first),
-        first_low=(VECTORS, first_low),
-        qkv=(VECTORS, qkv),
+        first=(IN_HBM, first),
         lse=(VECTORS, lse),
         norm_grad=(VECTORS, norm_grad),
         att=(IN_HBM, att),
@@ -645,18 +656,19 @@
         held=pltpu.VMEM((width, 4 * width), LOW),
         mask=pltpu.VMEM((count, count), f32),
         mixed_grad=pltpu.VMEM(size, LOW),
+        total=pltpu.VMEM(size, f32),
         qkv_grad=pltpu.VMEM((count, 3 * width), LOW),
         turned=pltpu.VMEM((width, 2 * count), LOW),
         whole=pltpu.VMEM((width, 4 * width), LOW),
         norm_rows=pltpu.VMEM((NORM_COLS, width), LOW),
         extra=pltpu.VMEM((width, NORM_COLS), LOW),
-        sem=pltpu.SemaphoreType.DMA((4 + len(late) + 2 + 2 * (4 * width // TILE),)),
+        sem=pltpu.SemaphoreType.DMA((6 + len(late) + 2 + 2 * (4 * width // TILE),)),
     )
     return launch(
         body,
         given,
         dict(
-            input_grad=(VECTORS, size, f32),
+            input_grad=(IN_HBM, size, f32),
             send=(IN_HBM, (width // 2, wide), LOW),
             keep=(IN_HBM, (width // 2, wide), LOW),
         ),
@@ -834,6 +846,7 @@
         for cut in (slice(0, half // 2), slice(half // 2, half)):
             send = add_low(*(part[cut] for part in after(terms, earlier)))
             others.append(route.second(send))
+            self.others = others
             earlier = yield send
         moving = None
         for j in range(count):
@@ -993,11 +1006,11 @@
         next(up_steps)
         next(in_steps)
         order = [down_steps, up_steps, up_steps, down_steps, up_steps, in_steps, down_steps]
-        order += [up_steps, in_steps, down_steps, up_steps, in_steps, down_steps, up_steps]
-        order += [in_steps, up_steps, in_steps]
+        order += [up_steps, in_steps, down_steps, in_steps, up_steps, down_steps, in_steps]
+        order += [up_steps, in_steps, up_steps]
         earlier = a.input_grad
-        for chain in order:
-            earlier = chain.send(earlier)
+        for turn, chain in enumerate(order):
+            earlier = chain.send((earlier, up_sum.others) if turn == 6 else earlier)
         for chain in (down_steps, up_steps):
             for earlier in iter(functools.partial(advance, chain, earlier), None):
                 pass

time: 342 us -> 336 us (0.982)
  transfers between devices with their start and end apart: 62 -> 62, of which waited for: 24 -> 27; matrix products, arithmetic and copies ran while one was open for 8% -> 9% of each run, Pallas kernels for 9% -> 9%
where the time goes in v7:
time: 336 us; the launch traced here: 333 us
  waiting for transfers between devices  174 us (52%)
  Pallas kernels  88 us (26%)
  other arithmetic  30.7 us (9%)
  starting transfers between devices  29.4 us (9%)
  local copies, waits for them, and re-layouts  8.34 us (2%)
    ppermute x62, waiting for transfers between devices, move(): return lax.ppermute(array, AXES, pairs)  174 us
    pallas_call x3, Pallas kernels, launch(): pl.pallas_call(kernel, out_shape=[jax.ShapeDtypeStruct(shape, kind) for _...  88 us
    ppermute x62, starting transfers between devices, move(): return lax.ppermute(array, AXES, pairs)  29.4 us
    convert_element_type x15, other arithmetic, add_low(): return add_all(*terms).astype(jnp.bfloat16)  17 us
  transfers between devices with their start and end apart: 62, of which 27 were waited for; matrix products, arithmetic and copies ran while one was open for 9% of the time, Pallas kernels for 9%

profile of v7, /device:TPU:0, one launch (start us, length us, event | category | flops | bytes accessed | tf_op | source)
XLA Modules:
  0.0 332.7 jit_solution(5215441414951336576)
XLA Ops:
  2.1 3.1 collective-permute-start.4
  7.4 6.0 %collective-permute-done.4 = bf16[32,4096]{1,0:T(8,128)(2,1)S(1)} collective-permute-done((bf16[32,4096]{1,0:T(8,128)(2,1)S(1)}, bf16[32,4096]{1,0:T(8,128)(2,1)S(1)}, u32[]{:S(2)}, u32[]{:S(2)}) %collective-permute-start.4) | collective-permute-done | bytes 262176 | tf_op jit(solution)/shard_map/ppermute | solution.py:708
  15.1 7.6 %collective-permute-done.5 = bf16[32,4096]{1,0:T(8,128)(2,1)S(1)} collective-permute-done((bf16[32,4096]{1,0:T(8,128)(2,1)S(1)}, bf16[32,4096]{1,0:T(8,128)(2,1)S(1)}, u32[]{:S(2)}, u32[]{:S(2)}) %collective-permute-start.5) | collective-permute-done | bytes 262176 | tf_op jit(solution)/shard_map/ppermute | solution.py:708
  22.9 10.9 %collective-permute-done.16 = bf16[32,4096]{1,0:T(8,128)(2,1)S(1)} collective-permute-done((bf16[32,4096]{1,0:T(8,128)(2,1)S(1)}, bf16[32,4096]{1,0:T(8,128)(2,1)S(1)}, u32[]{:S(2)}, u32[]{:S(2)}) %collective-permute-start.16) | collective-permute-done | bytes 262176 | tf_op jit(solution)/shard_map/ppermute | solution.py:708
  35.7 9.4 %collective-permute-done.8.refs_10_ = bf16[64,4224]{1,0:T(8,128)(2,1)S(1)} collective-permute-done((bf16[64,4224]{1,0:T(8,128)(2,1)S(1)}, bf16[64,4224]{1,0:T(8,128)(2,1)S(1)}, u32[]{:S(2)}, u32[]{:S(2)}) %collective-permute-start.8) | collective-permute-done | bytes 540704 | tf_op jit(solution)/shard_map/ppermute | solution.py:708
  48.0 8.5 %collective-permute-done.6.refs_27_ = bf16[64,4096]{1,0:T(8,128)(2,1)} collective-permute-done((bf16[64,4096]{1,0:T(8,128)(2,1)S(1)}, bf16[64,4096]{1,0:T(8,128)(2,1)}, u32[]{:S(2)}, u32[]{:S(2)}) %collective-permute-start.6) | collective-permute-done | bytes 524320 | tf_op jit(solution)/shard_map/ppermute | solution.py:708
  57.1 11.0 %collective-permute-done.14.refs_14_ = bf16[64,4224]{1,0:T(8,128)(2,1)} collective-permute-done((bf16[64,4224]{1,0:T(8,128)(2,1)S(1)}, bf16[64,4224]{1,0:T(8,128)(2,1)}, u32[]{:S(2)}, u32[]{:S(2)}) %collective-permute-start.14) | collective-permute-done | bytes 540704 | tf_op jit(solution)/shard_map/ppermute | solution.py:708
  69.8 9.5 %collective-permute-done.12.refs_31_ = bf16[64,4096]{1,0:T(8,128)(2,1)} collective-permute-done((bf16[64,4096]{1,0:T(8,128)(2,1)}, bf16[64,4096]{1,0:T(8,128)(2,1)}, u32[]{:S(2)}, u32[]{:S(2)}) %collective-permute-start.12) | collective-permute-done | bytes 524320 | tf_op jit(solution)/shard_map/ppermute | solution.py:708
  80.2 8.3 %collective-permute-done.18.refs_18_ = bf16[64,4224]{1,0:T(8,128)(2,1)} collective-permute-done((bf16[64,4224]{1,0:T(8,128)(2,1)}, bf16[64,4224]{1,0:T(8,128)(2,1)}, u32[]{:S(2)}, u32[]{:S(2)}) %collective-permute-start.18) | collective-permute-done | bytes 540704 | tf_op jit(solution)/shard_map/ppermute | solution.py:708
  90.3 1.8 fusion.refs_22_.refs_0_
  93.3 1.7 fusion.1.refs_7_
  95.7 3.3 collective-permute-done.24.refs_20_
  100.0 9.0 %collective-permute-done.21.refs_35_ = bf16[64,4096]{1,0:T(8,128)(2,1)S(1)} collective-permute-done((bf16[64,4096]{1,0:T(8,128)(2,1)}, bf16[64,4096]{1,0:T(8,128)(2,1)S(1)}, u32[]{:S(2)}, u32[]{:S(2)}) %collective-permute-start.21) | collective-permute-done | bytes 524320 | tf_op jit(solution)/shard_map/ppermute | solution.py:708
  109.0 6.7 %collective-permute-done.32.refs_33_ = bf16[64,4096]{1,0:T(8,128)(2,1)S(1)} collective-permute-done((bf16[64,4096]{1,0:T(8,128)(2,1)}, bf16[64,4096]{1,0:T(8,128)(2,1)S(1)}, u32[]{:S(2)}, u32[]{:S(2)}) %collective-permute-start.32) | collective-permute-done | bytes 524320 | tf_op jit(solution)/shard_map/ppermute | solution.py:708
  119.9 5.6 %collective-permute-done.35.refs_37_ = bf16[64,4096]{1,0:T(8,128)(2,1)} collective-permute-done((bf16[64,4096]{1,0:T(8,128)(2,1)S(1)}, bf16[64,4096]{1,0:T(8,128)(2,1)}, u32[]{:S(2)}, u32[]{:S(2)}) %collective-permute-start.35) | collective-permute-done | bytes 524320 | tf_op jit(solution)/shard_map/ppermute | solution.py:708
  130.8 58.1 %shard_map.251 = (bf16[256,3072]{1,0:T(8,128)(2,1)}, bf16[256,1024]{1,0:T(8,128)(2,1)}, f32[8,2,256]{2,1,0:T(2,128)}, bf16[256,1024]{1,0:T(8,128)(2,1)}, bf16[25...) custom-call(s32[1,4]{1,0:T(1,128)} %refs_0_.3, ...), custom_call_target="tpu_custom_call" | custom-call | flops 233001975808 | bytes 50331648 | tf_op jit(solution)/shard_map/pallas_call | solution.py:48
  189.3 10.4 %shard_map.252 = (bf16[512,4096]{1,0:T(8,128)(2,1)}, bf16[512,4096]{1,0:T(8,128)(2,1)}) custom-call(bf16[1024,1024]{1,0:T(8,128)(2,1)} %fusion.refs_22_.refs_0_, bf16[256,1024]{1,0:T(8,128)(2,1)} %get-tuple-element.155.refs_1_, bf16[256,1024]{1,0:T(8,128)(2,1)} %get-tuple-element.156.refs_2_, bf16[256,4096]{1,0:T(8,128)(2,1)} %get-tuple-element.157.refs_3_, ...), custom_call_target="tpu_custom_call" | custom-call | flops 42949672960 | bytes 16777216 | tf_op jit(solution)/shard_map/pallas_call | solution.py:48
  199.9 1.8 add_convert_fusion.5
  202.8 1.8 add_convert_fusion.4
  205.6 19.5 %shard_map.253 = (f32[256,1024]{1,0:T(8,128)}, bf16[512,4224]{1,0:T(8,128)(2,1)}, bf16[512,4224]{1,0:T(8,128)(2,1)}) custom-call(s32[1,4]{1,0:T(1,128)} %refs_0_.3, f32[256,1024]{1,0:T(8,128)} %get-tuple-element.164.refs_1_, f32[8,2,256]{2,1,0:T(2,128)} %get-tuple-element.165.refs_2_, f32[4,1024]{1,0:T(4,128)} %get-tuple-element.166.refs_3_, ...), custom_call_target="tpu_custom_call" | custom-call | flops 65498251264 | bytes 16777216 | tf_op jit(solution)/shard_map/pallas_call | solution.py:48
  227.0 1.9 add_convert_fusion.3
  232.6 10.5 %collective-permute-done.48 = bf16[64,4096]{1,0:T(8,128)(2,1)S(1)} collective-permute-done((bf16[64,4096]{1,0:T(8,128)(2,1)S(1)}, bf16[64,4096]{1,0:T(8,128)(2,1)S(1)}, u32[]{:S(2)}, u32[]{:S(2)}) %collective-permute-start.48) | collective-permute-done | bytes 524320 | tf_op jit(solution)/shard_map/ppermute | solution.py:708
  247.7 7.4 %collective-permute-done.52 = bf16[128,4096]{1,0:T(8,128)(2,1)S(1)} collective-permute-done((bf16[128,4096]{1,0:T(8,128)(2,1)S(1)}, bf16[128,4096]{1,0:T(8,128)(2,1)S(1)}, u32[]{:S(2)}, u32[]{:S(2)}) %collective-permute-start.52) | collective-permute-done | bytes 1048608 | tf_op jit(solution)/shard_map/ppermute | solution.py:708
  255.1 6.3 %collective-permute-done.51 = bf16[64,4096]{1,0:T(8,128)(2,1)S(1)} collective-permute-done((bf16[64,4096]{1,0:T(8,128)(2,1)S(1)}, bf16[64,4096]{1,0:T(8,128)(2,1)S(1)}, u32[]{:S(2)}, u32[]{:S(2)}) %collective-permute-start.51) | collective-permute-done | bytes 524320 | tf_op jit(solution)/shard_map/ppermute | solution.py:708
  262.9 9.7 %collective-permute-done.50 = bf16[64,4096]{1,0:T(8,128)(2,1)S(1)} collective-permute-done((bf16[64,4096]{1,0:T(8,128)(2,1)S(1)}, bf16[64,4096]{1,0:T(8,128)(2,1)S(1)}, u32[]{:S(2)}, u32[]{:S(2)}) %collective-permute-start.50) | collective-permute-done | bytes 524320 | tf_op jit(solution)/shard_map/ppermute | solution.py:708
  274.0 4.3 %collective-permute-done.49 = bf16[256,4224]{1,0:T(8,128)(2,1)S(1)} collective-permute-done((bf16[256,4224]{1,0:T(8,128)(2,1)S(1)}, bf16[256,4224]{1,0:T(8,128)(2,1)S(1)}, u32[]{:S(2)}, u32[]{:S(2)}) %collective-permute-start.49) | collective-permute-done | bytes 2162720 | tf_op jit(solution)/shard_map/ppermute | solution.py:708
  279.8 2.8 collective-permute-done.54
  285.1 8.9 %collective-permute-done.53 = bf16[128,4224]{1,0:T(8,128)(2,1)S(1)} collective-permute-done((bf16[128,4224]{1,0:T(8,128)(2,1)S(1)}, bf16[128,4224]{1,0:T(8,128)(2,1)S(1)}, u32[]{:S(2)}, u32[]{:S(2)}) %collective-permute-start.53) | collective-permute-done | bytes 1081376 | tf_op jit(solution)/shard_map/ppermute | solution.py:708
  296.8 8.6 %collective-permute-done.55 = bf16[32,4224]{1,0:T(8,128)(2,1)S(1)} collective-permute-done((bf16[32,4224]{1,0:T(8,128)(2,1)S(1)}, bf16[32,4224]{1,0:T(8,128)(2,1)S(1)}, u32[]{:S(2)}, u32[]{:S(2)}) %collective-permute-start.55) | collective-permute-done | bytes 270368 | tf_op jit(solution)/shard_map/ppermute | solution.py:708
  305.6 11.0 %collective-permute-done.59 = bf16[64,4096]{1,0:T(8,128)(2,1)S(1)} collective-permute-done((bf16[64,4096]{1,0:T(8,128)(2,1)S(1)}, bf16[64,4096]{1,0:T(8,128)(2,1)S(1)}, u32[]{:S(2)}, u32[]{:S(2)}) %collective-permute-start.59) | collective-permute-done | bytes 524320 | tf_op jit(solution)/shard_map/ppermute | solution.py:708
  320.4 4.0 %collective-permute-done.61 = bf16[32,4096]{1,0:T(8,128)(2,1)S(1)} collective-permute-done((bf16[32,4096]{1,0:T(8,128)(2,1)S(1)}, bf16[32,4096]{1,0:T(8,128)(2,1)S(1)}, u32[]{:S(2)}, u32[]{:S(2)}) %collective-permute-start.61) | collective-permute-done | bytes 262176 | tf_op jit(solution)/shard_map/ppermute | solution.py:708
  324.4 1.7 fusion.6
  (226 shorter events, 59.7 us)
Async XLA Ops:
  6.8 15.9 %collective-permute-start = (bf16[32,4224]{1,0:T(8,128)(2,1)S(1)}, bf16[32,4224]{1,0:T(8,128)(2,1)S(1)}, u32[]{:S(2)}, u32[]{:S(2)}) collective-permute-start(bf16[32,4224]{1,0:T(8,128)(2,1)S(1)} %pad_maximum_fusion.4), channel_id=1, source_target_pairs={{0,2},{1,5},{2,0},{3,7},{4,6},{5,1},{6,4},{7,3},{8,10},{9,13},{10,... | collective-permute-start | bytes 811016 | tf_op jit(solution)/shard_map/ppermute | solution.py:708
  13.5 22.2 %collective-permute-start.10 = (bf16[64,4096]{1,0:T(8,128)(2,1)S(1)}, bf16[64,4096]{1,0:T(8,128)(2,1)S(1)}, u32[]{:S(2)}, u32[]{:S(2)}) collective-permute-start(bf16[64,4096]{1,0:T(8,128)(2,1)S(1)} %pad_maximum_fusion.3.refs_23_), channel_id=1, source_target_pairs={{0,4},{1,3},{2,6},{3,1},{4,0},{5,7},{6,2},{7,5},{8,12},{9,11},{10,... | collective-permute-start | bytes 1572872 | tf_op jit(solution)/shard_map/ppermute | solution.py:708
  22.8 22.4 %collective-permute-start.8 = (bf16[64,4224]{1,0:T(8,128)(2,1)S(1)}, bf16[64,4224]{1,0:T(8,128)(2,1)S(1)}, u32[]{:S(2)}, u32[]{:S(2)}) collective-permute-start(bf16[64,4224]{1,0:T(8,128)(2,1)S(1)} %pad_maximum_fusion.2.refs_6_), channel_id=1, source_target_pairs={{0,8},{1,9},{2,10},{3,11},{4,12},{5,13},{6,14},{7,15},{8,16},{9,17... | collective-permute-start | bytes 1622024 | tf_op jit(solution)/shard_map/ppermute | solution.py:708
  33.9 23.2 %collective-permute-start.19 = (bf16[128,4096]{1,0:T(8,128)(2,1)S(1)}, bf16[128,4096]{1,0:T(8,128)(2,1)S(1)}, u32[]{:S(2)}, u32[]{:S(2)}) collective-permute-start(bf16[128,4096]{1,0:T(8,128)(2,1)S(1)} %pad_maximum_fusion.refs_39_), channel_id=1, source_target_pairs={{0,2},{1,5},{2,0},{3,7},{4,6},{5,1},{6,4},{7,3},{8,10},{9,13},{10,... | collective-permute-start | bytes 3145736 | tf_op jit(solution)/shard_map/ppermute | solution.py:708
  35.7 20.8 %collective-permute-start.6 = (bf16[64,4096]{1,0:T(8,128)(2,1)S(1)}, bf16[64,4096]{1,0:T(8,128)(2,1)}, u32[]{:S(2)}, u32[]{:S(2)}) collective-permute-start(bf16[64,4096]{1,0:T(8,128)(2,1)S(1)} %pad_maximum_fusion.3.refs_23_), channel_id=1, source_target_pairs={{0,8},{1,9},{2,10},{3,11},{4,12},{5,13},{6,14},{7,15},{8,16},{9,17... | collective-permute-start | bytes 1572872 | tf_op jit(solution)/shard_map/ppermute | solution.py:708
  45.7 22.4 %collective-permute-start.14 = (bf16[64,4224]{1,0:T(8,128)(2,1)S(1)}, bf16[64,4224]{1,0:T(8,128)(2,1)}, u32[]{:S(2)}, u32[]{:S(2)}) collective-permute-start(bf16[64,4224]{1,0:T(8,128)(2,1)S(1)} %collective-permute-done.8.refs_10_), channel_id=1, source_target_pairs={{0,8},{1,9},{2,10},{3,11},{4,12},{5,13},{6,14},{7,15},{8,16},{9,17... | collective-permute-start | bytes 1622024 | tf_op jit(solution)/shard_map/ppermute | solution.py:708
  46.5 22.1 %collective-permute-start.2 = (bf16[64,4224]{1,0:T(8,128)(2,1)S(1)}, bf16[64,4224]{1,0:T(8,128)(2,1)S(1)}, u32[]{:S(2)}, u32[]{:S(2)}) collective-permute-start(bf16[64,4224]{1,0:T(8,128)(2,1)S(1)} %pad_maximum_fusion.2.refs_6_), channel_id=1, source_target_pairs={{0,4},{1,3},{2,6},{3,1},{4,0},{5,7},{6,2},{7,5},{8,12},{9,11},{10,... | collective-permute-start | bytes 1622024 | tf_op jit(solution)/shard_map/ppermute | solution.py:708
  56.5 13.2 %collective-permute-start.29 = (bf16[64,4096]{1,0:T(8,128)(2,1)}, bf16[64,4096]{1,0:T(8,128)(2,1)}, u32[]{:S(2)}, u32[]{:S(2)}) collective-permute-start(bf16[64,4096]{1,0:T(8,128)(2,1)} %collective-permute-done.6.refs_27_), channel_id=1, source_target_pairs={{0,4},{1,3},{2,6},{3,1},{4,0},{5,7},{6,2},{7,5},{8,12},{9,11},{10,... | collective-permute-start | bytes 1572872 | tf_op jit(solution)/shard_map/ppermute | solution.py:708
  57.1 22.2 %collective-permute-start.12 = (bf16[64,4096]{1,0:T(8,128)(2,1)}, bf16[64,4096]{1,0:T(8,128)(2,1)}, u32[]{:S(2)}, u32[]{:S(2)}) collective-permute-start(bf16[64,4096]{1,0:T(8,128)(2,1)} %collective-permute-done.6.refs_27_), channel_id=1, source_target_pairs={{0,8},{1,9},{2,10},{3,11},{4,12},{5,13},{6,14},{7,15},{8,16},{9,17... | collective-permute-start | bytes 1572872 | tf_op jit(solution)/shard_map/ppermute | solution.py:708
  68.1 21.2 %collective-permute-start.20 = (bf16[128,4096]{1,0:T(8,128)(2,1)S(1)}, bf16[128,4096]{1,0:T(8,128)(2,1)}, u32[]{:S(2)}, u32[]{:S(2)}) collective-permute-start(bf16[128,4096]{1,0:T(8,128)(2,1)S(1)} %collective-permute-done.19.refs_41_), channel_id=1, source_target_pairs={{0,4},{1,3},{2,6},{3,1},{4,0},{5,7},{6,2},{7,5},{8,12},{9,11},{10,... | collective-permute-start | bytes 3145736 | tf_op jit(solution)/shard_map/ppermute | solution.py:708
  68.6 19.8 %collective-permute-start.18 = (bf16[64,4224]{1,0:T(8,128)(2,1)}, bf16[64,4224]{1,0:T(8,128)(2,1)}, u32[]{:S(2)}, u32[]{:S(2)}) collective-permute-start(bf16[64,4224]{1,0:T(8,128)(2,1)} %collective-permute-done.14.refs_14_), channel_id=1, source_target_pairs={{0,8},{1,9},{2,10},{3,11},{4,12},{5,13},{6,14},{7,15},{8,16},{9,17... | collective-permute-start | bytes 1622024 | tf_op jit(solution)/shard_map/ppermute | solution.py:708
  69.8 18.9 %collective-permute-start.7 = (bf16[64,4224]{1,0:T(8,128)(2,1)}, bf16[64,4224]{1,0:T(8,128)(2,1)}, u32[]{:S(2)}, u32[]{:S(2)}) collective-permute-start(bf16[64,4224]{1,0:T(8,128)(2,1)} %copy-done.27), channel_id=1, source_target_pairs={{0,1},{1,0},{2,3},{3,2},{4,5},{5,4},{6,7},{7,6},{8,9},{9,8},{10,11... | collective-permute-start | bytes 1622024 | tf_op jit(solution)/shard_map/ppermute | solution.py:708
  92.1 23.6 %collective-permute-start.39 = (bf16[128,4096]{1,0:T(8,128)(2,1)S(1)}, bf16[128,4096]{1,0:T(8,128)(2,1)S(1)}, u32[]{:S(2)}, u32[]{:S(2)}) collective-permute-start(bf16[128,4096]{1,0:T(8,128)(2,1)S(1)} %pad_maximum_fusion.refs_39_), channel_id=1, source_target_pairs={{0,4},{1,3},{2,6},{3,1},{4,0},{5,7},{6,2},{7,5},{8,12},{9,11},{10,... | collective-permute-start | bytes 3145736 | tf_op jit(solution)/shard_map/ppermute | solution.py:708
  93.2 15.9 %collective-permute-start.21 = (bf16[64,4096]{1,0:T(8,128)(2,1)}, bf16[64,4096]{1,0:T(8,128)(2,1)S(1)}, u32[]{:S(2)}, u32[]{:S(2)}) collective-permute-start(bf16[64,4096]{1,0:T(8,128)(2,1)} %collective-permute-done.12.refs_31_), channel_id=1, source_target_pairs={{0,8},{1,9},{2,10},{3,11},{4,12},{5,13},{6,14},{7,15},{8,16},{9,17... | collective-permute-start | bytes 1572872 | tf_op jit(solution)/shard_map/ppermute | solution.py:708
  95.1 22.2 %collective-permute-start.38 = (bf16[128,4096]{1,0:T(8,128)(2,1)S(1)}, bf16[128,4096]{1,0:T(8,128)(2,1)S(1)}, u32[]{:S(2)}, u32[]{:S(2)}) collective-permute-start(bf16[128,4096]{1,0:T(8,128)(2,1)S(1)} %collective-permute-done.19.refs_41_), channel_id=1, source_target_pairs={{0,1},{1,0},{2,3},{3,2},{4,5},{5,4},{6,7},{7,6},{8,9},{9,8},{10,11... | collective-permute-start | bytes 3145736 | tf_op jit(solution)/shard_map/ppermute | solution.py:708
  95.2 22.1 %collective-permute-start.37 = (bf16[128,4096]{1,0:T(8,128)(2,1)S(1)}, bf16[128,4096]{1,0:T(8,128)(2,1)S(1)}, u32[]{:S(2)}, u32[]{:S(2)}) collective-permute-start(bf16[128,4096]{1,0:T(8,128)(2,1)S(1)} %pad_maximum_fusion.refs_39_), channel_id=1, source_target_pairs={{0,1},{1,0},{2,3},{3,2},{4,5},{5,4},{6,7},{7,6},{8,9},{9,8},{10,11... | collective-permute-start | bytes 3145736 | tf_op jit(solution)/shard_map/ppermute | solution.py:708
  99.0 16.7 %collective-permute-start.32 = (bf16[64,4096]{1,0:T(8,128)(2,1)}, bf16[64,4096]{1,0:T(8,128)(2,1)S(1)}, u32[]{:S(2)}, u32[]{:S(2)}) collective-permute-start(bf16[64,4096]{1,0:T(8,128)(2,1)} %collective-permute-done.12.refs_31_), channel_id=1, source_target_pairs={{0,4},{1,3},{2,6},{3,1},{4,0},{5,7},{6,2},{7,5},{8,12},{9,11},{10,... | collective-permute-start | bytes 1572872 | tf_op jit(solution)/shard_map/ppermute | solution.py:708
  199.7 27.3 %collective-permute-start.44 = (bf16[512,4096]{1,0:T(8,128)(2,1)}, bf16[512,4096]{1,0:T(8,128)(2,1)}, u32[]{:S(2)}, u32[]{:S(2)}) collective-permute-start(bf16[512,4096]{1,0:T(8,128)(2,1)} %get-tuple-element.159), channel_id=1, source_target_pairs={{0,1},{1,0},{2,3},{3,2},{4,5},{5,4},{6,7},{7,6},{8,9},{9,8},{10,11... | collective-permute-start | bytes 12582920 | tf_op jit(solution)/shard_map/ppermute | solution.py:708
  201.7 23.5 %collective-permute-start.45 = (bf16[128,4096]{1,0:T(8,128)(2,1)S(1)}, bf16[128,4096]{1,0:T(8,128)(2,1)}, u32[]{:S(2)}, u32[]{:S(2)}) collective-permute-start(bf16[128,4096]{1,0:T(8,128)(2,1)S(1)} %add_convert_fusion.5), channel_id=1, source_target_pairs={{0,4},{1,3},{2,6},{3,1},{4,0},{5,7},{6,2},{7,5},{8,12},{9,11},{10,... | collective-permute-start | bytes 3145736 | tf_op jit(solution)/shard_map/ppermute | solution.py:708
  204.6 28.0 %collective-permute-start.47 = (bf16[128,4096]{1,0:T(8,128)(2,1)S(1)}, bf16[128,4096]{1,0:T(8,128)(2,1)S(1)}, u32[]{:S(2)}, u32[]{:S(2)}) collective-permute-start(bf16[128,4096]{1,0:T(8,128)(2,1)S(1)} %add_convert_fusion.4), channel_id=1, source_target_pairs={{0,4},{1,3},{2,6},{3,1},{4,0},{5,7},{6,2},{7,5},{8,12},{9,11},{10,... | collective-permute-start | bytes 3145736 | tf_op jit(solution)/shard_map/ppermute | solution.py:708
  225.1 20.9 %collective-permute-start.43 = (bf16[512,4224]{1,0:T(8,128)(2,1)}, bf16[512,4224]{1,0:T(8,128)(2,1)S(1)}, u32[]{:S(2)}, u32[]{:S(2)}) collective-permute-start(bf16[512,4224]{1,0:T(8,128)(2,1)} %get-tuple-element.177), channel_id=1, source_target_pairs={{0,1},{1,0},{2,3},{3,2},{4,5},{5,4},{6,7},{7,6},{8,9},{9,8},{10,11... | collective-permute-start | bytes 12976136 | tf_op jit(solution)/shard_map/ppermute | solution.py:708
  226.9 16.2 %collective-permute-start.48 = (bf16[64,4096]{1,0:T(8,128)(2,1)S(1)}, bf16[64,4096]{1,0:T(8,128)(2,1)S(1)}, u32[]{:S(2)}, u32[]{:S(2)}) collective-permute-start(bf16[64,4096]{1,0:T(8,128)(2,1)S(1)} %add_convert_fusion.11), channel_id=1, source_target_pairs={{0,8},{1,9},{2,10},{3,11},{4,12},{5,13},{6,14},{7,15},{8,16},{9,17... | collective-permute-start | bytes 1572872 | tf_op jit(solution)/shard_map/ppermute | solution.py:708
  229.0 15.8 %collective-permute-start.46 = (bf16[128,4096]{1,0:T(8,128)(2,1)S(1)}, bf16[128,4096]{1,0:T(8,128)(2,1)S(1)}, u32[]{:S(2)}, u32[]{:S(2)}) collective-permute-start(bf16[128,4096]{1,0:T(8,128)(2,1)S(1)} %add_convert_fusion.3), channel_id=1, source_target_pairs={{0,4},{1,3},{2,6},{3,1},{4,0},{5,7},{6,2},{7,5},{8,12},{9,11},{10,... | collective-permute-start | bytes 3145736 | tf_op jit(solution)/shard_map/ppermute | solution.py:708
  231.6 23.5 %collective-permute-start.52 = (bf16[128,4096]{1,0:T(8,128)(2,1)S(1)}, bf16[128,4096]{1,0:T(8,128)(2,1)S(1)}, u32[]{:S(2)}, u32[]{:S(2)}) collective-permute-start(bf16[128,4096]{1,0:T(8,128)(2,1)S(1)} %add_convert_fusion.2), channel_id=1, source_target_pairs={{0,4},{1,3},{2,6},{3,1},{4,0},{5,7},{6,2},{7,5},{8,12},{9,11},{10,... | collective-permute-start | bytes 3145736 | tf_op jit(solution)/shard_map/ppermute | solution.py:708
  244.7 16.7 %collective-permute-start.51 = (bf16[64,4096]{1,0:T(8,128)(2,1)S(1)}, bf16[64,4096]{1,0:T(8,128)(2,1)S(1)}, u32[]{:S(2)}, u32[]{:S(2)}) collective-permute-start(bf16[64,4096]{1,0:T(8,128)(2,1)S(1)} %add_convert_fusion.10), channel_id=1, source_target_pairs={{0,8},{1,9},{2,10},{3,11},{4,12},{5,13},{6,14},{7,15},{8,16},{9,17... | collective-permute-start | bytes 1572872 | tf_op jit(solution)/shard_map/ppermute | solution.py:708
  246.6 31.7 %collective-permute-start.49 = (bf16[256,4224]{1,0:T(8,128)(2,1)S(1)}, bf16[256,4224]{1,0:T(8,128)(2,1)S(1)}, u32[]{:S(2)}, u32[]{:S(2)}) collective-permute-start(bf16[256,4224]{1,0:T(8,128)(2,1)S(1)} %add_convert_fusion), channel_id=1, source_target_pairs={{0,4},{1,3},{2,6},{3,1},{4,0},{5,7},{6,2},{7,5},{8,12},{9,11},{10,... | collective-permute-start | bytes 6488072 | tf_op jit(solution)/shard_map/ppermute | solution.py:708
  247.7 25.0 %collective-permute-start.50 = (bf16[64,4096]{1,0:T(8,128)(2,1)S(1)}, bf16[64,4096]{1,0:T(8,128)(2,1)S(1)}, u32[]{:S(2)}, u32[]{:S(2)}) collective-permute-start(bf16[64,4096]{1,0:T(8,128)(2,1)S(1)} %add_convert_fusion.9), channel_id=1, source_target_pairs={{0,8},{1,9},{2,10},{3,11},{4,12},{5,13},{6,14},{7,15},{8,16},{9,17... | collective-permute-start | bytes 1572872 | tf_op jit(solution)/shard_map/ppermute | solution.py:708
  262.9 19.7 %collective-permute-start.54 = (bf16[64,4096]{1,0:T(8,128)(2,1)S(1)}, bf16[64,4096]{1,0:T(8,128)(2,1)S(1)}, u32[]{:S(2)}, u32[]{:S(2)}) collective-permute-start(bf16[64,4096]{1,0:T(8,128)(2,1)S(1)} %add_convert_fusion.8), channel_id=1, source_target_pairs={{0,8},{1,9},{2,10},{3,11},{4,12},{5,13},{6,14},{7,15},{8,16},{9,17... | collective-permute-start | bytes 1572872 | tf_op jit(solution)/shard_map/ppermute | solution.py:708
  278.7 15.2 %collective-permute-start.53 = (bf16[128,4224]{1,0:T(8,128)(2,1)S(1)}, bf16[128,4224]{1,0:T(8,128)(2,1)S(1)}, u32[]{:S(2)}, u32[]{:S(2)}) collective-permute-start(bf16[128,4224]{1,0:T(8,128)(2,1)S(1)} %add_convert_fusion.1), channel_id=1, source_target_pairs={{0,2},{1,5},{2,0},{3,7},{4,6},{5,1},{6,4},{7,3},{8,10},{9,13},{10,... | collective-permute-start | bytes 3244040 | tf_op jit(solution)/shard_map/ppermute | solution.py:708
  279.8 15.0 %collective-permute-start.57 = (bf16[64,4096]{1,0:T(8,128)(2,1)S(1)}, bf16[64,4096]{1,0:T(8,128)(2,1)S(1)}, u32[]{:S(2)}, u32[]{:S(2)}) collective-permute-start(bf16[64,4096]{1,0:T(8,128)(2,1)S(1)} %add_convert_fusion.7), channel_id=1, source_target_pairs={{0,8},{1,9},{2,10},{3,11},{4,12},{5,13},{6,14},{7,15},{8,16},{9,17... | collective-permute-start | bytes 1572872 | tf_op jit(solution)/shard_map/ppermute | solution.py:708
  296.1 20.5 %collective-permute-start.59 = (bf16[64,4096]{1,0:T(8,128)(2,1)S(1)}, bf16[64,4096]{1,0:T(8,128)(2,1)S(1)}, u32[]{:S(2)}, u32[]{:S(2)}) collective-permute-start(bf16[64,4096]{1,0:T(8,128)(2,1)S(1)} %add_convert_fusion.6), channel_id=1, source_target_pairs={{0,8},{1,9},{2,10},{3,11},{4,12},{5,13},{6,14},{7,15},{8,16},{9,17... | collective-permute-start | bytes 1572872 | tf_op jit(solution)/shard_map/ppermute | solution.py:708
  305.5 14.6 %collective-permute-start.58 = (bf16[32,4224]{1,0:T(8,128)(2,1)S(1)}, bf16[32,4224]{1,0:T(8,128)(2,1)S(1)}, u32[]{:S(2)}, u32[]{:S(2)}) collective-permute-start(bf16[32,4224]{1,0:T(8,128)(2,1)S(1)} %add_convert_fusion.13), channel_id=1, source_target_pairs={{0,8},{1,9},{2,10},{3,11},{4,12},{5,13},{6,14},{7,15},{8,16},{9,17... | collective-permute-start | bytes 811016 | tf_op jit(solution)/shard_map/ppermute | solution.py:708
  (71 other events, 795.1 us)

commit v8 on v7

--- a/solution.py
+++ b/solution.py
@@ -768,7 +768,8 @@
         for k in range(last + 1):
             blocks = [(k, 0), (k, 1)]
             add(which, chain[k], 0, blocks, ())
-            add(which, others[which][k], 1, blocks, pairs[1][min(k + 1 + which, last)])
+            late = others[1][last] if (which, k) == (1, last - 1) else pairs[1][min(k + 1 + which, last)]
+            add(which, others[which][k], 1, blocks, late)
     rows = range(last + 1)
     add(2, base, 0, [(k, 0) for k in rows], (pairs[0][last], besides))
     add(2, first, 0, [(k, 1) for k in rows], pairs[1][max(last - 1, 0)])

time: 336 us -> 336 us (level)
  starting transfers between devices: 29.4 us -> 32.9 us
    ppermute x62, starting transfers between devices: 29.4 us -> 32.9 us  [move(): return lax.ppermute(array, AXES, pairs)]
  transfers between devices with their start and end apart: 62 -> 62, of which waited for: 27 -> 30; matrix products, arithmetic and copies ran while one was open for 9% -> 9% of each run, Pallas kernels for 9% -> 9%
where the time goes in v8:
time: 336 us; the launch traced here: 333 us
  waiting for transfers between devices  172 us (51%)
  Pallas kernels  88 us (26%)
  starting transfers between devices  32.9 us (10%)
  other arithmetic  30.8 us (9%)
  local copies, waits for them, and re-layouts  6.75 us (2%)
    ppermute x62, waiting for transfers between devices, move(): return lax.ppermute(array, AXES, pairs)  172 us
    pallas_call x3, Pallas kernels, launch(): pl.pallas_call(kernel, out_shape=[jax.ShapeDtypeStruct(shape, kind) for _...  88 us
    ppermute x62, starting transfers between devices, move(): return lax.ppermute(array, AXES, pairs)  32.9 us
    convert_element_type x15, other arithmetic, add_low(): return add_all(*terms).astype(jnp.bfloat16)  17 us
  transfers between devices with their start and end apart: 62, of which 30 were waited for; matrix products, arithmetic and copies ran while one was open for 9% of the time, Pallas kernels for 9%

profile of v8, /device:TPU:0, one launch (start us, length us, event | category | flops | bytes accessed | tf_op | source)
XLA Modules:
  0.0 332.6 jit_solution(15761987951553894539)
XLA Ops:
  2.1 3.1 collective-permute-start.4
  7.4 6.0 %collective-permute-done.4 = bf16[32,4096]{1,0:T(8,128)(2,1)S(1)} collective-permute-done((bf16[32,4096]{1,0:T(8,128)(2,1)S(1)}, bf16[32,4096]{1,0:T(8,128)(2,1)S(1)}, u32[]{:S(2)}, u32[]{:S(2)}) %collective-permute-start.4) | collective-permute-done | bytes 262176 | tf_op jit(solution)/shard_map/ppermute | solution.py:708
  15.1 7.6 %collective-permute-done.5 = bf16[32,4096]{1,0:T(8,128)(2,1)S(1)} collective-permute-done((bf16[32,4096]{1,0:T(8,128)(2,1)S(1)}, bf16[32,4096]{1,0:T(8,128)(2,1)S(1)}, u32[]{:S(2)}, u32[]{:S(2)}) %collective-permute-start.5) | collective-permute-done | bytes 262176 | tf_op jit(solution)/shard_map/ppermute | solution.py:708
  22.9 10.9 %collective-permute-done.16 = bf16[32,4096]{1,0:T(8,128)(2,1)S(1)} collective-permute-done((bf16[32,4096]{1,0:T(8,128)(2,1)S(1)}, bf16[32,4096]{1,0:T(8,128)(2,1)S(1)}, u32[]{:S(2)}, u32[]{:S(2)}) %collective-permute-start.16) | collective-permute-done | bytes 262176 | tf_op jit(solution)/shard_map/ppermute | solution.py:708
  36.8 8.0 %collective-permute-done.8.refs_10_ = bf16[64,4224]{1,0:T(8,128)(2,1)S(1)} collective-permute-done((bf16[64,4224]{1,0:T(8,128)(2,1)S(1)}, bf16[64,4224]{1,0:T(8,128)(2,1)S(1)}, u32[]{:S(2)}, u32[]{:S(2)}) %collective-permute-start.8) | collective-permute-done | bytes 540704 | tf_op jit(solution)/shard_map/ppermute | solution.py:708
  46.3 2.2 collective-permute-done.2.refs_8_
  50.1 6.0 %collective-permute-done.6.refs_27_ = bf16[64,4096]{1,0:T(8,128)(2,1)} collective-permute-done((bf16[64,4096]{1,0:T(8,128)(2,1)S(1)}, bf16[64,4096]{1,0:T(8,128)(2,1)}, u32[]{:S(2)}, u32[]{:S(2)}) %collective-permute-start.6) | collective-permute-done | bytes 524320 | tf_op jit(solution)/shard_map/ppermute | solution.py:708
  56.9 2.3 collective-permute-done.19.refs_41_
  59.3 6.4 %collective-permute-done.14.refs_14_ = bf16[64,4224]{1,0:T(8,128)(2,1)} collective-permute-done((bf16[64,4224]{1,0:T(8,128)(2,1)S(1)}, bf16[64,4224]{1,0:T(8,128)(2,1)}, u32[]{:S(2)}, u32[]{:S(2)}) %collective-permute-start.14) | collective-permute-done | bytes 540704 | tf_op jit(solution)/shard_map/ppermute | solution.py:708
  69.4 6.8 %collective-permute-done.12.refs_31_ = bf16[64,4096]{1,0:T(8,128)(2,1)} collective-permute-done((bf16[64,4096]{1,0:T(8,128)(2,1)}, bf16[64,4096]{1,0:T(8,128)(2,1)}, u32[]{:S(2)}, u32[]{:S(2)}) %collective-permute-start.12) | collective-permute-done | bytes 524320 | tf_op jit(solution)/shard_map/ppermute | solution.py:708
  78.5 9.3 %collective-permute-done.18.refs_18_ = bf16[64,4224]{1,0:T(8,128)(2,1)} collective-permute-done((bf16[64,4224]{1,0:T(8,128)(2,1)}, bf16[64,4224]{1,0:T(8,128)(2,1)}, u32[]{:S(2)}, u32[]{:S(2)}) %collective-permute-start.18) | collective-permute-done | bytes 540704 | tf_op jit(solution)/shard_map/ppermute | solution.py:708
  89.6 1.8 fusion.refs_22_.refs_0_
  95.7 14.0 %collective-permute-done.21.refs_35_ = bf16[64,4096]{1,0:T(8,128)(2,1)S(1)} collective-permute-done((bf16[64,4096]{1,0:T(8,128)(2,1)}, bf16[64,4096]{1,0:T(8,128)(2,1)S(1)}, u32[]{:S(2)}, u32[]{:S(2)}) %collective-permute-start.21) | collective-permute-done | bytes 524320 | tf_op jit(solution)/shard_map/ppermute | solution.py:708
  113.8 5.5 %collective-permute-done.32.refs_33_ = bf16[64,4096]{1,0:T(8,128)(2,1)} collective-permute-done((bf16[64,4096]{1,0:T(8,128)(2,1)}, bf16[64,4096]{1,0:T(8,128)(2,1)}, u32[]{:S(2)}, u32[]{:S(2)}) %collective-permute-start.32) | collective-permute-done | bytes 524320 | tf_op jit(solution)/shard_map/ppermute | solution.py:708
  119.8 5.0 %collective-permute-done.33.refs_37_ = bf16[64,4096]{1,0:T(8,128)(2,1)} collective-permute-done((bf16[64,4096]{1,0:T(8,128)(2,1)S(1)}, bf16[64,4096]{1,0:T(8,128)(2,1)}, u32[]{:S(2)}, u32[]{:S(2)}) %collective-permute-start.33) | collective-permute-done | bytes 524320 | tf_op jit(solution)/shard_map/ppermute | solution.py:708
  130.6 58.1 %shard_map.251 = (bf16[256,3072]{1,0:T(8,128)(2,1)}, bf16[256,1024]{1,0:T(8,128)(2,1)}, f32[8,2,256]{2,1,0:T(2,128)}, bf16[256,1024]{1,0:T(8,128)(2,1)}, bf16[25...) custom-call(s32[1,4]{1,0:T(1,128)} %refs_0_.3, ...), custom_call_target="tpu_custom_call" | custom-call | flops 233001975808 | bytes 50331648 | tf_op jit(solution)/shard_map/pallas_call | solution.py:48
  188.9 10.4 %shard_map.252 = (bf16[512,4096]{1,0:T(8,128)(2,1)}, bf16[512,4096]{1,0:T(8,128)(2,1)}) custom-call(bf16[1024,1024]{1,0:T(8,128)(2,1)} %fusion.refs_22_.refs_0_, bf16[256,1024]{1,0:T(8,128)(2,1)} %get-tuple-element.155.refs_1_, bf16[256,1024]{1,0:T(8,128)(2,1)} %get-tuple-element.156.refs_2_, bf16[256,4096]{1,0:T(8,128)(2,1)} %get-tuple-element.157.refs_3_, ...), custom_call_target="tpu_custom_call" | custom-call | flops 42949672960 | bytes 16777216 | tf_op jit(solution)/shard_map/pallas_call | solution.py:48
  199.8 1.8 add_convert_fusion.5
  202.1 1.8 add_convert_fusion.4
  205.5 19.5 %shard_map.253 = (f32[256,1024]{1,0:T(8,128)}, bf16[512,4224]{1,0:T(8,128)(2,1)}, bf16[512,4224]{1,0:T(8,128)(2,1)}) custom-call(s32[1,4]{1,0:T(1,128)} %refs_0_.3, f32[256,1024]{1,0:T(8,128)} %get-tuple-element.164.refs_1_, f32[8,2,256]{2,1,0:T(2,128)} %get-tuple-element.165.refs_2_, f32[4,1024]{1,0:T(4,128)} %get-tuple-element.166.refs_3_, ...), custom_call_target="tpu_custom_call" | custom-call | flops 65498251264 | bytes 16777216 | tf_op jit(solution)/shard_map/pallas_call | solution.py:48
  226.9 1.9 add_convert_fusion.3
  232.5 10.5 %collective-permute-done.48 = bf16[64,4096]{1,0:T(8,128)(2,1)S(1)} collective-permute-done((bf16[64,4096]{1,0:T(8,128)(2,1)S(1)}, bf16[64,4096]{1,0:T(8,128)(2,1)S(1)}, u32[]{:S(2)}, u32[]{:S(2)}) %collective-permute-start.48) | collective-permute-done | bytes 524320 | tf_op jit(solution)/shard_map/ppermute | solution.py:708
  247.0 8.0 %collective-permute-done.52 = bf16[128,4096]{1,0:T(8,128)(2,1)S(1)} collective-permute-done((bf16[128,4096]{1,0:T(8,128)(2,1)S(1)}, bf16[128,4096]{1,0:T(8,128)(2,1)S(1)}, u32[]{:S(2)}, u32[]{:S(2)}) %collective-permute-start.52) | collective-permute-done | bytes 1048608 | tf_op jit(solution)/shard_map/ppermute | solution.py:708
  255.0 6.3 %collective-permute-done.51 = bf16[64,4096]{1,0:T(8,128)(2,1)S(1)} collective-permute-done((bf16[64,4096]{1,0:T(8,128)(2,1)S(1)}, bf16[64,4096]{1,0:T(8,128)(2,1)S(1)}, u32[]{:S(2)}, u32[]{:S(2)}) %collective-permute-start.51) | collective-permute-done | bytes 524320 | tf_op jit(solution)/shard_map/ppermute | solution.py:708
  262.8 9.7 %collective-permute-done.50 = bf16[64,4096]{1,0:T(8,128)(2,1)S(1)} collective-permute-done((bf16[64,4096]{1,0:T(8,128)(2,1)S(1)}, bf16[64,4096]{1,0:T(8,128)(2,1)S(1)}, u32[]{:S(2)}, u32[]{:S(2)}) %collective-permute-start.50) | collective-permute-done | bytes 524320 | tf_op jit(solution)/shard_map/ppermute | solution.py:708
  273.8 4.3 %collective-permute-done.49 = bf16[256,4224]{1,0:T(8,128)(2,1)S(1)} collective-permute-done((bf16[256,4224]{1,0:T(8,128)(2,1)S(1)}, bf16[256,4224]{1,0:T(8,128)(2,1)S(1)}, u32[]{:S(2)}, u32[]{:S(2)}) %collective-permute-start.49) | collective-permute-done | bytes 2162720 | tf_op jit(solution)/shard_map/ppermute | solution.py:708
  279.1 3.4 %collective-permute-done.54 = bf16[64,4096]{1,0:T(8,128)(2,1)S(1)} collective-permute-done((bf16[64,4096]{1,0:T(8,128)(2,1)S(1)}, bf16[64,4096]{1,0:T(8,128)(2,1)S(1)}, u32[]{:S(2)}, u32[]{:S(2)}) %collective-permute-start.54) | collective-permute-done | bytes 524320 | tf_op jit(solution)/shard_map/ppermute | solution.py:708
  284.4 9.5 %collective-permute-done.53 = bf16[128,4224]{1,0:T(8,128)(2,1)S(1)} collective-permute-done((bf16[128,4224]{1,0:T(8,128)(2,1)S(1)}, bf16[128,4224]{1,0:T(8,128)(2,1)S(1)}, u32[]{:S(2)}, u32[]{:S(2)}) %collective-permute-start.53) | collective-permute-done | bytes 1081376 | tf_op jit(solution)/shard_map/ppermute | solution.py:708
  296.7 8.6 %collective-permute-done.55 = bf16[32,4224]{1,0:T(8,128)(2,1)S(1)} collective-permute-done((bf16[32,4224]{1,0:T(8,128)(2,1)S(1)}, bf16[32,4224]{1,0:T(8,128)(2,1)S(1)}, u32[]{:S(2)}, u32[]{:S(2)}) %collective-permute-start.55) | collective-permute-done | bytes 270368 | tf_op jit(solution)/shard_map/ppermute | solution.py:708
  305.5 11.0 %collective-permute-done.59 = bf16[64,4096]{1,0:T(8,128)(2,1)S(1)} collective-permute-done((bf16[64,4096]{1,0:T(8,128)(2,1)S(1)}, bf16[64,4096]{1,0:T(8,128)(2,1)S(1)}, u32[]{:S(2)}, u32[]{:S(2)}) %collective-permute-start.59) | collective-permute-done | bytes 524320 | tf_op jit(solution)/shard_map/ppermute | solution.py:708
  318.2 1.8 collective-permute-done.58
  320.3 4.0 %collective-permute-done.61 = bf16[32,4096]{1,0:T(8,128)(2,1)S(1)} collective-permute-done((bf16[32,4096]{1,0:T(8,128)(2,1)S(1)}, bf16[32,4096]{1,0:T(8,128)(2,1)S(1)}, u32[]{:S(2)}, u32[]{:S(2)}) %collective-permute-start.61) | collective-permute-done | bytes 262176 | tf_op jit(solution)/shard_map/ppermute | solution.py:708
  (220 shorter events, 65.4 us)
Async XLA Ops:
  6.8 15.9 %collective-permute-start = (bf16[32,4224]{1,0:T(8,128)(2,1)S(1)}, bf16[32,4224]{1,0:T(8,128)(2,1)S(1)}, u32[]{:S(2)}, u32[]{:S(2)}) collective-permute-start(bf16[32,4224]{1,0:T(8,128)(2,1)S(1)} %pad_maximum_fusion.4), channel_id=1, source_target_pairs={{0,2},{1,5},{2,0},{3,7},{4,6},{5,1},{6,4},{7,3},{8,10},{9,13},{10,... | collective-permute-start | bytes 811016 | tf_op jit(solution)/shard_map/ppermute | solution.py:708
  13.5 23.2 %collective-permute-start.10 = (bf16[64,4096]{1,0:T(8,128)(2,1)S(1)}, bf16[64,4096]{1,0:T(8,128)(2,1)S(1)}, u32[]{:S(2)}, u32[]{:S(2)}) collective-permute-start(bf16[64,4096]{1,0:T(8,128)(2,1)S(1)} %pad_maximum_fusion.3.refs_23_), channel_id=1, source_target_pairs={{0,4},{1,3},{2,6},{3,1},{4,0},{5,7},{6,2},{7,5},{8,12},{9,11},{10,... | collective-permute-start | bytes 1572872 | tf_op jit(solution)/shard_map/ppermute | solution.py:708
  22.8 21.9 %collective-permute-start.8 = (bf16[64,4224]{1,0:T(8,128)(2,1)S(1)}, bf16[64,4224]{1,0:T(8,128)(2,1)S(1)}, u32[]{:S(2)}, u32[]{:S(2)}) collective-permute-start(bf16[64,4224]{1,0:T(8,128)(2,1)S(1)} %pad_maximum_fusion.2.refs_6_), channel_id=1, source_target_pairs={{0,8},{1,9},{2,10},{3,11},{4,12},{5,13},{6,14},{7,15},{8,16},{9,17... | collective-permute-start | bytes 1622024 | tf_op jit(solution)/shard_map/ppermute | solution.py:708
  33.9 25.3 %collective-permute-start.19 = (bf16[128,4096]{1,0:T(8,128)(2,1)S(1)}, bf16[128,4096]{1,0:T(8,128)(2,1)S(1)}, u32[]{:S(2)}, u32[]{:S(2)}) collective-permute-start(bf16[128,4096]{1,0:T(8,128)(2,1)S(1)} %pad_maximum_fusion.refs_39_), channel_id=1, source_target_pairs={{0,2},{1,5},{2,0},{3,7},{4,6},{5,1},{6,4},{7,3},{8,10},{9,13},{10,... | collective-permute-start | bytes 3145736 | tf_op jit(solution)/shard_map/ppermute | solution.py:708
  36.7 19.3 %collective-permute-start.6 = (bf16[64,4096]{1,0:T(8,128)(2,1)S(1)}, bf16[64,4096]{1,0:T(8,128)(2,1)}, u32[]{:S(2)}, u32[]{:S(2)}) collective-permute-start(bf16[64,4096]{1,0:T(8,128)(2,1)S(1)} %pad_maximum_fusion.3.refs_23_), channel_id=1, source_target_pairs={{0,8},{1,9},{2,10},{3,11},{4,12},{5,13},{6,14},{7,15},{8,16},{9,17... | collective-permute-start | bytes 1572872 | tf_op jit(solution)/shard_map/ppermute | solution.py:708
  45.5 20.1 %collective-permute-start.14 = (bf16[64,4224]{1,0:T(8,128)(2,1)S(1)}, bf16[64,4224]{1,0:T(8,128)(2,1)}, u32[]{:S(2)}, u32[]{:S(2)}) collective-permute-start(bf16[64,4224]{1,0:T(8,128)(2,1)S(1)} %collective-permute-done.8.refs_10_), channel_id=1, source_target_pairs={{0,8},{1,9},{2,10},{3,11},{4,12},{5,13},{6,14},{7,15},{8,16},{9,17... | collective-permute-start | bytes 1622024 | tf_op jit(solution)/shard_map/ppermute | solution.py:708
  48.5 18.2 %collective-permute-start.1 = (bf16[64,4224]{1,0:T(8,128)(2,1)S(1)}, bf16[64,4224]{1,0:T(8,128)(2,1)S(1)}, u32[]{:S(2)}, u32[]{:S(2)}) collective-permute-start(bf16[64,4224]{1,0:T(8,128)(2,1)S(1)} %pad_maximum_fusion.2.refs_6_), channel_id=1, source_target_pairs={{0,1},{1,0},{2,3},{3,2},{4,5},{5,4},{6,7},{7,6},{8,9},{9,8},{10,11... | collective-permute-start | bytes 1622024 | tf_op jit(solution)/shard_map/ppermute | solution.py:708
  59.3 16.9 %collective-permute-start.12 = (bf16[64,4096]{1,0:T(8,128)(2,1)}, bf16[64,4096]{1,0:T(8,128)(2,1)}, u32[]{:S(2)}, u32[]{:S(2)}) collective-permute-start(bf16[64,4096]{1,0:T(8,128)(2,1)} %collective-permute-done.6.refs_27_), channel_id=1, source_target_pairs={{0,8},{1,9},{2,10},{3,11},{4,12},{5,13},{6,14},{7,15},{8,16},{9,17... | collective-permute-start | bytes 1572872 | tf_op jit(solution)/shard_map/ppermute | solution.py:708
  65.6 23.9 %collective-permute-start.20 = (bf16[128,4096]{1,0:T(8,128)(2,1)S(1)}, bf16[128,4096]{1,0:T(8,128)(2,1)}, u32[]{:S(2)}, u32[]{:S(2)}) collective-permute-start(bf16[128,4096]{1,0:T(8,128)(2,1)S(1)} %collective-permute-done.19.refs_41_), channel_id=1, source_target_pairs={{0,4},{1,3},{2,6},{3,1},{4,0},{5,7},{6,2},{7,5},{8,12},{9,11},{10,... | collective-permute-start | bytes 3145736 | tf_op jit(solution)/shard_map/ppermute | solution.py:708
  66.8 21.0 %collective-permute-start.18 = (bf16[64,4224]{1,0:T(8,128)(2,1)}, bf16[64,4224]{1,0:T(8,128)(2,1)}, u32[]{:S(2)}, u32[]{:S(2)}) collective-permute-start(bf16[64,4224]{1,0:T(8,128)(2,1)} %collective-permute-done.14.refs_14_), channel_id=1, source_target_pairs={{0,8},{1,9},{2,10},{3,11},{4,12},{5,13},{6,14},{7,15},{8,16},{9,17... | collective-permute-start | bytes 1622024 | tf_op jit(solution)/shard_map/ppermute | solution.py:708
  76.9 14.5 %collective-permute-start.15 = (bf16[64,4224]{1,0:T(8,128)(2,1)}, bf16[64,4224]{1,0:T(8,128)(2,1)}, u32[]{:S(2)}, u32[]{:S(2)}) collective-permute-start(bf16[64,4224]{1,0:T(8,128)(2,1)} %collective-permute-done.14.refs_14_), channel_id=1, source_target_pairs={{0,1},{1,0},{2,3},{3,2},{4,5},{5,4},{6,7},{7,6},{8,9},{9,8},{10,11... | collective-permute-start | bytes 1622024 | tf_op jit(solution)/shard_map/ppermute | solution.py:708
  78.4 13.6 %collective-permute-start.31 = (bf16[64,4096]{1,0:T(8,128)(2,1)}, bf16[64,4096]{1,0:T(8,128)(2,1)}, u32[]{:S(2)}, u32[]{:S(2)}) collective-permute-start(bf16[64,4096]{1,0:T(8,128)(2,1)} %collective-permute-done.12.refs_31_), channel_id=1, source_target_pairs={{0,1},{1,0},{2,3},{3,2},{4,5},{5,4},{6,7},{7,6},{8,9},{9,8},{10,11... | collective-permute-start | bytes 1572872 | tf_op jit(solution)/shard_map/ppermute | solution.py:708
  88.5 21.2 %collective-permute-start.39 = (bf16[128,4096]{1,0:T(8,128)(2,1)S(1)}, bf16[128,4096]{1,0:T(8,128)(2,1)}, u32[]{:S(2)}, u32[]{:S(2)}) collective-permute-start(bf16[128,4096]{1,0:T(8,128)(2,1)S(1)} %pad_maximum_fusion.refs_39_), channel_id=1, source_target_pairs={{0,4},{1,3},{2,6},{3,1},{4,0},{5,7},{6,2},{7,5},{8,12},{9,11},{10,... | collective-permute-start | bytes 3145736 | tf_op jit(solution)/shard_map/ppermute | solution.py:708
  91.4 20.9 %collective-permute-start.38 = (bf16[128,4096]{1,0:T(8,128)(2,1)S(1)}, bf16[128,4096]{1,0:T(8,128)(2,1)S(1)}, u32[]{:S(2)}, u32[]{:S(2)}) collective-permute-start(bf16[128,4096]{1,0:T(8,128)(2,1)S(1)} %collective-permute-done.19.refs_41_), channel_id=1, source_target_pairs={{0,1},{1,0},{2,3},{3,2},{4,5},{5,4},{6,7},{7,6},{8,9},{9,8},{10,11... | collective-permute-start | bytes 3145736 | tf_op jit(solution)/shard_map/ppermute | solution.py:708
  92.0 18.2 %collective-permute-start.24 = (bf16[64,4224]{1,0:T(8,128)(2,1)}, bf16[64,4224]{1,0:T(8,128)(2,1)}, u32[]{:S(2)}, u32[]{:S(2)}) collective-permute-start(bf16[64,4224]{1,0:T(8,128)(2,1)} %collective-permute-done.18.refs_18_), channel_id=1, source_target_pairs={{0,4},{1,3},{2,6},{3,1},{4,0},{5,7},{6,2},{7,5},{8,12},{9,11},{10,... | collective-permute-start | bytes 1622024 | tf_op jit(solution)/shard_map/ppermute | solution.py:708
  93.6 16.0 %collective-permute-start.21 = (bf16[64,4096]{1,0:T(8,128)(2,1)}, bf16[64,4096]{1,0:T(8,128)(2,1)S(1)}, u32[]{:S(2)}, u32[]{:S(2)}) collective-permute-start(bf16[64,4096]{1,0:T(8,128)(2,1)} %collective-permute-done.12.refs_31_), channel_id=1, source_target_pairs={{0,8},{1,9},{2,10},{3,11},{4,12},{5,13},{6,14},{7,15},{8,16},{9,17... | collective-permute-start | bytes 1572872 | tf_op jit(solution)/shard_map/ppermute | solution.py:708
  95.5 16.7 %collective-permute-start.37 = (bf16[128,4096]{1,0:T(8,128)(2,1)S(1)}, bf16[128,4096]{1,0:T(8,128)(2,1)S(1)}, u32[]{:S(2)}, u32[]{:S(2)}) collective-permute-start(bf16[128,4096]{1,0:T(8,128)(2,1)S(1)} %pad_maximum_fusion.refs_39_), channel_id=1, source_target_pairs={{0,1},{1,0},{2,3},{3,2},{4,5},{5,4},{6,7},{7,6},{8,9},{9,8},{10,11... | collective-permute-start | bytes 3145736 | tf_op jit(solution)/shard_map/ppermute | solution.py:708
  199.3 27.6 %collective-permute-start.44 = (bf16[512,4096]{1,0:T(8,128)(2,1)}, bf16[512,4096]{1,0:T(8,128)(2,1)}, u32[]{:S(2)}, u32[]{:S(2)}) collective-permute-start(bf16[512,4096]{1,0:T(8,128)(2,1)} %get-tuple-element.159), channel_id=1, source_target_pairs={{0,1},{1,0},{2,3},{3,2},{4,5},{5,4},{6,7},{7,6},{8,9},{9,8},{10,11... | collective-permute-start | bytes 12582920 | tf_op jit(solution)/shard_map/ppermute | solution.py:708
  201.6 23.6 %collective-permute-start.45 = (bf16[128,4096]{1,0:T(8,128)(2,1)S(1)}, bf16[128,4096]{1,0:T(8,128)(2,1)}, u32[]{:S(2)}, u32[]{:S(2)}) collective-permute-start(bf16[128,4096]{1,0:T(8,128)(2,1)S(1)} %add_convert_fusion.5), channel_id=1, source_target_pairs={{0,4},{1,3},{2,6},{3,1},{4,0},{5,7},{6,2},{7,5},{8,12},{9,11},{10,... | collective-permute-start | bytes 3145736 | tf_op jit(solution)/shard_map/ppermute | solution.py:708
  203.9 28.6 %collective-permute-start.47 = (bf16[128,4096]{1,0:T(8,128)(2,1)S(1)}, bf16[128,4096]{1,0:T(8,128)(2,1)S(1)}, u32[]{:S(2)}, u32[]{:S(2)}) collective-permute-start(bf16[128,4096]{1,0:T(8,128)(2,1)S(1)} %add_convert_fusion.4), channel_id=1, source_target_pairs={{0,4},{1,3},{2,6},{3,1},{4,0},{5,7},{6,2},{7,5},{8,12},{9,11},{10,... | collective-permute-start | bytes 3145736 | tf_op jit(solution)/shard_map/ppermute | solution.py:708
  225.0 20.9 %collective-permute-start.43 = (bf16[512,4224]{1,0:T(8,128)(2,1)}, bf16[512,4224]{1,0:T(8,128)(2,1)S(1)}, u32[]{:S(2)}, u32[]{:S(2)}) collective-permute-start(bf16[512,4224]{1,0:T(8,128)(2,1)} %get-tuple-element.177), channel_id=1, source_target_pairs={{0,1},{1,0},{2,3},{3,2},{4,5},{5,4},{6,7},{7,6},{8,9},{9,8},{10,11... | collective-permute-start | bytes 12976136 | tf_op jit(solution)/shard_map/ppermute | solution.py:708
  226.8 16.2 %collective-permute-start.48 = (bf16[64,4096]{1,0:T(8,128)(2,1)S(1)}, bf16[64,4096]{1,0:T(8,128)(2,1)S(1)}, u32[]{:S(2)}, u32[]{:S(2)}) collective-permute-start(bf16[64,4096]{1,0:T(8,128)(2,1)S(1)} %add_convert_fusion.11), channel_id=1, source_target_pairs={{0,8},{1,9},{2,10},{3,11},{4,12},{5,13},{6,14},{7,15},{8,16},{9,17... | collective-permute-start | bytes 1572872 | tf_op jit(solution)/shard_map/ppermute | solution.py:708
  228.9 15.8 %collective-permute-start.46 = (bf16[128,4096]{1,0:T(8,128)(2,1)S(1)}, bf16[128,4096]{1,0:T(8,128)(2,1)S(1)}, u32[]{:S(2)}, u32[]{:S(2)}) collective-permute-start(bf16[128,4096]{1,0:T(8,128)(2,1)S(1)} %add_convert_fusion.3), channel_id=1, source_target_pairs={{0,4},{1,3},{2,6},{3,1},{4,0},{5,7},{6,2},{7,5},{8,12},{9,11},{10,... | collective-permute-start | bytes 3145736 | tf_op jit(solution)/shard_map/ppermute | solution.py:708
  230.9 24.1 %collective-permute-start.52 = (bf16[128,4096]{1,0:T(8,128)(2,1)S(1)}, bf16[128,4096]{1,0:T(8,128)(2,1)S(1)}, u32[]{:S(2)}, u32[]{:S(2)}) collective-permute-start(bf16[128,4096]{1,0:T(8,128)(2,1)S(1)} %add_convert_fusion.2), channel_id=1, source_target_pairs={{0,4},{1,3},{2,6},{3,1},{4,0},{5,7},{6,2},{7,5},{8,12},{9,11},{10,... | collective-permute-start | bytes 3145736 | tf_op jit(solution)/shard_map/ppermute | solution.py:708
  244.6 16.7 %collective-permute-start.51 = (bf16[64,4096]{1,0:T(8,128)(2,1)S(1)}, bf16[64,4096]{1,0:T(8,128)(2,1)S(1)}, u32[]{:S(2)}, u32[]{:S(2)}) collective-permute-start(bf16[64,4096]{1,0:T(8,128)(2,1)S(1)} %add_convert_fusion.10), channel_id=1, source_target_pairs={{0,8},{1,9},{2,10},{3,11},{4,12},{5,13},{6,14},{7,15},{8,16},{9,17... | collective-permute-start | bytes 1572872 | tf_op jit(solution)/shard_map/ppermute | solution.py:708
  246.5 31.7 %collective-permute-start.49 = (bf16[256,4224]{1,0:T(8,128)(2,1)S(1)}, bf16[256,4224]{1,0:T(8,128)(2,1)S(1)}, u32[]{:S(2)}, u32[]{:S(2)}) collective-permute-start(bf16[256,4224]{1,0:T(8,128)(2,1)S(1)} %add_convert_fusion), channel_id=1, source_target_pairs={{0,4},{1,3},{2,6},{3,1},{4,0},{5,7},{6,2},{7,5},{8,12},{9,11},{10,... | collective-permute-start | bytes 6488072 | tf_op jit(solution)/shard_map/ppermute | solution.py:708
  247.0 25.5 %collective-permute-start.50 = (bf16[64,4096]{1,0:T(8,128)(2,1)S(1)}, bf16[64,4096]{1,0:T(8,128)(2,1)S(1)}, u32[]{:S(2)}, u32[]{:S(2)}) collective-permute-start(bf16[64,4096]{1,0:T(8,128)(2,1)S(1)} %add_convert_fusion.9), channel_id=1, source_target_pairs={{0,8},{1,9},{2,10},{3,11},{4,12},{5,13},{6,14},{7,15},{8,16},{9,17... | collective-permute-start | bytes 1572872 | tf_op jit(solution)/shard_map/ppermute | solution.py:708
  262.8 19.7 %collective-permute-start.54 = (bf16[64,4096]{1,0:T(8,128)(2,1)S(1)}, bf16[64,4096]{1,0:T(8,128)(2,1)S(1)}, u32[]{:S(2)}, u32[]{:S(2)}) collective-permute-start(bf16[64,4096]{1,0:T(8,128)(2,1)S(1)} %add_convert_fusion.8), channel_id=1, source_target_pairs={{0,8},{1,9},{2,10},{3,11},{4,12},{5,13},{6,14},{7,15},{8,16},{9,17... | collective-permute-start | bytes 1572872 | tf_op jit(solution)/shard_map/ppermute | solution.py:708
  278.6 15.2 %collective-permute-start.53 = (bf16[128,4224]{1,0:T(8,128)(2,1)S(1)}, bf16[128,4224]{1,0:T(8,128)(2,1)S(1)}, u32[]{:S(2)}, u32[]{:S(2)}) collective-permute-start(bf16[128,4224]{1,0:T(8,128)(2,1)S(1)} %add_convert_fusion.1), channel_id=1, source_target_pairs={{0,2},{1,5},{2,0},{3,7},{4,6},{5,1},{6,4},{7,3},{8,10},{9,13},{10,... | collective-permute-start | bytes 3244040 | tf_op jit(solution)/shard_map/ppermute | solution.py:708
  279.1 15.1 %collective-permute-start.57 = (bf16[64,4096]{1,0:T(8,128)(2,1)S(1)}, bf16[64,4096]{1,0:T(8,128)(2,1)S(1)}, u32[]{:S(2)}, u32[]{:S(2)}) collective-permute-start(bf16[64,4096]{1,0:T(8,128)(2,1)S(1)} %add_convert_fusion.7), channel_id=1, source_target_pairs={{0,8},{1,9},{2,10},{3,11},{4,12},{5,13},{6,14},{7,15},{8,16},{9,17... | collective-permute-start | bytes 1572872 | tf_op jit(solution)/shard_map/ppermute | solution.py:708
  295.4 21.1 %collective-permute-start.59 = (bf16[64,4096]{1,0:T(8,128)(2,1)S(1)}, bf16[64,4096]{1,0:T(8,128)(2,1)S(1)}, u32[]{:S(2)}, u32[]{:S(2)}) collective-permute-start(bf16[64,4096]{1,0:T(8,128)(2,1)S(1)} %add_convert_fusion.6), channel_id=1, source_target_pairs={{0,8},{1,9},{2,10},{3,11},{4,12},{5,13},{6,14},{7,15},{8,16},{9,17... | collective-permute-start | bytes 1572872 | tf_op jit(solution)/shard_map/ppermute | solution.py:708
  305.4 14.6 %collective-permute-start.58 = (bf16[32,4224]{1,0:T(8,128)(2,1)S(1)}, bf16[32,4224]{1,0:T(8,128)(2,1)S(1)}, u32[]{:S(2)}, u32[]{:S(2)}) collective-permute-start(bf16[32,4224]{1,0:T(8,128)(2,1)S(1)} %add_convert_fusion.13), channel_id=1, source_target_pairs={{0,8},{1,9},{2,10},{3,11},{4,12},{5,13},{6,14},{7,15},{8,16},{9,17... | collective-permute-start | bytes 811016 | tf_op jit(solution)/shard_map/ppermute | solution.py:708
  (68 other events, 771.1 us)
